TPU v7x, 32 devices: a whole 2x2x4 slice. The times are simulated.
32 devices in a mesh: dp: 16 (over z, x, core), tensor: 2 (over y).
Axes of the slice: x: 2, y: 2, z: 4, core: 2. Of those that a mesh axis runs over, the one named last changes fastest.
Arguments:
- tokens: bfloat16 [4096, 512], P(('dp', 'tensor')), may hold values from -7 to 7, as said below
- norm_gains: float32 [5, 512], replicated, may hold values from 0.25 to 1.75
- first_in: bfloat16 [512, 2048], P('dp', 'tensor'), may hold values from -0.25 to 0.25
- first_out: bfloat16 [512, 2048], P('dp', 'tensor'), may hold values from -0.125 to 0.125
- attention_in: bfloat16 [4, 512, 512], P(None, 'dp', 'tensor'), may hold values from -0.25 to 0.25
- attention_out: bfloat16 [512, 512], P('dp', 'tensor'), may hold values from -1 to 1
- head_biases: float32 [2, 512], P(None, 'tensor'), may hold values from -3 to 3
- gated_in: bfloat16 [2, 512, 512], P(None, 'dp', 'tensor'), may hold values from -0.25 to 0.25
- pointwise_out: bfloat16 [512, 512], P('dp', 'tensor'), may hold values from -0.25 to 0.25
- depth_kernel: float32 [31, 512], P(None, 'tensor'), may hold values from -1 to 1
- batch_scale: float32 [512], P('tensor'), may hold values from 0.25 to 1.75
- batch_shift: float32 [512], P('tensor'), may hold values from -3 to 3
- second_in: bfloat16 [512, 2048], P('dp', 'tensor'), may hold values from -0.25 to 0.25
- second_out: bfloat16 [512, 2048], P('dp', 'tensor'), may hold values from -0.125 to 0.125
- cotangent: bfloat16 [4096, 512], P(('dp', 'tensor')), may hold values from -6 to 6
Outputs:
- block_out: bfloat16 [4096, 512], P(('dp', 'tensor'))
- grad_tokens: float32 [4096, 512], P(('dp', 'tensor'))
- grad_gains: float32 [5, 512], replicated
- grad_first_in: float32 [512, 2048], P('dp', 'tensor')
- grad_first_out: float32 [512, 2048], P('dp', 'tensor')
- grad_attention_in: float32 [4, 512, 512], P(None, 'dp', 'tensor')
- grad_attention_out: float32 [512, 512], P('dp', 'tensor')
- grad_head_biases: float32 [2, 512], P(None, 'tensor')
- grad_gated_in: float32 [2, 512, 512], P(None, 'dp', 'tensor')
- grad_pointwise_out: float32 [512, 512], P('dp', 'tensor')
- grad_kernel: float32 [31, 512], P(None, 'tensor')
- grad_batch_scale: float32 [512], P('tensor')
- grad_batch_shift: float32 [512], P('tensor')
- grad_second_in: float32 [512, 2048], P('dp', 'tensor')
- grad_second_out: float32 [512, 2048], P('dp', 'tensor')
Inputs may be any that keep to these rules, and one draw needn't show every extreme that they name: `tokens`: the block's input.
All inputs are finite; a program needn't handle non-finite values.
Results may differ from a plain program's by a relative error of at most 0.029.
Values may be sent and summed in bfloat16 or wider, within the bound.
No kernel may reach another device: no remote copies, remote signals or barrier semaphores. Data moves between devices by JAX's collectives and lax.ppermute only.
A program may use at most 128 MiB of HBM per device.

v0:
```python
import math

import jax
import jax.numpy as jnp
from jax import lax
from jax.sharding import PartitionSpec as P

HEAD_TOTAL = 8


EPSILON = 1e-05
FULL_PRECISION = lax.Precision.HIGHEST


def matmul(left_side, right_side):
    return jnp.dot(left_side, right_side, preferred_element_type=jnp.float32)


def right_transposed(left_side, right_side):
    return lax.dot_general(
        left_side, right_side, (((1,), (1,)), ((), ())), preferred_element_type=jnp.float32
    )


def left_transposed(left_side, right_side):
    return lax.dot_general(
        left_side, right_side, (((0,), (0,)), ((), ())), preferred_element_type=jnp.float32
    )


def swish_slope(pre_value, gate_sigma):
    return gate_sigma * (1.0 + pre_value * (1.0 - gate_sigma))


def norm_rows(residual, norm_gain):
    centred = residual - jnp.mean(residual, -1, keepdims=True)
    factor = lax.rsqrt(jnp.mean(centred * centred, -1, keepdims=True) + EPSILON)
    normed = centred * factor
    return (normed * norm_gain, normed, factor)


def norm_back(gradient, normed, factor, norm_gain):
    scaled = gradient * norm_gain
    inner_sum = (
        scaled
        - jnp.mean(scaled, -1, keepdims=True)
        - normed * jnp.mean(scaled * normed, -1, keepdims=True)
    )
    return (factor * inner_sum, jnp.sum(gradient * normed, 0))


def sinusoid(length, features):
    offsets = jnp.arange(2 * length - 1, dtype=jnp.float32) - (length - 1)
    half_width = features // 2
    frequency = jnp.exp(
        jnp.arange(half_width, dtype=jnp.float32) * (-math.log(10000.0) / half_width)
    )
    angles = offsets[:, None] * frequency[None, :]
    return jnp.concatenate([jnp.sin(angles), jnp.cos(angles)], 1)


def shift_relative(unscaled_scores):
    head_count = unscaled_scores.shape[0]
    length = unscaled_scores.shape[1]
    wide = unscaled_scores.shape[2]
    flattened = unscaled_scores.reshape(head_count, length * wide)[
        :, length - 1 : length - 1 + length * (wide - 1)
    ]
    return flattened.reshape(head_count, length, wide - 1)[:, :, :length]


def unshift_relative(grad_scores, wide):
    head_count = grad_scores.shape[0]
    length = grad_scores.shape[1]
    widened = jnp.pad(grad_scores, ((0, 0), (0, 0), (0, wide - 1 - length)))
    flattened = widened.reshape(head_count, length * (wide - 1))
    flattened = jnp.pad(flattened, ((0, 0), (length - 1, 1)))
    return flattened.reshape(head_count, length, wide)


def split_heads(matrix, head_count):
    return matrix.reshape(matrix.shape[0], head_count, matrix.shape[1] // head_count)


def tap_windows(padded, kernel_width, length):
    return jnp.stack([padded[tap_index : tap_index + length] for tap_index in range(kernel_width)])


def depthwise(padded, depth_kernel, length):
    windows = tap_windows(padded, depth_kernel.shape[0], length)
    return jnp.einsum(
        "klc,kc->lc",
        windows,
        depth_kernel,
        precision=FULL_PRECISION,
        preferred_element_type=jnp.float32,
    )


def gather_weights(stacked, single):
    return (
        lax.all_gather(stacked, "dp", axis=1, tiled=True),
        lax.all_gather(single, "dp", axis=0, tiled=True),
    )


def regather_weights(stacked, single):
    return (
        lax.all_gather(stacked, "dp", axis=1, tiled=True),
        lax.all_gather(single, "dp", axis=0, tiled=True),
    )


def gather_rows(entries):
    return lax.all_gather(entries, "tensor", axis=0, tiled=True)


def scatter_rows(partial_value):
    return lax.psum_scatter(
        partial_value.astype(jnp.bfloat16), "tensor", scatter_dimension=0, tiled=True
    ).astype(jnp.float32)


def gather_grads(gradient):
    return lax.all_gather(gradient, "tensor", axis=0, tiled=True)


def scatter_grads(partial_value):
    return lax.psum_scatter(
        partial_value.astype(jnp.bfloat16), "tensor", scatter_dimension=0, tiled=True
    ).astype(jnp.float32)


def reduce_weights(stacked, single):
    return (stacked, single)


def feed_forward(residual, norm_gain, weights):
    weight_in = weights[0][0]
    weight_out = weights[1]
    gained, normed, factor = norm_rows(residual, norm_gain)
    gathered = gather_rows(gained.astype(jnp.bfloat16))
    hidden_pre = matmul(gathered, weight_in)
    gate_sigma = jax.nn.sigmoid(hidden_pre)
    hidden = (hidden_pre * gate_sigma).astype(jnp.bfloat16)
    branch = scatter_rows(right_transposed(hidden, weight_out))
    return (residual + 0.5 * branch, (normed, factor, gathered, hidden_pre, gate_sigma, hidden))


def feed_back(grad_residual, norm_gain, weights, stored):
    weight_in = weights[0][0]
    weight_out = weights[1]
    normed, factor, gathered, hidden_pre, gate_sigma, hidden = stored
    grad_branch = gather_grads((0.5 * grad_residual).astype(jnp.bfloat16))
    grad_hidden = matmul(grad_branch, weight_out)
    grad_pre = (grad_hidden * swish_slope(hidden_pre, gate_sigma)).astype(jnp.bfloat16)
    grad_out = left_transposed(grad_branch, hidden)
    grad_in = left_transposed(gathered, grad_pre)
    grad_entries = scatter_grads(right_transposed(grad_pre, weight_in))
    grad_norm, grad_gain = norm_back(grad_entries, normed, factor, norm_gain)
    return (grad_residual + grad_norm, grad_gain, reduce_weights(grad_in[None], grad_out))


def score_block(query_content, query_position, key_rows, position_rows, head_count):
    score_scale = (query_content.shape[1] // head_count) ** (-0.5)
    content = jnp.einsum(
        "ihd,jhd->hij",
        split_heads(query_content, head_count),
        split_heads(key_rows, head_count),
        preferred_element_type=jnp.float32,
    )
    unscaled_scores = jnp.einsum(
        "tox,box->otb",
        split_heads(query_position, head_count),
        split_heads(position_rows, head_count),
        preferred_element_type=jnp.float32,
    )
    return (content + shift_relative(unscaled_scores)) * score_scale


def attention_forward(residual, norm_gain, weights, head_biases, position_table, head_count):
    projections = weights[0]
    weight_out = weights[1]
    gained, normed, factor = norm_rows(residual, norm_gain)
    gathered = gather_rows(gained.astype(jnp.bfloat16))
    queries = matmul(gathered, projections[0])
    key_rows = matmul(gathered, projections[1]).astype(jnp.bfloat16)
    value_rows = matmul(gathered, projections[2]).astype(jnp.bfloat16)
    query_content = (queries + head_biases[0]).astype(jnp.bfloat16)
    query_position = (queries + head_biases[1]).astype(jnp.bfloat16)
    position_rows = matmul(position_table, projections[3]).astype(jnp.bfloat16)
    scores = score_block(query_content, query_position, key_rows, position_rows, head_count)
    row_top = jnp.max(scores, -1, keepdims=True)
    lifted = jnp.exp(scores - row_top)
    row_total = jnp.sum(lifted, -1, keepdims=True)
    probability = lifted / row_total
    log_total = row_top + jnp.log(row_total)
    mixture = jnp.einsum(
        "hij,jhd->ihd",
        probability.astype(jnp.bfloat16),
        split_heads(value_rows, head_count),
        preferred_element_type=jnp.float32,
    )
    attended = mixture.reshape(mixture.shape[0], -1).astype(jnp.bfloat16)
    branch = scatter_rows(right_transposed(attended, weight_out))
    return (
        residual + branch,
        (
            normed,
            factor,
            gathered,
            query_content,
            query_position,
            key_rows,
            value_rows,
            position_rows,
            log_total,
            attended,
        ),
    )


def attention_back(grad_residual, norm_gain, weights, position_table, head_count, stored):
    projections = weights[0]
    weight_out = weights[1]
    (
        normed,
        factor,
        gathered,
        query_content,
        query_position,
        key_rows,
        value_rows,
        position_rows,
        log_total,
        attended,
    ) = stored
    grad_branch = gather_grads(grad_residual.astype(jnp.bfloat16))
    grad_out = left_transposed(grad_branch, attended)
    grad_attended = matmul(grad_branch, weight_out).astype(jnp.bfloat16)
    scores = score_block(query_content, query_position, key_rows, position_rows, head_count)
    probability = jnp.exp(scores - log_total)
    grad_heads = split_heads(grad_attended, head_count)
    grad_probability = jnp.einsum(
        "ihd,jhd->hij",
        grad_heads,
        split_heads(value_rows, head_count),
        preferred_element_type=jnp.float32,
    )
    grad_values = jnp.einsum(
        "hij,ihd->jhd",
        probability.astype(jnp.bfloat16),
        grad_heads,
        preferred_element_type=jnp.float32,
    )
    inner_sum = jnp.sum(probability * grad_probability, -1, keepdims=True)
    score_scale = (query_content.shape[1] // head_count) ** (-0.5)
    grad_scores = (probability * (grad_probability - inner_sum)).astype(jnp.bfloat16) * score_scale
    grad_content_q = jnp.einsum(
        "hij,jhd->ihd",
        grad_scores,
        split_heads(key_rows, head_count),
        preferred_element_type=jnp.float32,
    )
    grad_keys = jnp.einsum(
        "hij,ihd->jhd",
        grad_scores,
        split_heads(query_content, head_count),
        preferred_element_type=jnp.float32,
    )
    grad_raw = unshift_relative(grad_scores, position_rows.shape[0])
    grad_position_q = jnp.einsum(
        "wul,lwp->uwp",
        grad_raw,
        split_heads(position_rows, head_count),
        preferred_element_type=jnp.float32,
    )
    grad_positions = jnp.einsum(
        "lxz,xln->zln",
        grad_raw,
        split_heads(query_position, head_count),
        preferred_element_type=jnp.float32,
    )
    row_count = gathered.shape[0]
    grad_queries = (grad_content_q + grad_position_q).reshape(row_count, -1).astype(jnp.bfloat16)
    grad_keys = grad_keys.reshape(row_count, -1).astype(jnp.bfloat16)
    grad_values = grad_values.reshape(row_count, -1).astype(jnp.bfloat16)
    grad_positions = grad_positions.reshape(position_rows.shape[0], -1).astype(jnp.bfloat16)
    grad_biases = jnp.stack(
        [jnp.sum(grad_content_q, 0).reshape(-1), jnp.sum(grad_position_q, 0).reshape(-1)]
    )
    grad_projections = jnp.stack(
        [
            left_transposed(gathered, grad_queries),
            left_transposed(gathered, grad_keys),
            left_transposed(gathered, grad_values),
            left_transposed(position_table, grad_positions),
        ]
    )
    grad_entries = scatter_grads(
        right_transposed(grad_queries, projections[0])
        + right_transposed(grad_keys, projections[1])
        + right_transposed(grad_values, projections[2])
    )
    grad_norm, grad_gain = norm_back(grad_entries, normed, factor, norm_gain)
    return (
        grad_residual + grad_norm,
        grad_gain,
        grad_biases,
        reduce_weights(grad_projections, grad_out),
    )


def conv_forward(residual, norm_gain, weights, depth_kernel, batch_scale, batch_shift, token_count):
    gated_weights = weights[0]
    weight_out = weights[1]
    gained, normed, factor = norm_rows(residual, norm_gain)
    gathered = gather_rows(gained.astype(jnp.bfloat16))
    value_pre = matmul(gathered, gated_weights[0])
    gate_sigma = jax.nn.sigmoid(matmul(gathered, gated_weights[1]))
    glued = value_pre * gate_sigma
    half_width = (depth_kernel.shape[0] - 1) // 2
    padded = jnp.pad(glued, ((half_width, half_width), (0, 0)))
    length = gathered.shape[0]
    convolved = depthwise(padded, depth_kernel, length)
    column_sum, square_sum = lax.psum(
        (jnp.sum(convolved, 0), jnp.sum(convolved * convolved, 0)), "dp"
    )
    column_mean = column_sum / token_count
    inverse_deviation = lax.rsqrt(square_sum / token_count - column_mean * column_mean + EPSILON)
    standard = (convolved - column_mean) * inverse_deviation
    shifted = standard * batch_scale + batch_shift
    shift_sigma = jax.nn.sigmoid(shifted)
    activated = (shifted * shift_sigma).astype(jnp.bfloat16)
    branch = scatter_rows(right_transposed(activated, weight_out))
    return (
        residual + branch,
        (
            normed,
            factor,
            gathered,
            value_pre,
            gate_sigma,
            padded,
            standard,
            inverse_deviation,
            shifted,
            shift_sigma,
            activated,
        ),
    )


def conv_back(grad_residual, norm_gain, weights, depth_kernel, batch_scale, token_count, stored):
    gated_weights = weights[0]
    weight_out = weights[1]
    (
        normed,
        factor,
        gathered,
        value_pre,
        gate_sigma,
        padded,
        standard,
        inverse_deviation,
        shifted,
        shift_sigma,
        activated,
    ) = stored
    grad_branch = gather_grads(grad_residual.astype(jnp.bfloat16))
    grad_out = left_transposed(grad_branch, activated)
    grad_shifted = matmul(grad_branch, weight_out) * swish_slope(shifted, shift_sigma)
    shift_grad, scale_grad = lax.psum(
        (jnp.sum(grad_shifted, 0), jnp.sum(grad_shifted * standard, 0)), "dp"
    )
    grad_convolved = (
        inverse_deviation
        * batch_scale
        * (grad_shifted - shift_grad / token_count - standard * scale_grad / token_count)
    )
    kernel_width = depth_kernel.shape[0]
    half_width = (kernel_width - 1) // 2
    length = gathered.shape[0]
    padded_grad = jnp.pad(grad_convolved, ((half_width, half_width), (0, 0)))
    grad_glued = depthwise(padded_grad, depth_kernel[::-1], length)
    kernel_grad = jnp.einsum(
        "klc,lc->kc",
        tap_windows(padded, kernel_width, length),
        grad_convolved,
        precision=FULL_PRECISION,
        preferred_element_type=jnp.float32,
    )
    grad_value = (grad_glued * gate_sigma).astype(jnp.bfloat16)
    grad_gate = (grad_glued * value_pre * gate_sigma * (1.0 - gate_sigma)).astype(jnp.bfloat16)
    grad_gated = jnp.stack(
        [left_transposed(gathered, grad_value), left_transposed(gathered, grad_gate)]
    )
    grad_entries = scatter_grads(
        right_transposed(grad_value, gated_weights[0])
        + right_transposed(grad_gate, gated_weights[1])
    )
    grad_norm, grad_gain = norm_back(grad_entries, normed, factor, norm_gain)
    return (
        grad_residual + grad_norm,
        grad_gain,
        kernel_grad,
        shift_grad,
        scale_grad,
        reduce_weights(grad_gated, grad_out),
    )


def body(
    tokens,
    norm_gains,
    first_in,
    first_out,
    attention_in,
    attention_out,
    head_biases,
    gated_in,
    pointwise_out,
    depth_kernel,
    batch_scale,
    batch_shift,
    second_in,
    second_out,
    cotangent,
):
    local_heads = HEAD_TOTAL // lax.axis_size("tensor")
    length = tokens.shape[0] * lax.axis_size("tensor")
    token_count = float(length * lax.axis_size("dp"))
    position_table = sinusoid(length, tokens.shape[1]).astype(jnp.bfloat16)
    start_rows = tokens.astype(jnp.float32)
    first_weights = gather_weights(first_in[None], first_out)
    after_first, kept_first = feed_forward(start_rows, norm_gains[0], first_weights)
    attention_weights = gather_weights(attention_in, attention_out)
    after_attention, kept_attention = attention_forward(
        after_first, norm_gains[1], attention_weights, head_biases, position_table, local_heads
    )
    gated_weights = gather_weights(gated_in, pointwise_out)
    after_conv, kept_conv = conv_forward(
        after_attention,
        norm_gains[2],
        gated_weights,
        depth_kernel,
        batch_scale,
        batch_shift,
        token_count,
    )
    second_weights = gather_weights(second_in[None], second_out)
    after_second, kept_second = feed_forward(after_conv, norm_gains[3], second_weights)
    final_rows, normed_last, factor_last = norm_rows(after_second, norm_gains[4])
    block_out = final_rows.astype(jnp.bfloat16)
    grad_fourth, gain_last = norm_back(
        cotangent.astype(jnp.float32), normed_last, factor_last, norm_gains[4]
    )
    second_weights = regather_weights(second_in[None], second_out)
    grad_third, gain_fourth, second_grads = feed_back(
        grad_fourth, norm_gains[3], second_weights, kept_second
    )
    gated_weights = regather_weights(gated_in, pointwise_out)
    grad_second, gain_third, kernel_grad, shift_grad, scale_grad, gated_grads = conv_back(
        grad_third, norm_gains[2], gated_weights, depth_kernel, batch_scale, token_count, kept_conv
    )
    attention_weights = regather_weights(attention_in, attention_out)
    grad_first, gain_second, bias_grad, attention_grads = attention_back(
        grad_second, norm_gains[1], attention_weights, position_table, local_heads, kept_attention
    )
    first_weights = regather_weights(first_in[None], first_out)
    grad_start, gain_first, first_grads = feed_back(
        grad_first, norm_gains[0], first_weights, kept_first
    )
    kernel_total, bias_total = lax.psum((kernel_grad, bias_grad), "dp")
    gain_total = lax.psum(
        jnp.stack([gain_first, gain_second, gain_third, gain_fourth, gain_last]), ("dp", "tensor")
    )
    reduced = (
        lax.psum_scatter(first_grads[0], "dp", scatter_dimension=1, tiled=True),
        lax.psum_scatter(first_grads[1], "dp", scatter_dimension=0, tiled=True),
        lax.psum_scatter(attention_grads[0], "dp", scatter_dimension=1, tiled=True),
        lax.psum_scatter(attention_grads[1], "dp", scatter_dimension=0, tiled=True),
        lax.psum_scatter(gated_grads[0], "dp", scatter_dimension=1, tiled=True),
        lax.psum_scatter(gated_grads[1], "dp", scatter_dimension=0, tiled=True),
        lax.psum_scatter(second_grads[0], "dp", scatter_dimension=1, tiled=True),
        lax.psum_scatter(second_grads[1], "dp", scatter_dimension=0, tiled=True),
    )
    first_grads = (reduced[0], reduced[1])
    attention_grads = (reduced[2], reduced[3])
    gated_grads = (reduced[4], reduced[5])
    second_grads = (reduced[6], reduced[7])
    return (
        block_out,
        grad_start,
        gain_total,
        first_grads[0][0],
        first_grads[1],
        attention_grads[0],
        attention_grads[1],
        bias_total,
        gated_grads[0],
        gated_grads[1],
        kernel_total,
        scale_grad,
        shift_grad,
        second_grads[0][0],
        second_grads[1],
    )


def solution(mesh):
    placed = (
        P(("dp", "tensor"), None),
        P(),
        P("dp", "tensor"),
        P("dp", "tensor"),
        P(None, "dp", "tensor"),
        P("dp", "tensor"),
        P(None, "tensor"),
        P(None, "dp", "tensor"),
        P("dp", "tensor"),
        P(None, "tensor"),
        P("tensor"),
        P("tensor"),
        P("dp", "tensor"),
        P("dp", "tensor"),
        P(("dp", "tensor"), None),
    )
    return jax.shard_map(
        body,
        mesh=mesh,
        in_specs=placed,
        out_specs=(
            P(("dp", "tensor"), None),
            P(("dp", "tensor"), None),
            P(),
            P("dp", "tensor"),
            P("dp", "tensor"),
            P(None, "dp", "tensor"),
            P("dp", "tensor"),
            P(None, "tensor"),
            P(None, "dp", "tensor"),
            P("dp", "tensor"),
            P(None, "tensor"),
            P("tensor"),
            P("tensor"),
            P("dp", "tensor"),
            P("dp", "tensor"),
        ),
        check_vma=False,
    )
```

profile of v0, /device:TPU:0, one launch (start us, length us, event | category | flops | bytes accessed | tf_op | source)
XLA Modules:
  0.0 1029.8 jit_solution(5988033297141111255)
XLA Ops:
  14.1 7.1 all_gather.56
  21.3 23.0 %all_gather.61 = bf16[512,256]{1,0:T(8,128)(2,1)S(1)} all-gather(bf16[32,256]{1,0:T(8,128)(2,1)} %param.20), channel_id=1, replica_groups=mesh['dp'=16,'tensor'=2] {'dp'}, dimensions={0}, use_global_device_ids=true | all-gather | bytes 278528 | tf_op jit(solution)/shard_map/all_gather | solution.py:103
  45.0 5.9 all-gather.14.cloned.1.call-done
  52.5 37.4 %all-gather.8.cloned.1.call-done = bf16[512,1024]{1,0:T(8,128)(2,1)} async-done(((bf16[32,1024]{1,0:T(8,128)(2,1)}), bf16[512,1024]{1,0:T(8,128)(2,1)}) %all-gather.8.cloned.1.call-update) | async-done | bytes 1048592 | tf_op jit(solution)/shard_map/all_gather | solution.py:103
  89.9 2.4 convolution_convert_fusion.7
  92.4 2.2 fusion.16
  94.7 34.3 %all-gather.10.cloned.1.call-done = bf16[4,512,256]{2,1,0:T(8,128)(2,1)} async-done(((bf16[4,32,256]{2,1,0:T(8,128)(2,1)}), bf16[4,512,256]{2,1,0:T(8,128)(2,1)}) %all-gather.10.cloned.1.call-update) | async-done | bytes 1048592 | tf_op jit(solution)/shard_map/all_gather | solution.py:102
  130.4 12.0 %reduce-scatter.17.cloned.1.call-done = bf16[128,512]{1,0:T(8,128)(2,1)} async-done(((bf16[256,512]{1,0:T(8,128)(2,1)}), bf16[128,512]{1,0:T(8,128)(2,1)}) %reduce-scatter.17.cloned.1.call-update) | async-done | bytes 131088 | tf_op jit(solution)/shard_map/reduce_scatter | solution.py:119
  145.5 5.9 all_gather.59
  153.8 3.7 reshape.216
  157.5 2.7 slice.349
  160.3 3.9 reshape.217
  170.2 22.1 %all_gather.64 = bf16[512,256]{1,0:T(8,128)(2,1)S(1)} all-gather(bf16[32,256]{1,0:T(8,128)(2,1)S(1)} %copy-done.52), channel_id=1, replica_groups=mesh['dp'=16,'tensor'=2] {'dp'}, dimensions={0}, use_global_device_ids=true | all-gather | bytes 278528 | tf_op jit(solution)/shard_map/all_gather | solution.py:103
  192.3 18.9 %all_gather.63 = bf16[2,512,256]{2,1,0:T(8,128)(2,1)S(1)} all-gather(bf16[2,32,256]{2,1,0:T(8,128)(2,1)S(1)} %copy-done.47), channel_id=1, replica_groups=mesh['dp'=16,'tensor'=2] {'dp'}, dimensions={1}, use_global_device_ids=true | all-gather | bytes 557056 | tf_op jit(solution)/shard_map/all_gather | solution.py:102
  212.7 6.6 all_gather.62
  221.5 3.1 copy-done
  225.6 30.3 %all-reduce.6 = (f32[256]{0:T(256)S(1)}, f32[256]{0:T(256)S(1)}) all-reduce(f32[256]{0:T(256)S(1)} %get-tuple-element.28, f32[256]{0:T(256)S(1)} %get-tuple-element.27), channel_id=1, replica_groups=mesh['dp'=16,'tensor'=2] {'dp'}, use_global_device_ids=true, to_apply=%region_13.14 | all-reduce | flops 512 | bytes 4096 | tf_op jit(solution)/shard_map/psum | solution.py:326
  259.1 6.6 reduce-scatter.21.cloned.1.call-done
  267.1 5.9 all_gather.65
  273.0 33.1 %all-gather.16.cloned.1.call-done = bf16[512,1024]{1,0:T(8,128)(2,1)} async-done(((bf16[32,1024]{1,0:T(8,128)(2,1)}), bf16[512,1024]{1,0:T(8,128)(2,1)}) %all-gather.16.cloned.1.call-update) | async-done | bytes 1048592 | tf_op jit(solution)/shard_map/all_gather | solution.py:102
  306.0 2.6 fusion.235
  308.7 36.6 %all-gather.12.cloned.1.call-done = bf16[512,1024]{1,0:T(8,128)(2,1)} async-done(((bf16[32,1024]{1,0:T(8,128)(2,1)}), bf16[512,1024]{1,0:T(8,128)(2,1)}) %all-gather.12.cloned.1.call-update) | async-done | bytes 1048592 | tf_op jit(solution)/shard_map/all_gather | solution.py:103
  345.3 2.7 convolution_convert_fusion.3
  348.1 10.7 %reduce-scatter.23.cloned.1.call-done = bf16[128,512]{1,0:T(8,128)(2,1)} async-done(((bf16[256,512]{1,0:T(8,128)(2,1)}), bf16[128,512]{1,0:T(8,128)(2,1)}) %reduce-scatter.23.cloned.1.call-update) | async-done | bytes 131088 | tf_op jit(solution)/shard_map/reduce_scatter | solution.py:119
  361.0 1.8 fusion.168
  364.0 5.9 all_gather.68
  370.6 2.1 fusion.5
  375.5 11.0 %reduce-scatter.25.cloned.1.call-done = bf16[128,512]{1,0:T(8,128)(2,1)} async-done(((bf16[256,512]{1,0:T(8,128)(2,1)}), bf16[128,512]{1,0:T(8,128)(2,1)}) %reduce-scatter.25.cloned.1.call-update) | async-done | bytes 131088 | tf_op jit(solution)/shard_map/reduce_scatter | solution.py:129
  386.6 1.7 fusion.173
  388.3 2.0 fusion.222
  390.3 5.9 all_gather.69
  397.6 32.3 %all-reduce.5 = (f32[256]{0:T(256)S(1)}, f32[256]{0:T(256)S(1)}) all-reduce(f32[256]{0:T(256)S(1)} %get-tuple-element.26, f32[256]{0:T(256)S(1)} %get-tuple-element.25), channel_id=1, replica_groups=mesh['dp'=16,'tensor'=2] {'dp'}, use_global_device_ids=true, to_apply=%region_28.29 | all-reduce | flops 512 | bytes 4096 | tf_op jit(solution)/shard_map/psum | solution.py:373
  434.5 8.0 reduce-scatter.27.cloned.1.call-done
  444.2 1.8 fusion.220
  446.0 6.1 all_gather.70
  454.4 2.3 fusion.236
  458.8 2.7 reshape.219
  461.5 2.9 pad.18
  464.4 3.0 reshape.220
  467.4 2.1 convolution_bitcast_fusion.9
  469.5 2.8 convolution_convert_fusion.9
  472.4 3.5 fusion.226
  478.6 1.9 fusion.9
  480.6 11.8 %reduce-scatter.29.cloned.1.call-done = bf16[128,512]{1,0:T(8,128)(2,1)} async-done(((bf16[256,512]{1,0:T(8,128)(2,1)}), bf16[128,512]{1,0:T(8,128)(2,1)}) %reduce-scatter.29.cloned.1.call-update) | async-done | bytes 131088 | tf_op jit(solution)/shard_map/reduce_scatter | solution.py:129
  493.5 1.9 multiply_convert_fusion.2
  495.4 6.0 all_gather.71
  502.1 2.1 fusion.6
  506.3 2.2 fusion.214
  508.6 2.1 fusion.237
  513.3 3.3 fusion.216
  516.7 1.8 convolution_bitcast_fusion
  522.9 3.1 fusion.215
  526.2 1.8 convolution_bitcast_fusion.1
  528.0 4.1 multiply_reduce_fusion
  532.3 61.0 %all-reduce.4 = (f32[2,256]{1,0:T(2,128)}, f32[31,256]{1,0:T(8,128)}) all-reduce(f32[2,256]{1,0:T(2,128)S(1)} %pad_maximum_fusion.5, f32[31,256]{1,0:T(8,128)S(1)} %bitcast.460), channel_id=1, replica_groups=mesh['dp'=16,'tensor'=2] {'dp'}, use_global_device_ids=true, to_apply=%region_51.52 | all-reduce | flops 8448 | bytes 67584 | tf_op jit(solution)/shard_map/psum | solution.py:474
  594.5 37.3 %psum.53 = f32[5,512]{1,0:T(8,128)} all-reduce(f32[5,512]{1,0:T(8,128)S(1)} %stack.338), channel_id=1, replica_groups=mesh['dp'=16,'tensor'=2] {'dp','tensor'}, use_global_device_ids=true, to_apply=%region_44.45 | all-reduce | flops 2560 | bytes 20480 | tf_op jit(solution)/shard_map/psum | solution.py:475
  631.8 1.8 fusion.163
  633.6 3.4 reduce-scatter.39.cloned.1.call-done
  637.0 60.5 %reduce-scatter.41.cloned.1.call-done = f32[2,32,256]{2,1,0:T(8,128)} async-done(((f32[2,512,256]{2,1,0:T(8,128)}), f32[2,32,256]{2,1,0:T(8,128)}) %reduce-scatter.41.cloned.1.call-update) | async-done | bytes 65552 | tf_op jit(solution)/shard_map/reduce_scatter | solution.py:483
  697.6 65.2 %reduce-scatter.47.cloned.1.call-done = f32[32,1024]{1,0:T(8,128)} async-done(((f32[512,1024]{1,0:T(8,128)}), f32[32,1024]{1,0:T(8,128)}) %reduce-scatter.47.cloned.1.call-update) | async-done | bytes 131088 | tf_op jit(solution)/shard_map/reduce_scatter | solution.py:486
  762.7 64.7 %reduce-scatter.45.cloned.1.call-done = f32[1,32,1024]{2,1,0:T(8,128)} async-done(((f32[1,512,1024]{2,1,0:T(8,128)}), f32[1,32,1024]{2,1,0:T(8,128)}) %reduce-scatter.45.cloned.1.call-update) | async-done | bytes 131088 | tf_op jit(solution)/shard_map/reduce_scatter | solution.py:485
  827.5 65.4 %reduce-scatter.37.cloned.1.call-done = f32[4,32,256]{2,1,0:T(8,128)} async-done(((f32[4,512,256]{2,1,0:T(8,128)}), f32[4,32,256]{2,1,0:T(8,128)}) %reduce-scatter.37.cloned.1.call-update) | async-done | bytes 131088 | tf_op jit(solution)/shard_map/reduce_scatter | solution.py:481
  892.8 64.7 %reduce-scatter.35.cloned.1.call-done = f32[32,1024]{1,0:T(8,128)} async-done(((f32[512,1024]{1,0:T(8,128)}), f32[32,1024]{1,0:T(8,128)}) %reduce-scatter.35.cloned.1.call-update) | async-done | bytes 131088 | tf_op jit(solution)/shard_map/reduce_scatter | solution.py:480
  957.6 65.3 %reduce-scatter.33.cloned.1.call-done = f32[1,32,1024]{2,1,0:T(8,128)} async-done(((f32[1,512,1024]{2,1,0:T(8,128)}), f32[1,32,1024]{2,1,0:T(8,128)}) %reduce-scatter.33.cloned.1.call-update) | async-done | bytes 131088 | tf_op jit(solution)/shard_map/reduce_scatter | solution.py:479
  (358 shorter events, 64.6 us)
Async XLA Ops:
  7.2 135.2 %copy-start.1 = (bf16[128,512]{1,0:T(8,128)(2,1)S(1)}, bf16[128,512]{1,0:T(8,128)(2,1)}, u32[]{:S(2)}) copy-start(bf16[128,512]{1,0:T(8,128)(2,1)} %param.15) | copy-start | bytes 393220
  7.2 43.7 %all-gather.14.cloned.1.call-start = ((), (), s32[]{:S(2)}) async-start(), calls=%async_computation.35 | async-start | bytes 1114112 | tf_op jit(solution)/shard_map/all_gather | solution.py:102
  7.9 82.0 %all-gather.8.cloned.1.call-start = ((), (), s32[]{:S(2)}) async-start(), calls=%async_computation.16 | async-start | bytes 1114112 | tf_op jit(solution)/shard_map/all_gather | solution.py:103
  8.7 120.4 %all-gather.10.cloned.1.call-start = ((), (), s32[]{:S(2)}) async-start(), calls=%async_computation.18 | async-start | bytes 1114112 | tf_op jit(solution)/shard_map/all_gather | solution.py:102
  9.4 132.9 %reduce-scatter.17.cloned.1.call-start = ((), (), s32[]{:S(2)}) async-start(), calls=%async_computation.17 | async-start | bytes 393216 | tf_op jit(solution)/shard_map/reduce_scatter | solution.py:119
  10.5 143.3 %copy-start.53 = (f32[128]{0:T(128)}, f32[128]{0:T(128)S(1)}, u32[]{:S(2)}) copy-start(f32[128]{0:T(128)S(1)} %broadcast_multiply_fusion.16) | copy-start | bytes 1540
  13.1 253.9 %copy-start.46 = (f32[1,512]{1,0:T(1,128)}, f32[1,512]{1,0:T(1,128)S(1)}, u32[]{:S(2)}) copy-start(f32[1,512]{1,0:T(1,128)S(1)} %get-tuple-element.58) | copy-start | bytes 6148
  21.2 123.2 %copy-start.13 = (bf16[256,512]{1,0:T(8,128)(2,1)}, bf16[256,512]{1,0:T(8,128)(2,1)S(1)}, u32[]{:S(2)}) copy-start(bf16[256,512]{1,0:T(8,128)(2,1)S(1)} %all_gather.56) | copy-start | bytes 786436
  44.2 124.9 %copy-start.11 = (bf16[512,256]{1,0:T(8,128)(2,1)}, bf16[512,256]{1,0:T(8,128)(2,1)S(1)}, u32[]{:S(2)}) copy-start(bf16[512,256]{1,0:T(8,128)(2,1)S(1)} %all_gather.61) | copy-start | bytes 786436
  52.5 100.2 %copy-start.26 = (f32[256,1024]{1,0:T(8,128)}, f32[256,1024]{1,0:T(8,128)S(1)}, u32[]{:S(2)}) copy-start(f32[256,1024]{1,0:T(8,128)S(1)} %fusion.233) | copy-start | bytes 3145732
  92.4 118.8 %reduce-scatter.19.cloned.1.call-start = ((), (), s32[]{:S(2)}) async-start(), calls=%async_computation.19 | async-start | bytes 393216 | tf_op jit(solution)/shard_map/reduce_scatter | solution.py:119
  94.7 49.8 %copy-start.42 = (bf16[511,256]{1,0:T(8,128)(2,1)}, bf16[511,256]{1,0:T(8,128)(2,1)S(1)}, u32[]{:S(2)}) copy-start(bf16[511,256]{1,0:T(8,128)(2,1)S(1)} %get-tuple-element.63) | copy-start | bytes 784900
  94.7 58.0 %copy-start.43 = (bf16[511,256]{1,0:T(8,128)(2,1)}, bf16[511,256]{1,0:T(8,128)(2,1)S(1)}, u32[]{:S(2)}) copy-start(bf16[511,256]{1,0:T(8,128)(2,1)S(1)} %get-tuple-element.64) | copy-start | bytes 784900
  130.3 33.8 %copy-start.27 = (bf16[511,256]{0,1:T(8,128)(2,1)}, bf16[511,256]{0,1:T(8,128)(2,1)S(1)}, u32[]{:S(2)}) copy-start(bf16[511,256]{0,1:T(8,128)(2,1)S(1)} %convolution_convert_fusion.6) | copy-start | bytes 784900
  143.4 16.9 %copy-start.55 = (f32[128]{0:T(128)}, f32[128]{0:T(128)S(1)}, u32[]{:S(2)}) copy-start(f32[128]{0:T(128)S(1)} %broadcast_multiply_fusion.15) | copy-start | bytes 1540
  144.5 15.8 %copy-start.66 = (f32[128]{0:T(128)}, f32[128]{0:T(128)S(1)}, u32[]{:S(2)}) copy-start(f32[128]{0:T(128)S(1)} %add_rsqrt_fusion.4) | copy-start | bytes 1540
  152.7 14.4 %copy-start.36 = (bf16[256,256]{0,1:T(8,128)(2,1)}, bf16[256,256]{0,1:T(8,128)(2,1)S(1)}, u32[]{:S(2)}) copy-start(bf16[256,256]{0,1:T(8,128)(2,1)S(1)} %get-tuple-element.56) | copy-start | bytes 393220
  164.1 28.2 %copy-start.47 = (bf16[2,32,256]{2,1,0:T(8,128)(2,1)S(1)}, bf16[2,32,256]{2,1,0:T(8,128)(2,1)}, u32[]{:S(2)}) copy-start(bf16[2,32,256]{2,1,0:T(8,128)(2,1)} %param.22) | copy-start | bytes 98308
  164.1 47.0 %copy-start.2 = (bf16[128,512]{1,0:T(8,128)(2,1)S(1)}, bf16[128,512]{1,0:T(8,128)(2,1)}, u32[]{:S(2)}) copy-start(bf16[128,512]{1,0:T(8,128)(2,1)} %reduce-scatter.17.cloned.1.call-done) | copy-start | bytes 393220
  167.6 53.2 %copy-start.48 = (f32[4,256]{1,0:T(4,128)}, f32[4,256]{1,0:T(4,128)S(1)}, u32[]{:S(2)}) copy-start(f32[4,256]{1,0:T(4,128)S(1)} %fusion.14) | copy-start | bytes 12292
  168.8 52.0 %copy-start.34 = (bf16[256,256]{0,1:T(8,128)(2,1)}, bf16[256,256]{0,1:T(8,128)(2,1)S(1)}, u32[]{:S(2)}) copy-start(bf16[256,256]{0,1:T(8,128)(2,1)S(1)} %convolution_convert_fusion.13) | copy-start | bytes 393220
  169.1 51.9 %copy-start.32 = (bf16[4,64,256]{2,1,0:T(8,128)(2,1)}, bf16[4,64,256]{2,1,0:T(8,128)(2,1)S(1)}, u32[]{:S(2)}) copy-start(bf16[4,64,256]{2,1,0:T(8,128)(2,1)S(1)} %convolution_convert_fusion.11) | copy-start | bytes 393220
  170.2 95.5 %reduce-scatter.21.cloned.1.call-start = ((), (), s32[]{:S(2)}) async-start(), calls=%async_computation.20 | async-start | bytes 393216 | tf_op jit(solution)/shard_map/reduce_scatter | solution.py:119
  192.3 64.3 %copy-start.44 = (bf16[512,256]{1,0:T(8,128)(2,1)}, bf16[512,256]{1,0:T(8,128)(2,1)S(1)}, u32[]{:S(2)}) copy-start(bf16[512,256]{1,0:T(8,128)(2,1)S(1)} %all_gather.64) | copy-start | bytes 786436
  221.0 35.0 %copy-start.79 = (f32[256]{0:T(256)S(1)}, f32[256]{0:T(256)}, u32[]{:S(2)}) copy-start(f32[256]{0:T(256)} %param.25) | copy-start | bytes 3076
  221.0 35.6 %copy-start.80 = (f32[256]{0:T(256)S(1)}, f32[256]{0:T(256)}, u32[]{:S(2)}) copy-start(f32[256]{0:T(256)} %param.26) | copy-start | bytes 3076
  225.6 33.5 %copy-start.8 = (f32[256,256]{0,1:T(8,128)}, f32[256,256]{0,1:T(8,128)S(1)}, u32[]{:S(2)}) copy-start(f32[256,256]{0,1:T(8,128)S(1)} %multiply_reduce_fusion.2) | copy-start | bytes 786436
  257.6 48.5 %all-gather.16.cloned.1.call-start = ((), (), s32[]{:S(2)}) async-start(), calls=%async_computation.36 | async-start | bytes 1114112 | tf_op jit(solution)/shard_map/all_gather | solution.py:102
  258.3 87.0 %all-gather.12.cloned.1.call-start = ((), (), s32[]{:S(2)}) async-start(), calls=%async_computation.21 | async-start | bytes 1114112 | tf_op jit(solution)/shard_map/all_gather | solution.py:103
  259.1 99.7 %reduce-scatter.23.cloned.1.call-start = ((), (), s32[]{:S(2)}) async-start(), calls=%async_computation.22 | async-start | bytes 393216 | tf_op jit(solution)/shard_map/reduce_scatter | solution.py:119
  266.7 81.4 %copy-start.59 = (f32[128]{0:T(128)}, f32[128]{0:T(128)S(1)}, u32[]{:S(2)}) copy-start(f32[128]{0:T(128)S(1)} %broadcast_multiply_fusion.13) | copy-start | bytes 1540
  266.9 81.2 %copy-start.69 = (f32[128]{0:T(128)}, f32[128]{0:T(128)S(1)}, u32[]{:S(2)}) copy-start(f32[128]{0:T(128)S(1)} %add_rsqrt_fusion.2) | copy-start | bytes 1540
  273.0 33.1 %copy-start.15 = (bf16[256,512]{1,0:T(8,128)(2,1)}, bf16[256,512]{1,0:T(8,128)(2,1)S(1)}, u32[]{:S(2)}) copy-start(bf16[256,512]{1,0:T(8,128)(2,1)S(1)} %all_gather.65) | copy-start | bytes 786436
  308.7 64.8 %copy-start.4 = (bf16[512,1024]{1,0:T(8,128)(2,1)S(1)}, bf16[512,1024]{1,0:T(8,128)(2,1)}, u32[]{:S(2)}) copy-start(bf16[512,1024]{1,0:T(8,128)(2,1)} %all-gather.16.cloned.1.call-done) | copy-start | bytes 3145732
  348.1 38.5 %reduce-scatter.25.cloned.1.call-start = ((), (), s32[]{:S(2)}) async-start(), calls=%async_computation.23 | async-start | bytes 393216 | tf_op jit(solution)/shard_map/reduce_scatter | solution.py:129
  358.8 29.5 %copy-start.7 = (bf16[128,512]{1,0:T(8,128)(2,1)S(1)}, bf16[128,512]{1,0:T(8,128)(2,1)}, u32[]{:S(2)}) copy-start(bf16[128,512]{1,0:T(8,128)(2,1)} %reduce-scatter.23.cloned.1.call-done) | copy-start | bytes 393220
  374.7 67.8 %reduce-scatter.27.cloned.1.call-start = ((), (), s32[]{:S(2)}) async-start(), calls=%async_computation.24 | async-start | bytes 393216 | tf_op jit(solution)/shard_map/reduce_scatter | solution.py:129
  396.2 33.7 %copy-start.39 = (bf16[256,512]{1,0:T(8,128)(2,1)}, bf16[256,512]{1,0:T(8,128)(2,1)S(1)}, u32[]{:S(2)}) copy-start(bf16[256,512]{1,0:T(8,128)(2,1)S(1)} %all_gather.69) | copy-start | bytes 786436
  431.8 20.4 %copy-start.12 = (bf16[512,256]{1,0:T(8,128)(2,1)S(1)}, bf16[512,256]{1,0:T(8,128)(2,1)}, u32[]{:S(2)}) copy-start(bf16[512,256]{1,0:T(8,128)(2,1)} %copy-done.11) | copy-start | bytes 786436
  433.1 13.0 %copy-start.21 = (bf16[256,256]{1,0:T(8,128)(2,1)}, bf16[256,256]{1,0:T(8,128)(2,1)S(1)}, u32[]{:S(2)}) copy-start(bf16[256,256]{1,0:T(8,128)(2,1)S(1)} %get-tuple-element.51) | copy-start | bytes 393220
  433.1 23.6 %copy-start.23 = (bf16[256,256]{1,0:T(8,128)(2,1)}, bf16[256,256]{1,0:T(8,128)(2,1)S(1)}, u32[]{:S(2)}) copy-start(bf16[256,256]{1,0:T(8,128)(2,1)S(1)} %get-tuple-element.50) | copy-start | bytes 393220
  434.4 58.0 %reduce-scatter.29.cloned.1.call-start = ((), (), s32[]{:S(2)}) async-start(), calls=%async_computation.25 | async-start | bytes 393216 | tf_op jit(solution)/shard_map/reduce_scatter | solution.py:129
  434.4 18.0 %copy-start.50 = (f32[4,256]{1,0:T(4,128)}, f32[4,256]{1,0:T(4,128)S(1)}, u32[]{:S(2)}) copy-start(f32[4,256]{1,0:T(4,128)S(1)} %log_add_fusion) | copy-start | bytes 12292
  452.2 17.4 %copy-start.10 = (bf16[256,512]{1,0:T(8,128)(2,1)}, bf16[256,512]{1,0:T(8,128)(2,1)S(1)}, u32[]{:S(2)}) copy-start(bf16[256,512]{1,0:T(8,128)(2,1)S(1)} %all_gather.70) | copy-start | bytes 786436
  452.7 16.8 %copy-start.51 = (f32[4,256]{1,0:T(4,128)S(1)}, f32[4,256]{1,0:T(4,128)}, u32[]{:S(2)}) copy-start(f32[4,256]{1,0:T(4,128)} %copy-done.50) | copy-start | bytes 12292
  457.7 34.7 %copy-start.56 = (f32[128]{0:T(128)S(1)}, f32[128]{0:T(128)}, u32[]{:S(2)}) copy-start(f32[128]{0:T(128)} %copy-done.55) | copy-start | bytes 1540
  472.4 33.9 %copy-start.9 = (f32[256,256]{0,1:T(8,128)S(1)}, f32[256,256]{0,1:T(8,128)}, u32[]{:S(2)}) copy-start(f32[256,256]{0,1:T(8,128)} %copy-done.8) | copy-start | bytes 786436
  475.9 29.1 %copy-start.3 = (bf16[512,1024]{1,0:T(8,128)(2,1)S(1)}, bf16[512,1024]{1,0:T(8,128)(2,1)}, u32[]{:S(2)}) copy-start(bf16[512,1024]{1,0:T(8,128)(2,1)} %all-gather.14.cloned.1.call-done) | copy-start | bytes 3145732
  480.5 112.8 %reduce-scatter.31.cloned.1.call-start = ((), (), s32[]{:S(2)}) async-start(), calls=%async_computation.26 | async-start | bytes 393216 | tf_op jit(solution)/shard_map/reduce_scatter | solution.py:129
  495.4 16.5 %copy-start.22 = (bf16[256,256]{1,0:T(8,128)(2,1)S(1)}, bf16[256,256]{1,0:T(8,128)(2,1)}, u32[]{:S(2)}) copy-start(bf16[256,256]{1,0:T(8,128)(2,1)} %copy-done.21) | copy-start | bytes 393220
  506.2 127.4 %reduce-scatter.43.cloned.1.call-start = ((), (), s32[]{:S(2)}) async-start(), calls=%async_computation.32 | async-start | bytes 557056 | tf_op jit(solution)/shard_map/reduce_scatter | solution.py:484
  508.5 128.5 %reduce-scatter.39.cloned.1.call-start = ((), (), s32[]{:S(2)}) async-start(), calls=%async_computation.30 | async-start | bytes 557056 | tf_op jit(solution)/shard_map/reduce_scatter | solution.py:482
  510.6 186.9 %reduce-scatter.41.cloned.1.call-start = ((), (), s32[]{:S(2)}) async-start(), calls=%async_computation.31 | async-start | bytes 1114112 | tf_op jit(solution)/shard_map/reduce_scatter | solution.py:483
  513.2 249.5 %reduce-scatter.47.cloned.1.call-start = ((), (), s32[]{:S(2)}) async-start(), calls=%async_computation.34 | async-start | bytes 2228224 | tf_op jit(solution)/shard_map/reduce_scatter | solution.py:486
  516.6 310.9 %reduce-scatter.45.cloned.1.call-start = ((), (), s32[]{:S(2)}) async-start(), calls=%async_computation.33 | async-start | bytes 2228224 | tf_op jit(solution)/shard_map/reduce_scatter | solution.py:485
  518.5 374.4 %reduce-scatter.37.cloned.1.call-start = ((), (), s32[]{:S(2)}) async-start(), calls=%async_computation.29 | async-start | bytes 2228224 | tf_op jit(solution)/shard_map/reduce_scatter | solution.py:481
  522.6 434.9 %reduce-scatter.35.cloned.1.call-start = ((), (), s32[]{:S(2)}) async-start(), calls=%async_computation.28 | async-start | bytes 2228224 | tf_op jit(solution)/shard_map/reduce_scatter | solution.py:480
  526.0 67.3 %copy-start.54 = (f32[128]{0:T(128)S(1)}, f32[128]{0:T(128)}, u32[]{:S(2)}) copy-start(f32[128]{0:T(128)} %copy-done.53) | copy-start | bytes 1540
  526.0 67.3 %copy-start.65 = (f32[128]{0:T(128)S(1)}, f32[128]{0:T(128)}, u32[]{:S(2)}) copy-start(f32[128]{0:T(128)} %copy-done.64) | copy-start | bytes 1540
  526.0 68.4 %copy-start.60 = (f32[512]{0:T(512)S(1)}, f32[512]{0:T(512)}, u32[]{:S(2)}) copy-start(f32[512]{0:T(512)} %get-tuple-element.15) | copy-start | bytes 6148
  526.1 68.4 %copy-start.61 = (f32[512]{0:T(512)S(1)}, f32[512]{0:T(512)}, u32[]{:S(2)}) copy-start(f32[512]{0:T(512)} %get-tuple-element.17) | copy-start | bytes 6148
  526.1 68.4 %copy-start.62 = (f32[512]{0:T(512)S(1)}, f32[512]{0:T(512)}, u32[]{:S(2)}) copy-start(f32[512]{0:T(512)} %get-tuple-element.19) | copy-start | bytes 6148
  526.1 105.8 %copy-start.31 = (f32[128,512]{1,0:T(8,128)S(1)}, f32[128,512]{1,0:T(8,128)}, u32[]{:S(2)}) copy-start(f32[128,512]{1,0:T(8,128)} %get-tuple-element.41) | copy-start | bytes 786436
  526.1 496.8 %reduce-scatter.33.cloned.1.call-start = ((), (), s32[]{:S(2)}) async-start(), calls=%async_computation.27 | async-start | bytes 2228224 | tf_op jit(solution)/shard_map/reduce_scatter | solution.py:479
  (38 other events, 188.8 us)
Sparse Core Ops, SparseCore 0:
  10.2 40.6 all-gather.13
  53.0 36.8 all-gather.7
  92.1 36.8 all-gather.9
  131.7 10.5 reduce-scatter.16
  170.3 11.6 reduce-scatter.18
  257.7 7.9 reduce-scatter.20
  268.1 37.9 all-gather.15
  308.4 36.8 all-gather.11
  348.2 10.5 reduce-scatter.22
  374.8 11.6 reduce-scatter.24
  434.5 7.9 reduce-scatter.26
  480.6 11.6 reduce-scatter.28
  506.3 11.6 reduce-scatter.30
  522.0 55.7 reduce-scatter.42
  582.2 54.7 reduce-scatter.38
  641.1 56.4 reduce-scatter.40
  702.2 60.5 reduce-scatter.46
  766.9 60.5 reduce-scatter.44
  832.2 60.5 reduce-scatter.36
  897.0 60.5 reduce-scatter.34
  962.3 60.5 reduce-scatter.32
where the time goes:
time: 1030 us
  waiting for transfers between devices  600 us (58%)
  blocking collectives  274 us (27%)
  matrix products  63.4 us (6%)
  other arithmetic  40.2 us (4%)
  local copies, waits for them, and re-layouts  34.3 us (3%)
  between operations  16.1 us (2%)
    all_gather x2, waiting for transfers between devices, gather_weights(): lax.all_gather(single, 'dp', axis=0, tiled=True)  74.1 us
    all_gather x3, waiting for transfers between devices, gather_weights(): lax.all_gather(stacked, 'dp', axis=1, tiled=True)  73.3 us
    reduce_scatter x1, waiting for transfers between devices, body(): lax.psum_scatter(attention_grads[0], 'dp', scatter_dimension=1, tiled=True)  65.4 us
    reduce_scatter x1, waiting for transfers between devices, body(): lax.psum_scatter(first_grads[0], 'dp', scatter_dimension=1, tiled=True)  65.3 us
    reduce_scatter x1, waiting for transfers between devices, body(): lax.psum_scatter(second_grads[1], 'dp', scatter_dimension=0, tiled=True)  65.2 us
    reduce_scatter x1, waiting for transfers between devices, body(): lax.psum_scatter(second_grads[0], 'dp', scatter_dimension=1, tiled=True)  64.7 us
    reduce_scatter x1, waiting for transfers between devices, body(): lax.psum_scatter(first_grads[1], 'dp', scatter_dimension=0, tiled=True)  64.7 us
    psum x1, blocking collectives, body(): kernel_total, bias_total = lax.psum((kernel_grad, bias_grad), 'dp')  61 us
  transfers between devices with their start and end apart: 21, of which 18 were waited for; matrix products, arithmetic and copies ran while one was open for 4% of the time, Pallas kernels for 0%

commit v1 on v0

v1 whole, which is shorter than its diff:
```python
import math

import jax
import jax.numpy as jnp
from jax import lax
from jax.experimental import pallas as pl
from jax.experimental.pallas import tpu as pltpu
from jax.sharding import PartitionSpec as P

HEAD_TOTAL = 8
EPSILON = 1e-05
BF16 = jnp.bfloat16
F32 = jnp.float32


def matmul(left_side, right_side):
    return jnp.dot(left_side, right_side, preferred_element_type=F32)


def right_transposed(left_side, right_side):
    return lax.dot_general(
        left_side, right_side, (((1,), (1,)), ((), ())), preferred_element_type=F32
    )


def left_transposed(left_side, right_side):
    return lax.dot_general(
        left_side, right_side, (((0,), (0,)), ((), ())), preferred_element_type=F32
    )


def swish_slope(pre_value, gate_sigma):
    return gate_sigma * (1.0 + pre_value * (1.0 - gate_sigma))


def norm_parts(residual):
    centred = residual - jnp.mean(residual, -1, keepdims=True)
    factor = lax.rsqrt(jnp.mean(centred * centred, -1, keepdims=True) + EPSILON)
    return centred * factor, factor


def norm_back(gradient, normed, factor, norm_gain):
    scaled = gradient * norm_gain
    inner_sum = (
        scaled
        - jnp.mean(scaled, -1, keepdims=True)
        - normed * jnp.mean(scaled * normed, -1, keepdims=True)
    )
    return factor * inner_sum, jnp.sum(gradient * normed, 0, keepdims=True)


def sinusoid(length, features):
    offsets = jnp.arange(2 * length, dtype=F32) - (length - 1)
    half_width = features // 2
    frequency = jnp.exp(jnp.arange(half_width, dtype=F32) * (-math.log(10000.0) / half_width))
    angles = offsets[:, None] * frequency[None, :]
    table = jnp.concatenate([jnp.sin(angles), jnp.cos(angles)], 1)
    return jnp.where(offsets[:, None] < length, table, 0.0)


def on_chip(function, name, operands, results, scratch=(), flops=300_000_000):
    count = len(operands)
    total = count + len(results)

    def kernel(*refs):
        function(refs[:count], refs[count:total], refs[total:])

    moved = sum(value.size * value.dtype.itemsize for value in operands)
    moved += sum(math.prod(shape) * jnp.dtype(kind).itemsize for shape, kind in results)
    return pl.pallas_call(
        kernel,
        out_shape=[jax.ShapeDtypeStruct(shape, kind) for shape, kind in results],
        in_specs=[pl.BlockSpec(memory_space=pltpu.VMEM)] * count,
        out_specs=[pl.BlockSpec(memory_space=pltpu.VMEM)] * len(results),
        scratch_shapes=list(scratch),
        compiler_params=pltpu.CompilerParams(vmem_limit_bytes=40 * 1024 * 1024),
        cost_estimate=pl.CostEstimate(flops=flops, bytes_accessed=moved, transcendentals=0),
        name=name,
    )(*operands)


def swap(value):
    return lax.ppermute(value, "tensor", [(0, 1), (1, 0)])


def both_halves(own):
    other = swap(own)
    first = lax.axis_index("tensor") == 0
    return jnp.concatenate([jnp.where(first, own, other), jnp.where(first, other, own)], 0)


def sum_over(value, axis):
    size = lax.axis_size(axis)
    if size & (size - 1):
        return lax.psum(value, axis)
    step = 1
    while step < size:
        value = value + lax.ppermute(value, axis, [(k, k ^ step) for k in range(size)])
        step *= 2
    return value


def ff_forward_body(row, residual, gain_ref, weight_ref, outs):
    entries_ref, pre_ref, hidden_ref, part_ref = outs
    half = weight_ref.shape[1] // 2
    normed, _ = norm_parts(residual)
    entries = (normed * gain_ref[row : row + 1, :]).astype(BF16)
    entries_ref[...] = entries
    pre = matmul(entries, weight_ref[:, :half])
    pre_ref[...] = pre
    hidden = (pre * jax.nn.sigmoid(pre)).astype(BF16)
    hidden_ref[...] = hidden
    part_ref[...] = right_transposed(hidden, weight_ref[:, half:]).astype(BF16)


def first_forward(tokens, gains, weights):
    rows, width = tokens.shape
    hidden = weights.shape[1] // 2

    def body(ins, outs, _):
        ff_forward_body(0, ins[0][...].astype(F32), ins[1], ins[2], outs)

    return on_chip(
        body,
        "first_forward",
        (tokens, gains, weights),
        (
            ((rows, width), BF16),
            ((rows, hidden), F32),
            ((rows, hidden), BF16),
            ((rows, width), BF16),
        ),
    )


def second_forward(residual, own, other, gains, weights):
    rows, width = residual.shape
    hidden = weights.shape[1] // 2

    def body(ins, outs, _):
        after = ins[0][...] + (ins[1][...].astype(F32) + ins[2][...].astype(F32))
        outs[0][...] = after
        ff_forward_body(3, after, ins[3], ins[4], outs[1:])

    return on_chip(
        body,
        "second_forward",
        (residual, own, other, gains, weights),
        (
            ((rows, width), F32),
            ((rows, width), BF16),
            ((rows, hidden), F32),
            ((rows, hidden), BF16),
            ((rows, width), BF16),
        ),
    )


def ff_back_body(gradient, pre_ref, weight_ref, branch_ref, slope_ref):
    half = weight_ref.shape[1] // 2
    branch = (0.5 * gradient).astype(BF16)
    branch_ref[...] = branch
    grad_hidden = matmul(branch, weight_ref[:, half:])
    pre = pre_ref[...]
    grad_pre = (grad_hidden * swish_slope(pre, jax.nn.sigmoid(pre))).astype(BF16)
    slope_ref[...] = grad_pre
    return right_transposed(grad_pre, weight_ref[:, :half])


def second_back(residual, own, other, cotangent, pre, gains, weights):
    rows, width = residual.shape
    hidden = weights.shape[1] // 2

    def body(ins, outs, _):
        x_ref, own_ref, other_ref, cot_ref, pre_ref, gain_ref, weight_ref = ins
        out_ref, grad_ref, branch_ref, slope_ref, part_ref, gain_grad_ref = outs
        after = x_ref[...] + 0.5 * (own_ref[...].astype(F32) + other_ref[...].astype(F32))
        normed, factor = norm_parts(after)
        gain = gain_ref[4:5, :]
        out_ref[...] = (normed * gain).astype(BF16)
        gradient, gain_grad_ref[...] = norm_back(
            cot_ref[...].astype(F32), normed, factor, gain
        )
        grad_ref[...] = gradient
        part_ref[...] = ff_back_body(gradient, pre_ref, weight_ref, branch_ref, slope_ref).astype(
            BF16
        )

    return on_chip(
        body,
        "second_back",
        (residual, own, other, cotangent, pre, gains, weights),
        (
            ((rows, width), BF16),
            ((rows, width), F32),
            ((rows, width), BF16),
            ((rows, hidden), BF16),
            ((rows, width), BF16),
            ((1, width), F32),
        ),
    )


def ff_weight_grads(entries, grad_pre, branch, hidden, name):
    width = entries.shape[1]
    half = hidden.shape[1]

    def body(ins, outs, _):
        outs[0][:, :half] = left_transposed(ins[0][...], ins[1][...]).astype(BF16)
        outs[0][:, half:] = left_transposed(ins[2][...], ins[3][...]).astype(BF16)

    return on_chip(
        body, name, (entries, grad_pre, branch, hidden), (((width, 2 * half), BF16),)
    )[0]


def position_forward(table, weights, columns):
    def body(ins, outs, _):
        outs[0][...] = matmul(ins[0][...], ins[1][:, 3 * columns : 4 * columns]).astype(BF16)

    return on_chip(body, "position_forward", (table, weights), (((table.shape[0], columns), BF16),))[0]


def attention_forward(tokens, own, other, gains, weights, positions, biases, heads):
    rows, width = tokens.shape
    columns = biases.shape[1]
    features = columns // heads
    scale = features ** (-0.5)

    def body(ins, outs, _):
        x_ref, own_ref, other_ref, gain_ref, weight_ref, table_ref, bias_ref = ins
        after_ref, e_ref, qc_ref, qp_ref, k_ref, v_ref, prob_ref, mix_ref, part_ref = outs
        after = x_ref[...].astype(F32) + 0.5 * (
            own_ref[...].astype(F32) + other_ref[...].astype(F32)
        )
        after_ref[...] = after
        normed, _ = norm_parts(after)
        entries = (normed * gain_ref[1:2, :]).astype(BF16)
        e_ref[...] = entries
        joined = matmul(entries, weight_ref[:, : 3 * columns])
        queries = joined[:, :columns]
        content_q = (queries + bias_ref[0:1, :]).astype(BF16)
        position_q = (queries + bias_ref[1:2, :]).astype(BF16)
        keys = joined[:, columns : 2 * columns].astype(BF16)
        values = joined[:, 2 * columns :].astype(BF16)
        qc_ref[...] = content_q
        qp_ref[...] = position_q
        k_ref[...] = keys
        v_ref[...] = values
        mixed = []
        for head in range(heads):
            part = slice(head * features, (head + 1) * features)
            content = right_transposed(content_q[:, part], keys[:, part])
            raw = right_transposed(position_q[:, part], table_ref[:, part])
            shifted = pltpu.roll(raw, rows + 1, 1, stride=1, stride_axis=0)[:, :rows]
            scores = (content + shifted) * scale
            lifted = jnp.exp(scores - jnp.max(scores, -1, keepdims=True))
            probability = lifted / jnp.sum(lifted, -1, keepdims=True)
            prob_ref[head] = probability
            mixed.append(matmul(probability.astype(BF16), values[:, part]))
        attended = jnp.concatenate(mixed, 1).astype(BF16)
        mix_ref[...] = attended
        part_ref[...] = right_transposed(attended, weight_ref[:, 4 * columns :]).astype(BF16)

    local = ((rows, columns), BF16)
    return on_chip(
        body,
        "attention_forward",
        (tokens, own, other, gains, weights, positions, biases),
        (
            ((rows, width), F32),
            ((rows, width), BF16),
            local,
            local,
            local,
            local,
            ((heads, rows, rows), F32),
            local,
            ((rows, width), BF16),
        ),
    )


def attention_back(gradient, own, other, residual, gains, weights, positions, kept, heads):
    rows, width = residual.shape
    columns = positions.shape[1]
    features = columns // heads
    scale = features ** (-0.5)

    def body(ins, outs, _):
        (
            grad_ref,
            own_ref,
            other_ref,
            x_ref,
            gain_ref,
            weight_ref,
            table_ref,
            qc_ref,
            qp_ref,
            k_ref,
            v_ref,
            prob_ref,
        ) = ins
        total_ref, branch_ref, joined_ref, table_grad_ref, part_ref, gain_grad_ref, bias_ref = outs
        normed, factor = norm_parts(x_ref[...])
        passed, gain_grad_ref[...] = norm_back(
            own_ref[...].astype(F32) + other_ref[...].astype(F32), normed, factor, gain_ref[2:3, :]
        )
        total = grad_ref[...] + passed
        total_ref[...] = total
        branch = total.astype(BF16)
        branch_ref[...] = branch
        grad_mixed = matmul(branch, weight_ref[:, 4 * columns :]).astype(BF16)
        line = lax.broadcasted_iota(jnp.int32, (rows, rows), 0)
        place = lax.broadcasted_iota(jnp.int32, (rows, rows), 1)
        flip = (line + place == rows - 1).astype(F32).astype(BF16)
        content_q = qc_ref[...]
        keys = k_ref[...]
        values = v_ref[...]
        flipped_q = matmul(flip, qp_ref[...]).astype(BF16)
        zeros = jnp.zeros((rows, rows), F32)
        from_content, from_position, to_keys, to_values, to_table = [], [], [], [], []
        for head in range(heads):
            part = slice(head * features, (head + 1) * features)
            probability = prob_ref[head]
            grad_probability = right_transposed(grad_mixed[:, part], values[:, part])
            to_values.append(left_transposed(probability.astype(BF16), grad_mixed[:, part]))
            inner = jnp.sum(probability * grad_probability, -1, keepdims=True)
            grad_scores = (probability * (grad_probability - inner)).astype(BF16) * scale
            grad_scores = grad_scores.astype(BF16)
            from_content.append(matmul(grad_scores, keys[:, part]))
            to_keys.append(left_transposed(grad_scores, content_q[:, part]))
            flipped = jnp.concatenate([matmul(flip, grad_scores), zeros], 1)
            spread = pltpu.roll(flipped, 0, 1, stride=1, stride_axis=0).astype(BF16)
            from_position.append(matmul(spread, table_ref[:, part]))
            to_table.append(left_transposed(spread, flipped_q[:, part]))
        grad_content = jnp.concatenate(from_content, 1)
        grad_position = jnp.concatenate(from_position, 1)
        high = grad_position.astype(BF16)
        low = (grad_position - high.astype(F32)).astype(BF16)
        grad_position = matmul(flip, high) + matmul(flip, low)
        bias_ref[0:1, :] = jnp.sum(grad_content, 0, keepdims=True)
        bias_ref[1:2, :] = jnp.sum(grad_position, 0, keepdims=True)
        joined = jnp.concatenate(
            [grad_content + grad_position] + to_keys + to_values, 1
        ).astype(BF16)
        joined_ref[...] = joined
        table_grad_ref[...] = jnp.concatenate(to_table, 1).astype(BF16)
        part_ref[...] = right_transposed(joined, weight_ref[:, : 3 * columns]).astype(BF16)

    return on_chip(
        body,
        "attention_back",
        (gradient, own, other, residual, gains, weights, positions) + tuple(kept),
        (
            ((rows, width), F32),
            ((rows, width), BF16),
            ((rows, 3 * columns), BF16),
            ((2 * rows, columns), BF16),
            ((rows, width), BF16),
            ((1, width), F32),
            ((2, columns), F32),
        ),
    )


def attention_weight_grads(entries, joined, table, table_grad, branch, attended):
    width = entries.shape[1]
    columns = attended.shape[1]

    def body(ins, outs, _):
        out_ref = outs[0]
        out_ref[:, : 3 * columns] = left_transposed(ins[0][...], ins[1][...]).astype(BF16)
        out_ref[:, 3 * columns : 4 * columns] = left_transposed(ins[2][...], ins[3][...]).astype(
            BF16
        )
        out_ref[:, 4 * columns :] = left_transposed(ins[4][...], ins[5][...]).astype(BF16)

    return on_chip(
        body,
        "attention_weight_grads",
        (entries, joined, table, table_grad, branch, attended),
        (((width, 5 * columns), BF16),),
    )[0]


PAD = 16


def conv_forward(residual, own, other, gains, weights, depth_kernel):
    rows, width = residual.shape
    taps, columns = depth_kernel.shape
    half_taps = (taps - 1) // 2

    def body(ins, outs, scratch):
        x_ref, own_ref, other_ref, gain_ref, weight_ref, tap_ref = ins
        after_ref, c_ref, value_ref, gate_ref, conv_ref, sums_ref = outs
        padded = scratch[0]
        after = x_ref[...] + (own_ref[...].astype(F32) + other_ref[...].astype(F32))
        after_ref[...] = after
        normed, _ = norm_parts(after)
        entries = (normed * gain_ref[2:3, :]).astype(BF16)
        c_ref[...] = entries
        joined = matmul(entries, weight_ref[:, : 2 * columns])
        value = joined[:, :columns]
        gate = jax.nn.sigmoid(joined[:, columns:])
        value_ref[...] = value
        gate_ref[...] = gate
        padded[:PAD, :] = jnp.zeros((PAD, columns), F32)
        padded[PAD + rows :, :] = jnp.zeros((PAD, columns), F32)
        padded[PAD : PAD + rows, :] = value * gate
        total = jnp.zeros((rows, columns), F32)
        for tap in range(taps):
            start = PAD - half_taps + tap
            total = total + tap_ref[tap : tap + 1, :] * padded[start : start + rows, :]
        conv_ref[...] = total
        sums_ref[0:1, :] = jnp.sum(total, 0, keepdims=True)
        sums_ref[1:2, :] = jnp.sum(total * total, 0, keepdims=True)

    local = ((rows, columns), F32)
    return on_chip(
        body,
        "conv_forward",
        (residual, own, other, gains, weights, depth_kernel),
        (((rows, width), F32), ((rows, width), BF16), local, local, local, ((2, columns), F32)),
        scratch=(pltpu.VMEM((rows + 2 * PAD, columns), F32),),
    )


def batch_norm(conv_ref, sums_ref, batch_ref, token_count):
    column_mean = sums_ref[0:1, :] / token_count
    inverse = lax.rsqrt(sums_ref[1:2, :] / token_count - column_mean * column_mean + EPSILON)
    standard = (conv_ref[...] - column_mean) * inverse
    return standard, inverse, standard * batch_ref[0:1, :] + batch_ref[1:2, :]


def norm_forward(convolved, sums, batch, weights, token_count):
    rows, columns = convolved.shape
    width = weights.shape[0]

    def body(ins, outs, _):
        conv_ref, sums_ref, batch_ref, weight_ref = ins
        _, _, shifted = batch_norm(conv_ref, sums_ref, batch_ref, token_count)
        activated = (shifted * jax.nn.sigmoid(shifted)).astype(BF16)
        outs[0][...] = activated
        outs[1][...] = right_transposed(activated, weight_ref[:, 2 * columns :]).astype(BF16)

    return on_chip(
        body,
        "norm_forward",
        (convolved, sums, batch, weights),
        (((rows, columns), BF16), ((rows, width), BF16)),
    )


def norm_backward(gradient, own, other, residual, gains, weights, convolved, sums, batch, count):
    rows, columns = convolved.shape
    width = weights.shape[0]

    def body(ins, outs, _):
        grad_ref, own_ref, other_ref, x_ref, gain_ref, weight_ref, conv_ref, sums_ref, batch_ref = (
            ins
        )
        total_ref, branch_ref, shifted_ref, grad_sums_ref, gain_grad_ref = outs
        normed, factor = norm_parts(x_ref[...])
        passed, gain_grad_ref[...] = norm_back(
            own_ref[...].astype(F32) + other_ref[...].astype(F32), normed, factor, gain_ref[3:4, :]
        )
        total = grad_ref[...] + passed
        total_ref[...] = total
        branch = total.astype(BF16)
        branch_ref[...] = branch
        standard, _, shifted = batch_norm(conv_ref, sums_ref, batch_ref, count)
        grad_shifted = matmul(branch, weight_ref[:, 2 * columns :]) * swish_slope(
            shifted, jax.nn.sigmoid(shifted)
        )
        shifted_ref[...] = grad_shifted
        grad_sums_ref[0:1, :] = jnp.sum(grad_shifted, 0, keepdims=True)
        grad_sums_ref[1:2, :] = jnp.sum(grad_shifted * standard, 0, keepdims=True)

    return on_chip(
        body,
        "norm_backward",
        (gradient, own, other, residual, gains, weights, convolved, sums, batch),
        (
            ((rows, width), F32),
            ((rows, width), BF16),
            ((rows, columns), F32),
            ((2, columns), F32),
            ((1, width), F32),
        ),
    )


def conv_backward(
    grad_shifted, grad_sums, convolved, sums, batch, value, gate, weights, depth_kernel, count
):
    rows, columns = convolved.shape
    width = weights.shape[0]
    taps = depth_kernel.shape[0]
    half_taps = (taps - 1) // 2

    def body(ins, outs, scratch):
        (
            shifted_ref,
            grad_sums_ref,
            conv_ref,
            sums_ref,
            batch_ref,
            value_ref,
            gate_ref,
            weight_ref,
            tap_ref,
        ) = ins
        grad_conv_ref, joined_ref, part_ref = outs
        padded = scratch[0]
        standard, inverse, _ = batch_norm(conv_ref, sums_ref, batch_ref, count)
        grad_conv = (inverse * batch_ref[0:1, :]) * (
            shifted_ref[...]
            - grad_sums_ref[0:1, :] / count
            - standard * (grad_sums_ref[1:2, :] / count)
        )
        grad_conv_ref[...] = grad_conv
        padded[:PAD, :] = jnp.zeros((PAD, columns), F32)
        padded[PAD + rows :, :] = jnp.zeros((PAD, columns), F32)
        padded[PAD : PAD + rows, :] = grad_conv
        total = jnp.zeros((rows, columns), F32)
        for tap in range(taps):
            start = PAD + half_taps - tap
            total = total + tap_ref[tap : tap + 1, :] * padded[start : start + rows, :]
        gate_sigma = gate_ref[...]
        grad_value = total * gate_sigma
        joined = jnp.concatenate(
            [grad_value, grad_value * value_ref[...] * (1.0 - gate_sigma)], 1
        ).astype(BF16)
        joined_ref[...] = joined
        part_ref[...] = right_transposed(joined, weight_ref[:, : 2 * columns]).astype(BF16)

    return on_chip(
        body,
        "conv_backward",
        (grad_shifted, grad_sums, convolved, sums, batch, value, gate, weights, depth_kernel),
        (((rows, columns), F32), ((rows, 2 * columns), BF16), ((rows, width), BF16)),
        scratch=(pltpu.VMEM((rows + 2 * PAD, columns), F32),),
    )


def conv_weight_grads(entries, joined, branch, activated, value, gate, grad_conv, taps):
    rows, columns = grad_conv.shape
    width = entries.shape[1]
    half_taps = (taps - 1) // 2

    def body(ins, outs, scratch):
        e_ref, joined_ref, branch_ref, y_ref, value_ref, gate_ref, grad_ref = ins
        out_ref, tap_ref = outs
        padded = scratch[0]
        out_ref[:, : 2 * columns] = left_transposed(e_ref[...], joined_ref[...]).astype(BF16)
        out_ref[:, 2 * columns :] = left_transposed(branch_ref[...], y_ref[...]).astype(BF16)
        padded[:PAD, :] = jnp.zeros((PAD, columns), F32)
        padded[PAD + rows :, :] = jnp.zeros((PAD, columns), F32)
        padded[PAD : PAD + rows, :] = value_ref[...] * gate_ref[...]
        grad_conv_value = grad_ref[...]
        for tap in range(taps):
            start = PAD - half_taps + tap
            tap_ref[tap : tap + 1, :] = jnp.sum(
                padded[start : start + rows, :] * grad_conv_value, 0, keepdims=True
            )

    return on_chip(
        body,
        "conv_weight_grads",
        (entries, joined, branch, activated, value, gate, grad_conv),
        (((width, 3 * columns), BF16), ((taps, columns), F32)),
        scratch=(pltpu.VMEM((rows + 2 * PAD, columns), F32),),
    )


def first_back(gradient, own, other, residual, pre, gains, weights):
    rows, width = residual.shape
    hidden = weights.shape[1] // 2

    def body(ins, outs, _):
        grad_ref, own_ref, other_ref, x_ref, pre_ref, gain_ref, weight_ref = ins
        total_ref, branch_ref, slope_ref, part_ref, gain_grad_ref = outs
        normed, factor = norm_parts(x_ref[...])
        passed, gain_grad_ref[...] = norm_back(
            own_ref[...].astype(F32) + other_ref[...].astype(F32), normed, factor, gain_ref[1:2, :]
        )
        total = grad_ref[...] + passed
        total_ref[...] = total
        part_ref[...] = ff_back_body(total, pre_ref, weight_ref, branch_ref, slope_ref).astype(BF16)

    return on_chip(
        body,
        "first_back",
        (gradient, own, other, residual, pre, gains, weights),
        (
            ((rows, width), F32),
            ((rows, width), BF16),
            ((rows, hidden), BF16),
            ((rows, width), BF16),
            ((1, width), F32),
        ),
    )


def input_back(gradient, own, other, tokens, gains):
    rows, width = tokens.shape

    def body(ins, outs, _):
        grad_ref, own_ref, other_ref, x_ref, gain_ref = ins
        normed, factor = norm_parts(x_ref[...].astype(F32))
        passed, outs[1][...] = norm_back(
            own_ref[...].astype(F32) + other_ref[...].astype(F32), normed, factor, gain_ref[0:1, :]
        )
        outs[0][...] = grad_ref[...] + passed

    return on_chip(
        body,
        "input_back",
        (gradient, own, other, tokens, gains),
        (((rows, width), F32), ((1, width), F32)),
        flops=1_000_000,
    )


def own_rows(whole, count):
    return lax.dynamic_slice_in_dim(whole, lax.axis_index("tensor") * count, count, 0)


def columns_of(stacked):
    return [stacked[index] for index in range(stacked.shape[0])]


def scatter_weights(grads):
    return lax.psum_scatter(grads, "dp", scatter_dimension=0, tiled=True).astype(F32)


def stacked_columns(pieces, count):
    width = pieces.shape[1] // count
    return jnp.stack([pieces[:, index * width : (index + 1) * width] for index in range(count)])


def body(
    tokens,
    norm_gains,
    first_in,
    first_out,
    attention_in,
    attention_out,
    head_biases,
    gated_in,
    pointwise_out,
    depth_kernel,
    batch_scale,
    batch_shift,
    second_in,
    second_out,
    cotangent,
):
    own_count = tokens.shape[0]
    local_heads = HEAD_TOTAL // lax.axis_size("tensor")
    length = own_count * lax.axis_size("tensor")
    token_count = float(length * lax.axis_size("dp"))
    columns = attention_out.shape[1]
    hidden = first_in.shape[1]
    table = sinusoid(length, tokens.shape[1]).astype(BF16)
    batch = jnp.stack([batch_scale, batch_shift])

    def gather(pieces):
        return lax.all_gather(jnp.concatenate(pieces, 1), "dp", axis=0, tiled=True)

    first_weights = gather([first_in, first_out])
    rest = gather(
        columns_of(attention_in)
        + [attention_out]
        + columns_of(gated_in)
        + [pointwise_out, second_in, second_out]
    )
    attention_weights = rest[:, : 5 * columns]
    conv_weights = rest[:, 5 * columns : 8 * columns]
    second_weights = rest[:, 8 * columns :]

    tokens_all = both_halves(tokens)
    cotangent_all = both_halves(cotangent)

    entries1, pre1, hidden1, part1 = first_forward(tokens_all, norm_gains, first_weights)
    other1 = swap(part1)
    positions = position_forward(table, attention_weights, columns)
    after1, entries2, qc, qp, keys, values, prob, attended, part2 = attention_forward(
        tokens_all, part1, other1, norm_gains, attention_weights, positions, head_biases, local_heads
    )
    other2 = swap(part2)
    after2, entries3, value_pre, gate, convolved, sums = conv_forward(
        after1, part2, other2, norm_gains, conv_weights, depth_kernel
    )
    sums = sum_over(sums, "dp")
    activated, part3 = norm_forward(convolved, sums, batch, conv_weights, token_count)
    other3 = swap(part3)
    after3, entries4, pre4, hidden4, part4 = second_forward(
        after2, part3, other3, norm_gains, second_weights
    )
    other4 = swap(part4)
    out_all, grad4, branch4, slope4, part5, gain5 = second_back(
        after3, part4, other4, cotangent_all, pre4, norm_gains, second_weights
    )
    block_out = own_rows(out_all, own_count)
    other5 = swap(part5)
    grads_second = ff_weight_grads(entries4, slope4, branch4, hidden4, "second_weight_grads")
    grad3, branch3, grad_shifted, grad_sums, gain4 = norm_backward(
        grad4, part5, other5, after3, norm_gains, conv_weights, convolved, sums, batch, token_count
    )
    grad_sums = sum_over(grad_sums, "dp")
    grad_conv, joined3, part6 = conv_backward(
        grad_shifted,
        grad_sums,
        convolved,
        sums,
        batch,
        value_pre,
        gate,
        conv_weights,
        depth_kernel,
        token_count,
    )
    other6 = swap(part6)
    grads_conv, tap_grads = conv_weight_grads(
        entries3, joined3, branch3, activated, value_pre, gate, grad_conv, depth_kernel.shape[0]
    )
    grad2, branch2, joined2, table_grad, part7, gain3, bias_grads = attention_back(
        grad3,
        part6,
        other6,
        after2,
        norm_gains,
        attention_weights,
        positions,
        (qc, qp, keys, values, prob),
        local_heads,
    )
    other7 = swap(part7)
    grads_attention = attention_weight_grads(
        entries2, joined2, table, table_grad, branch2, attended
    )
    grad1, branch1, slope1, part8, gain2 = first_back(
        grad2, part7, other7, after1, pre1, norm_gains, first_weights
    )
    grads_first = ff_weight_grads(entries1, slope1, branch1, hidden1, "first_weight_grads")
    other_start = (1 - lax.axis_index("tensor")) * own_count
    other8 = swap(lax.dynamic_slice_in_dim(part8, other_start, own_count, 0))
    grad_start, gain1 = input_back(
        own_rows(grad1, own_count), own_rows(part8, own_count), other8, tokens, norm_gains
    )

    reduced_a = scatter_weights(jnp.concatenate([grads_second, grads_conv], 1))
    reduced_b = scatter_weights(jnp.concatenate([grads_attention, grads_first], 1))
    reduced_second = reduced_a[:, : 2 * hidden]
    reduced_conv = reduced_a[:, 2 * hidden :]
    reduced_attention = reduced_b[:, : 5 * columns]
    reduced_first = reduced_b[:, 5 * columns :]

    gains = jnp.concatenate([gain1, 0.5 * gain2, 0.5 * gain3, 0.5 * gain4, 0.5 * gain5], 0)
    packed = jnp.concatenate(
        [jnp.reshape(value, (-1, 128)) for value in (gains, tap_grads, bias_grads)], 0
    )
    packed = sum_over(packed, "dp")
    gain_rows = gains.size // 128
    tap_rows = tap_grads.size // 128
    gain_total = sum_over(packed[:gain_rows].reshape(gains.shape), "tensor")
    tap_total = packed[gain_rows : gain_rows + tap_rows].reshape(tap_grads.shape)
    bias_total = packed[gain_rows + tap_rows :].reshape(bias_grads.shape)
    return (
        block_out,
        grad_start,
        gain_total,
        reduced_first[:, :hidden],
        reduced_first[:, hidden:],
        stacked_columns(reduced_attention[:, : 4 * columns], 4),
        reduced_attention[:, 4 * columns :],
        bias_total,
        stacked_columns(reduced_conv[:, : 2 * columns], 2),
        reduced_conv[:, 2 * columns :],
        tap_total,
        grad_sums[1],
        grad_sums[0],
        reduced_second[:, :hidden],
        reduced_second[:, hidden:],
    )


def solution(mesh):
    placed = (
        P(("dp", "tensor"), None),
        P(),
        P("dp", "tensor"),
        P("dp", "tensor"),
        P(None, "dp", "tensor"),
        P("dp", "tensor"),
        P(None, "tensor"),
        P(None, "dp", "tensor"),
        P("dp", "tensor"),
        P(None, "tensor"),
        P("tensor"),
        P("tensor"),
        P("dp", "tensor"),
        P("dp", "tensor"),
        P(("dp", "tensor"), None),
    )
    return jax.shard_map(
        body,
        mesh=mesh,
        in_specs=placed,
        out_specs=(
            P(("dp", "tensor"), None),
            P(("dp", "tensor"), None),
            P(),
            P("dp", "tensor"),
            P("dp", "tensor"),
            P(None, "dp", "tensor"),
            P("dp", "tensor"),
            P(None, "tensor"),
            P(None, "dp", "tensor"),
            P("dp", "tensor"),
            P(None, "tensor"),
            P("tensor"),
            P("tensor"),
            P("dp", "tensor"),
            P("dp", "tensor"),
        ),
        check_vma=False,
    )
```

time: 1030 us -> 329 us (0.32)
  waiting for transfers between devices: 600 us -> 216 us
  blocking collectives: 274 us -> 0 us
  matrix products: 63.4 us -> 0 us
  starting transfers between devices: 1.12 us -> 29.1 us
  other arithmetic: 40.2 us -> 13.4 us
  Pallas kernels: 0 us -> 21.1 us
    reduce_scatter x16 -> x2, waiting for transfers between devices: 449 us -> 74.7 us  [scatter_weights(): lax.psum_scatter(grads, 'dp', scatter_dimension=0, tiled=True).astype(F32)]
    psum x4 -> x0, blocking collectives: 161 us -> none  [the longest x1 61 us: body(): kernel_total, bias_total = lax.psum((kernel_grad, bias_grad), 'dp')]
    all_gather x11 -> x0, blocking collectives: 113 us -> none  [the longest x2 45 us: gather_weights(): lax.all_gather(single, 'dp', axis=0, tiled=True)]
    all_gather x5 -> x2, waiting for transfers between devices: 147 us -> 71.9 us  [gather(): return lax.all_gather(jnp.concatenate(pieces, 1), 'dp', axis=0, tiled=True)]
    ppermute x0 -> x23, waiting for transfers between devices: none -> 69.1 us  [the longest x10 40.5 us: swap(): return lax.ppermute(value, 'tensor', [(0, 1), (1, 0)])]
    dot_general x44 -> x0, matrix products: 61.8 us -> none  [the longest x12 17.8 us: left_transposed(): lax.dot_general(left_side, right_side, (((0,), (0,)), ((), ())), preferre...]
    ppermute x0 -> x23, starting transfers between devices: none -> 28.9 us  [the longest x10 15.4 us: swap(): return lax.ppermute(value, 'tensor', [(0, 1), (1, 0)])]
    pallas_call x0 -> x16, Pallas kernels: none -> 21.1 us  [on_chip(): pl.pallas_call(kernel, out_shape=[jax.ShapeDtypeStruct(shape, kind) for s...]
  transfers between devices with their start and end apart: 21 -> 27, of which waited for: 18 -> 26; matrix products, arithmetic and copies ran while one was open for 4% -> 7% of each run, Pallas kernels for 0% -> 3%
where the time goes in v1:
time: 329 us; the launch traced here: 327 us
  waiting for transfers between devices  216 us (66%)
  local copies, waits for them, and re-layouts  33.8 us (10%)
  starting transfers between devices  29.1 us (9%)
  Pallas kernels  21.1 us (6%)
  between operations  14.3 us (4%)
  other arithmetic  13.4 us (4%)
    reduce_scatter x2, waiting for transfers between devices, scatter_weights(): lax.psum_scatter(grads, 'dp', scatter_dimension=0, tiled=True).astype(F32)  74.7 us
    all_gather x2, waiting for transfers between devices, gather(): return lax.all_gather(jnp.concatenate(pieces, 1), 'dp', axis=0, tiled=True)  71.9 us
    ppermute x10, waiting for transfers between devices, swap(): return lax.ppermute(value, 'tensor', [(0, 1), (1, 0)])  40.5 us
    ppermute x13, waiting for transfers between devices, sum_over(): lax.ppermute(value, axis, [(k, k ^ step) for k in range(size)])  28.6 us
    unnamed x105, local copies, waits for them, and re-layouts  22.7 us
    pallas_call x16, Pallas kernels, on_chip(): pl.pallas_call(kernel, out_shape=[jax.ShapeDtypeStruct(shape, kind) for s...  21.1 us
    ppermute x10, starting transfers between devices, swap(): return lax.ppermute(value, 'tensor', [(0, 1), (1, 0)])  15.4 us
    ppermute x13, starting transfers between devices, sum_over(): lax.ppermute(value, axis, [(k, k ^ step) for k in range(size)])  13.5 us
  transfers between devices with their start and end apart: 27, of which 26 were waited for; matrix products, arithmetic and copies ran while one was open for 7% of the time, Pallas kernels for 3%

profile of v1, /device:TPU:0, one launch (start us, length us, event | category | flops | bytes accessed | tf_op | source)
XLA Modules:
  0.0 327.5 jit_solution(7232135046145578095)
XLA Ops:
  7.2 1.5 pad_maximum_fusion.4
  17.1 3.0 collective-permute-start
  20.2 2.2 multiply_sine_fusion
  22.5 2.2 collective-permute-done
  24.6 2.0 collective-permute-done.9
  26.6 1.7 broadcast_select_fusion.1
  28.3 26.5 %all-gather.3.cloned.1.call-done.refs_2_.refs_6_ = bf16[512,2048]{1,0:T(8,128)(2,1)} async-done(((bf16[32,2048]{1,0:T(8,128)(2,1)}), bf16[512,2048]{1,0:T(8,128)(2,1)}) %all-gather.3.cloned.1.call-update) | async-done | bytes 2097168 | tf_op jit(solution)/shard_map/all_gather | solution.py:672
  54.9 1.6 copy-done
  57.4 1.0 copy-done.3
  60.0 1.5 collective-permute-start.1
  61.6 45.4 %all-gather.5.cloned.1.call-done = bf16[512,4096]{1,0:T(8,128)(2,1)} async-done(((bf16[32,4096]{1,0:T(8,128)(2,1)}), bf16[512,4096]{1,0:T(8,128)(2,1)}) %all-gather.5.cloned.1.call-update) | async-done | bytes 4194320 | tf_op jit(solution)/shard_map/all_gather | solution.py:672
  107.0 1.6 slice.124.refs_1_.refs_4_.refs_5_
  109.6 3.3 attention_forward.1
  114.2 1.5 collective-permute-start.2
  115.8 6.9 %collective-permute-done.2.refs_2_ = bf16[256,512]{1,0:T(8,128)(2,1)S(1)} collective-permute-done((bf16[256,512]{1,0:T(8,128)(2,1)S(1)}, bf16[256,512]{1,0:T(8,128)(2,1)S(1)}, u32[]{:S(2)}, u32[]{:S(2)}) %collective-permute-start.2) | collective-permute-done | bytes 262176 | tf_op jit(solution)/shard_map/ppermute | solution.py:83
  122.7 1.8 conv_forward.1
  124.6 1.1 collective-permute-done.3
  126.3 3.0 collective-permute-done.4
  129.3 1.5 collective-permute-start.5
  130.8 2.1 collective-permute-done.5
  132.9 1.8 collective-permute-start.6
  134.8 2.7 collective-permute-done.6
  137.7 1.5 collective-permute-start.7
  139.5 5.3 %collective-permute-done.7.refs_2_ = bf16[256,512]{1,0:T(8,128)(2,1)S(1)} collective-permute-done((bf16[256,512]{1,0:T(8,128)(2,1)S(1)}, bf16[256,512]{1,0:T(8,128)(2,1)S(1)}, u32[]{:S(2)}, u32[]{:S(2)}) %collective-permute-start.7) | collective-permute-done | bytes 262176 | tf_op jit(solution)/shard_map/ppermute | solution.py:83
  144.8 1.0 second_forward.1
  145.8 1.6 collective-permute-start.8
  147.4 6.4 %collective-permute-done.8.refs_2_ = bf16[256,512]{1,0:T(8,128)(2,1)S(1)} collective-permute-done((bf16[256,512]{1,0:T(8,128)(2,1)S(1)}, bf16[256,512]{1,0:T(8,128)(2,1)S(1)}, u32[]{:S(2)}, u32[]{:S(2)}) %collective-permute-start.8) | collective-permute-done | bytes 262176 | tf_op jit(solution)/shard_map/ppermute | solution.py:83
  153.8 1.3 second_back.1
  155.1 1.6 collective-permute-start.10
  156.7 4.9 %collective-permute-done.10.refs_2_ = bf16[256,512]{1,0:T(8,128)(2,1)S(1)} collective-permute-done((bf16[256,512]{1,0:T(8,128)(2,1)S(1)}, bf16[256,512]{1,0:T(8,128)(2,1)S(1)}, u32[]{:S(2)}, u32[]{:S(2)}) %collective-permute-start.10) | collective-permute-done | bytes 262176 | tf_op jit(solution)/shard_map/ppermute | solution.py:83
  163.0 1.2 collective-permute-done.11
  164.7 3.0 collective-permute-done.12
  167.7 1.5 collective-permute-start.13
  169.2 2.1 collective-permute-done.13
  171.3 1.8 collective-permute-start.14
  173.8 1.9 collective-permute-done.14
  175.8 1.6 conv_backward.1
  178.1 2.1 conv_weight_grads.1
  180.2 1.8 pad_maximum_fusion.1
  182.1 1.6 collective-permute-start.15
  183.6 5.1 %collective-permute-done.15.refs_2_ = bf16[256,512]{1,0:T(8,128)(2,1)S(1)} collective-permute-done((bf16[256,512]{1,0:T(8,128)(2,1)}, bf16[256,512]{1,0:T(8,128)(2,1)S(1)}, u32[]{:S(2)}, u32[]{:S(2)}) %collective-permute-start.15) | collective-permute-done | bytes 262176 | tf_op jit(solution)/shard_map/ppermute | solution.py:83
  188.7 1.3 copy-done.6
  190.0 1.1 copy-done.10
  195.7 3.6 %attention_back.1 = (f32[256,512]{1,0:T(8,128)S(1)}, bf16[256,512]{1,0:T(8,128)(2,1)S(1)}, bf16[256,768]{1,0:T(8,128)(2,1)S(1)}, bf16[512,256]{1,0:T(8,128)(2,1)...) custom-call(f32[256,512]{1,0:T(8,128)S(1)} %copy-done.10, ...), custom_call_target="tpu_custom_call" | custom-call | flops 300000000 | bytes 6436864 | tf_op jit(solution)/shard_map/attention_back/pallas_call | solution.py:70
  199.4 1.5 collective-permute-start.16
  201.5 4.3 %collective-permute-done.16.refs_2_ = bf16[256,512]{1,0:T(8,128)(2,1)S(1)} collective-permute-done((bf16[256,512]{1,0:T(8,128)(2,1)S(1)}, bf16[256,512]{1,0:T(8,128)(2,1)S(1)}, u32[]{:S(2)}, u32[]{:S(2)}) %collective-permute-start.16) | collective-permute-done | bytes 262176 | tf_op jit(solution)/shard_map/ppermute | solution.py:83
  205.8 1.2 first_back.1
  207.8 2.0 pad_maximum_fusion
  210.6 1.5 collective-permute-start.17
  212.2 3.5 %collective-permute-done.17.refs_2_ = bf16[128,512]{1,0:T(8,128)(2,1)S(1)} collective-permute-done((bf16[128,512]{1,0:T(8,128)(2,1)S(1)}, bf16[128,512]{1,0:T(8,128)(2,1)S(1)}, u32[]{:S(2)}, u32[]{:S(2)}) %collective-permute-start.17) | collective-permute-done | bytes 131104 | tf_op jit(solution)/shard_map/ppermute | solution.py:83
  215.7 1.0 input_back.1
  216.8 1.2 collective-permute-done.18
  218.7 3.4 %collective-permute-done.19 = f32[86,128]{1,0:T(8,128)S(1)} collective-permute-done((f32[86,128]{1,0:T(8,128)S(1)}, f32[86,128]{1,0:T(8,128)S(1)}, u32[]{:S(2)}, u32[]{:S(2)}) %collective-permute-start.19) | collective-permute-done | bytes 44064 | tf_op jit(solution)/shard_map/ppermute | solution.py:98
  222.2 1.5 collective-permute-start.20
  223.7 3.5 %collective-permute-done.20 = f32[86,128]{1,0:T(8,128)S(1)} collective-permute-done((f32[86,128]{1,0:T(8,128)S(1)}, f32[86,128]{1,0:T(8,128)S(1)}, u32[]{:S(2)}, u32[]{:S(2)}) %collective-permute-start.20) | collective-permute-done | bytes 44064 | tf_op jit(solution)/shard_map/ppermute | solution.py:98
  227.2 1.8 collective-permute-start.21
  229.7 3.0 collective-permute-done.21
  232.7 1.6 collective-permute-start.22
  237.1 8.9 %reduce-scatter.5.cloned.1.call-done = bf16[32,2816]{1,0:T(8,128)(2,1)} async-done(((bf16[512,2816]{1,0:T(8,128)(2,1)}), bf16[32,2816]{1,0:T(8,128)(2,1)}) %reduce-scatter.5.cloned.1.call-update) | async-done | bytes 180240 | tf_op jit(solution)/shard_map/reduce_scatter | solution.py:637
  246.9 1.4 slice.138
  249.0 1.6 fusion.2
  250.5 65.8 %reduce-scatter.3.cloned.1.call-done = bf16[32,3328]{1,0:T(8,128)(2,1)} async-done(((bf16[512,3328]{1,0:T(8,128)(2,1)}), bf16[32,3328]{1,0:T(8,128)(2,1)}) %reduce-scatter.3.cloned.1.call-update) | async-done | bytes 213008 | tf_op jit(solution)/shard_map/reduce_scatter | solution.py:637
  318.0 1.6 fusion.1
  319.6 1.3 slice.134
  (173 shorter events, 32.5 us)
Async XLA Ops:
  7.2 47.7 %copy-start.2 = (f32[5,512]{1,0:T(8,128)S(1)}, f32[5,512]{1,0:T(8,128)}, u32[]{:S(2)}) copy-start(f32[5,512]{1,0:T(8,128)} %refs_4_.5) | copy-start | bytes 30724
  7.2 47.7 %all-gather.3.cloned.1.call-start = ((), (), s32[]{:S(2)}) async-start(), calls=%async_computation.2 | async-start | bytes 2228224 | tf_op jit(solution)/shard_map/all_gather | solution.py:672
  8.8 98.2 %all-gather.5.cloned.1.call-start = ((), (), s32[]{:S(2)}) async-start(), calls=%async_computation.3 | async-start | bytes 4456448 | tf_op jit(solution)/shard_map/all_gather | solution.py:672
  17.0 229.0 %reduce-scatter.5.cloned.1.call-start = ((), (), s32[]{:S(2)}) async-start(), calls=%async_computation.5 | async-start | bytes 3063808 | tf_op jit(solution)/shard_map/reduce_scatter | solution.py:637
  17.1 7.6 %collective-permute-start = (bf16[128,512]{1,0:T(8,128)(2,1)}, bf16[128,512]{1,0:T(8,128)(2,1)S(1)}, u32[]{:S(2)}, u32[]{:S(2)}) collective-permute-start(bf16[128,512]{1,0:T(8,128)(2,1)} %refs_3_.7), channel_id=1, source_target_pairs={{0,1},{1,0},{2,3},{3,2},{4,5},{5,4},{6,7},{7,6},{8,9},{9,8},{10,11... | collective-permute-start | bytes 393224 | tf_op jit(solution)/shard_map/ppermute | solution.py:83
  20.1 6.5 %collective-permute-start.9 = (bf16[128,512]{1,0:T(8,128)(2,1)}, bf16[128,512]{1,0:T(8,128)(2,1)S(1)}, u32[]{:S(2)}, u32[]{:S(2)}) collective-permute-start(bf16[128,512]{1,0:T(8,128)(2,1)} %param.29), channel_id=1, source_target_pairs={{0,1},{1,0},{2,3},{3,2},{4,5},{5,4},{6,7},{7,6},{8,9},{9,8},{10,11... | collective-permute-start | bytes 393224 | tf_op jit(solution)/shard_map/ppermute | solution.py:83
  54.9 1.6 copy-start
  57.4 1.0 copy-start.3
  58.5 0.8 copy-start.7
  60.0 48.9 %collective-permute-start.1 = (bf16[256,512]{1,0:T(8,128)(2,1)S(1)}, bf16[256,512]{1,0:T(8,128)(2,1)S(1)}, u32[]{:S(2)}, u32[]{:S(2)}) collective-permute-start(bf16[256,512]{1,0:T(8,128)(2,1)S(1)} %get-tuple-element.71.refs_1_), channel_id=1, source_target_pairs={{0,1},{1,0},{2,3},{3,2},{4,5},{5,4},{6,7},{7,6},{8,9},{9,8},{10,11... | collective-permute-start | bytes 786440 | tf_op jit(solution)/shard_map/ppermute | solution.py:83
  107.0 8.7 %copy-start.42 = (bf16[512,4096]{1,0:T(8,128)(2,1)S(1)}, bf16[512,4096]{1,0:T(8,128)(2,1)}, u32[]{:S(2)}) copy-start(bf16[512,4096]{1,0:T(8,128)(2,1)} %all-gather.5.cloned.1.call-done) | copy-start | bytes 12582916
  108.5 14.1 %copy-start.18 = (f32[31,256]{1,0:T(8,128)S(1)}, f32[31,256]{1,0:T(8,128)}, u32[]{:S(2)}) copy-start(f32[31,256]{1,0:T(8,128)} %refs_8_.1) | copy-start | bytes 95236
  109.6 25.2 %copy-start.46 = (f32[256]{0:T(256)S(1)}, f32[256]{0:T(256)}, u32[]{:S(2)}) copy-start(f32[256]{0:T(256)} %param.26) | copy-start | bytes 3076
  109.6 25.2 %copy-start.47 = (f32[256]{0:T(256)S(1)}, f32[256]{0:T(256)}, u32[]{:S(2)}) copy-start(f32[256]{0:T(256)} %param.25) | copy-start | bytes 3076
  114.1 8.5 %copy-start.19 = (bf16[256,256]{1,0:T(8,128)(2,1)}, bf16[256,256]{1,0:T(8,128)(2,1)S(1)}, u32[]{:S(2)}) copy-start(bf16[256,256]{1,0:T(8,128)(2,1)S(1)} %get-tuple-element.90.refs_7_) | copy-start | bytes 393220
  114.1 23.3 %copy-start.25 = (bf16[256,256]{1,0:T(8,128)(2,1)}, bf16[256,256]{1,0:T(8,128)(2,1)S(1)}, u32[]{:S(2)}) copy-start(bf16[256,256]{1,0:T(8,128)(2,1)S(1)} %get-tuple-element.93.refs_10_) | copy-start | bytes 393220
  114.1 25.4 %copy-start.5 = (f32[4,256,256]{2,1,0:T(8,128)}, f32[4,256,256]{2,1,0:T(8,128)S(1)}, u32[]{:S(2)}) copy-start(f32[4,256,256]{2,1,0:T(8,128)S(1)} %get-tuple-element.94.refs_11_) | copy-start | bytes 3145732
  114.1 25.4 %copy-start.14 = (bf16[256,512]{1,0:T(8,128)(2,1)}, bf16[256,512]{1,0:T(8,128)(2,1)S(1)}, u32[]{:S(2)}) copy-start(bf16[256,512]{1,0:T(8,128)(2,1)S(1)} %get-tuple-element.113.refs_0_) | copy-start | bytes 786436
  114.2 8.5 %collective-permute-start.2 = (bf16[256,512]{1,0:T(8,128)(2,1)S(1)}, bf16[256,512]{1,0:T(8,128)(2,1)S(1)}, u32[]{:S(2)}, u32[]{:S(2)}) collective-permute-start(bf16[256,512]{1,0:T(8,128)(2,1)S(1)} %get-tuple-element.73.refs_1_), channel_id=1, source_target_pairs={{0,1},{1,0},{2,3},{3,2},{4,5},{5,4},{6,7},{7,6},{8,9},{9,8},{10,11... | collective-permute-start | bytes 786440 | tf_op jit(solution)/shard_map/ppermute | solution.py:83
  124.5 1.2 collective-permute-start.3
  125.7 3.6 %collective-permute-start.4 = (f32[2,256]{1,0:T(2,128)S(1)}, f32[2,256]{1,0:T(2,128)S(1)}, u32[]{:S(2)}, u32[]{:S(2)}) collective-permute-start(f32[2,256]{1,0:T(2,128)S(1)} %add.59), channel_id=1, source_target_pairs={{0,4},{2,6},{4,0},{6,2},{8,12},{10,14},{12,8},{14,10},{16,20},{18,... | collective-permute-start | bytes 6152 | tf_op jit(solution)/shard_map/ppermute | solution.py:98
  129.3 3.6 %collective-permute-start.5 = (f32[2,256]{1,0:T(2,128)S(1)}, f32[2,256]{1,0:T(2,128)S(1)}, u32[]{:S(2)}, u32[]{:S(2)}) collective-permute-start(f32[2,256]{1,0:T(2,128)S(1)} %add.60), channel_id=1, source_target_pairs={{0,8},{2,10},{4,12},{6,14},{8,0},{10,2},{12,4},{14,6},{16,24},{18,... | collective-permute-start | bytes 6152 | tf_op jit(solution)/shard_map/ppermute | solution.py:98
  132.9 4.5 %collective-permute-start.6 = (f32[2,256]{1,0:T(2,128)S(1)}, f32[2,256]{1,0:T(2,128)S(1)}, u32[]{:S(2)}, u32[]{:S(2)}) collective-permute-start(f32[2,256]{1,0:T(2,128)S(1)} %add.61), channel_id=1, source_target_pairs={{0,16},{2,18},{4,20},{6,22},{8,24},{10,26},{12,28},{14,30},{16,0},... | collective-permute-start | bytes 6152 | tf_op jit(solution)/shard_map/ppermute | solution.py:98
  137.7 9.7 %copy-start.43 = (bf16[128,512]{1,0:T(8,128)(2,1)S(1)}, bf16[128,512]{1,0:T(8,128)(2,1)}, u32[]{:S(2)}) copy-start(bf16[128,512]{1,0:T(8,128)(2,1)} %get-tuple-element.135) | copy-start | bytes 393220
  137.7 9.7 %copy-start.44 = (bf16[128,512]{1,0:T(8,128)(2,1)S(1)}, bf16[128,512]{1,0:T(8,128)(2,1)}, u32[]{:S(2)}) copy-start(bf16[128,512]{1,0:T(8,128)(2,1)} %get-tuple-element.136) | copy-start | bytes 393220
  137.7 7.1 %collective-permute-start.7 = (bf16[256,512]{1,0:T(8,128)(2,1)S(1)}, bf16[256,512]{1,0:T(8,128)(2,1)S(1)}, u32[]{:S(2)}, u32[]{:S(2)}) collective-permute-start(bf16[256,512]{1,0:T(8,128)(2,1)S(1)} %get-tuple-element.77.refs_1_), channel_id=1, source_target_pairs={{0,1},{1,0},{2,3},{3,2},{4,5},{5,4},{6,7},{7,6},{8,9},{9,8},{10,11... | collective-permute-start | bytes 786440 | tf_op jit(solution)/shard_map/ppermute | solution.py:83
  145.8 8.0 %collective-permute-start.8 = (bf16[256,512]{1,0:T(8,128)(2,1)S(1)}, bf16[256,512]{1,0:T(8,128)(2,1)S(1)}, u32[]{:S(2)}, u32[]{:S(2)}) collective-permute-start(bf16[256,512]{1,0:T(8,128)(2,1)S(1)} %get-tuple-element.79.refs_1_), channel_id=1, source_target_pairs={{0,1},{1,0},{2,3},{3,2},{4,5},{5,4},{6,7},{7,6},{8,9},{9,8},{10,11... | collective-permute-start | bytes 786440 | tf_op jit(solution)/shard_map/ppermute | solution.py:83
  155.1 18.8 %copy-start.27 = (bf16[256,512]{1,0:T(8,128)(2,1)}, bf16[256,512]{1,0:T(8,128)(2,1)S(1)}, u32[]{:S(2)}) copy-start(bf16[256,512]{1,0:T(8,128)(2,1)S(1)} %get-tuple-element.81) | copy-start | bytes 786436
  155.1 18.8 %copy-start.33 = (f32[1,512]{1,0:T(1,128)}, f32[1,512]{1,0:T(1,128)S(1)}, u32[]{:S(2)}) copy-start(f32[1,512]{1,0:T(1,128)S(1)} %get-tuple-element.105) | copy-start | bytes 6148
  155.1 6.4 %collective-permute-start.10 = (bf16[256,512]{1,0:T(8,128)(2,1)S(1)}, bf16[256,512]{1,0:T(8,128)(2,1)S(1)}, u32[]{:S(2)}, u32[]{:S(2)}) collective-permute-start(bf16[256,512]{1,0:T(8,128)(2,1)S(1)} %get-tuple-element.83.refs_1_), channel_id=1, source_target_pairs={{0,1},{1,0},{2,3},{3,2},{4,5},{5,4},{6,7},{7,6},{8,9},{9,8},{10,11... | collective-permute-start | bytes 786440 | tf_op jit(solution)/shard_map/ppermute | solution.py:83
  162.1 0.8 copy-start.9
  162.9 15.1 %copy-start.35 = (f32[1,512]{1,0:T(1,128)}, f32[1,512]{1,0:T(1,128)S(1)}, u32[]{:S(2)}) copy-start(f32[1,512]{1,0:T(1,128)S(1)} %get-tuple-element.104) | copy-start | bytes 6148
  162.9 1.2 collective-permute-start.11
  164.1 3.6 %collective-permute-start.12 = (f32[2,256]{1,0:T(2,128)S(1)}, f32[2,256]{1,0:T(2,128)S(1)}, u32[]{:S(2)}, u32[]{:S(2)}) collective-permute-start(f32[2,256]{1,0:T(2,128)S(1)} %add.64), channel_id=1, source_target_pairs={{0,4},{2,6},{4,0},{6,2},{8,12},{10,14},{12,8},{14,10},{16,20},{18,... | collective-permute-start | bytes 6152 | tf_op jit(solution)/shard_map/ppermute | solution.py:98
  167.7 3.6 %collective-permute-start.13 = (f32[2,256]{1,0:T(2,128)S(1)}, f32[2,256]{1,0:T(2,128)S(1)}, u32[]{:S(2)}, u32[]{:S(2)}) collective-permute-start(f32[2,256]{1,0:T(2,128)S(1)} %add.65), channel_id=1, source_target_pairs={{0,8},{2,10},{4,12},{6,14},{8,0},{10,2},{12,4},{14,6},{16,24},{18,... | collective-permute-start | bytes 6152 | tf_op jit(solution)/shard_map/ppermute | solution.py:98
  171.3 4.5 %collective-permute-start.14 = (f32[2,256]{1,0:T(2,128)S(1)}, f32[2,256]{1,0:T(2,128)S(1)}, u32[]{:S(2)}, u32[]{:S(2)}) collective-permute-start(f32[2,256]{1,0:T(2,128)S(1)} %add.66), channel_id=1, source_target_pairs={{0,16},{2,18},{4,20},{6,22},{8,24},{10,26},{12,28},{14,30},{16,0},... | collective-permute-start | bytes 6152 | tf_op jit(solution)/shard_map/ppermute | solution.py:98
  175.8 4.4 %copy-start.31 = (f32[2,256]{1,0:T(2,128)}, f32[2,256]{1,0:T(2,128)S(1)}, u32[]{:S(2)}) copy-start(f32[2,256]{1,0:T(2,128)S(1)} %add.67.refs_1_) | copy-start | bytes 6148
  180.2 1.8 copy-start.29
  182.0 18.9 %copy-start.15 = (bf16[256,512]{1,0:T(8,128)(2,1)S(1)}, bf16[256,512]{1,0:T(8,128)(2,1)}, u32[]{:S(2)}) copy-start(bf16[256,512]{1,0:T(8,128)(2,1)} %copy-done.14) | copy-start | bytes 786436
  182.0 134.4 %reduce-scatter.3.cloned.1.call-start = ((), (), s32[]{:S(2)}) async-start(), calls=%async_computation.4 | async-start | bytes 3620864 | tf_op jit(solution)/shard_map/reduce_scatter | solution.py:637
  182.1 6.6 %collective-permute-start.15 = (bf16[256,512]{1,0:T(8,128)(2,1)}, bf16[256,512]{1,0:T(8,128)(2,1)S(1)}, u32[]{:S(2)}, u32[]{:S(2)}) collective-permute-start(bf16[256,512]{1,0:T(8,128)(2,1)} %copy-done.16), channel_id=1, source_target_pairs={{0,1},{1,0},{2,3},{3,2},{4,5},{5,4},{6,7},{7,6},{8,9},{9,8},{10,11... | collective-permute-start | bytes 786440 | tf_op jit(solution)/shard_map/ppermute | solution.py:83
  188.7 1.3 copy-start.6
  190.0 1.1 copy-start.10
  191.0 1.0 copy-start.17
  192.0 0.9 copy-start.20
  192.9 0.9 copy-start.22
  193.8 0.9 copy-start.24
  194.8 0.9 copy-start.26
  195.7 10.1 %copy-start.1 = (bf16[512,2048]{1,0:T(8,128)(2,1)S(1)}, bf16[512,2048]{1,0:T(8,128)(2,1)}, u32[]{:S(2)}) copy-start(bf16[512,2048]{1,0:T(8,128)(2,1)} %all-gather.3.cloned.1.call-done.refs_2_.refs_6_) | copy-start | bytes 6291460
  195.7 10.1 %copy-start.4 = (f32[256,1024]{1,0:T(8,128)S(1)}, f32[256,1024]{1,0:T(8,128)}, u32[]{:S(2)}) copy-start(f32[256,1024]{1,0:T(8,128)} %copy-done.3) | copy-start | bytes 3145732
  199.3 7.7 %copy-start.37 = (f32[1,512]{1,0:T(1,128)}, f32[1,512]{1,0:T(1,128)S(1)}, u32[]{:S(2)}) copy-start(f32[1,512]{1,0:T(1,128)S(1)} %get-tuple-element.103) | copy-start | bytes 6148
  199.3 7.7 %copy-start.39 = (f32[2,256]{1,0:T(2,128)}, f32[2,256]{1,0:T(2,128)S(1)}, u32[]{:S(2)}) copy-start(f32[2,256]{1,0:T(2,128)S(1)} %get-tuple-element.112) | copy-start | bytes 6148
  199.4 6.4 %collective-permute-start.16 = (bf16[256,512]{1,0:T(8,128)(2,1)S(1)}, bf16[256,512]{1,0:T(8,128)(2,1)S(1)}, u32[]{:S(2)}, u32[]{:S(2)}) collective-permute-start(bf16[256,512]{1,0:T(8,128)(2,1)S(1)} %get-tuple-element.96.refs_1_), channel_id=1, source_target_pairs={{0,1},{1,0},{2,3},{3,2},{4,5},{5,4},{6,7},{7,6},{8,9},{9,8},{10,11... | collective-permute-start | bytes 786440 | tf_op jit(solution)/shard_map/ppermute | solution.py:83
  201.5 5.5 %copy-start.8 = (bf16[256,1024]{1,0:T(8,128)(2,1)S(1)}, bf16[256,1024]{1,0:T(8,128)(2,1)}, u32[]{:S(2)}) copy-start(bf16[256,1024]{1,0:T(8,128)(2,1)} %copy-done.7) | copy-start | bytes 1572868
  201.5 5.5 %copy-start.13 = (bf16[256,512]{1,0:T(8,128)(2,1)S(1)}, bf16[256,512]{1,0:T(8,128)(2,1)}, u32[]{:S(2)}) copy-start(bf16[256,512]{1,0:T(8,128)(2,1)} %copy-done.12) | copy-start | bytes 786436
  209.8 5.9 %copy-start.11 = (bf16[128,512]{1,0:T(8,128)(2,1)S(1)}, bf16[128,512]{1,0:T(8,128)(2,1)}, u32[]{:S(2)}) copy-start(bf16[128,512]{1,0:T(8,128)(2,1)} %refs_3_.7) | copy-start | bytes 393220
  209.8 19.2 %copy-start.28 = (bf16[256,512]{1,0:T(8,128)(2,1)S(1)}, bf16[256,512]{1,0:T(8,128)(2,1)}, u32[]{:S(2)}) copy-start(bf16[256,512]{1,0:T(8,128)(2,1)} %copy-done.27) | copy-start | bytes 786436
  209.8 24.5 %copy-start.32 = (f32[2,256]{1,0:T(2,128)S(1)}, f32[2,256]{1,0:T(2,128)}, u32[]{:S(2)}) copy-start(f32[2,256]{1,0:T(2,128)} %copy-done.31) | copy-start | bytes 6148
  210.6 5.0 %collective-permute-start.17 = (bf16[128,512]{1,0:T(8,128)(2,1)S(1)}, bf16[128,512]{1,0:T(8,128)(2,1)S(1)}, u32[]{:S(2)}, u32[]{:S(2)}) collective-permute-start(bf16[128,512]{1,0:T(8,128)(2,1)S(1)} %get-tuple-element.133), channel_id=1, source_target_pairs={{0,1},{1,0},{2,3},{3,2},{4,5},{5,4},{6,7},{7,6},{8,9},{9,8},{10,11... | collective-permute-start | bytes 393224 | tf_op jit(solution)/shard_map/ppermute | solution.py:83
  216.7 1.3 collective-permute-start.18
  218.0 4.1 %collective-permute-start.19 = (f32[86,128]{1,0:T(8,128)S(1)}, f32[86,128]{1,0:T(8,128)S(1)}, u32[]{:S(2)}, u32[]{:S(2)}) collective-permute-start(f32[86,128]{1,0:T(8,128)S(1)} %fusion.4), channel_id=1, source_target_pairs={{0,4},{2,6},{4,0},{6,2},{8,12},{10,14},{12,8},{14,10},{16,20},{18,... | collective-permute-start | bytes 132104 | tf_op jit(solution)/shard_map/ppermute | solution.py:98
  222.2 5.0 %collective-permute-start.20 = (f32[86,128]{1,0:T(8,128)S(1)}, f32[86,128]{1,0:T(8,128)S(1)}, u32[]{:S(2)}, u32[]{:S(2)}) collective-permute-start(f32[86,128]{1,0:T(8,128)S(1)} %add.70), channel_id=1, source_target_pairs={{0,8},{2,10},{4,12},{6,14},{8,0},{10,2},{12,4},{14,6},{16,24},{18,... | collective-permute-start | bytes 132104 | tf_op jit(solution)/shard_map/ppermute | solution.py:98
  227.2 5.5 %collective-permute-start.21 = (f32[86,128]{1,0:T(8,128)S(1)}, f32[86,128]{1,0:T(8,128)S(1)}, u32[]{:S(2)}, u32[]{:S(2)}) collective-permute-start(f32[86,128]{1,0:T(8,128)S(1)} %add.71), channel_id=1, source_target_pairs={{0,16},{2,18},{4,20},{6,22},{8,24},{10,26},{12,28},{14,30},{16,0},... | collective-permute-start | bytes 132104 | tf_op jit(solution)/shard_map/ppermute | solution.py:98
  232.7 3.8 %collective-permute-start.22 = (f32[5,512]{1,0:T(8,128)S(1)}, f32[5,512]{1,0:T(8,128)S(1)}, u32[]{:S(2)}, u32[]{:S(2)}) collective-permute-start(f32[5,512]{1,0:T(8,128)S(1)} %reshape.64), channel_id=1, source_target_pairs={{0,1},{1,0},{2,3},{3,2},{4,5},{5,4},{6,7},{7,6},{8,9},{9,8},{10,11... | collective-permute-start | bytes 30728 | tf_op jit(solution)/shard_map/ppermute | solution.py:98
  (11 other events, 7.9 us)
Sparse Core Ops, SparseCore 0:
  10.8 44.0 all-gather.2
  57.6 49.3 all-gather.4
  182.1 63.8 reduce-scatter.4
  250.2 66.1 reduce-scatter.2

commit v2 on v1

--- a/solution.py
+++ b/solution.py
@@ -89,15 +89,131 @@
     return jnp.concatenate([jnp.where(first, own, other), jnp.where(first, other, own)], 0)
 
 
+def own_half(value):
+    half = value.shape[0] // 2
+    return jnp.where(lax.axis_index("tensor") == 0, value[:half], value[half:])
+
+
+def other_half(value):
+    half = value.shape[0] // 2
+    return jnp.where(lax.axis_index("tensor") == 0, value[half:], value[:half])
+
+
+def shift(value, axis, mask):
+    return lax.ppermute(value, axis, [(k, k ^ mask) for k in range(lax.axis_size(axis))])
+
+
 def sum_over(value, axis):
     size = lax.axis_size(axis)
     if size & (size - 1):
         return lax.psum(value, axis)
     step = 1
     while step < size:
-        value = value + lax.ppermute(value, axis, [(k, k ^ step) for k in range(size)])
-        step *= 2
+        if step >= 4 and step * 4 <= size:
+            near, far, both = (shift(value, axis, step * times) for times in (1, 2, 3))
+            value = (value + near) + (far + both)
+            step *= 4
+        else:
+            value = value + shift(value, axis, step)
+            step *= 2
     return value
+
+
+GATHER_ORDERS = ((8, 4, 2, 1), (8, 2, 4, 1))
+SCATTER_ORDERS = ((1, 2, 4, 8), (1, 4, 2, 8))
+
+
+def doubling():
+    return lax.axis_size("dp") == 16
+
+
+def distances(order):
+    blocks = [0]
+    for mask in order:
+        blocks = blocks + [block ^ mask for block in blocks]
+    return blocks
+
+
+def halving(order):
+    return distances(order[::-1])
+
+
+def gather_stage(pair, stage):
+    return tuple(
+        jnp.concatenate([value, shift(value, "dp", order[stage])], 0)
+        for value, order in zip(pair, GATHER_ORDERS)
+    )
+
+
+def gather_last(pair):
+    return tuple((value, shift(value, "dp", 1)) for value in pair)
+
+
+def tie(values, *others):
+    return lax.optimization_barrier((values, others))[0]
+
+
+def assemble(ref, target_ref, order, half, matrices, first_column):
+    device = lax.axis_index("dp")
+    blocks = distances(order)
+    count = len(blocks) // 2
+    rows = target_ref.shape[0] // len(blocks)
+    columns = ref.shape[1]
+    for place in range(count):
+        owner = device ^ blocks[half * count + place]
+        target = pl.ds(pl.multiple_of(owner * rows, rows), rows)
+        for matrix in range(matrices):
+            start = (place * matrices + matrix) * rows
+            left = first_column + matrix * columns
+            target_ref[target, left : left + columns] = ref[start : start + rows, :]
+
+
+def scatter_split(total_ref, keep_ref, send_ref, order, matrices):
+    device = lax.axis_index("dp")
+    blocks = halving(order)
+    count = len(blocks) // 2
+    rows = total_ref.shape[0] // len(blocks)
+    columns = keep_ref.shape[1]
+    for place, block in enumerate(blocks):
+        source = pl.ds(pl.multiple_of((device ^ block) * rows, rows), rows)
+        for matrix in range(matrices):
+            piece = total_ref[source, matrix * columns : (matrix + 1) * columns]
+            start = ((place % count) * matrices + matrix) * rows
+            if place < count:
+                keep_ref[start : start + rows, :] = piece
+            else:
+                send_ref[start : start + rows, :] = piece.astype(BF16)
+
+
+def scatter_stage(keeps, sends, stage, name):
+    arrived = [
+        shift(send, "dp", order[stage]) for send, order in zip(sends, SCATTER_ORDERS)
+    ]
+    groups = len(keeps)
+    last = stage == len(SCATTER_ORDERS[0]) - 1
+    results = []
+    for keep in keeps:
+        rows, columns = keep.shape
+        if last:
+            results.append(((rows, columns), F32))
+        else:
+            results.append(((rows // 2, columns), F32))
+            results.append(((rows // 2, columns), BF16))
+
+    def body(ins, outs, _):
+        for group in range(groups):
+            total = ins[group][...] + ins[groups + group][...].astype(F32)
+            if last:
+                outs[group][...] = total
+            else:
+                half = total.shape[0] // 2
+                outs[2 * group][...] = total[:half]
+                outs[2 * group + 1][...] = total[half:].astype(BF16)
+
+    values = on_chip(body, name, tuple(keeps) + tuple(arrived), tuple(results), flops=1_000_000)
+    if last:
+        return values, None
+    return values[0::2], values[1::2]
 
 
 def ff_forward_body(row, residual, gain_ref, weight_ref, outs):
@@ -177,7 +293,7 @@
         after = x_ref[...] + 0.5 * (own_ref[...].astype(F32) + other_ref[...].astype(F32))
         normed, factor = norm_parts(after)
         gain = gain_ref[4:5, :]
-        out_ref[...] = (normed * gain).astype(BF16)
+        out_ref[...] = own_half(normed * gain).astype(BF16)
         gradient, gain_grad_ref[...] = norm_back(
             cot_ref[...].astype(F32), normed, factor, gain
         )
@@ -191,7 +307,7 @@
         "second_back",
         (residual, own, other, cotangent, pre, gains, weights),
         (
-            ((rows, width), BF16),
+            ((rows // 2, width), BF16),
             ((rows, width), F32),
             ((rows, width), BF16),
             ((rows, hidden), BF16),
@@ -211,6 +327,52 @@
 
     return on_chip(
         body, name, (entries, grad_pre, branch, hidden), (((width, 2 * half), BF16),)
+    )[0]
+
+
+def ff_weight_split(entries, grad_pre, branch, hidden, name):
+    width = entries.shape[1]
+    half = hidden.shape[1]
+
+    def body(ins, outs, scratch):
+        for group in range(2):
+            scratch[0][...] = left_transposed(ins[2 * group][...], ins[2 * group + 1][...])
+            scatter_split(
+                scratch[0], outs[2 * group], outs[2 * group + 1], SCATTER_ORDERS[group], 1
+            )
+
+    halves = (((width // 2, half), F32), ((width // 2, half), BF16))
+    values = on_chip(
+        body,
+        name,
+        (entries, grad_pre, branch, hidden),
+        halves + halves,
+        scratch=(pltpu.VMEM((width, half), F32),),
+    )
+    return values[0::2], values[1::2]
+
+
+def ff_assemble(pairs, width):
+    columns = pairs[0][0].shape[1]
+
+    def body(ins, outs, _):
+        for group in range(2):
+            for half in range(2):
+                assemble(
+                    ins[2 * group + half],
+                    outs[0],
+                    GATHER_ORDERS[group],
+                    half,
+                    1,
+                    group * columns,
+                )
+
+    return on_chip(
+        body,
+        "first_assemble",
+        pairs[0] + pairs[1],
+        (((width, 2 * columns), BF16),),
+        flops=1_000_000,
     )[0]
 
 
@@ -260,7 +422,7 @@
             mixed.append(matmul(probability.astype(BF16), values[:, part]))
         attended = jnp.concatenate(mixed, 1).astype(BF16)
         mix_ref[...] = attended
-        part_ref[...] = right_transposed(attended, weight_ref[:, 4 * columns :]).astype(BF16)
+        part_ref[...] = right_transposed(attended, weight_ref[:, 4 * columns : 5 * columns]).astype(BF16)
 
     local = ((rows, columns), BF16)
     return on_chip(
@@ -311,7 +473,7 @@
         total_ref[...] = total
         branch = total.astype(BF16)
         branch_ref[...] = branch
-        grad_mixed = matmul(branch, weight_ref[:, 4 * columns :]).astype(BF16)
+        grad_mixed = matmul(branch, weight_ref[:, 4 * columns : 5 * columns]).astype(BF16)
         line = lax.broadcasted_iota(jnp.int32, (rows, rows), 0)
         place = lax.broadcasted_iota(jnp.int32, (rows, rows), 1)
         flip = (line + place == rows - 1).astype(F32).astype(BF16)
@@ -365,24 +527,75 @@
     )
 
 
-def attention_weight_grads(entries, joined, table, table_grad, branch, attended):
+def mixed_assemble(pairs, width):
+    columns = pairs[0][0].shape[1]
+
+    def body(ins, outs, _):
+        for group in range(2):
+            for half in range(2):
+                assemble(
+                    ins[2 * group + half],
+                    outs[0],
+                    GATHER_ORDERS[group],
+                    half,
+                    4,
+                    4 * group * columns,
+                )
+
+    return on_chip(
+        body,
+        "mixed_assemble",
+        pairs[0] + pairs[1],
+        (((width, 8 * columns), BF16),),
+        flops=1_000_000,
+    )[0]
+
+
+def mixed_weight_grads(attention_parts, conv_parts, split):
+    entries, joined, table, table_grad, branch, attended = attention_parts
+    conv_entries, conv_joined, conv_branch, activated = conv_parts
     width = entries.shape[1]
     columns = attended.shape[1]
 
-    def body(ins, outs, _):
-        out_ref = outs[0]
-        out_ref[:, : 3 * columns] = left_transposed(ins[0][...], ins[1][...]).astype(BF16)
-        out_ref[:, 3 * columns : 4 * columns] = left_transposed(ins[2][...], ins[3][...]).astype(
-            BF16
-        )
-        out_ref[:, 4 * columns :] = left_transposed(ins[4][...], ins[5][...]).astype(BF16)
-
-    return on_chip(
-        body,
-        "attention_weight_grads",
-        (entries, joined, table, table_grad, branch, attended),
-        (((width, 5 * columns), BF16),),
-    )[0]
+    def whole(ins, target_ref):
+        target_ref[:, : 3 * columns] = left_transposed(ins[0][...], ins[1][...])
+        target_ref[:, 3 * columns : 4 * columns] = left_transposed(ins[2][...], ins[3][...])
+        target_ref[:, 4 * columns : 5 * columns] = left_transposed(ins[4][...], ins[5][...])
+        target_ref[:, 5 * columns : 7 * columns] = left_transposed(ins[6][...], ins[7][...])
+        target_ref[:, 7 * columns :] = left_transposed(ins[8][...], ins[9][...])
+
+    def body(ins, outs, scratch):
+        if not split:
+            whole(ins, outs[0])
+            return
+        whole(ins, scratch[0])
+        for group in range(2):
+            part = scratch[0].at[:, 4 * group * columns : 4 * (group + 1) * columns]
+            scatter_split(part, outs[2 * group], outs[2 * group + 1], SCATTER_ORDERS[group], 4)
+
+    operands = (
+        entries,
+        joined,
+        table,
+        table_grad,
+        branch,
+        attended,
+        conv_entries,
+        conv_joined,
+        conv_branch,
+        activated,
+    )
+    if not split:
+        return on_chip(body, "mixed_weight_grads", operands, (((width, 8 * columns), F32),))[0]
+    halves = (((2 * width, columns), F32), ((2 * width, columns), BF16))
+    values = on_chip(
+        body,
+        "mixed_weight_grads",
+        operands,
+        halves + halves,
+        scratch=(pltpu.VMEM((width, 8 * columns), F32),),
+    )
+    return values[0::2], values[1::2]
 
 
 PAD = 16
@@ -402,7 +615,7 @@
         normed, _ = norm_parts(after)
         entries = (normed * gain_ref[2:3, :]).astype(BF16)
         c_ref[...] = entries
-        joined = matmul(entries, weight_ref[:, : 2 * columns])
+        joined = matmul(entries, weight_ref[:, 5 * columns : 7 * columns])
         value = joined[:, :columns]
         gate = jax.nn.sigmoid(joined[:, columns:])
         value_ref[...] = value
@@ -444,7 +657,7 @@
         _, _, shifted = batch_norm(conv_ref, sums_ref, batch_ref, token_count)
         activated = (shifted * jax.nn.sigmoid(shifted)).astype(BF16)
         outs[0][...] = activated
-        outs[1][...] = right_transposed(activated, weight_ref[:, 2 * columns :]).astype(BF16)
+        outs[1][...] = right_transposed(activated, weight_ref[:, 7 * columns :]).astype(BF16)
 
     return on_chip(
         body,
@@ -472,7 +685,7 @@
         branch = total.astype(BF16)
         branch_ref[...] = branch
         standard, _, shifted = batch_norm(conv_ref, sums_ref, batch_ref, count)
-        grad_shifted = matmul(branch, weight_ref[:, 2 * columns :]) * swish_slope(
+        grad_shifted = matmul(branch, weight_ref[:, 7 * columns :]) * swish_slope(
             shifted, jax.nn.sigmoid(shifted)
         )
         shifted_ref[...] = grad_shifted
@@ -535,7 +748,7 @@
             [grad_value, grad_value * value_ref[...] * (1.0 - gate_sigma)], 1
         ).astype(BF16)
         joined_ref[...] = joined
-        part_ref[...] = right_transposed(joined, weight_ref[:, : 2 * columns]).astype(BF16)
+        part_ref[...] = right_transposed(joined, weight_ref[:, 5 * columns : 7 * columns]).astype(BF16)
 
     return on_chip(
         body,
@@ -546,34 +759,31 @@
     )
 
 
-def conv_weight_grads(entries, joined, branch, activated, value, gate, grad_conv, taps):
+def tap_gradients(value, gate, grad_conv, taps):
     rows, columns = grad_conv.shape
-    width = entries.shape[1]
     half_taps = (taps - 1) // 2
 
     def body(ins, outs, scratch):
-        e_ref, joined_ref, branch_ref, y_ref, value_ref, gate_ref, grad_ref = ins
-        out_ref, tap_ref = outs
+        value_ref, gate_ref, grad_ref = ins
         padded = scratch[0]
-        out_ref[:, : 2 * columns] = left_transposed(e_ref[...], joined_ref[...]).astype(BF16)
-        out_ref[:, 2 * columns :] = left_transposed(branch_ref[...], y_ref[...]).astype(BF16)
         padded[:PAD, :] = jnp.zeros((PAD, columns), F32)
         padded[PAD + rows :, :] = jnp.zeros((PAD, columns), F32)
         padded[PAD : PAD + rows, :] = value_ref[...] * gate_ref[...]
         grad_conv_value = grad_ref[...]
         for tap in range(taps):
             start = PAD - half_taps + tap
-            tap_ref[tap : tap + 1, :] = jnp.sum(
+            outs[0][tap : tap + 1, :] = jnp.sum(
                 padded[start : start + rows, :] * grad_conv_value, 0, keepdims=True
             )
 
     return on_chip(
         body,
-        "conv_weight_grads",
-        (entries, joined, branch, activated, value, gate, grad_conv),
-        (((width, 3 * columns), BF16), ((taps, columns), F32)),
+        "tap_gradients",
+        (value, gate, grad_conv),
+        (((taps, columns), F32),),
         scratch=(pltpu.VMEM((rows + 2 * PAD, columns), F32),),
-    )
+        flops=10_000_000,
+    )[0]
 
 
 def first_back(gradient, own, other, residual, pre, gains, weights):
@@ -582,24 +792,27 @@
 
     def body(ins, outs, _):
         grad_ref, own_ref, other_ref, x_ref, pre_ref, gain_ref, weight_ref = ins
-        total_ref, branch_ref, slope_ref, part_ref, gain_grad_ref = outs
+        total_ref, branch_ref, slope_ref, keep_ref, send_ref, gain_grad_ref = outs
         normed, factor = norm_parts(x_ref[...])
         passed, gain_grad_ref[...] = norm_back(
             own_ref[...].astype(F32) + other_ref[...].astype(F32), normed, factor, gain_ref[1:2, :]
         )
         total = grad_ref[...] + passed
-        total_ref[...] = total
-        part_ref[...] = ff_back_body(total, pre_ref, weight_ref, branch_ref, slope_ref).astype(BF16)
+        total_ref[...] = own_half(total)
+        part = ff_back_body(total, pre_ref, weight_ref, branch_ref, slope_ref)
+        keep_ref[...] = own_half(part)
+        send_ref[...] = other_half(part).astype(BF16)
 
     return on_chip(
         body,
         "first_back",
         (gradient, own, other, residual, pre, gains, weights),
         (
-            ((rows, width), F32),
+            ((rows // 2, width), F32),
             ((rows, width), BF16),
             ((rows, hidden), BF16),
-            ((rows, width), BF16),
+            ((rows // 2, width), F32),
+            ((rows // 2, width), BF16),
             ((1, width), F32),
         ),
     )
@@ -625,21 +838,17 @@
     )
 
 
-def own_rows(whole, count):
-    return lax.dynamic_slice_in_dim(whole, lax.axis_index("tensor") * count, count, 0)
-
-
-def columns_of(stacked):
-    return [stacked[index] for index in range(stacked.shape[0])]
-
-
-def scatter_weights(grads):
-    return lax.psum_scatter(grads, "dp", scatter_dimension=0, tiled=True).astype(F32)
+def reduce_plain(grads):
+    return lax.psum_scatter(grads.astype(BF16), "dp", scatter_dimension=0, tiled=True).astype(F32)
 
 
 def stacked_columns(pieces, count):
     width = pieces.shape[1] // count
     return jnp.stack([pieces[:, index * width : (index + 1) * width] for index in range(count)])
+
+
+def unstacked(stacked):
+    return [stacked[index] for index in range(stacked.shape[0])]
 
 
 def body(
@@ -659,57 +868,70 @@
     second_out,
     cotangent,
 ):
-    own_count = tokens.shape[0]
     local_heads = HEAD_TOTAL // lax.axis_size("tensor")
-    length = own_count * lax.axis_size("tensor")
+    length = tokens.shape[0] * lax.axis_size("tensor")
     token_count = float(length * lax.axis_size("dp"))
     columns = attention_out.shape[1]
     hidden = first_in.shape[1]
-    table = sinusoid(length, tokens.shape[1]).astype(BF16)
+    width = tokens.shape[1]
+    table = sinusoid(length, width).astype(BF16)
     batch = jnp.stack([batch_scale, batch_shift])
+    split = doubling()
 
     def gather(pieces):
         return lax.all_gather(jnp.concatenate(pieces, 1), "dp", axis=0, tiled=True)
 
-    first_weights = gather([first_in, first_out])
-    rest = gather(
-        columns_of(attention_in)
-        + [attention_out]
-        + columns_of(gated_in)
-        + [pointwise_out, second_in, second_out]
-    )
-    attention_weights = rest[:, : 5 * columns]
-    conv_weights = rest[:, 5 * columns : 8 * columns]
-    second_weights = rest[:, 8 * columns :]
-
     tokens_all = both_halves(tokens)
     cotangent_all = both_halves(cotangent)
 
+    if split:
+        batch_one = (first_in, first_out)
+        batch_two = (
+            attention_in.reshape(-1, columns),
+            jnp.concatenate([attention_out, gated_in.reshape(-1, columns), pointwise_out], 0),
+        )
+        for stage in range(3):
+            batch_one = gather_stage(batch_one, stage)
+            batch_two = gather_stage(tie(batch_two, batch_one), stage)
+        second_pieces = tie((second_in, second_out), batch_one)
+        batch_one = gather_last(batch_one)
+        first_weights = ff_assemble(batch_one, width)
+        batch_two = gather_last(tie(batch_two, batch_one))
+        mixed_weights = mixed_assemble(batch_two, width)
+        second_weights = gather(second_pieces)
+    else:
+        first_weights = gather([first_in, first_out])
+        mixed_weights = gather(
+            unstacked(attention_in) + [attention_out] + unstacked(gated_in) + [pointwise_out]
+        )
+        second_weights = gather([second_in, second_out])
+
     entries1, pre1, hidden1, part1 = first_forward(tokens_all, norm_gains, first_weights)
     other1 = swap(part1)
-    positions = position_forward(table, attention_weights, columns)
+    positions = position_forward(table, mixed_weights, columns)
     after1, entries2, qc, qp, keys, values, prob, attended, part2 = attention_forward(
-        tokens_all, part1, other1, norm_gains, attention_weights, positions, head_biases, local_heads
+        tokens_all, part1, other1, norm_gains, mixed_weights, positions, head_biases, local_heads
     )
     other2 = swap(part2)
     after2, entries3, value_pre, gate, convolved, sums = conv_forward(
-        after1, part2, other2, norm_gains, conv_weights, depth_kernel
+        after1, part2, other2, norm_gains, mixed_weights, depth_kernel
     )
     sums = sum_over(sums, "dp")
-    activated, part3 = norm_forward(convolved, sums, batch, conv_weights, token_count)
+    activated, part3 = norm_forward(convolved, sums, batch, mixed_weights, token_count)
     other3 = swap(part3)
     after3, entries4, pre4, hidden4, part4 = second_forward(
         after2, part3, other3, norm_gains, second_weights
     )
     other4 = swap(part4)
-    out_all, grad4, branch4, slope4, part5, gain5 = second_back(
+    block_out, grad4, branch4, slope4, part5, gain5 = second_back(
         after3, part4, other4, cotangent_all, pre4, norm_gains, second_weights
     )
-    block_out = own_rows(out_all, own_count)
     other5 = swap(part5)
     grads_second = ff_weight_grads(entries4, slope4, branch4, hidden4, "second_weight_grads")
+    other5 = tie(other5, grads_second)
+    reduced_second = reduce_plain(grads_second)
     grad3, branch3, grad_shifted, grad_sums, gain4 = norm_backward(
-        grad4, part5, other5, after3, norm_gains, conv_weights, convolved, sums, batch, token_count
+        grad4, part5, other5, after3, norm_gains, mixed_weights, convolved, sums, batch, token_count
     )
     grad_sums = sum_over(grad_sums, "dp")
     grad_conv, joined3, part6 = conv_backward(
@@ -720,45 +942,55 @@
         batch,
         value_pre,
         gate,
-        conv_weights,
+        mixed_weights,
         depth_kernel,
         token_count,
     )
     other6 = swap(part6)
-    grads_conv, tap_grads = conv_weight_grads(
-        entries3, joined3, branch3, activated, value_pre, gate, grad_conv, depth_kernel.shape[0]
-    )
+    tap_grads = tap_gradients(value_pre, gate, grad_conv, depth_kernel.shape[0])
     grad2, branch2, joined2, table_grad, part7, gain3, bias_grads = attention_back(
         grad3,
         part6,
         other6,
         after2,
         norm_gains,
-        attention_weights,
+        mixed_weights,
         positions,
         (qc, qp, keys, values, prob),
         local_heads,
     )
     other7 = swap(part7)
-    grads_attention = attention_weight_grads(
-        entries2, joined2, table, table_grad, branch2, attended
-    )
-    grad1, branch1, slope1, part8, gain2 = first_back(
+    mixed_grads = mixed_weight_grads(
+        (entries2, joined2, table, table_grad, branch2, attended),
+        (entries3, joined3, branch3, activated),
+        split,
+    )
+    grad1, branch1, slope1, keep8, send8, gain2 = first_back(
         grad2, part7, other7, after1, pre1, norm_gains, first_weights
     )
-    grads_first = ff_weight_grads(entries1, slope1, branch1, hidden1, "first_weight_grads")
-    other_start = (1 - lax.axis_index("tensor")) * own_count
-    other8 = swap(lax.dynamic_slice_in_dim(part8, other_start, own_count, 0))
-    grad_start, gain1 = input_back(
-        own_rows(grad1, own_count), own_rows(part8, own_count), other8, tokens, norm_gains
-    )
-
-    reduced_a = scatter_weights(jnp.concatenate([grads_second, grads_conv], 1))
-    reduced_b = scatter_weights(jnp.concatenate([grads_attention, grads_first], 1))
-    reduced_second = reduced_a[:, : 2 * hidden]
-    reduced_conv = reduced_a[:, 2 * hidden :]
-    reduced_attention = reduced_b[:, : 5 * columns]
-    reduced_first = reduced_b[:, 5 * columns :]
+    if split:
+        first_grads = ff_weight_split(entries1, slope1, branch1, hidden1, "first_weight_grads")
+        for stage in range(4):
+            mixed_grads = scatter_stage(*mixed_grads, stage, "mixed_sum")
+            first_grads = scatter_stage(*first_grads, stage, "first_sum")
+        (mixed_a, mixed_b), (reduced_in, reduced_out) = mixed_grads[0], first_grads[0]
+        rows = mixed_a.shape[0] // 4
+        reduced_attention = mixed_a.reshape(4, rows, columns)
+        reduced_mixing = mixed_b[:rows]
+        reduced_gated = mixed_b[rows : 3 * rows].reshape(2, rows, columns)
+        reduced_pointwise = mixed_b[3 * rows :]
+    else:
+        first_grads = reduce_plain(
+            ff_weight_grads(entries1, slope1, branch1, hidden1, "first_weight_grads")
+        )
+        reduced_in, reduced_out = first_grads[:, :hidden], first_grads[:, hidden:]
+        mixed = reduce_plain(mixed_grads)
+        reduced_attention = stacked_columns(mixed[:, : 4 * columns], 4)
+        reduced_mixing = mixed[:, 4 * columns : 5 * columns]
+        reduced_gated = stacked_columns(mixed[:, 5 * columns : 7 * columns], 2)
+        reduced_pointwise = mixed[:, 7 * columns :]
+    other8 = swap(send8)
+    grad_start, gain1 = input_back(grad1, keep8, other8, tokens, norm_gains)
 
     gains = jnp.concatenate([gain1, 0.5 * gain2, 0.5 * gain3, 0.5 * gain4, 0.5 * gain5], 0)
     packed = jnp.concatenate(
@@ -774,13 +1006,13 @@
         block_out,
         grad_start,
         gain_total,
-        reduced_first[:, :hidden],
-        reduced_first[:, hidden:],
-        stacked_columns(reduced_attention[:, : 4 * columns], 4),
-        reduced_attention[:, 4 * columns :],
+        reduced_in,
+        reduced_out,
+        reduced_attention,
+        reduced_mixing,
         bias_total,
-        stacked_columns(reduced_conv[:, : 2 * columns], 2),
-        reduced_conv[:, 2 * columns :],
+        reduced_gated,
+        reduced_pointwise,
         tap_total,
         grad_sums[1],
         grad_sums[0],

time: 329 us -> 255 us (0.78)
  waiting for transfers between devices: 216 us -> 83.9 us
  starting transfers between devices: 29.1 us -> 64.1 us
  local copies, waits for them, and re-layouts: 33.8 us -> 49.4 us
  Pallas kernels: 21.1 us -> 30.8 us
    reduce_scatter x2 -> x1, waiting for transfers between devices: 74.7 us -> 0.01 us  [reduce_plain(): lax.psum_scatter(grads.astype(BF16), 'dp', scatter_dimension=0, tiled=True)]
    all_gather x2 -> x1, waiting for transfers between devices: 71.9 us -> 0.01 us  [gather(): return lax.all_gather(jnp.concatenate(pieces, 1), 'dp', axis=0, tiled=True)]
    ppermute x13 -> x48, starting transfers between devices: 13.5 us -> 54.1 us  [shift(): lax.ppermute(value, axis, [(k, k ^ mask) for k in range(lax.axis_size(axi...]
    ppermute x13 -> x48, waiting for transfers between devices: 28.6 us -> 49.4 us  [shift(): lax.ppermute(value, axis, [(k, k ^ mask) for k in range(lax.axis_size(axi...]
    unnamed x105 -> x192, local copies, waits for them, and re-layouts: 22.7 us -> 41.9 us
    pallas_call x16 -> x26, Pallas kernels: 21.1 us -> 30.8 us  [on_chip(): pl.pallas_call(kernel, out_shape=[jax.ShapeDtypeStruct(shape, kind) for s...]
    ppermute x10, waiting for transfers between devices: 40.5 us -> 34.4 us  [swap(): return lax.ppermute(value, 'tensor', [(0, 1), (1, 0)])]
    ppermute x10, starting transfers between devices: 15.4 us -> 9.92 us  [swap(): return lax.ppermute(value, 'tensor', [(0, 1), (1, 0)])]
  transfers between devices with their start and end apart: 27 -> 60, of which waited for: 26 -> 35; matrix products, arithmetic and copies ran while one was open for 7% -> 7% of each run, Pallas kernels for 3% -> 11%
where the time goes in v2:
time: 255 us; the launch traced here: 253 us
  waiting for transfers between devices  83.9 us (33%)
  starting transfers between devices  64.1 us (25%)
  local copies, waits for them, and re-layouts  49.4 us (19%)
  Pallas kernels  30.8 us (12%)
  between operations  14.9 us (6%)
  other arithmetic  10.3 us (4%)
    ppermute x48, starting transfers between devices, shift(): lax.ppermute(value, axis, [(k, k ^ mask) for k in range(lax.axis_size(axi...  54.1 us
    ppermute x48, waiting for transfers between devices, shift(): lax.ppermute(value, axis, [(k, k ^ mask) for k in range(lax.axis_size(axi...  49.4 us
    unnamed x192, local copies, waits for them, and re-layouts  41.9 us
    ppermute x10, waiting for transfers between devices, swap(): return lax.ppermute(value, 'tensor', [(0, 1), (1, 0)])  34.4 us
    pallas_call x26, Pallas kernels, on_chip(): pl.pallas_call(kernel, out_shape=[jax.ShapeDtypeStruct(shape, kind) for s...  30.8 us
    ppermute x10, starting transfers between devices, swap(): return lax.ppermute(value, 'tensor', [(0, 1), (1, 0)])  9.92 us
  transfers between devices with their start and end apart: 60, of which 35 were waited for; matrix products, arithmetic and copies ran while one was open for 7% of the time, Pallas kernels for 11%

profile of v2, /device:TPU:0, one launch (start us, length us, event | category | flops | bytes accessed | tf_op | source)
XLA Modules:
  0.0 253.3 jit_solution(15132947377096029328)
XLA Ops:
  7.3 4.1 %collective-permute-start.1 = (bf16[32,1024]{1,0:T(8,128)(2,1)}, bf16[32,1024]{1,0:T(8,128)(2,1)S(1)}, u32[]{:S(2)}, u32[]{:S(2)}) collective-permute-start(bf16[32,1024]{1,0:T(8,128)(2,1)} %param.17), channel_id=1, source_target_pairs={{0,16},{2,18},{4,20},{6,22},{8,24},{10,26},{12,28},{14,30},{16,0},... | collective-permute-start | bytes 196616 | tf_op jit(solution)/shard_map/ppermute | solution.py:103
  12.3 2.9 %collective-permute-done.1 = bf16[32,1024]{1,0:T(8,128)(2,1)S(1)} collective-permute-done((bf16[32,1024]{1,0:T(8,128)(2,1)}, bf16[32,1024]{1,0:T(8,128)(2,1)S(1)}, u32[]{:S(2)}, u32[]{:S(2)}) %collective-permute-start.1) | collective-permute-done | bytes 65568 | tf_op jit(solution)/shard_map/ppermute | solution.py:103
  15.3 2.2 collective-permute-start.2
  18.4 1.6 collective-permute-start.6
  21.1 1.6 collective-permute-start.3
  24.5 4.6 %collective-permute-done.3 = bf16[128,1024]{1,0:T(8,128)(2,1)S(1)} collective-permute-done((bf16[128,1024]{1,0:T(8,128)(2,1)S(1)}, bf16[128,1024]{1,0:T(8,128)(2,1)S(1)}, u32[]{:S(2)}, u32[]{:S(2)}) %collective-permute-start.3) | collective-permute-done | bytes 262176 | tf_op jit(solution)/shard_map/ppermute | solution.py:103
  29.2 1.4 collective-permute-done.7
  31.4 3.3 %collective-permute-start.10 = (bf16[128,256]{1,0:T(8,128)(2,1)S(1)}, bf16[128,256]{1,0:T(8,128)(2,1)S(1)}, u32[]{:S(2)}, u32[]{:S(2)}) collective-permute-start(bf16[128,256]{1,0:T(8,128)(2,1)S(1)} %bitcast.9), channel_id=1, source_target_pairs={{0,16},{2,18},{4,20},{6,22},{8,24},{10,26},{12,28},{14,30},{16,0},... | collective-permute-start | bytes 196616 | tf_op jit(solution)/shard_map/ppermute | solution.py:103
  34.7 1.5 collective-permute-start.26
  36.4 2.4 collective-permute-done.10
  38.8 2.8 %collective-permute-done.11 = bf16[128,256]{1,0:T(8,128)(2,1)S(1)} collective-permute-done((bf16[128,256]{1,0:T(8,128)(2,1)S(1)}, bf16[128,256]{1,0:T(8,128)(2,1)S(1)}, u32[]{:S(2)}, u32[]{:S(2)}) %collective-permute-start.11) | collective-permute-done | bytes 65568 | tf_op jit(solution)/shard_map/ppermute | solution.py:103
  41.6 1.7 collective-permute-start.12
  43.3 1.5 collective-permute-start.13
  44.8 2.0 collective-permute-done.12
  46.8 1.5 collective-permute-done.13
  48.9 1.5 collective-permute-start.14
  51.3 3.0 %multiply_sine_fusion = (bf16[512,256]{1,0:T(8,128)(2,1)}, bf16[512,256]{1,0:T(8,128)(2,1)}) fusion(f32[256]{0:T(256)S(1)} %multiply_exponential_fusion, f32[512]{0:T(512)S(1)} %iota_add_fusion), kind=kLoop, calls=%fused_computation.3 | loop fusion | flops 393216 | bytes 527360 | tf_op jit(solution)/shard_map/sin | solution.py:57
  54.3 2.9 %collective-permute-done.14 = bf16[512,256]{1,0:T(8,128)(2,1)S(1)} collective-permute-done((bf16[512,256]{1,0:T(8,128)(2,1)S(1)}, bf16[512,256]{1,0:T(8,128)(2,1)S(1)}, u32[]{:S(2)}, u32[]{:S(2)}) %collective-permute-start.14) | collective-permute-done | bytes 262176 | tf_op jit(solution)/shard_map/ppermute | solution.py:103
  60.0 2.1 collective-permute-done
  62.1 1.7 broadcast_select_fusion.1
  67.1 4.9 %collective-permute-done.9.refs_2_ = bf16[256,512]{1,0:T(8,128)(2,1)S(1)} collective-permute-done((bf16[256,512]{1,0:T(8,128)(2,1)S(1)}, bf16[256,512]{1,0:T(8,128)(2,1)S(1)}, u32[]{:S(2)}, u32[]{:S(2)}) %collective-permute-start.9) | collective-permute-done | bytes 262176 | tf_op jit(solution)/shard_map/ppermute | solution.py:83
  72.0 3.3 %attention_forward.1 = (f32[256,512]{1,0:T(8,128)S(1)}, bf16[256,512]{1,0:T(8,128)(2,1)S(1)}, bf16[256,256]{1,0:T(8,128)(2,1)S(1)}, bf16[256,256]{1,0:T(8,128)(2...) custom-call(bf16[256,512]{1,0:T(8,128)(2,1)S(1)} %pad_maximum_fusion, ...), custom_call_target="tpu_custom_call" | custom-call | flops 300000000 | bytes 5910528 | tf_op jit(solution)/shard_map/attention_forward/pallas_call | solution.py:70
  80.6 5.6 %collective-permute-done.18.refs_2_ = bf16[256,512]{1,0:T(8,128)(2,1)S(1)} collective-permute-done((bf16[256,512]{1,0:T(8,128)(2,1)S(1)}, bf16[256,512]{1,0:T(8,128)(2,1)S(1)}, u32[]{:S(2)}, u32[]{:S(2)}) %collective-permute-start.18) | collective-permute-done | bytes 262176 | tf_op jit(solution)/shard_map/ppermute | solution.py:83
  86.1 1.8 conv_forward.1
  90.7 1.8 collective-permute-start.20
  92.5 1.8 collective-permute-done.20
  94.2 1.3 collective-permute-start.23
  96.4 2.2 collective-permute-start.21
  102.9 4.6 %collective-permute-done.24.refs_2_ = bf16[256,512]{1,0:T(8,128)(2,1)S(1)} collective-permute-done((bf16[256,512]{1,0:T(8,128)(2,1)S(1)}, bf16[256,512]{1,0:T(8,128)(2,1)S(1)}, u32[]{:S(2)}, u32[]{:S(2)}) %collective-permute-start.24) | collective-permute-done | bytes 262176 | tf_op jit(solution)/shard_map/ppermute | solution.py:83
  108.2 1.6 copy-done.3
  114.9 5.3 %collective-permute-done.25.refs_2_ = bf16[256,512]{1,0:T(8,128)(2,1)S(1)} collective-permute-done((bf16[256,512]{1,0:T(8,128)(2,1)S(1)}, bf16[256,512]{1,0:T(8,128)(2,1)S(1)}, u32[]{:S(2)}, u32[]{:S(2)}) %collective-permute-start.25) | collective-permute-done | bytes 262176 | tf_op jit(solution)/shard_map/ppermute | solution.py:83
  120.2 1.7 second_back.1
  124.2 1.3 copy-done.2
  126.7 5.5 %collective-permute-done.27.refs_2_ = bf16[256,512]{1,0:T(8,128)(2,1)S(1)} collective-permute-done((bf16[256,512]{1,0:T(8,128)(2,1)}, bf16[256,512]{1,0:T(8,128)(2,1)S(1)}, u32[]{:S(2)}, u32[]{:S(2)}) %collective-permute-start.27) | collective-permute-done | bytes 262176 | tf_op jit(solution)/shard_map/ppermute | solution.py:83
  139.3 1.8 collective-permute-start.29
  141.1 1.8 collective-permute-done.29
  142.8 2.4 collective-permute-start.32
  148.2 1.5 collective-permute-done.31
  149.9 1.8 conv_backward.1
  153.2 4.9 %collective-permute-done.33.refs_2_ = bf16[256,512]{1,0:T(8,128)(2,1)S(1)} collective-permute-done((bf16[256,512]{1,0:T(8,128)(2,1)S(1)}, bf16[256,512]{1,0:T(8,128)(2,1)S(1)}, u32[]{:S(2)}, u32[]{:S(2)}) %collective-permute-start.33) | collective-permute-done | bytes 262176 | tf_op jit(solution)/shard_map/ppermute | solution.py:83
  158.2 4.3 %attention_back.1 = (f32[256,512]{1,0:T(8,128)S(1)}, bf16[256,512]{1,0:T(8,128)(2,1)S(1)}, bf16[256,768]{1,0:T(8,128)(2,1)S(1)}, bf16[512,256]{1,0:T(8,128)(2,1)...) custom-call(f32[256,512]{1,0:T(8,128)S(1)} %get-tuple-element.145.refs_0_, ...), custom_call_target="tpu_custom_call" | custom-call | flops 300000000 | bytes 7223296 | tf_op jit(solution)/shard_map/attention_back/pallas_call | solution.py:70
  167.1 1.6 tap_gradients.1
  169.3 1.4 reshape.76
  179.2 2.0 mixed_weight_grads.1
  184.9 1.2 copy-done.17
  187.2 2.3 first_back.1
  189.5 1.2 collective-permute-start.35
  190.7 1.8 first_weight_grads.1
  193.6 1.4 collective-permute-done.35.refs_2_
  198.2 1.2 copy-done.15
  199.4 1.4 mixed_sum.4
  200.7 1.4 collective-permute-start.52
  204.8 5.7 %collective-permute-done.37 = f32[86,128]{1,0:T(8,128)S(1)} collective-permute-done((f32[86,128]{1,0:T(8,128)S(1)}, f32[86,128]{1,0:T(8,128)S(1)}, u32[]{:S(2)}, u32[]{:S(2)}) %collective-permute-start.37) | collective-permute-done | bytes 44064 | tf_op jit(solution)/shard_map/ppermute | solution.py:103
  210.5 1.7 collective-permute-start.40
  213.1 1.8 collective-permute-start.38
  214.9 2.0 first_sum.4
  217.0 1.3 collective-permute-start.44
  218.5 2.0 collective-permute-start.54
  221.2 1.4 collective-permute-start.41
  222.6 5.3 %collective-permute-done.54.refs_2_ = bf16[256,256]{1,0:T(8,128)(2,1)S(1)} collective-permute-done((bf16[256,256]{1,0:T(8,128)(2,1)S(1)}, bf16[256,256]{1,0:T(8,128)(2,1)S(1)}, u32[]{:S(2)}, u32[]{:S(2)}) %collective-permute-start.54) | collective-permute-done | bytes 131104 | tf_op jit(solution)/shard_map/ppermute | solution.py:103
  228.9 2.0 collective-permute-start.57
  236.5 1.8 collective-permute-start.48
  241.7 2.5 collective-permute-done.49.refs_3_
  244.9 1.6 fusion.1
  (326 shorter events, 85.1 us)
Async XLA Ops:
  7.2 24.1 %copy-start.90 = (bf16[32,256]{1,0:T(8,128)(2,1)S(1)}, bf16[32,256]{1,0:T(8,128)(2,1)}, u32[]{:S(2)}) copy-start(bf16[32,256]{1,0:T(8,128)(2,1)} %param.23) | copy-start | bytes 49156
  7.2 24.2 %copy-start.88 = (bf16[4,32,256]{2,1,0:T(8,128)(2,1)S(1)}, bf16[4,32,256]{2,1,0:T(8,128)(2,1)}, u32[]{:S(2)}) copy-start(bf16[4,32,256]{2,1,0:T(8,128)(2,1)} %param.19) | copy-start | bytes 196612
  7.2 27.5 %copy-start.84 = (bf16[128,512]{1,0:T(8,128)(2,1)S(1)}, bf16[128,512]{1,0:T(8,128)(2,1)}, u32[]{:S(2)}) copy-start(bf16[128,512]{1,0:T(8,128)(2,1)} %param.29) | copy-start | bytes 393220
  7.3 101.0 %all-gather.2.cloned.1.call-start = ((), (), s32[]{:S(2)}) async-start(), calls=%async_computation.1 | async-start | bytes 2228224 | tf_op jit(solution)/shard_map/all_gather | solution.py:882
  7.3 8.0 %collective-permute-start.1 = (bf16[32,1024]{1,0:T(8,128)(2,1)}, bf16[32,1024]{1,0:T(8,128)(2,1)S(1)}, u32[]{:S(2)}, u32[]{:S(2)}) collective-permute-start(bf16[32,1024]{1,0:T(8,128)(2,1)} %param.17), channel_id=1, source_target_pairs={{0,16},{2,18},{4,20},{6,22},{8,24},{10,26},{12,28},{14,30},{16,0},... | collective-permute-start | bytes 196616 | tf_op jit(solution)/shard_map/ppermute | solution.py:103
  11.4 7.0 %collective-permute-start.5 = (bf16[32,1024]{1,0:T(8,128)(2,1)}, bf16[32,1024]{1,0:T(8,128)(2,1)S(1)}, u32[]{:S(2)}, u32[]{:S(2)}) collective-permute-start(bf16[32,1024]{1,0:T(8,128)(2,1)} %param.18), channel_id=1, source_target_pairs={{0,16},{2,18},{4,20},{6,22},{8,24},{10,26},{12,28},{14,30},{16,0},... | collective-permute-start | bytes 196616 | tf_op jit(solution)/shard_map/ppermute | solution.py:103
  15.3 5.8 %collective-permute-start.2 = (bf16[64,1024]{1,0:T(8,128)(2,1)S(1)}, bf16[64,1024]{1,0:T(8,128)(2,1)S(1)}, u32[]{:S(2)}, u32[]{:S(2)}) collective-permute-start(bf16[64,1024]{1,0:T(8,128)(2,1)S(1)} %get-tuple-element.239), channel_id=1, source_target_pairs={{0,8},{2,10},{4,12},{6,14},{8,0},{10,2},{12,4},{14,6},{16,24},{18,... | collective-permute-start | bytes 393224 | tf_op jit(solution)/shard_map/ppermute | solution.py:103
  18.4 5.4 %collective-permute-start.6 = (bf16[64,1024]{1,0:T(8,128)(2,1)S(1)}, bf16[64,1024]{1,0:T(8,128)(2,1)S(1)}, u32[]{:S(2)}, u32[]{:S(2)}) collective-permute-start(bf16[64,1024]{1,0:T(8,128)(2,1)S(1)} %get-tuple-element.233), channel_id=1, source_target_pairs={{0,4},{2,6},{4,0},{6,2},{8,12},{10,14},{12,8},{14,10},{16,20},{18,... | collective-permute-start | bytes 393224 | tf_op jit(solution)/shard_map/ppermute | solution.py:103
  21.1 36.0 %copy-start.28 = (bf16[128,512]{1,0:T(8,128)(2,1)S(1)}, bf16[128,512]{1,0:T(8,128)(2,1)}, u32[]{:S(2)}) copy-start(bf16[128,512]{1,0:T(8,128)(2,1)} %refs_3_.7) | copy-start | bytes 393220
  21.1 8.0 %collective-permute-start.3 = (bf16[128,1024]{1,0:T(8,128)(2,1)S(1)}, bf16[128,1024]{1,0:T(8,128)(2,1)S(1)}, u32[]{:S(2)}, u32[]{:S(2)}) collective-permute-start(bf16[128,1024]{1,0:T(8,128)(2,1)S(1)} %get-tuple-element.229), channel_id=1, source_target_pairs={{0,4},{2,6},{4,0},{6,2},{8,12},{10,14},{12,8},{14,10},{16,20},{18,... | collective-permute-start | bytes 786440 | tf_op jit(solution)/shard_map/ppermute | solution.py:103
  23.9 6.7 %collective-permute-start.7 = (bf16[128,1024]{1,0:T(8,128)(2,1)S(1)}, bf16[128,1024]{1,0:T(8,128)(2,1)S(1)}, u32[]{:S(2)}, u32[]{:S(2)}) collective-permute-start(bf16[128,1024]{1,0:T(8,128)(2,1)S(1)} %get-tuple-element.227), channel_id=1, source_target_pairs={{0,8},{2,10},{4,12},{6,14},{8,0},{10,2},{12,4},{14,6},{16,24},{18,... | collective-permute-start | bytes 786440 | tf_op jit(solution)/shard_map/ppermute | solution.py:103
  31.3 213.6 %reduce-scatter.2.cloned.1.call-start = ((), (), s32[]{:S(2)}) async-start(), calls=%async_computation.2 | async-start | bytes 2228224 | tf_op jit(solution)/shard_map/reduce_scatter | solution.py:842
  31.4 7.4 %collective-permute-start.10 = (bf16[128,256]{1,0:T(8,128)(2,1)S(1)}, bf16[128,256]{1,0:T(8,128)(2,1)S(1)}, u32[]{:S(2)}, u32[]{:S(2)}) collective-permute-start(bf16[128,256]{1,0:T(8,128)(2,1)S(1)} %bitcast.9), channel_id=1, source_target_pairs={{0,16},{2,18},{4,20},{6,22},{8,24},{10,26},{12,28},{14,30},{16,0},... | collective-permute-start | bytes 196616 | tf_op jit(solution)/shard_map/ppermute | solution.py:103
  34.7 24.6 %collective-permute-start.26 = (bf16[128,512]{1,0:T(8,128)(2,1)S(1)}, bf16[128,512]{1,0:T(8,128)(2,1)S(1)}, u32[]{:S(2)}, u32[]{:S(2)}) collective-permute-start(bf16[128,512]{1,0:T(8,128)(2,1)S(1)} %copy-done.84), channel_id=1, source_target_pairs={{0,1},{1,0},{2,3},{3,2},{4,5},{5,4},{6,7},{7,6},{8,9},{9,8},{10,11... | collective-permute-start | bytes 393224 | tf_op jit(solution)/shard_map/ppermute | solution.py:83
  36.3 5.3 %collective-permute-start.11 = (bf16[128,256]{1,0:T(8,128)(2,1)S(1)}, bf16[128,256]{1,0:T(8,128)(2,1)S(1)}, u32[]{:S(2)}, u32[]{:S(2)}) collective-permute-start(bf16[128,256]{1,0:T(8,128)(2,1)S(1)} %pad_maximum_fusion.9), channel_id=1, source_target_pairs={{0,16},{2,18},{4,20},{6,22},{8,24},{10,26},{12,28},{14,30},{16,0},... | collective-permute-start | bytes 196616 | tf_op jit(solution)/shard_map/ppermute | solution.py:103
  41.6 5.2 %collective-permute-start.12 = (bf16[256,256]{1,0:T(8,128)(2,1)S(1)}, bf16[256,256]{1,0:T(8,128)(2,1)S(1)}, u32[]{:S(2)}, u32[]{:S(2)}) collective-permute-start(bf16[256,256]{1,0:T(8,128)(2,1)S(1)} %pad_maximum_fusion.6), channel_id=1, source_target_pairs={{0,8},{2,10},{4,12},{6,14},{8,0},{10,2},{12,4},{14,6},{16,24},{18,... | collective-permute-start | bytes 393224 | tf_op jit(solution)/shard_map/ppermute | solution.py:103
  43.3 5.0 %collective-permute-start.13 = (bf16[256,256]{1,0:T(8,128)(2,1)S(1)}, bf16[256,256]{1,0:T(8,128)(2,1)S(1)}, u32[]{:S(2)}, u32[]{:S(2)}) collective-permute-start(bf16[256,256]{1,0:T(8,128)(2,1)S(1)} %pad_maximum_fusion.7), channel_id=1, source_target_pairs={{0,4},{2,6},{4,0},{6,2},{8,12},{10,14},{12,8},{14,10},{16,20},{18,... | collective-permute-start | bytes 393224 | tf_op jit(solution)/shard_map/ppermute | solution.py:103
  48.3 10.5 %collective-permute-start.4 = (bf16[256,1024]{1,0:T(8,128)(2,1)S(1)}, bf16[256,1024]{1,0:T(8,128)(2,1)S(1)}, u32[]{:S(2)}, u32[]{:S(2)}) collective-permute-start(bf16[256,1024]{1,0:T(8,128)(2,1)S(1)} %constant_dynamic-update-slice_fusion.5.refs_0_), channel_id=1, source_target_pairs={{0,2},{2,0},{4,6},{6,4},{8,10},{10,8},{12,14},{14,12},{16,18},{18,... | collective-permute-start | bytes 1572872 | tf_op jit(solution)/shard_map/ppermute | solution.py:103
  48.4 10.4 %collective-permute-start.8 = (bf16[256,1024]{1,0:T(8,128)(2,1)S(1)}, bf16[256,1024]{1,0:T(8,128)(2,1)S(1)}, u32[]{:S(2)}, u32[]{:S(2)}) collective-permute-start(bf16[256,1024]{1,0:T(8,128)(2,1)S(1)} %constant_dynamic-update-slice_fusion.14.refs_2_), channel_id=1, source_target_pairs={{0,2},{2,0},{4,6},{6,4},{8,10},{10,8},{12,14},{14,12},{16,18},{18,... | collective-permute-start | bytes 1572872 | tf_op jit(solution)/shard_map/ppermute | solution.py:103
  48.9 8.3 %collective-permute-start.14 = (bf16[512,256]{1,0:T(8,128)(2,1)S(1)}, bf16[512,256]{1,0:T(8,128)(2,1)S(1)}, u32[]{:S(2)}, u32[]{:S(2)}) collective-permute-start(bf16[512,256]{1,0:T(8,128)(2,1)S(1)} %pad_maximum_fusion.3), channel_id=1, source_target_pairs={{0,4},{2,6},{4,0},{6,2},{8,12},{10,14},{12,8},{14,10},{16,20},{18,... | collective-permute-start | bytes 786440 | tf_op jit(solution)/shard_map/ppermute | solution.py:103
  50.4 8.4 %collective-permute-start.15 = (bf16[512,256]{1,0:T(8,128)(2,1)S(1)}, bf16[512,256]{1,0:T(8,128)(2,1)S(1)}, u32[]{:S(2)}, u32[]{:S(2)}) collective-permute-start(bf16[512,256]{1,0:T(8,128)(2,1)S(1)} %pad_maximum_fusion.4), channel_id=1, source_target_pairs={{0,8},{2,10},{4,12},{6,14},{8,0},{10,2},{12,4},{14,6},{16,24},{18,... | collective-permute-start | bytes 786440 | tf_op jit(solution)/shard_map/ppermute | solution.py:103
  57.2 5.0 %collective-permute-start = (bf16[128,512]{1,0:T(8,128)(2,1)S(1)}, bf16[128,512]{1,0:T(8,128)(2,1)S(1)}, u32[]{:S(2)}, u32[]{:S(2)}) collective-permute-start(bf16[128,512]{1,0:T(8,128)(2,1)S(1)} %copy-done.28), channel_id=1, source_target_pairs={{0,1},{1,0},{2,3},{3,2},{4,5},{5,4},{6,7},{7,6},{8,9},{9,8},{10,11... | collective-permute-start | bytes 393224 | tf_op jit(solution)/shard_map/ppermute | solution.py:83
  58.8 7.6 %collective-permute-start.16 = (bf16[1024,256]{1,0:T(8,128)(2,1)S(1)}, bf16[1024,256]{1,0:T(8,128)(2,1)S(1)}, u32[]{:S(2)}, u32[]{:S(2)}) collective-permute-start(bf16[1024,256]{1,0:T(8,128)(2,1)S(1)} %pad_maximum_fusion.refs_0_), channel_id=1, source_target_pairs={{0,2},{2,0},{4,6},{6,4},{8,10},{10,8},{12,14},{14,12},{16,18},{18,... | collective-permute-start | bytes 1572872 | tf_op jit(solution)/shard_map/ppermute | solution.py:103
  58.9 7.6 %collective-permute-start.17 = (bf16[1024,256]{1,0:T(8,128)(2,1)S(1)}, bf16[1024,256]{1,0:T(8,128)(2,1)S(1)}, u32[]{:S(2)}, u32[]{:S(2)}) collective-permute-start(bf16[1024,256]{1,0:T(8,128)(2,1)S(1)} %pad_maximum_fusion.1.refs_2_), channel_id=1, source_target_pairs={{0,2},{2,0},{4,6},{6,4},{8,10},{10,8},{12,14},{14,12},{16,18},{18,... | collective-permute-start | bytes 1572872 | tf_op jit(solution)/shard_map/ppermute | solution.py:103
  65.6 6.4 %collective-permute-start.9 = (bf16[256,512]{1,0:T(8,128)(2,1)S(1)}, bf16[256,512]{1,0:T(8,128)(2,1)S(1)}, u32[]{:S(2)}, u32[]{:S(2)}) collective-permute-start(bf16[256,512]{1,0:T(8,128)(2,1)S(1)} %get-tuple-element.117.refs_1_), channel_id=1, source_target_pairs={{0,1},{1,0},{2,3},{3,2},{4,5},{5,4},{6,7},{7,6},{8,9},{9,8},{10,11... | collective-permute-start | bytes 786440 | tf_op jit(solution)/shard_map/ppermute | solution.py:83
  79.7 6.4 %collective-permute-start.18 = (bf16[256,512]{1,0:T(8,128)(2,1)S(1)}, bf16[256,512]{1,0:T(8,128)(2,1)S(1)}, u32[]{:S(2)}, u32[]{:S(2)}) collective-permute-start(bf16[256,512]{1,0:T(8,128)(2,1)S(1)} %get-tuple-element.127.refs_1_), channel_id=1, source_target_pairs={{0,1},{1,0},{2,3},{3,2},{4,5},{5,4},{6,7},{7,6},{8,9},{9,8},{10,11... | collective-permute-start | bytes 786440 | tf_op jit(solution)/shard_map/ppermute | solution.py:83
  89.5 1.2 collective-permute-start.19
  90.7 3.6 %collective-permute-start.20 = (f32[2,256]{1,0:T(2,128)S(1)}, f32[2,256]{1,0:T(2,128)S(1)}, u32[]{:S(2)}, u32[]{:S(2)}) collective-permute-start(f32[2,256]{1,0:T(2,128)S(1)} %add.58), channel_id=1, source_target_pairs={{0,4},{2,6},{4,0},{6,2},{8,12},{10,14},{12,8},{14,10},{16,20},{18,... | collective-permute-start | bytes 6152 | tf_op jit(solution)/shard_map/ppermute | solution.py:103
  94.2 5.4 %collective-permute-start.23 = (f32[2,256]{1,0:T(2,128)S(1)}, f32[2,256]{1,0:T(2,128)S(1)}, u32[]{:S(2)}, u32[]{:S(2)}) collective-permute-start(f32[2,256]{1,0:T(2,128)S(1)} %add.59), channel_id=1, source_target_pairs={{0,24},{2,26},{4,28},{6,30},{8,16},{10,18},{12,20},{14,22},{16,8},... | collective-permute-start | bytes 6152 | tf_op jit(solution)/shard_map/ppermute | solution.py:103
  95.5 4.5 %collective-permute-start.22 = (f32[2,256]{1,0:T(2,128)S(1)}, f32[2,256]{1,0:T(2,128)S(1)}, u32[]{:S(2)}, u32[]{:S(2)}) collective-permute-start(f32[2,256]{1,0:T(2,128)S(1)} %add.59), channel_id=1, source_target_pairs={{0,16},{2,18},{4,20},{6,22},{8,24},{10,26},{12,28},{14,30},{16,0},... | collective-permute-start | bytes 6152 | tf_op jit(solution)/shard_map/ppermute | solution.py:103
  96.4 3.8 %collective-permute-start.21 = (f32[2,256]{1,0:T(2,128)S(1)}, f32[2,256]{1,0:T(2,128)S(1)}, u32[]{:S(2)}, u32[]{:S(2)}) collective-permute-start(f32[2,256]{1,0:T(2,128)S(1)} %add.59), channel_id=1, source_target_pairs={{0,8},{2,10},{4,12},{6,14},{8,0},{10,2},{12,4},{14,6},{16,24},{18,... | collective-permute-start | bytes 6152 | tf_op jit(solution)/shard_map/ppermute | solution.py:103
  101.2 6.4 %collective-permute-start.24 = (bf16[256,512]{1,0:T(8,128)(2,1)S(1)}, bf16[256,512]{1,0:T(8,128)(2,1)S(1)}, u32[]{:S(2)}, u32[]{:S(2)}) collective-permute-start(bf16[256,512]{1,0:T(8,128)(2,1)S(1)} %get-tuple-element.131.refs_1_), channel_id=1, source_target_pairs={{0,1},{1,0},{2,3},{3,2},{4,5},{5,4},{6,7},{7,6},{8,9},{9,8},{10,11... | collective-permute-start | bytes 786440 | tf_op jit(solution)/shard_map/ppermute | solution.py:83
  113.8 6.4 %collective-permute-start.25 = (bf16[256,512]{1,0:T(8,128)(2,1)S(1)}, bf16[256,512]{1,0:T(8,128)(2,1)S(1)}, u32[]{:S(2)}, u32[]{:S(2)}) collective-permute-start(bf16[256,512]{1,0:T(8,128)(2,1)S(1)} %get-tuple-element.135.refs_1_), channel_id=1, source_target_pairs={{0,1},{1,0},{2,3},{3,2},{4,5},{5,4},{6,7},{7,6},{8,9},{9,8},{10,11... | collective-permute-start | bytes 786440 | tf_op jit(solution)/shard_map/ppermute | solution.py:83
  125.6 6.6 %collective-permute-start.27 = (bf16[256,512]{1,0:T(8,128)(2,1)}, bf16[256,512]{1,0:T(8,128)(2,1)S(1)}, u32[]{:S(2)}, u32[]{:S(2)}) collective-permute-start(bf16[256,512]{1,0:T(8,128)(2,1)} %copy-done.31), channel_id=1, source_target_pairs={{0,1},{1,0},{2,3},{3,2},{4,5},{5,4},{6,7},{7,6},{8,9},{9,8},{10,11... | collective-permute-start | bytes 786440 | tf_op jit(solution)/shard_map/ppermute | solution.py:83
  138.0 1.2 collective-permute-start.28
  139.3 3.6 %collective-permute-start.29 = (f32[2,256]{1,0:T(2,128)S(1)}, f32[2,256]{1,0:T(2,128)S(1)}, u32[]{:S(2)}, u32[]{:S(2)}) collective-permute-start(f32[2,256]{1,0:T(2,128)S(1)} %add.63), channel_id=1, source_target_pairs={{0,4},{2,6},{4,0},{6,2},{8,12},{10,14},{12,8},{14,10},{16,20},{18,... | collective-permute-start | bytes 6152 | tf_op jit(solution)/shard_map/ppermute | solution.py:103
  142.8 5.4 %collective-permute-start.32 = (f32[2,256]{1,0:T(2,128)S(1)}, f32[2,256]{1,0:T(2,128)S(1)}, u32[]{:S(2)}, u32[]{:S(2)}) collective-permute-start(f32[2,256]{1,0:T(2,128)S(1)} %add.64), channel_id=1, source_target_pairs={{0,24},{2,26},{4,28},{6,30},{8,16},{10,18},{12,20},{14,22},{16,8},... | collective-permute-start | bytes 6152 | tf_op jit(solution)/shard_map/ppermute | solution.py:103
  145.2 4.5 %collective-permute-start.31 = (f32[2,256]{1,0:T(2,128)S(1)}, f32[2,256]{1,0:T(2,128)S(1)}, u32[]{:S(2)}, u32[]{:S(2)}) collective-permute-start(f32[2,256]{1,0:T(2,128)S(1)} %add.64), channel_id=1, source_target_pairs={{0,16},{2,18},{4,20},{6,22},{8,24},{10,26},{12,28},{14,30},{16,0},... | collective-permute-start | bytes 6152 | tf_op jit(solution)/shard_map/ppermute | solution.py:103
  146.3 3.6 %collective-permute-start.30 = (f32[2,256]{1,0:T(2,128)S(1)}, f32[2,256]{1,0:T(2,128)S(1)}, u32[]{:S(2)}, u32[]{:S(2)}) collective-permute-start(f32[2,256]{1,0:T(2,128)S(1)} %add.64), channel_id=1, source_target_pairs={{0,8},{2,10},{4,12},{6,14},{8,0},{10,2},{12,4},{14,6},{16,24},{18,... | collective-permute-start | bytes 6152 | tf_op jit(solution)/shard_map/ppermute | solution.py:103
  151.7 6.4 %collective-permute-start.33 = (bf16[256,512]{1,0:T(8,128)(2,1)S(1)}, bf16[256,512]{1,0:T(8,128)(2,1)S(1)}, u32[]{:S(2)}, u32[]{:S(2)}) collective-permute-start(bf16[256,512]{1,0:T(8,128)(2,1)S(1)} %get-tuple-element.150.refs_1_), channel_id=1, source_target_pairs={{0,1},{1,0},{2,3},{3,2},{4,5},{5,4},{6,7},{7,6},{8,9},{9,8},{10,11... | collective-permute-start | bytes 786440 | tf_op jit(solution)/shard_map/ppermute | solution.py:83
  165.6 19.3 %collective-permute-start.34 = (bf16[256,512]{1,0:T(8,128)(2,1)}, bf16[256,512]{1,0:T(8,128)(2,1)}, u32[]{:S(2)}, u32[]{:S(2)}) collective-permute-start(bf16[256,512]{1,0:T(8,128)(2,1)} %get-tuple-element.157.refs_1_), channel_id=1, source_target_pairs={{0,1},{1,0},{2,3},{3,2},{4,5},{5,4},{6,7},{7,6},{8,9},{9,8},{10,11... | collective-permute-start | bytes 786440 | tf_op jit(solution)/shard_map/ppermute | solution.py:83
  183.2 14.9 %collective-permute-start.50 = (bf16[1024,256]{1,0:T(8,128)(2,1)}, bf16[1024,256]{1,0:T(8,128)(2,1)}, u32[]{:S(2)}, u32[]{:S(2)}) collective-permute-start(bf16[1024,256]{1,0:T(8,128)(2,1)} %get-tuple-element.203), channel_id=1, source_target_pairs={{0,2},{2,0},{4,6},{6,4},{8,10},{10,8},{12,14},{14,12},{16,18},{18,... | collective-permute-start | bytes 1572872 | tf_op jit(solution)/shard_map/ppermute | solution.py:103
  183.2 14.9 %collective-permute-start.51 = (bf16[1024,256]{1,0:T(8,128)(2,1)}, bf16[1024,256]{1,0:T(8,128)(2,1)}, u32[]{:S(2)}, u32[]{:S(2)}) collective-permute-start(bf16[1024,256]{1,0:T(8,128)(2,1)} %get-tuple-element.204), channel_id=1, source_target_pairs={{0,2},{2,0},{4,6},{6,4},{8,10},{10,8},{12,14},{14,12},{16,18},{18,... | collective-permute-start | bytes 1572872 | tf_op jit(solution)/shard_map/ppermute | solution.py:103
  189.5 5.5 %collective-permute-start.35 = (bf16[128,512]{1,0:T(8,128)(2,1)S(1)}, bf16[128,512]{1,0:T(8,128)(2,1)S(1)}, u32[]{:S(2)}, u32[]{:S(2)}) collective-permute-start(bf16[128,512]{1,0:T(8,128)(2,1)S(1)} %get-tuple-element.161), channel_id=1, source_target_pairs={{0,1},{1,0},{2,3},{3,2},{4,5},{5,4},{6,7},{7,6},{8,9},{9,8},{10,11... | collective-permute-start | bytes 393224 | tf_op jit(solution)/shard_map/ppermute | solution.py:83
  192.5 19.7 %collective-permute-start.42 = (bf16[256,1024]{1,0:T(8,128)(2,1)}, bf16[256,1024]{1,0:T(8,128)(2,1)}, u32[]{:S(2)}, u32[]{:S(2)}) collective-permute-start(bf16[256,1024]{1,0:T(8,128)(2,1)} %get-tuple-element.176), channel_id=1, source_target_pairs={{0,2},{2,0},{4,6},{6,4},{8,10},{10,8},{12,14},{14,12},{16,18},{18,... | collective-permute-start | bytes 1572872 | tf_op jit(solution)/shard_map/ppermute | solution.py:103
  192.5 20.6 %collective-permute-start.43 = (bf16[256,1024]{1,0:T(8,128)(2,1)}, bf16[256,1024]{1,0:T(8,128)(2,1)}, u32[]{:S(2)}, u32[]{:S(2)}) collective-permute-start(bf16[256,1024]{1,0:T(8,128)(2,1)} %get-tuple-element.177), channel_id=1, source_target_pairs={{0,2},{2,0},{4,6},{6,4},{8,10},{10,8},{12,14},{14,12},{16,18},{18,... | collective-permute-start | bytes 1572872 | tf_op jit(solution)/shard_map/ppermute | solution.py:103
  198.1 5.0 %collective-permute-start.36 = (f32[86,128]{1,0:T(8,128)S(1)}, f32[86,128]{1,0:T(8,128)S(1)}, u32[]{:S(2)}, u32[]{:S(2)}) collective-permute-start(f32[86,128]{1,0:T(8,128)S(1)} %pad_maximum_fusion.10), channel_id=1, source_target_pairs={{0,2},{2,0},{4,6},{6,4},{8,10},{10,8},{12,14},{14,12},{16,18},{18,... | collective-permute-start | bytes 132104 | tf_op jit(solution)/shard_map/ppermute | solution.py:103
  200.7 16.2 %collective-permute-start.52 = (bf16[512,256]{1,0:T(8,128)(2,1)S(1)}, bf16[512,256]{1,0:T(8,128)(2,1)S(1)}, u32[]{:S(2)}, u32[]{:S(2)}) collective-permute-start(bf16[512,256]{1,0:T(8,128)(2,1)S(1)} %get-tuple-element.207), channel_id=1, source_target_pairs={{0,4},{2,6},{4,0},{6,2},{8,12},{10,14},{12,8},{14,10},{16,20},{18,... | collective-permute-start | bytes 786440 | tf_op jit(solution)/shard_map/ppermute | solution.py:103
  202.1 16.2 %collective-permute-start.53 = (bf16[512,256]{1,0:T(8,128)(2,1)S(1)}, bf16[512,256]{1,0:T(8,128)(2,1)S(1)}, u32[]{:S(2)}, u32[]{:S(2)}) collective-permute-start(bf16[512,256]{1,0:T(8,128)(2,1)S(1)} %get-tuple-element.208), channel_id=1, source_target_pairs={{0,8},{2,10},{4,12},{6,14},{8,0},{10,2},{12,4},{14,6},{16,24},{18,... | collective-permute-start | bytes 786440 | tf_op jit(solution)/shard_map/ppermute | solution.py:103
  203.9 6.6 %collective-permute-start.37 = (f32[86,128]{1,0:T(8,128)S(1)}, f32[86,128]{1,0:T(8,128)S(1)}, u32[]{:S(2)}, u32[]{:S(2)}) collective-permute-start(f32[86,128]{1,0:T(8,128)S(1)} %fusion.4), channel_id=1, source_target_pairs={{0,4},{2,6},{4,0},{6,2},{8,12},{10,14},{12,8},{14,10},{16,20},{18,... | collective-permute-start | bytes 132104 | tf_op jit(solution)/shard_map/ppermute | solution.py:103
  210.5 8.0 %collective-permute-start.40 = (f32[86,128]{1,0:T(8,128)S(1)}, f32[86,128]{1,0:T(8,128)S(1)}, u32[]{:S(2)}, u32[]{:S(2)}) collective-permute-start(f32[86,128]{1,0:T(8,128)S(1)} %add.69), channel_id=1, source_target_pairs={{0,24},{2,26},{4,28},{6,30},{8,16},{10,18},{12,20},{14,22},{16,8},... | collective-permute-start | bytes 132104 | tf_op jit(solution)/shard_map/ppermute | solution.py:103
  212.2 8.3 %collective-permute-start.39 = (f32[86,128]{1,0:T(8,128)S(1)}, f32[86,128]{1,0:T(8,128)S(1)}, u32[]{:S(2)}, u32[]{:S(2)}) collective-permute-start(f32[86,128]{1,0:T(8,128)S(1)} %add.69), channel_id=1, source_target_pairs={{0,16},{2,18},{4,20},{6,22},{8,24},{10,26},{12,28},{14,30},{16,0},... | collective-permute-start | bytes 132104 | tf_op jit(solution)/shard_map/ppermute | solution.py:103
  213.1 8.1 %collective-permute-start.38 = (f32[86,128]{1,0:T(8,128)S(1)}, f32[86,128]{1,0:T(8,128)S(1)}, u32[]{:S(2)}, u32[]{:S(2)}) collective-permute-start(f32[86,128]{1,0:T(8,128)S(1)} %add.69), channel_id=1, source_target_pairs={{0,8},{2,10},{4,12},{6,14},{8,0},{10,2},{12,4},{14,6},{16,24},{18,... | collective-permute-start | bytes 132104 | tf_op jit(solution)/shard_map/ppermute | solution.py:103
  217.0 13.9 %collective-permute-start.44 = (bf16[128,1024]{1,0:T(8,128)(2,1)}, bf16[128,1024]{1,0:T(8,128)(2,1)S(1)}, u32[]{:S(2)}, u32[]{:S(2)}) collective-permute-start(bf16[128,1024]{1,0:T(8,128)(2,1)} %get-tuple-element.180), channel_id=1, source_target_pairs={{0,4},{2,6},{4,0},{6,2},{8,12},{10,14},{12,8},{14,10},{16,20},{18,... | collective-permute-start | bytes 786440 | tf_op jit(solution)/shard_map/ppermute | solution.py:103
  218.3 12.6 %collective-permute-start.45 = (bf16[128,1024]{1,0:T(8,128)(2,1)S(1)}, bf16[128,1024]{1,0:T(8,128)(2,1)S(1)}, u32[]{:S(2)}, u32[]{:S(2)}) collective-permute-start(bf16[128,1024]{1,0:T(8,128)(2,1)S(1)} %get-tuple-element.181), channel_id=1, source_target_pairs={{0,8},{2,10},{4,12},{6,14},{8,0},{10,2},{12,4},{14,6},{16,24},{18,... | collective-permute-start | bytes 786440 | tf_op jit(solution)/shard_map/ppermute | solution.py:103
  218.5 9.4 %collective-permute-start.54 = (bf16[256,256]{1,0:T(8,128)(2,1)S(1)}, bf16[256,256]{1,0:T(8,128)(2,1)S(1)}, u32[]{:S(2)}, u32[]{:S(2)}) collective-permute-start(bf16[256,256]{1,0:T(8,128)(2,1)S(1)} %get-tuple-element.211), channel_id=1, source_target_pairs={{0,8},{2,10},{4,12},{6,14},{8,0},{10,2},{12,4},{14,6},{16,24},{18,... | collective-permute-start | bytes 393224 | tf_op jit(solution)/shard_map/ppermute | solution.py:103
  220.5 7.4 %collective-permute-start.55 = (bf16[256,256]{1,0:T(8,128)(2,1)S(1)}, bf16[256,256]{1,0:T(8,128)(2,1)S(1)}, u32[]{:S(2)}, u32[]{:S(2)}) collective-permute-start(bf16[256,256]{1,0:T(8,128)(2,1)S(1)} %get-tuple-element.212), channel_id=1, source_target_pairs={{0,4},{2,6},{4,0},{6,2},{8,12},{10,14},{12,8},{14,10},{16,20},{18,... | collective-permute-start | bytes 393224 | tf_op jit(solution)/shard_map/ppermute | solution.py:103
  221.2 12.6 %collective-permute-start.41 = (f32[5,512]{1,0:T(8,128)S(1)}, f32[5,512]{1,0:T(8,128)S(1)}, u32[]{:S(2)}, u32[]{:S(2)}) collective-permute-start(f32[5,512]{1,0:T(8,128)S(1)} %reshape.78), channel_id=1, source_target_pairs={{0,1},{1,0},{2,3},{3,2},{4,5},{5,4},{6,7},{7,6},{8,9},{9,8},{10,11... | collective-permute-start | bytes 30728 | tf_op jit(solution)/shard_map/ppermute | solution.py:103
  227.9 6.6 %collective-permute-start.56 = (bf16[128,256]{1,0:T(8,128)(2,1)S(1)}, bf16[128,256]{1,0:T(8,128)(2,1)S(1)}, u32[]{:S(2)}, u32[]{:S(2)}) collective-permute-start(bf16[128,256]{1,0:T(8,128)(2,1)S(1)} %get-tuple-element.215), channel_id=1, source_target_pairs={{0,16},{2,18},{4,20},{6,22},{8,24},{10,26},{12,28},{14,30},{16,0},... | collective-permute-start | bytes 196616 | tf_op jit(solution)/shard_map/ppermute | solution.py:103
  228.9 6.3 %collective-permute-start.57 = (bf16[128,256]{1,0:T(8,128)(2,1)S(1)}, bf16[128,256]{1,0:T(8,128)(2,1)S(1)}, u32[]{:S(2)}, u32[]{:S(2)}) collective-permute-start(bf16[128,256]{1,0:T(8,128)(2,1)S(1)} %get-tuple-element.216), channel_id=1, source_target_pairs={{0,16},{2,18},{4,20},{6,22},{8,24},{10,26},{12,28},{14,30},{16,0},... | collective-permute-start | bytes 196616 | tf_op jit(solution)/shard_map/ppermute | solution.py:103
  231.0 5.4 %collective-permute-start.46 = (bf16[64,1024]{1,0:T(8,128)(2,1)S(1)}, bf16[64,1024]{1,0:T(8,128)(2,1)S(1)}, u32[]{:S(2)}, u32[]{:S(2)}) collective-permute-start(bf16[64,1024]{1,0:T(8,128)(2,1)S(1)} %get-tuple-element.184), channel_id=1, source_target_pairs={{0,8},{2,10},{4,12},{6,14},{8,0},{10,2},{12,4},{14,6},{16,24},{18,... | collective-permute-start | bytes 393224 | tf_op jit(solution)/shard_map/ppermute | solution.py:103
  231.4 5.0 %collective-permute-start.47 = (bf16[64,1024]{1,0:T(8,128)(2,1)S(1)}, bf16[64,1024]{1,0:T(8,128)(2,1)S(1)}, u32[]{:S(2)}, u32[]{:S(2)}) collective-permute-start(bf16[64,1024]{1,0:T(8,128)(2,1)S(1)} %get-tuple-element.185), channel_id=1, source_target_pairs={{0,4},{2,6},{4,0},{6,2},{8,12},{10,14},{12,8},{14,10},{16,20},{18,... | collective-permute-start | bytes 393224 | tf_op jit(solution)/shard_map/ppermute | solution.py:103
  236.5 5.2 %collective-permute-start.48 = (bf16[32,1024]{1,0:T(8,128)(2,1)S(1)}, bf16[32,1024]{1,0:T(8,128)(2,1)S(1)}, u32[]{:S(2)}, u32[]{:S(2)}) collective-permute-start(bf16[32,1024]{1,0:T(8,128)(2,1)S(1)} %get-tuple-element.188), channel_id=1, source_target_pairs={{0,16},{2,18},{4,20},{6,22},{8,24},{10,26},{12,28},{14,30},{16,0},... | collective-permute-start | bytes 196616 | tf_op jit(solution)/shard_map/ppermute | solution.py:103
  238.2 6.0 %collective-permute-start.49 = (bf16[32,1024]{1,0:T(8,128)(2,1)S(1)}, bf16[32,1024]{1,0:T(8,128)(2,1)S(1)}, u32[]{:S(2)}, u32[]{:S(2)}) collective-permute-start(bf16[32,1024]{1,0:T(8,128)(2,1)S(1)} %get-tuple-element.189), channel_id=1, source_target_pairs={{0,16},{2,18},{4,20},{6,22},{8,24},{10,26},{12,28},{14,30},{16,0},... | collective-permute-start | bytes 196616 | tf_op jit(solution)/shard_map/ppermute | solution.py:103
  (90 other events, 534.9 us)
Sparse Core Ops, SparseCore 0:
  31.4 43.7 all-gather.1
  125.7 60.9 reduce-scatter.1

commit v3 on v2

--- a/solution.py
+++ b/solution.py
@@ -58,22 +58,90 @@
     return jnp.where(offsets[:, None] < length, table, 0.0)
 
 
-def on_chip(function, name, operands, results, scratch=(), flops=300_000_000):
+class Fetched:
+    def __init__(self, source, buffer, semaphore):
+        self.copy = pltpu.make_async_copy(source, buffer, semaphore)
+        self.copy.start()
+        self.buffer = buffer
+        self.shape = buffer.shape
+        self.pending = True
+
+    def finish(self):
+        if self.pending:
+            self.copy.wait()
+            self.pending = False
+
+    def __getitem__(self, index):
+        self.finish()
+        return self.buffer[index]
+
+
+class Stored:
+    def __init__(self, target, buffer, semaphore):
+        self.copy = pltpu.make_async_copy(buffer, target, semaphore)
+        self.buffer = buffer
+        self.shape = buffer.shape
+        self.started = False
+
+    def start(self):
+        if not self.started:
+            self.copy.start()
+            self.started = True
+
+    def finish(self):
+        self.start()
+        self.copy.wait()
+
+    def __getitem__(self, index):
+        return self.buffer[index]
+
+    def __setitem__(self, index, value):
+        self.buffer[index] = value
+        if index is Ellipsis:
+            self.start()
+
+
+def far(shape, kind):
+    return (shape, kind, True)
+
+
+def on_chip(function, name, operands, results, scratch=(), flops=300_000_000, fetch=()):
     count = len(operands)
     total = count + len(results)
+    fetch = tuple(sorted(fetch))
+    distant = [index for index, result in enumerate(results) if len(result) == 3]
+    buffers = [pltpu.VMEM(operands[index].shape, operands[index].dtype) for index in fetch]
+    buffers += [pltpu.VMEM(results[index][0], results[index][1]) for index in distant]
+    moves = len(buffers)
+    semaphores = [pltpu.SemaphoreType.DMA((moves,))] if moves else []
 
     def kernel(*refs):
-        function(refs[:count], refs[count:total], refs[total:])
+        ins, outs = list(refs[:count]), list(refs[count:total])
+        spaces = refs[total : total + moves]
+        if moves:
+            semaphore = refs[total + moves]
+        for place, index in enumerate(fetch):
+            ins[index] = Fetched(ins[index], spaces[place], semaphore.at[place])
+        for place, index in enumerate(distant, len(fetch)):
+            outs[index] = Stored(outs[index], spaces[place], semaphore.at[place])
+        function(ins, outs, refs[total + moves + len(semaphores) :])
+        for index in fetch:
+            ins[index].finish()
+        for index in distant:
+            outs[index].finish()
+
+    def place(is_far):
+        return pl.BlockSpec(memory_space=pltpu.HBM if is_far else pltpu.VMEM)
 
     moved = sum(value.size * value.dtype.itemsize for value in operands)
-    moved += sum(math.prod(shape) * jnp.dtype(kind).itemsize for shape, kind in results)
+    moved += sum(math.prod(r[0]) * jnp.dtype(r[1]).itemsize for r in results)
     return pl.pallas_call(
         kernel,
-        out_shape=[jax.ShapeDtypeStruct(shape, kind) for shape, kind in results],
-        in_specs=[pl.BlockSpec(memory_space=pltpu.VMEM)] * count,
-        out_specs=[pl.BlockSpec(memory_space=pltpu.VMEM)] * len(results),
-        scratch_shapes=list(scratch),
-        compiler_params=pltpu.CompilerParams(vmem_limit_bytes=40 * 1024 * 1024),
+        out_shape=[jax.ShapeDtypeStruct(r[0], r[1]) for r in results],
+        in_specs=[place(index in fetch) for index in range(count)],
+        out_specs=[place(index in distant) for index in range(len(results))],
+        scratch_shapes=buffers + semaphores + list(scratch),
+        compiler_params=pltpu.CompilerParams(vmem_limit_bytes=32 * 1024 * 1024),
         cost_estimate=pl.CostEstimate(flops=flops, bytes_accessed=moved, transcendentals=0),
         name=name,
     )(*operands)
@@ -185,7 +253,7 @@
                 send_ref[start : start + rows, :] = piece.astype(BF16)
 
 
-def scatter_stage(keeps, sends, stage, name):
+def scatter_stage(keeps, sends, stage, name, fetch=()):
     arrived = [
         shift(send, "dp", order[stage]) for send, order in zip(sends, SCATTER_ORDERS)
     ]
@@ -210,7 +278,7 @@
                 outs[2 * group][...] = total[:half]
                 outs[2 * group + 1][...] = total[half:].astype(BF16)
 
-    values = on_chip(body, name, tuple(keeps) + tuple(arrived), tuple(results), flops=1_000_000)
+    values = on_chip(body, name, tuple(keeps) + tuple(arrived), tuple(results), flops=1_000_000, fetch=fetch)
     if last:
         return values, None
     return values[0::2], values[1::2]
@@ -231,22 +299,33 @@
 
 def first_forward(tokens, gains, weights):
     rows, width = tokens.shape
-    hidden = weights.shape[1] // 2
-
-    def body(ins, outs, _):
-        ff_forward_body(0, ins[0][...].astype(F32), ins[1], ins[2], outs)
-
-    return on_chip(
-        body,
-        "first_forward",
-        (tokens, gains, weights),
-        (
-            ((rows, width), BF16),
-            ((rows, hidden), F32),
-            ((rows, hidden), BF16),
-            ((rows, width), BF16),
-        ),
-    )
+    split = isinstance(weights, tuple)
+    pieces = weights[0] + weights[1] if split else (weights,)
+    hidden = pieces[0].shape[1] if split else weights.shape[1] // 2
+
+    def body(ins, outs, scratch):
+        weight_ref = ins[2]
+        if split:
+            weight_ref = outs[4]
+            for group in range(2):
+                for half in range(2):
+                    piece = ins[2 + 2 * group + half]
+                    assemble(
+                        piece, weight_ref, GATHER_ORDERS[group], half, 1, group * hidden
+                    )
+            weight_ref.start()
+        ff_forward_body(0, ins[0][...].astype(F32), ins[1], weight_ref, outs[:4])
+
+    results = (
+        far((rows, width), BF16),
+        far((rows, hidden), F32),
+        far((rows, hidden), BF16),
+        ((rows, width), BF16),
+    )
+    if split:
+        results += (far((width, 2 * hidden), BF16),)
+    values = on_chip(body, "first_forward", (tokens, gains) + pieces, results)
+    return values if split else tuple(values) + (weights,)
 
 
 def second_forward(residual, own, other, gains, weights):
@@ -256,7 +335,8 @@
     def body(ins, outs, _):
         after = ins[0][...] + (ins[1][...].astype(F32) + ins[2][...].astype(F32))
         outs[0][...] = after
-        ff_forward_body(3, after, ins[3], ins[4], outs[1:])
+        outs[5][...] = after
+        ff_forward_body(3, after, ins[3], ins[4], outs[1:5])
 
     return on_chip(
         body,
@@ -264,11 +344,13 @@
         (residual, own, other, gains, weights),
         (
             ((rows, width), F32),
+            far((rows, width), BF16),
+            ((rows, hidden), F32),
+            far((rows, hidden), BF16),
             ((rows, width), BF16),
-            ((rows, hidden), F32),
-            ((rows, hidden), BF16),
-            ((rows, width), BF16),
+            far((rows, width), F32),
         ),
+        fetch=(4,),
     )
 
 
@@ -294,9 +376,8 @@
         normed, factor = norm_parts(after)
         gain = gain_ref[4:5, :]
         out_ref[...] = own_half(normed * gain).astype(BF16)
-        gradient, gain_grad_ref[...] = norm_back(
-            cot_ref[...].astype(F32), normed, factor, gain
-        )
+        gradient, gain_grad = norm_back(cot_ref[...].astype(F32), normed, factor, gain)
+        gain_grad_ref[...] = 0.5 * gain_grad
         grad_ref[...] = gradient
         part_ref[...] = ff_back_body(gradient, pre_ref, weight_ref, branch_ref, slope_ref).astype(
             BF16
@@ -312,8 +393,9 @@
             ((rows, width), BF16),
             ((rows, hidden), BF16),
             ((rows, width), BF16),
-            ((1, width), F32),
+            far((1, width), F32),
         ),
+        fetch=(3, 6),
     )
 
 
@@ -326,7 +408,11 @@
         outs[0][:, half:] = left_transposed(ins[2][...], ins[3][...]).astype(BF16)
 
     return on_chip(
-        body, name, (entries, grad_pre, branch, hidden), (((width, 2 * half), BF16),)
+        body,
+        name,
+        (entries, grad_pre, branch, hidden),
+        (far((width, 2 * half), BF16),),
+        fetch=(0, 3),
     )[0]
 
 
@@ -348,39 +434,18 @@
         (entries, grad_pre, branch, hidden),
         halves + halves,
         scratch=(pltpu.VMEM((width, half), F32),),
+        fetch=(0, 3),
     )
     return values[0::2], values[1::2]
-
-
-def ff_assemble(pairs, width):
-    columns = pairs[0][0].shape[1]
-
-    def body(ins, outs, _):
-        for group in range(2):
-            for half in range(2):
-                assemble(
-                    ins[2 * group + half],
-                    outs[0],
-                    GATHER_ORDERS[group],
-                    half,
-                    1,
-                    group * columns,
-                )
-
-    return on_chip(
-        body,
-        "first_assemble",
-        pairs[0] + pairs[1],
-        (((width, 2 * columns), BF16),),
-        flops=1_000_000,
-    )[0]
 
 
 def position_forward(table, weights, columns):
     def body(ins, outs, _):
         outs[0][...] = matmul(ins[0][...], ins[1][:, 3 * columns : 4 * columns]).astype(BF16)
 
-    return on_chip(body, "position_forward", (table, weights), (((table.shape[0], columns), BF16),))[0]
+    return on_chip(
+        body, "position_forward", (table, weights), (((table.shape[0], columns), BF16),)
+    )[0]
 
 
 def attention_forward(tokens, own, other, gains, weights, positions, biases, heads):
@@ -391,11 +456,12 @@
 
     def body(ins, outs, _):
         x_ref, own_ref, other_ref, gain_ref, weight_ref, table_ref, bias_ref = ins
-        after_ref, e_ref, qc_ref, qp_ref, k_ref, v_ref, prob_ref, mix_ref, part_ref = outs
+        after_ref, e_ref, kept_ref, prob_ref, mix_ref, part_ref, after_far_ref = outs
         after = x_ref[...].astype(F32) + 0.5 * (
             own_ref[...].astype(F32) + other_ref[...].astype(F32)
         )
         after_ref[...] = after
+        after_far_ref[...] = after
         normed, _ = norm_parts(after)
         entries = (normed * gain_ref[1:2, :]).astype(BF16)
         e_ref[...] = entries
@@ -405,10 +471,7 @@
         position_q = (queries + bias_ref[1:2, :]).astype(BF16)
         keys = joined[:, columns : 2 * columns].astype(BF16)
         values = joined[:, 2 * columns :].astype(BF16)
-        qc_ref[...] = content_q
-        qp_ref[...] = position_q
-        k_ref[...] = keys
-        v_ref[...] = values
+        kept_ref[...] = jnp.concatenate([content_q, position_q, keys, values], 1)
         mixed = []
         for head in range(heads):
             part = slice(head * features, (head + 1) * features)
@@ -424,21 +487,18 @@
         mix_ref[...] = attended
         part_ref[...] = right_transposed(attended, weight_ref[:, 4 * columns : 5 * columns]).astype(BF16)
 
-    local = ((rows, columns), BF16)
     return on_chip(
         body,
         "attention_forward",
         (tokens, own, other, gains, weights, positions, biases),
         (
             ((rows, width), F32),
+            far((rows, width), BF16),
+            far((rows, 4 * columns), BF16),
+            far((heads, rows, rows), F32),
+            far((rows, columns), BF16),
             ((rows, width), BF16),
-            local,
-            local,
-            local,
-            local,
-            ((heads, rows, rows), F32),
-            local,
-            ((rows, width), BF16),
+            far((rows, width), F32),
         ),
     )
 
@@ -458,17 +518,15 @@
             gain_ref,
             weight_ref,
             table_ref,
-            qc_ref,
-            qp_ref,
-            k_ref,
-            v_ref,
+            kept_ref,
             prob_ref,
         ) = ins
         total_ref, branch_ref, joined_ref, table_grad_ref, part_ref, gain_grad_ref, bias_ref = outs
         normed, factor = norm_parts(x_ref[...])
-        passed, gain_grad_ref[...] = norm_back(
+        passed, gain_grad = norm_back(
             own_ref[...].astype(F32) + other_ref[...].astype(F32), normed, factor, gain_ref[2:3, :]
         )
+        gain_grad_ref[...] = 0.5 * gain_grad
         total = grad_ref[...] + passed
         total_ref[...] = total
         branch = total.astype(BF16)
@@ -477,10 +535,10 @@
         line = lax.broadcasted_iota(jnp.int32, (rows, rows), 0)
         place = lax.broadcasted_iota(jnp.int32, (rows, rows), 1)
         flip = (line + place == rows - 1).astype(F32).astype(BF16)
-        content_q = qc_ref[...]
-        keys = k_ref[...]
-        values = v_ref[...]
-        flipped_q = matmul(flip, qp_ref[...]).astype(BF16)
+        content_q = kept_ref[:, :columns]
+        keys = kept_ref[:, 2 * columns : 3 * columns]
+        values = kept_ref[:, 3 * columns :]
+        flipped_q = matmul(flip, kept_ref[:, columns : 2 * columns]).astype(BF16)
         zeros = jnp.zeros((rows, rows), F32)
         from_content, from_position, to_keys, to_values, to_table = [], [], [], [], []
         for head in range(heads):
@@ -521,13 +579,14 @@
             ((rows, 3 * columns), BF16),
             ((2 * rows, columns), BF16),
             ((rows, width), BF16),
-            ((1, width), F32),
-            ((2, columns), F32),
+            far((1, width), F32),
+            far((2, columns), F32),
         ),
-    )
-
-
-def mixed_assemble(pairs, width):
+        fetch=(0, 3, 7, 8),
+    )
+
+
+def mixed_assemble(pairs, table, width):
     columns = pairs[0][0].shape[1]
 
     def body(ins, outs, _):
@@ -541,14 +600,14 @@
                     4,
                     4 * group * columns,
                 )
+        outs[1][...] = matmul(ins[4][...], outs[0][:, 3 * columns : 4 * columns]).astype(BF16)
 
     return on_chip(
         body,
         "mixed_assemble",
-        pairs[0] + pairs[1],
-        (((width, 8 * columns), BF16),),
-        flops=1_000_000,
-    )[0]
+        pairs[0] + pairs[1] + (table,),
+        (((width, 8 * columns), BF16), ((table.shape[0], columns), BF16)),
+    )
 
 
 def mixed_weight_grads(attention_parts, conv_parts, split):
@@ -585,15 +644,18 @@
         conv_branch,
         activated,
     )
+    fetch = (0, 5, 6, 7, 8, 9)
     if not split:
-        return on_chip(body, "mixed_weight_grads", operands, (((width, 8 * columns), F32),))[0]
-    halves = (((2 * width, columns), F32), ((2 * width, columns), BF16))
+        results = (((width, 8 * columns), F32),)
+        return on_chip(body, "mixed_weight_grads", operands, results, fetch=fetch)[0]
+    halves = (far((2 * width, columns), F32), ((2 * width, columns), BF16))
     values = on_chip(
         body,
         "mixed_weight_grads",
         operands,
         halves + halves,
         scratch=(pltpu.VMEM((width, 8 * columns), F32),),
+        fetch=fetch,
     )
     return values[0::2], values[1::2]
 
@@ -608,10 +670,11 @@
 
     def body(ins, outs, scratch):
         x_ref, own_ref, other_ref, gain_ref, weight_ref, tap_ref = ins
-        after_ref, c_ref, value_ref, gate_ref, conv_ref, sums_ref = outs
+        after_ref, c_ref, value_ref, gate_ref, conv_ref, sums_ref, after_far_ref, conv_far_ref = outs
         padded = scratch[0]
         after = x_ref[...] + (own_ref[...].astype(F32) + other_ref[...].astype(F32))
         after_ref[...] = after
+        after_far_ref[...] = after
         normed, _ = norm_parts(after)
         entries = (normed * gain_ref[2:3, :]).astype(BF16)
         c_ref[...] = entries
@@ -628,15 +691,25 @@
             start = PAD - half_taps + tap
             total = total + tap_ref[tap : tap + 1, :] * padded[start : start + rows, :]
         conv_ref[...] = total
+        conv_far_ref[...] = total
         sums_ref[0:1, :] = jnp.sum(total, 0, keepdims=True)
         sums_ref[1:2, :] = jnp.sum(total * total, 0, keepdims=True)
 
-    local = ((rows, columns), F32)
+    local = far((rows, columns), F32)
     return on_chip(
         body,
         "conv_forward",
         (residual, own, other, gains, weights, depth_kernel),
-        (((rows, width), F32), ((rows, width), BF16), local, local, local, ((2, columns), F32)),
+        (
+            ((rows, width), F32),
+            far((rows, width), BF16),
+            local,
+            local,
+            ((rows, columns), F32),
+            ((2, columns), F32),
+            far((rows, width), F32),
+            local,
+        ),
         scratch=(pltpu.VMEM((rows + 2 * PAD, columns), F32),),
     )
 
@@ -663,7 +736,7 @@
         body,
         "norm_forward",
         (convolved, sums, batch, weights),
-        (((rows, columns), BF16), ((rows, width), BF16)),
+        (far((rows, columns), BF16), ((rows, width), BF16)),
     )
 
 
@@ -677,9 +750,10 @@
         )
         total_ref, branch_ref, shifted_ref, grad_sums_ref, gain_grad_ref = outs
         normed, factor = norm_parts(x_ref[...])
-        passed, gain_grad_ref[...] = norm_back(
+        passed, gain_grad = norm_back(
             own_ref[...].astype(F32) + other_ref[...].astype(F32), normed, factor, gain_ref[3:4, :]
         )
+        gain_grad_ref[...] = 0.5 * gain_grad
         total = grad_ref[...] + passed
         total_ref[...] = total
         branch = total.astype(BF16)
@@ -697,12 +771,13 @@
         "norm_backward",
         (gradient, own, other, residual, gains, weights, convolved, sums, batch),
         (
-            ((rows, width), F32),
-            ((rows, width), BF16),
+            far((rows, width), F32),
+            far((rows, width), BF16),
             ((rows, columns), F32),
             ((2, columns), F32),
-            ((1, width), F32),
+            far((1, width), F32),
         ),
+        fetch=(3, 6),
     )
 
 
@@ -754,8 +829,9 @@
         body,
         "conv_backward",
         (grad_shifted, grad_sums, convolved, sums, batch, value, gate, weights, depth_kernel),
-        (((rows, columns), F32), ((rows, 2 * columns), BF16), ((rows, width), BF16)),
+        (((rows, columns), F32), far((rows, 2 * columns), BF16), ((rows, width), BF16)),
         scratch=(pltpu.VMEM((rows + 2 * PAD, columns), F32),),
+        fetch=(2, 5, 6),
     )
 
 
@@ -780,9 +856,10 @@
         body,
         "tap_gradients",
         (value, gate, grad_conv),
-        (((taps, columns), F32),),
+        (far((taps, columns), F32),),
         scratch=(pltpu.VMEM((rows + 2 * PAD, columns), F32),),
         flops=10_000_000,
+        fetch=(0, 1),
     )[0]
 
 
@@ -794,9 +871,10 @@
         grad_ref, own_ref, other_ref, x_ref, pre_ref, gain_ref, weight_ref = ins
         total_ref, branch_ref, slope_ref, keep_ref, send_ref, gain_grad_ref = outs
         normed, factor = norm_parts(x_ref[...])
-        passed, gain_grad_ref[...] = norm_back(
+        passed, gain_grad = norm_back(
             own_ref[...].astype(F32) + other_ref[...].astype(F32), normed, factor, gain_ref[1:2, :]
         )
+        gain_grad_ref[...] = 0.5 * gain_grad
         total = grad_ref[...] + passed
         total_ref[...] = own_half(total)
         part = ff_back_body(total, pre_ref, weight_ref, branch_ref, slope_ref)
@@ -813,28 +891,43 @@
             ((rows, hidden), BF16),
             ((rows // 2, width), F32),
             ((rows // 2, width), BF16),
-            ((1, width), F32),
+            far((1, width), F32),
         ),
-    )
-
-
-def input_back(gradient, own, other, tokens, gains):
+        fetch=(3, 4, 6),
+    )
+
+
+def input_back(gradient, own, other, tokens, gains, gain_grads, tap_grads, bias_grads):
     rows, width = tokens.shape
+    taps, columns = tap_grads.shape
+    upper = (taps + 1) // 2
+    packed_rows = -(-(6 + upper) // 8) * 8
 
     def body(ins, outs, _):
-        grad_ref, own_ref, other_ref, x_ref, gain_ref = ins
+        grad_ref, own_ref, other_ref, x_ref, gain_ref = ins[:5]
+        tap_ref, bias_ref = ins[9:]
+        packed = outs[1]
         normed, factor = norm_parts(x_ref[...].astype(F32))
-        passed, outs[1][...] = norm_back(
+        passed, gain_grad = norm_back(
             own_ref[...].astype(F32) + other_ref[...].astype(F32), normed, factor, gain_ref[0:1, :]
         )
         outs[0][...] = grad_ref[...] + passed
+        packed[...] = jnp.zeros((packed_rows, 2 * columns), F32)
+        packed[0:1, :] = gain_grad
+        for place in range(4):
+            packed[place + 1 : place + 2, :] = ins[5 + place][...]
+        packed[5:6, :columns] = bias_ref[0:1, :]
+        packed[5:6, columns:] = bias_ref[1:2, :]
+        packed[6 : 6 + upper, :columns] = tap_ref[:upper, :]
+        packed[6 : 6 + taps - upper, columns:] = tap_ref[upper:, :]
 
     return on_chip(
         body,
         "input_back",
-        (gradient, own, other, tokens, gains),
-        (((rows, width), F32), ((1, width), F32)),
+        (gradient, own, other, tokens, gains) + tuple(gain_grads) + (tap_grads, bias_grads),
+        (((rows, width), F32), ((packed_rows, 2 * columns), F32)),
         flops=1_000_000,
+        fetch=(5, 6, 7, 8, 9, 10),
     )
 
 
@@ -890,36 +983,41 @@
             attention_in.reshape(-1, columns),
             jnp.concatenate([attention_out, gated_in.reshape(-1, columns), pointwise_out], 0),
         )
-        for stage in range(3):
-            batch_one = gather_stage(batch_one, stage)
-            batch_two = gather_stage(tie(batch_two, batch_one), stage)
+        batch_one = gather_stage(batch_one, 0)
+        batch_one = gather_stage(tie(batch_one, tokens_all), 1)
+        batch_two = gather_stage(tie(batch_two, batch_one), 0)
+        batch_one = gather_stage(batch_one, 2)
         second_pieces = tie((second_in, second_out), batch_one)
+        batch_two = gather_stage(tie(batch_two, batch_one), 1)
         batch_one = gather_last(batch_one)
-        first_weights = ff_assemble(batch_one, width)
-        batch_two = gather_last(tie(batch_two, batch_one))
-        mixed_weights = mixed_assemble(batch_two, width)
+        batch_two = gather_stage(tie(batch_two, batch_one), 2)
         second_weights = gather(second_pieces)
     else:
-        first_weights = gather([first_in, first_out])
+        batch_one = gather([first_in, first_out])
         mixed_weights = gather(
             unstacked(attention_in) + [attention_out] + unstacked(gated_in) + [pointwise_out]
         )
         second_weights = gather([second_in, second_out])
-
-    entries1, pre1, hidden1, part1 = first_forward(tokens_all, norm_gains, first_weights)
+        positions = position_forward(table, mixed_weights, columns)
+
+    entries1, pre1, hidden1, part1, first_weights = first_forward(
+        tokens_all, norm_gains, batch_one
+    )
     other1 = swap(part1)
-    positions = position_forward(table, mixed_weights, columns)
-    after1, entries2, qc, qp, keys, values, prob, attended, part2 = attention_forward(
+    if split:
+        batch_two = gather_last(tie(batch_two, part1))
+        mixed_weights, positions = mixed_assemble(batch_two, table, width)
+    after1, entries2, kept, prob, attended, part2, after1_far = attention_forward(
         tokens_all, part1, other1, norm_gains, mixed_weights, positions, head_biases, local_heads
     )
     other2 = swap(part2)
-    after2, entries3, value_pre, gate, convolved, sums = conv_forward(
+    after2, entries3, value_pre, gate, convolved, sums, after2_far, conv_far = conv_forward(
         after1, part2, other2, norm_gains, mixed_weights, depth_kernel
     )
     sums = sum_over(sums, "dp")
     activated, part3 = norm_forward(convolved, sums, batch, mixed_weights, token_count)
     other3 = swap(part3)
-    after3, entries4, pre4, hidden4, part4 = second_forward(
+    after3, entries4, pre4, hidden4, part4, after3_far = second_forward(
         after2, part3, other3, norm_gains, second_weights
     )
     other4 = swap(part4)
@@ -931,13 +1029,22 @@
     other5 = tie(other5, grads_second)
     reduced_second = reduce_plain(grads_second)
     grad3, branch3, grad_shifted, grad_sums, gain4 = norm_backward(
-        grad4, part5, other5, after3, norm_gains, mixed_weights, convolved, sums, batch, token_count
+        grad4,
+        part5,
+        other5,
+        after3_far,
+        norm_gains,
+        mixed_weights,
+        conv_far,
+        sums,
+        batch,
+        token_count,
     )
     grad_sums = sum_over(grad_sums, "dp")
     grad_conv, joined3, part6 = conv_backward(
         grad_shifted,
         grad_sums,
-        convolved,
+        conv_far,
         sums,
         batch,
         value_pre,
@@ -952,11 +1059,11 @@
         grad3,
         part6,
         other6,
-        after2,
+        after2_far,
         norm_gains,
         mixed_weights,
         positions,
-        (qc, qp, keys, values, prob),
+        (kept, prob),
         local_heads,
     )
     other7 = swap(part7)
@@ -966,12 +1073,14 @@
         split,
     )
     grad1, branch1, slope1, keep8, send8, gain2 = first_back(
-        grad2, part7, other7, after1, pre1, norm_gains, first_weights
+        grad2, part7, other7, after1_far, pre1, norm_gains, first_weights
     )
     if split:
         first_grads = ff_weight_split(entries1, slope1, branch1, hidden1, "first_weight_grads")
         for stage in range(4):
-            mixed_grads = scatter_stage(*mixed_grads, stage, "mixed_sum")
+            mixed_grads = scatter_stage(
+                *mixed_grads, stage, "mixed_sum", (0, 1) if stage == 0 else ()
+            )
             first_grads = scatter_stage(*first_grads, stage, "first_sum")
         (mixed_a, mixed_b), (reduced_in, reduced_out) = mixed_grads[0], first_grads[0]
         rows = mixed_a.shape[0] // 4
@@ -990,18 +1099,24 @@
         reduced_gated = stacked_columns(mixed[:, 5 * columns : 7 * columns], 2)
         reduced_pointwise = mixed[:, 7 * columns :]
     other8 = swap(send8)
-    grad_start, gain1 = input_back(grad1, keep8, other8, tokens, norm_gains)
-
-    gains = jnp.concatenate([gain1, 0.5 * gain2, 0.5 * gain3, 0.5 * gain4, 0.5 * gain5], 0)
-    packed = jnp.concatenate(
-        [jnp.reshape(value, (-1, 128)) for value in (gains, tap_grads, bias_grads)], 0
+    grad_start, packed = input_back(
+        grad1,
+        keep8,
+        other8,
+        tokens,
+        norm_gains,
+        (gain2, gain3, gain4, gain5),
+        tap_grads,
+        bias_grads,
     )
     packed = sum_over(packed, "dp")
-    gain_rows = gains.size // 128
-    tap_rows = tap_grads.size // 128
-    gain_total = sum_over(packed[:gain_rows].reshape(gains.shape), "tensor")
-    tap_total = packed[gain_rows : gain_rows + tap_rows].reshape(tap_grads.shape)
-    bias_total = packed[gain_rows + tap_rows :].reshape(bias_grads.shape)
+    gain_total = sum_over(packed[:5], "tensor")
+    bias_total = packed[5].reshape(bias_grads.shape)
+    taps = tap_grads.shape[0]
+    upper = (taps + 1) // 2
+    tap_total = jnp.concatenate(
+        [packed[6 : 6 + upper, :columns], packed[6 : 6 + taps - upper, columns:]], 0
+    )
     return (
         block_out,
         grad_start,

time: 255 us -> 236 us (0.925)
  local copies, waits for them, and re-layouts: 49.4 us -> 24.8 us
  waiting for transfers between devices: 83.9 us -> 90.4 us
    unnamed x192 -> x110, local copies, waits for them, and re-layouts: 41.9 us -> 20.7 us
    ppermute x48, waiting for transfers between devices: 49.4 us -> 54.7 us  [shift(): lax.ppermute(value, axis, [(k, k ^ mask) for k in range(lax.axis_size(axi...]
    ppermute x10, starting transfers between devices: 9.92 us -> 14 us  [swap(): return lax.ppermute(value, 'tensor', [(0, 1), (1, 0)])]
    ppermute x48, starting transfers between devices: 54.1 us -> 50.4 us  [shift(): lax.ppermute(value, axis, [(k, k ^ mask) for k in range(lax.axis_size(axi...]
    reshape x6 -> x0, local copies, waits for them, and re-layouts: 3.19 us -> none  [the longest x3 1.97 us: body(): jnp.reshape(value, (-1, 128))]
    pallas_call x26 -> x24, Pallas kernels: 30.8 us -> 33 us  [on_chip(): pl.pallas_call(kernel, out_shape=[jax.ShapeDtypeStruct(r[0], r[1]) for r...]
  transfers between devices with their start and end apart: 60 -> 60, of which waited for: 35 -> 39; matrix products, arithmetic and copies ran while one was open for 7% -> 3% of each run, Pallas kernels for 11% -> 12%
where the time goes in v3:
time: 236 us
  waiting for transfers between devices  90.4 us (38%)
  starting transfers between devices  64.6 us (27%)
  Pallas kernels  33 us (14%)
  local copies, waits for them, and re-layouts  24.8 us (11%)
  between operations  14.9 us (6%)
  other arithmetic  7.98 us (3%)
    ppermute x48, waiting for transfers between devices, shift(): lax.ppermute(value, axis, [(k, k ^ mask) for k in range(lax.axis_size(axi...  54.7 us
    ppermute x48, starting transfers between devices, shift(): lax.ppermute(value, axis, [(k, k ^ mask) for k in range(lax.axis_size(axi...  50.4 us
    ppermute x10, waiting for transfers between devices, swap(): return lax.ppermute(value, 'tensor', [(0, 1), (1, 0)])  35.7 us
    pallas_call x24, Pallas kernels, on_chip(): pl.pallas_call(kernel, out_shape=[jax.ShapeDtypeStruct(r[0], r[1]) for r...  33 us
    unnamed x110, local copies, waits for them, and re-layouts  20.7 us
    ppermute x10, starting transfers between devices, swap(): return lax.ppermute(value, 'tensor', [(0, 1), (1, 0)])  14 us
  transfers between devices with their start and end apart: 60, of which 39 were waited for; matrix products, arithmetic and copies ran while one was open for 3% of the time, Pallas kernels for 12%

profile of v3, /device:TPU:0, one launch (start us, length us, event | category | flops | bytes accessed | tf_op | source)
XLA Modules:
  0.0 235.7 jit_solution(6167920636286644117)
XLA Ops:
  7.2 4.1 %collective-permute-start.1 = (bf16[32,1024]{1,0:T(8,128)(2,1)}, bf16[32,1024]{1,0:T(8,128)(2,1)S(1)}, u32[]{:S(2)}, u32[]{:S(2)}) collective-permute-start(bf16[32,1024]{1,0:T(8,128)(2,1)} %param.17), channel_id=1, source_target_pairs={{0,16},{2,18},{4,20},{6,22},{8,24},{10,26},{12,28},{14,30},{16,0},... | collective-permute-start | bytes 196616 | tf_op jit(solution)/shard_map/ppermute | solution.py:171
  11.4 1.8 collective-permute-start.26
  13.4 1.8 collective-permute-done.1
  16.0 2.0 collective-permute-done.2
  19.4 1.7 broadcast_select_fusion.1
  21.1 1.6 collective-permute-start.3
  22.8 1.6 collective-permute-start.6
  24.4 1.8 collective-permute-done.3
  26.2 1.6 collective-permute-start.4
  29.4 4.0 %collective-permute-done.4 = bf16[128,1024]{1,0:T(8,128)(2,1)S(1)} collective-permute-done((bf16[128,1024]{1,0:T(8,128)(2,1)S(1)}, bf16[128,1024]{1,0:T(8,128)(2,1)S(1)}, u32[]{:S(2)}, u32[]{:S(2)}) %collective-permute-start.4) | collective-permute-done | bytes 262176 | tf_op jit(solution)/shard_map/ppermute | solution.py:171
  33.5 1.7 collective-permute-done.7
  36.0 3.3 %collective-permute-start.10 = (bf16[128,256]{1,0:T(8,128)(2,1)S(1)}, bf16[128,256]{1,0:T(8,128)(2,1)S(1)}, u32[]{:S(2)}, u32[]{:S(2)}) collective-permute-start(bf16[128,256]{1,0:T(8,128)(2,1)S(1)} %bitcast.9), channel_id=1, source_target_pairs={{0,16},{2,18},{4,20},{6,22},{8,24},{10,26},{12,28},{14,30},{16,0},... | collective-permute-start | bytes 196616 | tf_op jit(solution)/shard_map/ppermute | solution.py:171
  39.9 2.1 collective-permute-done.10
  42.0 2.7 %collective-permute-done.11 = bf16[128,256]{1,0:T(8,128)(2,1)S(1)} collective-permute-done((bf16[128,256]{1,0:T(8,128)(2,1)S(1)}, bf16[128,256]{1,0:T(8,128)(2,1)S(1)}, u32[]{:S(2)}, u32[]{:S(2)}) %collective-permute-start.11) | collective-permute-done | bytes 65568 | tf_op jit(solution)/shard_map/ppermute | solution.py:171
  44.7 1.6 collective-permute-start.13
  46.4 5.7 %collective-permute-done.12 = bf16[256,256]{1,0:T(8,128)(2,1)S(1)} collective-permute-done((bf16[256,256]{1,0:T(8,128)(2,1)S(1)}, bf16[256,256]{1,0:T(8,128)(2,1)S(1)}, u32[]{:S(2)}, u32[]{:S(2)}) %collective-permute-start.12) | collective-permute-done | bytes 131104 | tf_op jit(solution)/shard_map/ppermute | solution.py:171
  52.2 1.5 collective-permute-start.14
  54.9 1.9 first_forward.1
  61.1 2.2 multiply_sine_fusion
  63.4 1.6 collective-permute-start.9
  65.7 6.1 %collective-permute-done.9.refs_2_ = bf16[256,512]{1,0:T(8,128)(2,1)S(1)} collective-permute-done((bf16[256,512]{1,0:T(8,128)(2,1)S(1)}, bf16[256,512]{1,0:T(8,128)(2,1)S(1)}, u32[]{:S(2)}, u32[]{:S(2)}) %collective-permute-start.9) | collective-permute-done | bytes 262176 | tf_op jit(solution)/shard_map/ppermute | solution.py:151
  71.8 4.7 %attention_forward.1 = (f32[256,512]{1,0:T(8,128)S(1)}, bf16[256,512]{1,0:T(8,128)(2,1)S(1)}, bf16[256,1024]{1,0:T(8,128)(2,1)S(1)}, f32[4,256,256]{2,1,0:T(8,12...) custom-call(bf16[256,512]{1,0:T(8,128)(2,1)S(1)} %pad_maximum_fusion.2.refs_0_, ...), custom_call_target="tpu_custom_call" | custom-call | flops 300000000 | bytes 6434816 | tf_op jit(solution)/shard_map/attention_forward/pallas_call | solution.py:138
  79.8 1.5 collective-permute-start.18
  81.3 6.0 %collective-permute-done.18.refs_2_ = bf16[256,512]{1,0:T(8,128)(2,1)S(1)} collective-permute-done((bf16[256,512]{1,0:T(8,128)(2,1)S(1)}, bf16[256,512]{1,0:T(8,128)(2,1)S(1)}, u32[]{:S(2)}, u32[]{:S(2)}) %collective-permute-start.18) | collective-permute-done | bytes 262176 | tf_op jit(solution)/shard_map/ppermute | solution.py:151
  87.3 2.4 %conv_forward.1 = (f32[256,512]{1,0:T(8,128)S(1)}, bf16[256,512]{1,0:T(8,128)(2,1)S(1)}, f32[256,256]{1,0:T(8,128)S(1)}, f32[256,256]{1,0:T(8,128)S(1)}, f32[256...) custom-call(f32[256,512]{1,0:T(8,128)S(1)} %get-tuple-element.136.refs_0_, ...), custom_call_target="tpu_custom_call" | custom-call | flops 300000000 | bytes 5549056 | tf_op jit(solution)/shard_map/conv_forward/pallas_call | solution.py:138
  93.3 2.8 %collective-permute-done.20 = f32[2,256]{1,0:T(2,128)S(1)} collective-permute-done((f32[2,256]{1,0:T(2,128)S(1)}, f32[2,256]{1,0:T(2,128)S(1)}, u32[]{:S(2)}, u32[]{:S(2)}) %collective-permute-start.20) | collective-permute-done | bytes 2080 | tf_op jit(solution)/shard_map/ppermute | solution.py:171
  96.1 2.5 %collective-permute-start.23 = (f32[2,256]{1,0:T(2,128)S(1)}, f32[2,256]{1,0:T(2,128)S(1)}, u32[]{:S(2)}, u32[]{:S(2)}) collective-permute-start(f32[2,256]{1,0:T(2,128)S(1)} %add.59), channel_id=1, source_target_pairs={{0,24},{2,26},{4,28},{6,30},{8,16},{10,18},{12,20},{14,22},{16,8},... | collective-permute-start | bytes 6152 | tf_op jit(solution)/shard_map/ppermute | solution.py:171
  99.0 1.5 collective-permute-start.21
  101.5 1.6 collective-permute-done.22
  104.3 1.5 collective-permute-start.24
  106.5 4.2 %collective-permute-done.24.refs_2_ = bf16[256,512]{1,0:T(8,128)(2,1)S(1)} collective-permute-done((bf16[256,512]{1,0:T(8,128)(2,1)S(1)}, bf16[256,512]{1,0:T(8,128)(2,1)S(1)}, u32[]{:S(2)}, u32[]{:S(2)}) %collective-permute-start.24) | collective-permute-done | bytes 262176 | tf_op jit(solution)/shard_map/ppermute | solution.py:151
  111.4 1.6 copy-done.1
  116.0 1.5 second_forward.1
  118.3 1.5 collective-permute-start.25
  119.8 4.9 %collective-permute-done.25.refs_2_ = bf16[256,512]{1,0:T(8,128)(2,1)S(1)} collective-permute-done((bf16[256,512]{1,0:T(8,128)(2,1)S(1)}, bf16[256,512]{1,0:T(8,128)(2,1)S(1)}, u32[]{:S(2)}, u32[]{:S(2)}) %collective-permute-start.25) | collective-permute-done | bytes 262176 | tf_op jit(solution)/shard_map/ppermute | solution.py:151
  124.7 2.2 second_back.1
  131.1 1.5 collective-permute-start.27
  132.7 5.1 %collective-permute-done.27.refs_2_ = bf16[256,512]{1,0:T(8,128)(2,1)S(1)} collective-permute-done((bf16[256,512]{1,0:T(8,128)(2,1)}, bf16[256,512]{1,0:T(8,128)(2,1)S(1)}, u32[]{:S(2)}, u32[]{:S(2)}) %collective-permute-start.27) | collective-permute-done | bytes 262176 | tf_op jit(solution)/shard_map/ppermute | solution.py:151
  143.7 2.9 %collective-permute-done.29 = f32[2,256]{1,0:T(2,128)S(1)} collective-permute-done((f32[2,256]{1,0:T(2,128)S(1)}, f32[2,256]{1,0:T(2,128)S(1)}, u32[]{:S(2)}, u32[]{:S(2)}) %collective-permute-start.29) | collective-permute-done | bytes 2080 | tf_op jit(solution)/shard_map/ppermute | solution.py:171
  146.6 2.4 %collective-permute-start.32 = (f32[2,256]{1,0:T(2,128)S(1)}, f32[2,256]{1,0:T(2,128)S(1)}, u32[]{:S(2)}, u32[]{:S(2)}) collective-permute-start(f32[2,256]{1,0:T(2,128)S(1)} %add.64), channel_id=1, source_target_pairs={{0,24},{2,26},{4,28},{6,30},{8,16},{10,18},{12,20},{14,22},{16,8},... | collective-permute-start | bytes 6152 | tf_op jit(solution)/shard_map/ppermute | solution.py:171
  149.0 2.0 collective-permute-start.30
  152.0 1.5 collective-permute-done.31
  153.5 2.3 conv_backward.1
  155.8 1.5 collective-permute-start.33
  157.3 4.9 %collective-permute-done.33.refs_2_ = bf16[256,512]{1,0:T(8,128)(2,1)S(1)} collective-permute-done((bf16[256,512]{1,0:T(8,128)(2,1)S(1)}, bf16[256,512]{1,0:T(8,128)(2,1)S(1)}, u32[]{:S(2)}, u32[]{:S(2)}) %collective-permute-start.33) | collective-permute-done | bytes 262176 | tf_op jit(solution)/shard_map/ppermute | solution.py:151
  162.3 4.3 %attention_back.1 = (f32[256,512]{1,0:T(8,128)S(1)}, bf16[256,512]{1,0:T(8,128)(2,1)S(1)}, bf16[256,768]{1,0:T(8,128)(2,1)S(1)}, bf16[512,256]{1,0:T(8,128)(2,1)...) custom-call(f32[256,512]{1,0:T(8,128)S(1)} %get-tuple-element.157.refs_0_, ...), custom_call_target="tpu_custom_call" | custom-call | flops 300000000 | bytes 7223296 | tf_op jit(solution)/shard_map/attention_back/pallas_call | solution.py:138
  166.5 1.5 collective-permute-start.34
  168.1 2.5 %mixed_weight_grads.1 = (f32[1024,256]{1,0:T(8,128)S(1)}, bf16[1024,256]{1,0:T(8,128)(2,1)S(1)}, f32[1024,256]{1,0:T(8,128)S(1)}, bf16[1024,256]{1,0:T(8,128)(2,1)S(1)}) custom-call(bf16[256,512]{1,0:T(8,128)(2,1)S(1)} %copy-done.35, bf16[256,768]{1,0:T(8,128)(2,1)S(1)} %get-tuple-element.205.refs_1_, bf16[512,512]{1,0:T(8,128)(2,1)S(1)} %fusion.refs_4_.refs_2_, ...), custom_call_target="tpu_custom_call" | custom-call | flops 300000000 | bytes 5898240 | tf_op jit(solution)/shard_map/mixed_weight_grads/pallas_call | solution.py:138
  171.2 1.8 collective-permute-done.34.refs_2_
  173.0 1.7 first_back.1
  178.1 1.9 tap_gradients.1.refs_9_
  179.9 2.2 collective-permute-done.35.refs_2_
  184.9 3.8 %collective-permute-done.37 = f32[24,512]{1,0:T(8,128)S(1)} collective-permute-done((f32[24,512]{1,0:T(8,128)S(1)}, f32[24,512]{1,0:T(8,128)S(1)}, u32[]{:S(2)}, u32[]{:S(2)}) %collective-permute-start.37) | collective-permute-done | bytes 49184 | tf_op jit(solution)/shard_map/ppermute | solution.py:171
  188.7 1.7 collective-permute-start.40
  191.3 1.8 collective-permute-start.38
  196.6 1.8 collective-permute-start.45
  198.5 4.3 %collective-permute-done.52.refs_2_ = bf16[512,256]{1,0:T(8,128)(2,1)S(1)} collective-permute-done((bf16[512,256]{1,0:T(8,128)(2,1)S(1)}, bf16[512,256]{1,0:T(8,128)(2,1)S(1)}, u32[]{:S(2)}, u32[]{:S(2)}) %collective-permute-start.52) | collective-permute-done | bytes 262176 | tf_op jit(solution)/shard_map/ppermute | solution.py:171
  205.3 1.5 collective-permute-start.41
  208.0 2.1 collective-permute-done.54.refs_2_
  211.0 2.1 collective-permute-start.57
  213.5 1.7 collective-permute-start.47
  218.5 2.4 %collective-permute-start.48 = (bf16[32,1024]{1,0:T(8,128)(2,1)S(1)}, bf16[32,1024]{1,0:T(8,128)(2,1)S(1)}, u32[]{:S(2)}, u32[]{:S(2)}) collective-permute-start(bf16[32,1024]{1,0:T(8,128)(2,1)S(1)} %get-tuple-element.200), channel_id=1, source_target_pairs={{0,16},{2,18},{4,20},{6,22},{8,24},{10,26},{12,28},{14,30},{16,0},... | collective-permute-start | bytes 196616 | tf_op jit(solution)/shard_map/ppermute | solution.py:171
  223.7 2.8 %collective-permute-done.49.refs_3_ = bf16[32,1024]{1,0:T(8,128)(2,1)S(1)} collective-permute-done((bf16[32,1024]{1,0:T(8,128)(2,1)S(1)}, bf16[32,1024]{1,0:T(8,128)(2,1)S(1)}, u32[]{:S(2)}, u32[]{:S(2)}) %collective-permute-start.49) | collective-permute-done | bytes 65568 | tf_op jit(solution)/shard_map/ppermute | solution.py:171
  227.2 1.6 fusion.1
  (235 shorter events, 60.5 us)
Async XLA Ops:
  7.2 104.2 %all-gather.2.cloned.1.call-start = ((), (), s32[]{:S(2)}) async-start(), calls=%async_computation.1 | async-start | bytes 2228224 | tf_op jit(solution)/shard_map/all_gather | solution.py:975
  7.2 8.0 %collective-permute-start.1 = (bf16[32,1024]{1,0:T(8,128)(2,1)}, bf16[32,1024]{1,0:T(8,128)(2,1)S(1)}, u32[]{:S(2)}, u32[]{:S(2)}) collective-permute-start(bf16[32,1024]{1,0:T(8,128)(2,1)} %param.17), channel_id=1, source_target_pairs={{0,16},{2,18},{4,20},{6,22},{8,24},{10,26},{12,28},{14,30},{16,0},... | collective-permute-start | bytes 196616 | tf_op jit(solution)/shard_map/ppermute | solution.py:171
  11.3 6.7 %collective-permute-start.2 = (bf16[32,1024]{1,0:T(8,128)(2,1)}, bf16[32,1024]{1,0:T(8,128)(2,1)S(1)}, u32[]{:S(2)}, u32[]{:S(2)}) collective-permute-start(bf16[32,1024]{1,0:T(8,128)(2,1)} %param.18), channel_id=1, source_target_pairs={{0,16},{2,18},{4,20},{6,22},{8,24},{10,26},{12,28},{14,30},{16,0},... | collective-permute-start | bytes 196616 | tf_op jit(solution)/shard_map/ppermute | solution.py:171
  11.4 7.5 %collective-permute-start.26 = (bf16[128,512]{1,0:T(8,128)(2,1)}, bf16[128,512]{1,0:T(8,128)(2,1)S(1)}, u32[]{:S(2)}, u32[]{:S(2)}) collective-permute-start(bf16[128,512]{1,0:T(8,128)(2,1)} %param.29), channel_id=1, source_target_pairs={{0,1},{1,0},{2,3},{3,2},{4,5},{5,4},{6,7},{7,6},{8,9},{9,8},{10,11... | collective-permute-start | bytes 393224 | tf_op jit(solution)/shard_map/ppermute | solution.py:151
  13.2 6.2 %collective-permute-start = (bf16[128,512]{1,0:T(8,128)(2,1)}, bf16[128,512]{1,0:T(8,128)(2,1)S(1)}, u32[]{:S(2)}, u32[]{:S(2)}) collective-permute-start(bf16[128,512]{1,0:T(8,128)(2,1)} %refs_3_.7), channel_id=1, source_target_pairs={{0,1},{1,0},{2,3},{3,2},{4,5},{5,4},{6,7},{7,6},{8,9},{9,8},{10,11... | collective-permute-start | bytes 393224 | tf_op jit(solution)/shard_map/ppermute | solution.py:151
  21.1 5.0 %collective-permute-start.3 = (bf16[64,1024]{1,0:T(8,128)(2,1)S(1)}, bf16[64,1024]{1,0:T(8,128)(2,1)S(1)}, u32[]{:S(2)}, u32[]{:S(2)}) collective-permute-start(bf16[64,1024]{1,0:T(8,128)(2,1)S(1)} %pad_maximum_fusion.6), channel_id=1, source_target_pairs={{0,8},{2,10},{4,12},{6,14},{8,0},{10,2},{12,4},{14,6},{16,24},{18,... | collective-permute-start | bytes 393224 | tf_op jit(solution)/shard_map/ppermute | solution.py:171
  22.8 32.1 %copy-start.4 = (f32[5,512]{1,0:T(8,128)S(1)}, f32[5,512]{1,0:T(8,128)}, u32[]{:S(2)}) copy-start(f32[5,512]{1,0:T(8,128)} %refs_4_.5) | copy-start | bytes 30724
  22.8 5.9 %collective-permute-start.6 = (bf16[64,1024]{1,0:T(8,128)(2,1)S(1)}, bf16[64,1024]{1,0:T(8,128)(2,1)S(1)}, u32[]{:S(2)}, u32[]{:S(2)}) collective-permute-start(bf16[64,1024]{1,0:T(8,128)(2,1)S(1)} %pad_maximum_fusion.7), channel_id=1, source_target_pairs={{0,4},{2,6},{4,0},{6,2},{8,12},{10,14},{12,8},{14,10},{16,20},{18,... | collective-permute-start | bytes 393224 | tf_op jit(solution)/shard_map/ppermute | solution.py:171
  26.2 7.3 %collective-permute-start.4 = (bf16[128,1024]{1,0:T(8,128)(2,1)S(1)}, bf16[128,1024]{1,0:T(8,128)(2,1)S(1)}, u32[]{:S(2)}, u32[]{:S(2)}) collective-permute-start(bf16[128,1024]{1,0:T(8,128)(2,1)S(1)} %get-tuple-element.243), channel_id=1, source_target_pairs={{0,4},{2,6},{4,0},{6,2},{8,12},{10,14},{12,8},{14,10},{16,20},{18,... | collective-permute-start | bytes 786440 | tf_op jit(solution)/shard_map/ppermute | solution.py:171
  28.7 6.4 %collective-permute-start.7 = (bf16[128,1024]{1,0:T(8,128)(2,1)S(1)}, bf16[128,1024]{1,0:T(8,128)(2,1)S(1)}, u32[]{:S(2)}, u32[]{:S(2)}) collective-permute-start(bf16[128,1024]{1,0:T(8,128)(2,1)S(1)} %get-tuple-element.239), channel_id=1, source_target_pairs={{0,8},{2,10},{4,12},{6,14},{8,0},{10,2},{12,4},{14,6},{16,24},{18,... | collective-permute-start | bytes 786440 | tf_op jit(solution)/shard_map/ppermute | solution.py:171
  35.9 191.4 %reduce-scatter.2.cloned.1.call-start = ((), (), s32[]{:S(2)}) async-start(), calls=%async_computation.2 | async-start | bytes 2228224 | tf_op jit(solution)/shard_map/reduce_scatter | solution.py:935
  36.0 6.0 %collective-permute-start.10 = (bf16[128,256]{1,0:T(8,128)(2,1)S(1)}, bf16[128,256]{1,0:T(8,128)(2,1)S(1)}, u32[]{:S(2)}, u32[]{:S(2)}) collective-permute-start(bf16[128,256]{1,0:T(8,128)(2,1)S(1)} %bitcast.9), channel_id=1, source_target_pairs={{0,16},{2,18},{4,20},{6,22},{8,24},{10,26},{12,28},{14,30},{16,0},... | collective-permute-start | bytes 196616 | tf_op jit(solution)/shard_map/ppermute | solution.py:171
  39.3 5.4 %collective-permute-start.11 = (bf16[128,256]{1,0:T(8,128)(2,1)S(1)}, bf16[128,256]{1,0:T(8,128)(2,1)S(1)}, u32[]{:S(2)}, u32[]{:S(2)}) collective-permute-start(bf16[128,256]{1,0:T(8,128)(2,1)S(1)} %pad_maximum_fusion.11), channel_id=1, source_target_pairs={{0,16},{2,18},{4,20},{6,22},{8,24},{10,26},{12,28},{14,30},{16,0},... | collective-permute-start | bytes 196616 | tf_op jit(solution)/shard_map/ppermute | solution.py:171
  39.4 12.8 %collective-permute-start.5 = (bf16[256,1024]{1,0:T(8,128)(2,1)S(1)}, bf16[256,1024]{1,0:T(8,128)(2,1)S(1)}, u32[]{:S(2)}, u32[]{:S(2)}) collective-permute-start(bf16[256,1024]{1,0:T(8,128)(2,1)S(1)} %constant_dynamic-update-slice_fusion.2.refs_2_), channel_id=1, source_target_pairs={{0,2},{2,0},{4,6},{6,4},{8,10},{10,8},{12,14},{14,12},{16,18},{18,... | collective-permute-start | bytes 1572872 | tf_op jit(solution)/shard_map/ppermute | solution.py:171
  39.4 12.8 %collective-permute-start.8 = (bf16[256,1024]{1,0:T(8,128)(2,1)S(1)}, bf16[256,1024]{1,0:T(8,128)(2,1)S(1)}, u32[]{:S(2)}, u32[]{:S(2)}) collective-permute-start(bf16[256,1024]{1,0:T(8,128)(2,1)S(1)} %constant_dynamic-update-slice_fusion.7.refs_4_), channel_id=1, source_target_pairs={{0,2},{2,0},{4,6},{6,4},{8,10},{10,8},{12,14},{14,12},{16,18},{18,... | collective-permute-start | bytes 1572872 | tf_op jit(solution)/shard_map/ppermute | solution.py:171
  44.7 7.4 %collective-permute-start.12 = (bf16[256,256]{1,0:T(8,128)(2,1)S(1)}, bf16[256,256]{1,0:T(8,128)(2,1)S(1)}, u32[]{:S(2)}, u32[]{:S(2)}) collective-permute-start(bf16[256,256]{1,0:T(8,128)(2,1)S(1)} %pad_maximum_fusion.8), channel_id=1, source_target_pairs={{0,8},{2,10},{4,12},{6,14},{8,0},{10,2},{12,4},{14,6},{16,24},{18,... | collective-permute-start | bytes 393224 | tf_op jit(solution)/shard_map/ppermute | solution.py:171
  44.7 7.4 %collective-permute-start.13 = (bf16[256,256]{1,0:T(8,128)(2,1)S(1)}, bf16[256,256]{1,0:T(8,128)(2,1)S(1)}, u32[]{:S(2)}, u32[]{:S(2)}) collective-permute-start(bf16[256,256]{1,0:T(8,128)(2,1)S(1)} %pad_maximum_fusion.9), channel_id=1, source_target_pairs={{0,4},{2,6},{4,0},{6,2},{8,12},{10,14},{12,8},{14,10},{16,20},{18,... | collective-permute-start | bytes 393224 | tf_op jit(solution)/shard_map/ppermute | solution.py:171
  52.2 6.9 %collective-permute-start.14 = (bf16[512,256]{1,0:T(8,128)(2,1)S(1)}, bf16[512,256]{1,0:T(8,128)(2,1)S(1)}, u32[]{:S(2)}, u32[]{:S(2)}) collective-permute-start(bf16[512,256]{1,0:T(8,128)(2,1)S(1)} %pad_maximum_fusion.3), channel_id=1, source_target_pairs={{0,4},{2,6},{4,0},{6,2},{8,12},{10,14},{12,8},{14,10},{16,20},{18,... | collective-permute-start | bytes 786440 | tf_op jit(solution)/shard_map/ppermute | solution.py:171
  53.7 6.8 %collective-permute-start.15 = (bf16[512,256]{1,0:T(8,128)(2,1)S(1)}, bf16[512,256]{1,0:T(8,128)(2,1)S(1)}, u32[]{:S(2)}, u32[]{:S(2)}) collective-permute-start(bf16[512,256]{1,0:T(8,128)(2,1)S(1)} %pad_maximum_fusion.4), channel_id=1, source_target_pairs={{0,8},{2,10},{4,12},{6,14},{8,0},{10,2},{12,4},{14,6},{16,24},{18,... | collective-permute-start | bytes 786440 | tf_op jit(solution)/shard_map/ppermute | solution.py:171
  60.6 4.6 %collective-permute-start.16 = (bf16[1024,256]{1,0:T(8,128)(2,1)S(1)}, bf16[1024,256]{1,0:T(8,128)(2,1)S(1)}, u32[]{:S(2)}, u32[]{:S(2)}) collective-permute-start(bf16[1024,256]{1,0:T(8,128)(2,1)S(1)} %pad_maximum_fusion.refs_0_), channel_id=1, source_target_pairs={{0,2},{2,0},{4,6},{6,4},{8,10},{10,8},{12,14},{14,12},{16,18},{18,... | collective-permute-start | bytes 1572872 | tf_op jit(solution)/shard_map/ppermute | solution.py:171
  60.6 4.5 %collective-permute-start.17 = (bf16[1024,256]{1,0:T(8,128)(2,1)S(1)}, bf16[1024,256]{1,0:T(8,128)(2,1)S(1)}, u32[]{:S(2)}, u32[]{:S(2)}) collective-permute-start(bf16[1024,256]{1,0:T(8,128)(2,1)S(1)} %pad_maximum_fusion.1.refs_2_), channel_id=1, source_target_pairs={{0,2},{2,0},{4,6},{6,4},{8,10},{10,8},{12,14},{14,12},{16,18},{18,... | collective-permute-start | bytes 1572872 | tf_op jit(solution)/shard_map/ppermute | solution.py:171
  63.4 8.4 %collective-permute-start.9 = (bf16[256,512]{1,0:T(8,128)(2,1)S(1)}, bf16[256,512]{1,0:T(8,128)(2,1)S(1)}, u32[]{:S(2)}, u32[]{:S(2)}) collective-permute-start(bf16[256,512]{1,0:T(8,128)(2,1)S(1)} %get-tuple-element.125.refs_1_), channel_id=1, source_target_pairs={{0,1},{1,0},{2,3},{3,2},{4,5},{5,4},{6,7},{7,6},{8,9},{9,8},{10,11... | collective-permute-start | bytes 786440 | tf_op jit(solution)/shard_map/ppermute | solution.py:151
  65.7 24.1 %copy-start.9 = (bf16[512,256]{1,0:T(8,128)(2,1)}, bf16[512,256]{1,0:T(8,128)(2,1)S(1)}, u32[]{:S(2)}) copy-start(bf16[512,256]{1,0:T(8,128)(2,1)S(1)} %get-tuple-element.135.refs_5_.refs_6_) | copy-start | bytes 786436
  65.7 21.7 %copy-start.38 = (f32[31,256]{1,0:T(8,128)S(1)}, f32[31,256]{1,0:T(8,128)}, u32[]{:S(2)}) copy-start(f32[31,256]{1,0:T(8,128)} %refs_8_.1) | copy-start | bytes 95236
  79.8 23.9 %copy-start.39 = (bf16[256,256]{1,0:T(8,128)(2,1)}, bf16[256,256]{1,0:T(8,128)(2,1)S(1)}, u32[]{:S(2)}) copy-start(bf16[256,256]{1,0:T(8,128)(2,1)S(1)} %get-tuple-element.208.refs_5_) | copy-start | bytes 393220
  79.8 7.5 %collective-permute-start.18 = (bf16[256,512]{1,0:T(8,128)(2,1)S(1)}, bf16[256,512]{1,0:T(8,128)(2,1)S(1)}, u32[]{:S(2)}, u32[]{:S(2)}) collective-permute-start(bf16[256,512]{1,0:T(8,128)(2,1)S(1)} %get-tuple-element.137.refs_1_), channel_id=1, source_target_pairs={{0,1},{1,0},{2,3},{3,2},{4,5},{5,4},{6,7},{7,6},{8,9},{9,8},{10,11... | collective-permute-start | bytes 786440 | tf_op jit(solution)/shard_map/ppermute | solution.py:151
  91.4 1.2 collective-permute-start.19
  92.5 3.6 %collective-permute-start.20 = (f32[2,256]{1,0:T(2,128)S(1)}, f32[2,256]{1,0:T(2,128)S(1)}, u32[]{:S(2)}, u32[]{:S(2)}) collective-permute-start(f32[2,256]{1,0:T(2,128)S(1)} %add.58), channel_id=1, source_target_pairs={{0,4},{2,6},{4,0},{6,2},{8,12},{10,14},{12,8},{14,10},{16,20},{18,... | collective-permute-start | bytes 6152 | tf_op jit(solution)/shard_map/ppermute | solution.py:171
  96.1 5.4 %collective-permute-start.23 = (f32[2,256]{1,0:T(2,128)S(1)}, f32[2,256]{1,0:T(2,128)S(1)}, u32[]{:S(2)}, u32[]{:S(2)}) collective-permute-start(f32[2,256]{1,0:T(2,128)S(1)} %add.59), channel_id=1, source_target_pairs={{0,24},{2,26},{4,28},{6,30},{8,16},{10,18},{12,20},{14,22},{16,8},... | collective-permute-start | bytes 6152 | tf_op jit(solution)/shard_map/ppermute | solution.py:171
  98.6 4.5 %collective-permute-start.22 = (f32[2,256]{1,0:T(2,128)S(1)}, f32[2,256]{1,0:T(2,128)S(1)}, u32[]{:S(2)}, u32[]{:S(2)}) collective-permute-start(f32[2,256]{1,0:T(2,128)S(1)} %add.59), channel_id=1, source_target_pairs={{0,16},{2,18},{4,20},{6,22},{8,24},{10,26},{12,28},{14,30},{16,0},... | collective-permute-start | bytes 6152 | tf_op jit(solution)/shard_map/ppermute | solution.py:171
  99.0 4.1 %collective-permute-start.21 = (f32[2,256]{1,0:T(2,128)S(1)}, f32[2,256]{1,0:T(2,128)S(1)}, u32[]{:S(2)}, u32[]{:S(2)}) collective-permute-start(f32[2,256]{1,0:T(2,128)S(1)} %add.59), channel_id=1, source_target_pairs={{0,8},{2,10},{4,12},{6,14},{8,0},{10,2},{12,4},{14,6},{16,24},{18,... | collective-permute-start | bytes 6152 | tf_op jit(solution)/shard_map/ppermute | solution.py:171
  104.3 6.4 %collective-permute-start.24 = (bf16[256,512]{1,0:T(8,128)(2,1)S(1)}, bf16[256,512]{1,0:T(8,128)(2,1)S(1)}, u32[]{:S(2)}, u32[]{:S(2)}) collective-permute-start(bf16[256,512]{1,0:T(8,128)(2,1)S(1)} %get-tuple-element.141.refs_1_), channel_id=1, source_target_pairs={{0,1},{1,0},{2,3},{3,2},{4,5},{5,4},{6,7},{7,6},{8,9},{9,8},{10,11... | collective-permute-start | bytes 786440 | tf_op jit(solution)/shard_map/ppermute | solution.py:151
  118.3 6.4 %collective-permute-start.25 = (bf16[256,512]{1,0:T(8,128)(2,1)S(1)}, bf16[256,512]{1,0:T(8,128)(2,1)S(1)}, u32[]{:S(2)}, u32[]{:S(2)}) collective-permute-start(bf16[256,512]{1,0:T(8,128)(2,1)S(1)} %get-tuple-element.145.refs_1_), channel_id=1, source_target_pairs={{0,1},{1,0},{2,3},{3,2},{4,5},{5,4},{6,7},{7,6},{8,9},{9,8},{10,11... | collective-permute-start | bytes 786440 | tf_op jit(solution)/shard_map/ppermute | solution.py:151
  131.1 6.6 %collective-permute-start.27 = (bf16[256,512]{1,0:T(8,128)(2,1)}, bf16[256,512]{1,0:T(8,128)(2,1)S(1)}, u32[]{:S(2)}, u32[]{:S(2)}) collective-permute-start(bf16[256,512]{1,0:T(8,128)(2,1)} %copy-done.26), channel_id=1, source_target_pairs={{0,1},{1,0},{2,3},{3,2},{4,5},{5,4},{6,7},{7,6},{8,9},{9,8},{10,11... | collective-permute-start | bytes 786440 | tf_op jit(solution)/shard_map/ppermute | solution.py:151
  141.8 1.2 collective-permute-start.28
  143.0 3.6 %collective-permute-start.29 = (f32[2,256]{1,0:T(2,128)S(1)}, f32[2,256]{1,0:T(2,128)S(1)}, u32[]{:S(2)}, u32[]{:S(2)}) collective-permute-start(f32[2,256]{1,0:T(2,128)S(1)} %add.63), channel_id=1, source_target_pairs={{0,4},{2,6},{4,0},{6,2},{8,12},{10,14},{12,8},{14,10},{16,20},{18,... | collective-permute-start | bytes 6152 | tf_op jit(solution)/shard_map/ppermute | solution.py:171
  146.6 5.4 %collective-permute-start.32 = (f32[2,256]{1,0:T(2,128)S(1)}, f32[2,256]{1,0:T(2,128)S(1)}, u32[]{:S(2)}, u32[]{:S(2)}) collective-permute-start(f32[2,256]{1,0:T(2,128)S(1)} %add.64), channel_id=1, source_target_pairs={{0,24},{2,26},{4,28},{6,30},{8,16},{10,18},{12,20},{14,22},{16,8},... | collective-permute-start | bytes 6152 | tf_op jit(solution)/shard_map/ppermute | solution.py:171
  149.0 4.5 %collective-permute-start.31 = (f32[2,256]{1,0:T(2,128)S(1)}, f32[2,256]{1,0:T(2,128)S(1)}, u32[]{:S(2)}, u32[]{:S(2)}) collective-permute-start(f32[2,256]{1,0:T(2,128)S(1)} %add.64), channel_id=1, source_target_pairs={{0,16},{2,18},{4,20},{6,22},{8,24},{10,26},{12,28},{14,30},{16,0},... | collective-permute-start | bytes 6152 | tf_op jit(solution)/shard_map/ppermute | solution.py:171
  149.0 4.5 %collective-permute-start.30 = (f32[2,256]{1,0:T(2,128)S(1)}, f32[2,256]{1,0:T(2,128)S(1)}, u32[]{:S(2)}, u32[]{:S(2)}) collective-permute-start(f32[2,256]{1,0:T(2,128)S(1)} %add.64), channel_id=1, source_target_pairs={{0,8},{2,10},{4,12},{6,14},{8,0},{10,2},{12,4},{14,6},{16,24},{18,... | collective-permute-start | bytes 6152 | tf_op jit(solution)/shard_map/ppermute | solution.py:171
  155.8 6.4 %collective-permute-start.33 = (bf16[256,512]{1,0:T(8,128)(2,1)S(1)}, bf16[256,512]{1,0:T(8,128)(2,1)S(1)}, u32[]{:S(2)}, u32[]{:S(2)}) collective-permute-start(bf16[256,512]{1,0:T(8,128)(2,1)S(1)} %get-tuple-element.162.refs_1_), channel_id=1, source_target_pairs={{0,1},{1,0},{2,3},{3,2},{4,5},{5,4},{6,7},{7,6},{8,9},{9,8},{10,11... | collective-permute-start | bytes 786440 | tf_op jit(solution)/shard_map/ppermute | solution.py:151
  166.5 6.4 %collective-permute-start.34 = (bf16[256,512]{1,0:T(8,128)(2,1)S(1)}, bf16[256,512]{1,0:T(8,128)(2,1)S(1)}, u32[]{:S(2)}, u32[]{:S(2)}) collective-permute-start(bf16[256,512]{1,0:T(8,128)(2,1)S(1)} %get-tuple-element.167.refs_1_), channel_id=1, source_target_pairs={{0,1},{1,0},{2,3},{3,2},{4,5},{5,4},{6,7},{7,6},{8,9},{9,8},{10,11... | collective-permute-start | bytes 786440 | tf_op jit(solution)/shard_map/ppermute | solution.py:151
  170.6 19.8 %collective-permute-start.50 = (bf16[1024,256]{1,0:T(8,128)(2,1)S(1)}, bf16[1024,256]{1,0:T(8,128)(2,1)S(1)}, u32[]{:S(2)}, u32[]{:S(2)}) collective-permute-start(bf16[1024,256]{1,0:T(8,128)(2,1)S(1)} %get-tuple-element.215), channel_id=1, source_target_pairs={{0,2},{2,0},{4,6},{6,4},{8,10},{10,8},{12,14},{14,12},{16,18},{18,... | collective-permute-start | bytes 1572872 | tf_op jit(solution)/shard_map/ppermute | solution.py:171
  170.7 20.7 %collective-permute-start.51 = (bf16[1024,256]{1,0:T(8,128)(2,1)S(1)}, bf16[1024,256]{1,0:T(8,128)(2,1)S(1)}, u32[]{:S(2)}, u32[]{:S(2)}) collective-permute-start(bf16[1024,256]{1,0:T(8,128)(2,1)S(1)} %get-tuple-element.216), channel_id=1, source_target_pairs={{0,2},{2,0},{4,6},{6,4},{8,10},{10,8},{12,14},{14,12},{16,18},{18,... | collective-permute-start | bytes 1572872 | tf_op jit(solution)/shard_map/ppermute | solution.py:171
  176.0 17.5 %collective-permute-start.42 = (bf16[256,1024]{1,0:T(8,128)(2,1)S(1)}, bf16[256,1024]{1,0:T(8,128)(2,1)S(1)}, u32[]{:S(2)}, u32[]{:S(2)}) collective-permute-start(bf16[256,1024]{1,0:T(8,128)(2,1)S(1)} %get-tuple-element.188), channel_id=1, source_target_pairs={{0,2},{2,0},{4,6},{6,4},{8,10},{10,8},{12,14},{14,12},{16,18},{18,... | collective-permute-start | bytes 1572872 | tf_op jit(solution)/shard_map/ppermute | solution.py:171
  176.1 17.8 %collective-permute-start.43 = (bf16[256,1024]{1,0:T(8,128)(2,1)S(1)}, bf16[256,1024]{1,0:T(8,128)(2,1)S(1)}, u32[]{:S(2)}, u32[]{:S(2)}) collective-permute-start(bf16[256,1024]{1,0:T(8,128)(2,1)S(1)} %get-tuple-element.189), channel_id=1, source_target_pairs={{0,2},{2,0},{4,6},{6,4},{8,10},{10,8},{12,14},{14,12},{16,18},{18,... | collective-permute-start | bytes 1572872 | tf_op jit(solution)/shard_map/ppermute | solution.py:171
  176.6 5.5 %collective-permute-start.35 = (bf16[128,512]{1,0:T(8,128)(2,1)S(1)}, bf16[128,512]{1,0:T(8,128)(2,1)S(1)}, u32[]{:S(2)}, u32[]{:S(2)}) collective-permute-start(bf16[128,512]{1,0:T(8,128)(2,1)S(1)} %get-tuple-element.173), channel_id=1, source_target_pairs={{0,1},{1,0},{2,3},{3,2},{4,5},{5,4},{6,7},{7,6},{8,9},{9,8},{10,11... | collective-permute-start | bytes 393224 | tf_op jit(solution)/shard_map/ppermute | solution.py:151
  183.2 1.3 collective-permute-start.36
  184.5 4.2 %collective-permute-start.37 = (f32[24,512]{1,0:T(8,128)S(1)}, f32[24,512]{1,0:T(8,128)S(1)}, u32[]{:S(2)}, u32[]{:S(2)}) collective-permute-start(f32[24,512]{1,0:T(8,128)S(1)} %add.68), channel_id=1, source_target_pairs={{0,4},{2,6},{4,0},{6,2},{8,12},{10,14},{12,8},{14,10},{16,20},{18,... | collective-permute-start | bytes 147464 | tf_op jit(solution)/shard_map/ppermute | solution.py:171
  188.7 6.6 %collective-permute-start.40 = (f32[24,512]{1,0:T(8,128)S(1)}, f32[24,512]{1,0:T(8,128)S(1)}, u32[]{:S(2)}, u32[]{:S(2)}) collective-permute-start(f32[24,512]{1,0:T(8,128)S(1)} %add.69), channel_id=1, source_target_pairs={{0,24},{2,26},{4,28},{6,30},{8,16},{10,18},{12,20},{14,22},{16,8},... | collective-permute-start | bytes 147464 | tf_op jit(solution)/shard_map/ppermute | solution.py:171
  190.4 6.2 %collective-permute-start.39 = (f32[24,512]{1,0:T(8,128)S(1)}, f32[24,512]{1,0:T(8,128)S(1)}, u32[]{:S(2)}, u32[]{:S(2)}) collective-permute-start(f32[24,512]{1,0:T(8,128)S(1)} %add.69), channel_id=1, source_target_pairs={{0,16},{2,18},{4,20},{6,22},{8,24},{10,26},{12,28},{14,30},{16,0},... | collective-permute-start | bytes 147464 | tf_op jit(solution)/shard_map/ppermute | solution.py:171
  191.3 7.1 %collective-permute-start.38 = (f32[24,512]{1,0:T(8,128)S(1)}, f32[24,512]{1,0:T(8,128)S(1)}, u32[]{:S(2)}, u32[]{:S(2)}) collective-permute-start(f32[24,512]{1,0:T(8,128)S(1)} %add.69), channel_id=1, source_target_pairs={{0,8},{2,10},{4,12},{6,14},{8,0},{10,2},{12,4},{14,6},{16,24},{18,... | collective-permute-start | bytes 147464 | tf_op jit(solution)/shard_map/ppermute | solution.py:171
  193.5 9.3 %collective-permute-start.52 = (bf16[512,256]{1,0:T(8,128)(2,1)S(1)}, bf16[512,256]{1,0:T(8,128)(2,1)S(1)}, u32[]{:S(2)}, u32[]{:S(2)}) collective-permute-start(bf16[512,256]{1,0:T(8,128)(2,1)S(1)} %get-tuple-element.219), channel_id=1, source_target_pairs={{0,4},{2,6},{4,0},{6,2},{8,12},{10,14},{12,8},{14,10},{16,20},{18,... | collective-permute-start | bytes 786440 | tf_op jit(solution)/shard_map/ppermute | solution.py:171
  193.9 9.2 %collective-permute-start.53 = (bf16[512,256]{1,0:T(8,128)(2,1)S(1)}, bf16[512,256]{1,0:T(8,128)(2,1)S(1)}, u32[]{:S(2)}, u32[]{:S(2)}) collective-permute-start(bf16[512,256]{1,0:T(8,128)(2,1)S(1)} %get-tuple-element.220), channel_id=1, source_target_pairs={{0,8},{2,10},{4,12},{6,14},{8,0},{10,2},{12,4},{14,6},{16,24},{18,... | collective-permute-start | bytes 786440 | tf_op jit(solution)/shard_map/ppermute | solution.py:171
  195.3 17.8 %collective-permute-start.44 = (bf16[128,1024]{1,0:T(8,128)(2,1)S(1)}, bf16[128,1024]{1,0:T(8,128)(2,1)S(1)}, u32[]{:S(2)}, u32[]{:S(2)}) collective-permute-start(bf16[128,1024]{1,0:T(8,128)(2,1)S(1)} %get-tuple-element.192), channel_id=1, source_target_pairs={{0,4},{2,6},{4,0},{6,2},{8,12},{10,14},{12,8},{14,10},{16,20},{18,... | collective-permute-start | bytes 786440 | tf_op jit(solution)/shard_map/ppermute | solution.py:171
  196.6 16.5 %collective-permute-start.45 = (bf16[128,1024]{1,0:T(8,128)(2,1)S(1)}, bf16[128,1024]{1,0:T(8,128)(2,1)S(1)}, u32[]{:S(2)}, u32[]{:S(2)}) collective-permute-start(bf16[128,1024]{1,0:T(8,128)(2,1)S(1)} %get-tuple-element.193), channel_id=1, source_target_pairs={{0,8},{2,10},{4,12},{6,14},{8,0},{10,2},{12,4},{14,6},{16,24},{18,... | collective-permute-start | bytes 786440 | tf_op jit(solution)/shard_map/ppermute | solution.py:171
  203.2 6.9 %collective-permute-start.54 = (bf16[256,256]{1,0:T(8,128)(2,1)S(1)}, bf16[256,256]{1,0:T(8,128)(2,1)S(1)}, u32[]{:S(2)}, u32[]{:S(2)}) collective-permute-start(bf16[256,256]{1,0:T(8,128)(2,1)S(1)} %get-tuple-element.223), channel_id=1, source_target_pairs={{0,8},{2,10},{4,12},{6,14},{8,0},{10,2},{12,4},{14,6},{16,24},{18,... | collective-permute-start | bytes 393224 | tf_op jit(solution)/shard_map/ppermute | solution.py:171
  203.9 6.2 %collective-permute-start.55 = (bf16[256,256]{1,0:T(8,128)(2,1)S(1)}, bf16[256,256]{1,0:T(8,128)(2,1)S(1)}, u32[]{:S(2)}, u32[]{:S(2)}) collective-permute-start(bf16[256,256]{1,0:T(8,128)(2,1)S(1)} %get-tuple-element.224), channel_id=1, source_target_pairs={{0,4},{2,6},{4,0},{6,2},{8,12},{10,14},{12,8},{14,10},{16,20},{18,... | collective-permute-start | bytes 393224 | tf_op jit(solution)/shard_map/ppermute | solution.py:171
  205.3 9.9 %collective-permute-start.41 = (f32[5,512]{1,0:T(8,128)S(1)}, f32[5,512]{1,0:T(8,128)S(1)}, u32[]{:S(2)}, u32[]{:S(2)}) collective-permute-start(f32[5,512]{1,0:T(8,128)S(1)} %slice.44), channel_id=1, source_target_pairs={{0,1},{1,0},{2,3},{3,2},{4,5},{5,4},{6,7},{7,6},{8,9},{9,8},{10,11... | collective-permute-start | bytes 30728 | tf_op jit(solution)/shard_map/ppermute | solution.py:171
  210.1 5.9 %collective-permute-start.56 = (bf16[128,256]{1,0:T(8,128)(2,1)S(1)}, bf16[128,256]{1,0:T(8,128)(2,1)S(1)}, u32[]{:S(2)}, u32[]{:S(2)}) collective-permute-start(bf16[128,256]{1,0:T(8,128)(2,1)S(1)} %get-tuple-element.227), channel_id=1, source_target_pairs={{0,16},{2,18},{4,20},{6,22},{8,24},{10,26},{12,28},{14,30},{16,0},... | collective-permute-start | bytes 196616 | tf_op jit(solution)/shard_map/ppermute | solution.py:171
  211.0 5.8 %collective-permute-start.57 = (bf16[128,256]{1,0:T(8,128)(2,1)S(1)}, bf16[128,256]{1,0:T(8,128)(2,1)S(1)}, u32[]{:S(2)}, u32[]{:S(2)}) collective-permute-start(bf16[128,256]{1,0:T(8,128)(2,1)S(1)} %get-tuple-element.228), channel_id=1, source_target_pairs={{0,16},{2,18},{4,20},{6,22},{8,24},{10,26},{12,28},{14,30},{16,0},... | collective-permute-start | bytes 196616 | tf_op jit(solution)/shard_map/ppermute | solution.py:171
  213.2 5.0 %collective-permute-start.46 = (bf16[64,1024]{1,0:T(8,128)(2,1)S(1)}, bf16[64,1024]{1,0:T(8,128)(2,1)S(1)}, u32[]{:S(2)}, u32[]{:S(2)}) collective-permute-start(bf16[64,1024]{1,0:T(8,128)(2,1)S(1)} %get-tuple-element.196), channel_id=1, source_target_pairs={{0,8},{2,10},{4,12},{6,14},{8,0},{10,2},{12,4},{14,6},{16,24},{18,... | collective-permute-start | bytes 393224 | tf_op jit(solution)/shard_map/ppermute | solution.py:171
  213.5 5.0 %collective-permute-start.47 = (bf16[64,1024]{1,0:T(8,128)(2,1)S(1)}, bf16[64,1024]{1,0:T(8,128)(2,1)S(1)}, u32[]{:S(2)}, u32[]{:S(2)}) collective-permute-start(bf16[64,1024]{1,0:T(8,128)(2,1)S(1)} %get-tuple-element.197), channel_id=1, source_target_pairs={{0,4},{2,6},{4,0},{6,2},{8,12},{10,14},{12,8},{14,10},{16,20},{18,... | collective-permute-start | bytes 393224 | tf_op jit(solution)/shard_map/ppermute | solution.py:171
  218.5 5.2 %collective-permute-start.48 = (bf16[32,1024]{1,0:T(8,128)(2,1)S(1)}, bf16[32,1024]{1,0:T(8,128)(2,1)S(1)}, u32[]{:S(2)}, u32[]{:S(2)}) collective-permute-start(bf16[32,1024]{1,0:T(8,128)(2,1)S(1)} %get-tuple-element.200), channel_id=1, source_target_pairs={{0,16},{2,18},{4,20},{6,22},{8,24},{10,26},{12,28},{14,30},{16,0},... | collective-permute-start | bytes 196616 | tf_op jit(solution)/shard_map/ppermute | solution.py:171
  220.8 5.7 %collective-permute-start.49 = (bf16[32,1024]{1,0:T(8,128)(2,1)S(1)}, bf16[32,1024]{1,0:T(8,128)(2,1)S(1)}, u32[]{:S(2)}, u32[]{:S(2)}) collective-permute-start(bf16[32,1024]{1,0:T(8,128)(2,1)S(1)} %get-tuple-element.201), channel_id=1, source_target_pairs={{0,16},{2,18},{4,20},{6,22},{8,24},{10,26},{12,28},{14,30},{16,0},... | collective-permute-start | bytes 196616 | tf_op jit(solution)/shard_map/ppermute | solution.py:171
  (50 other events, 346.1 us)
Sparse Core Ops, SparseCore 0:
  36.0 43.6 all-gather.1
  131.2 60.6 reduce-scatter.1

commit v4 on v2

v4 whole, which is shorter than its diff:
```python
import math

import jax
import jax.numpy as jnp
from jax import lax
from jax.experimental import pallas as pl
from jax.experimental.pallas import tpu as pltpu
from jax.sharding import PartitionSpec as P

HEAD_TOTAL = 8
EPSILON = 1e-05
BF16 = jnp.bfloat16
F32 = jnp.float32


def matmul(left_side, right_side):
    return jnp.dot(left_side, right_side, preferred_element_type=F32)


def right_transposed(left_side, right_side):
    return lax.dot_general(
        left_side, right_side, (((1,), (1,)), ((), ())), preferred_element_type=F32
    )


def left_transposed(left_side, right_side):
    return lax.dot_general(
        left_side, right_side, (((0,), (0,)), ((), ())), preferred_element_type=F32
    )


def swish_slope(pre_value, gate_sigma):
    return gate_sigma * (1.0 + pre_value * (1.0 - gate_sigma))


def norm_parts(residual):
    centred = residual - jnp.mean(residual, -1, keepdims=True)
    factor = lax.rsqrt(jnp.mean(centred * centred, -1, keepdims=True) + EPSILON)
    return centred * factor, factor


def norm_back(gradient, normed, factor, norm_gain):
    scaled = gradient * norm_gain
    inner_sum = (
        scaled
        - jnp.mean(scaled, -1, keepdims=True)
        - normed * jnp.mean(scaled * normed, -1, keepdims=True)
    )
    return factor * inner_sum, jnp.sum(gradient * normed, 0, keepdims=True)


def sinusoid(length, features):
    offsets = jnp.arange(2 * length, dtype=F32) - (length - 1)
    half_width = features // 2
    frequency = jnp.exp(jnp.arange(half_width, dtype=F32) * (-math.log(10000.0) / half_width))
    angles = offsets[:, None] * frequency[None, :]
    table = jnp.concatenate([jnp.sin(angles), jnp.cos(angles)], 1)
    return jnp.where(offsets[:, None] < length, table, 0.0)


def on_chip(function, name, operands, results, scratch=(), flops=300_000_000):
    count = len(operands)
    total = count + len(results)

    def kernel(*refs):
        function(refs[:count], refs[count:total], refs[total:])

    moved = sum(value.size * value.dtype.itemsize for value in operands)
    moved += sum(math.prod(shape) * jnp.dtype(kind).itemsize for shape, kind in results)
    return pl.pallas_call(
        kernel,
        out_shape=[jax.ShapeDtypeStruct(shape, kind) for shape, kind in results],
        in_specs=[pl.BlockSpec(memory_space=pltpu.VMEM)] * count,
        out_specs=[pl.BlockSpec(memory_space=pltpu.VMEM)] * len(results),
        scratch_shapes=list(scratch),
        compiler_params=pltpu.CompilerParams(vmem_limit_bytes=24 * 1024 * 1024),
        cost_estimate=pl.CostEstimate(flops=flops, bytes_accessed=moved, transcendentals=0),
        name=name,
    )(*operands)


def swap(value):
    return lax.ppermute(value, "tensor", [(0, 1), (1, 0)])


def both_halves(own):
    other = swap(own)
    first = lax.axis_index("tensor") == 0
    return jnp.concatenate([jnp.where(first, own, other), jnp.where(first, other, own)], 0)


def own_half(value):
    half = value.shape[0] // 2
    return jnp.where(lax.axis_index("tensor") == 0, value[:half], value[half:])


def other_half(value):
    half = value.shape[0] // 2
    return jnp.where(lax.axis_index("tensor") == 0, value[half:], value[:half])


def shift(value, axis, mask):
    return lax.ppermute(value, axis, [(k, k ^ mask) for k in range(lax.axis_size(axis))])


def sum_over(value, axis):
    size = lax.axis_size(axis)
    if size & (size - 1):
        return lax.psum(value, axis)
    step = 1
    while step < size:
        if step >= 4 and step * 4 <= size:
            near, far, both = (shift(value, axis, step * times) for times in (1, 2, 3))
            value = (value + near) + (far + both)
            step *= 4
        else:
            value = value + shift(value, axis, step)
            step *= 2
    return value


GATHER_ORDERS = ((8, 4, 2, 1), (8, 2, 4, 1))
SCATTER_ORDERS = ((1, 2, 4, 8), (1, 4, 2, 8))


def doubling():
    return lax.axis_size("dp") == 16


def distances(order):
    blocks = [0]
    for mask in order:
        blocks = blocks + [block ^ mask for block in blocks]
    return blocks


def halving(order):
    return distances(order[::-1])


def gather_send(pair, stage):
    return tuple(shift(value, "dp", order[stage]) for value, order in zip(pair, GATHER_ORDERS))


def gather_join(pair, arrived):
    def body(ins, outs, _):
        for group in range(2):
            rows = ins[group].shape[0]
            outs[group][:rows, :] = ins[group][...]
            outs[group][rows:, :] = ins[2 + group][...]

    results = tuple(((2 * value.shape[0], value.shape[1]), value.dtype) for value in pair)
    return tuple(on_chip(body, "gather_join", tuple(pair) + arrived, results, flops=1_000))


def gather_last(pair):
    return tuple((value, shift(value, "dp", 1)) for value in pair)


def tie(values, *others):
    return lax.optimization_barrier((values, others))[0]


def assemble(ref, target_ref, order, half, matrices, first_column):
    device = lax.axis_index("dp")
    blocks = distances(order)
    count = len(blocks) // 2
    rows = target_ref.shape[0] // len(blocks)
    columns = ref.shape[1]
    for place in range(count):
        owner = device ^ blocks[half * count + place]
        target = pl.ds(pl.multiple_of(owner * rows, rows), rows)
        for matrix in range(matrices):
            start = (place * matrices + matrix) * rows
            left = first_column + matrix * columns
            target_ref[target, left : left + columns] = ref[start : start + rows, :]


def scatter_split(total_ref, keep_ref, send_ref, order, matrices):
    device = lax.axis_index("dp")
    blocks = halving(order)
    count = len(blocks) // 2
    rows = total_ref.shape[0] // len(blocks)
    columns = keep_ref.shape[1]
    for place, block in enumerate(blocks):
        source = pl.ds(pl.multiple_of((device ^ block) * rows, rows), rows)
        for matrix in range(matrices):
            piece = total_ref[source, matrix * columns : (matrix + 1) * columns]
            start = ((place % count) * matrices + matrix) * rows
            if place < count:
                keep_ref[start : start + rows, :] = piece
            else:
                send_ref[start : start + rows, :] = piece.astype(BF16)


def scatter_send(sends, stage):
    return tuple(shift(send, "dp", order[stage]) for send, order in zip(sends, SCATTER_ORDERS))


def scatter_add(keeps, arrived, stage, name):
    groups = len(keeps)
    last = stage == len(SCATTER_ORDERS[0]) - 1
    results = []
    for keep in keeps:
        rows, columns = keep.shape
        if last:
            results.append(((rows, columns), F32))
        else:
            results.append(((rows // 2, columns), F32))
            results.append(((rows // 2, columns), BF16))

    def body(ins, outs, _):
        for group in range(groups):
            total = ins[group][...] + ins[groups + group][...].astype(F32)
            if last:
                outs[group][...] = total
            else:
                half = total.shape[0] // 2
                outs[2 * group][...] = total[:half]
                outs[2 * group + 1][...] = total[half:].astype(BF16)

    values = on_chip(body, name, tuple(keeps) + tuple(arrived), tuple(results), flops=1_000)
    if last:
        return values, ()
    return values[0::2], values[1::2]


def entries_of(residual, gain):
    return (norm_parts(residual)[0] * gain).astype(BF16)


def ff_forward_body(entries, weight_ref, part_ref):
    half = weight_ref.shape[1] // 2
    pre = matmul(entries, weight_ref[:, :half])
    hidden = (pre * jax.nn.sigmoid(pre)).astype(BF16)
    part_ref[...] = right_transposed(hidden, weight_ref[:, half:]).astype(BF16)
    return pre


def both_parts(own_ref, other_ref):
    return own_ref[...].astype(F32) + other_ref[...].astype(F32)


def first_forward(tokens, gains, weights):
    rows, width = tokens.shape
    split = isinstance(weights, tuple)
    pieces = weights[0] + weights[1] if split else (weights,)
    hidden = pieces[0].shape[1] if split else weights.shape[1] // 2

    def body(ins, outs, _):
        weight_ref = ins[2]
        if split:
            weight_ref = outs[2]
            for group in range(2):
                for half in range(2):
                    piece = ins[2 + 2 * group + half]
                    assemble(piece, weight_ref, GATHER_ORDERS[group], half, 1, group * hidden)
        entries = entries_of(ins[0][...].astype(F32), ins[1][0:1, :])
        outs[0][...] = ff_forward_body(entries, weight_ref, outs[1])

    results = (((rows, hidden), F32), ((rows, width), BF16))
    if split:
        results += (((width, 2 * hidden), BF16),)
    values = on_chip(body, "first_forward", (tokens, gains) + pieces, results)
    return values if split else tuple(values) + (weights,)


def ff_back_body(gradient, pre, weight_ref, grads_ref):
    width = gradient.shape[1]
    half = weight_ref.shape[1] // 2
    branch = (0.5 * gradient).astype(BF16)
    grads_ref[:, :width] = branch
    grad_hidden = matmul(branch, weight_ref[:, half:])
    sigma = jax.nn.sigmoid(pre)
    grad_pre = (grad_hidden * swish_slope(pre, sigma)).astype(BF16)
    grads_ref[:, width : width + half] = grad_pre
    grads_ref[:, width + half : width + 2 * half] = (pre * sigma).astype(BF16)
    return right_transposed(grad_pre, weight_ref[:, :half])


def second_weight_grads(rows_kept, width):
    half = (rows_kept.shape[1] - 2 * width) // 2

    def body(ins, outs, _):
        rows_ref = ins[0]
        outs[0][:, :half] = left_transposed(
            rows_ref[:, width : 2 * width], rows_ref[:, 2 * width : 2 * width + half]
        ).astype(BF16)
        outs[0][:, half:] = left_transposed(
            rows_ref[:, :width], rows_ref[:, 2 * width + half :]
        ).astype(BF16)

    return on_chip(body, "second_weight_grads", (rows_kept,), (((width, 2 * half), BF16),))[0]


def ff_weight_grads(grads, residual, gains, row, name):
    width = gains.shape[1]
    half = (grads.shape[1] - width) // 2

    def body(ins, outs, _):
        grads_ref, x_ref, gain_ref = ins
        entries = entries_of(x_ref[:, :width].astype(F32), gain_ref[row : row + 1, :])
        outs[0][:, :half] = left_transposed(entries, grads_ref[:, width : width + half]).astype(
            BF16
        )
        outs[0][:, half:] = left_transposed(
            grads_ref[:, :width], grads_ref[:, width + half :]
        ).astype(BF16)

    return on_chip(body, name, (grads, residual, gains), (((width, 2 * half), BF16),))[0]


def ff_weight_split(grads, residual, gains, row, name):
    width = gains.shape[1]
    half = (grads.shape[1] - width) // 2

    def body(ins, outs, scratch):
        grads_ref, x_ref, gain_ref = ins
        entries = entries_of(x_ref[:, :width].astype(F32), gain_ref[row : row + 1, :])
        scratch[0][...] = left_transposed(entries, grads_ref[:, width : width + half])
        scatter_split(scratch[0], outs[0], outs[1], SCATTER_ORDERS[0], 1)
        scratch[0][...] = left_transposed(grads_ref[:, :width], grads_ref[:, width + half :])
        scatter_split(scratch[0], outs[2], outs[3], SCATTER_ORDERS[1], 1)

    halves = (((width // 2, half), F32), ((width // 2, half), BF16))
    values = on_chip(
        body,
        name,
        (grads, residual, gains),
        halves + halves,
        scratch=(pltpu.VMEM((width, half), F32),),
    )
    return values[0::2], values[1::2]


def kept_residual(kept_ref, width):
    return kept_ref[:, :width].astype(F32) + kept_ref[:, width : 2 * width].astype(F32)


def position_forward(table, weights, columns):
    def body(ins, outs, _):
        outs[0][...] = matmul(ins[0][...], ins[1][:, 3 * columns : 4 * columns]).astype(BF16)

    return on_chip(
        body, "position_forward", (table, weights), (((table.shape[0], columns), BF16),)
    )[0]


def attention_forward(tokens, own, other, gains, weights, positions, biases, heads):
    rows, width = tokens.shape
    columns = biases.shape[1]
    features = columns // heads
    scale = features ** (-0.5)
    start = 2 * width

    def body(ins, outs, _):
        x_ref, own_ref, other_ref, gain_ref, weight_ref, table_ref, bias_ref = ins
        kept_ref, part_ref = outs
        after = x_ref[...].astype(F32) + 0.5 * both_parts(own_ref, other_ref)
        high = after.astype(BF16)
        kept_ref[:, :width] = high
        kept_ref[:, width : 2 * width] = (after - high.astype(F32)).astype(BF16)
        entries = entries_of(after, gain_ref[1:2, :])
        joined = matmul(entries, weight_ref[:, : 3 * columns])
        queries = joined[:, :columns]
        content_q = (queries + bias_ref[0:1, :]).astype(BF16)
        position_q = (queries + bias_ref[1:2, :]).astype(BF16)
        keys = joined[:, columns : 2 * columns].astype(BF16)
        values = joined[:, 2 * columns :].astype(BF16)
        kept_ref[:, start : start + columns] = content_q
        kept_ref[:, start + columns : start + 2 * columns] = position_q
        kept_ref[:, start + 2 * columns : start + 3 * columns] = keys
        kept_ref[:, start + 3 * columns : start + 4 * columns] = values
        mixed = []
        for head in range(heads):
            part = slice(head * features, (head + 1) * features)
            content = right_transposed(content_q[:, part], keys[:, part])
            raw = right_transposed(position_q[:, part], table_ref[:, part])
            shifted = pltpu.roll(raw, rows + 1, 1, stride=1, stride_axis=0)[:, :rows]
            scores = (content + shifted) * scale
            lifted = jnp.exp(scores - jnp.max(scores, -1, keepdims=True))
            probability = (lifted / jnp.sum(lifted, -1, keepdims=True)).astype(BF16)
            place = start + 5 * columns + head * rows
            kept_ref[:, place : place + rows] = probability
            mixed.append(matmul(probability, values[:, part]))
        attended = jnp.concatenate(mixed, 1).astype(BF16)
        kept_ref[:, start + 4 * columns : start + 5 * columns] = attended
        part_ref[...] = right_transposed(
            attended, weight_ref[:, 4 * columns : 5 * columns]
        ).astype(BF16)

    return on_chip(
        body,
        "attention_forward",
        (tokens, own, other, gains, weights, positions, biases),
        (((rows, start + 5 * columns + heads * rows), BF16), ((rows, width), BF16)),
    )


def attention_back(norm_grads, own, other, conv_kept, gains, weights, positions, kept, heads):
    rows, width = own.shape
    columns = positions.shape[1]
    features = columns // heads
    scale = features ** (-0.5)
    start = 2 * width

    def body(ins, outs, _):
        grad_ref, own_ref, other_ref, x_ref, gain_ref, weight_ref, table_ref, kept_ref = ins
        total_ref, joined_ref, table_grad_ref, part_ref, gain_grad_ref, bias_ref = outs
        normed, factor = norm_parts(x_ref[:, :width])
        passed, gain_grad = norm_back(
            both_parts(own_ref, other_ref), normed, factor, gain_ref[2:3, :]
        )
        gain_grad_ref[...] = 0.5 * gain_grad
        total = grad_ref[:, :width] + passed
        total_ref[...] = total
        grad_mixed = matmul(
            total.astype(BF16), weight_ref[:, 4 * columns : 5 * columns]
        ).astype(BF16)
        line = lax.broadcasted_iota(jnp.int32, (rows, rows), 0)
        place = lax.broadcasted_iota(jnp.int32, (rows, rows), 1)
        flip = (line + place == rows - 1).astype(F32).astype(BF16)
        content_q = kept_ref[:, start : start + columns]
        flipped_q = matmul(flip, kept_ref[:, start + columns : start + 2 * columns]).astype(BF16)
        keys = kept_ref[:, start + 2 * columns : start + 3 * columns]
        values = kept_ref[:, start + 3 * columns : start + 4 * columns]
        zeros = jnp.zeros((rows, rows), F32)
        from_content, from_position, to_keys, to_values, to_table = [], [], [], [], []
        for head in range(heads):
            part = slice(head * features, (head + 1) * features)
            left = start + 5 * columns + head * rows
            rounded = kept_ref[:, left : left + rows]
            probability = rounded.astype(F32)
            grad_probability = right_transposed(grad_mixed[:, part], values[:, part])
            to_values.append(left_transposed(rounded, grad_mixed[:, part]))
            inner = jnp.sum(probability * grad_probability, -1, keepdims=True)
            grad_scores = (probability * (grad_probability - inner)).astype(BF16) * scale
            grad_scores = grad_scores.astype(BF16)
            from_content.append(matmul(grad_scores, keys[:, part]))
            to_keys.append(left_transposed(grad_scores, content_q[:, part]))
            flipped = jnp.concatenate([matmul(flip, grad_scores), zeros], 1)
            spread = pltpu.roll(flipped, 0, 1, stride=1, stride_axis=0).astype(BF16)
            from_position.append(matmul(spread, table_ref[:, part]))
            to_table.append(left_transposed(spread, flipped_q[:, part]))
        grad_content = jnp.concatenate(from_content, 1)
        grad_position = jnp.concatenate(from_position, 1)
        high = grad_position.astype(BF16)
        low = (grad_position - high.astype(F32)).astype(BF16)
        grad_position = matmul(flip, high) + matmul(flip, low)
        bias_ref[0:1, :] = jnp.sum(grad_content, 0, keepdims=True)
        bias_ref[1:2, :] = jnp.sum(grad_position, 0, keepdims=True)
        joined = jnp.concatenate(
            [grad_content + grad_position] + to_keys + to_values, 1
        ).astype(BF16)
        joined_ref[...] = joined
        table_grad_ref[...] = jnp.concatenate(to_table, 1).astype(BF16)
        part_ref[...] = right_transposed(joined, weight_ref[:, : 3 * columns]).astype(BF16)

    return on_chip(
        body,
        "attention_back",
        (norm_grads, own, other, conv_kept, gains, weights, positions, kept),
        (
            ((rows, width), F32),
            ((rows, 3 * columns), BF16),
            ((2 * rows, columns), BF16),
            ((rows, width), BF16),
            ((1, width), F32),
            ((2, columns), F32),
        ),
    )


def mixed_assemble(pairs, table, width):
    columns = pairs[0][0].shape[1]

    def body(ins, outs, _):
        for group in range(2):
            for half in range(2):
                assemble(
                    ins[2 * group + half],
                    outs[0],
                    GATHER_ORDERS[group],
                    half,
                    4,
                    4 * group * columns,
                )
        outs[1][...] = matmul(ins[4][...], outs[0][:, 3 * columns : 4 * columns]).astype(BF16)

    return on_chip(
        body,
        "mixed_assemble",
        pairs[0] + pairs[1] + (table,),
        (((width, 8 * columns), BF16), ((table.shape[0], columns), BF16)),
    )


def mixed_weight_grads(joined, table, table_grad, total, kept, gains, conv_grads, split):
    width = gains.shape[1]
    columns = table_grad.shape[1]

    def whole(ins, target_ref):
        joined_ref, table_ref, table_grad_ref, total_ref, kept_ref, gain_ref, conv_ref = ins
        entries = entries_of(kept_residual(kept_ref, width), gain_ref[1:2, :])
        attended = kept_ref[:, 2 * width + 4 * columns : 2 * width + 5 * columns]
        target_ref[:, : 3 * columns] = left_transposed(entries, joined_ref[...])
        target_ref[:, 3 * columns : 4 * columns] = left_transposed(
            table_ref[...], table_grad_ref[...]
        )
        target_ref[:, 4 * columns : 5 * columns] = left_transposed(
            total_ref[...].astype(BF16), attended
        )
        target_ref[:, 5 * columns :] = conv_ref[...].astype(F32)

    def body(ins, outs, scratch):
        if not split:
            whole(ins, outs[0])
            return
        whole(ins, scratch[0])
        for group in range(2):
            part = scratch[0].at[:, 4 * group * columns : 4 * (group + 1) * columns]
            scatter_split(part, outs[2 * group], outs[2 * group + 1], SCATTER_ORDERS[group], 4)

    operands = (joined, table, table_grad, total, kept, gains, conv_grads)
    if not split:
        results = (((width, 8 * columns), F32),)
        return on_chip(body, "mixed_weight_grads", operands, results)[0]
    halves = (((2 * width, columns), F32), ((2 * width, columns), BF16))
    values = on_chip(
        body,
        "mixed_weight_grads",
        operands,
        halves + halves,
        scratch=(pltpu.VMEM((width, 8 * columns), F32),),
    )
    return values[0::2], values[1::2]


PAD = 16


def pad_rows(padded, rows, columns, value):
    padded[:PAD, :] = jnp.zeros((PAD, columns), F32)
    padded[PAD + rows :, :] = jnp.zeros((PAD, columns), F32)
    padded[PAD : PAD + rows, :] = value


def conv_forward(kept, own, other, gains, weights, depth_kernel):
    rows, width = own.shape
    taps, columns = depth_kernel.shape
    half_taps = (taps - 1) // 2

    def body(ins, outs, scratch):
        kept_ref, own_ref, other_ref, gain_ref, weight_ref, tap_ref = ins
        conv_ref, sums_ref = outs
        padded = scratch[0]
        after = kept_residual(kept_ref, width) + both_parts(own_ref, other_ref)
        conv_ref[:, :width] = after
        entries = entries_of(after, gain_ref[2:3, :])
        joined = matmul(entries, weight_ref[:, 5 * columns : 7 * columns])
        value = joined[:, :columns]
        gate = jax.nn.sigmoid(joined[:, columns:])
        conv_ref[:, width : width + columns] = value
        conv_ref[:, width + columns : width + 2 * columns] = gate
        pad_rows(padded, rows, columns, value * gate)
        total = jnp.zeros((rows, columns), F32)
        for tap in range(taps):
            start = PAD - half_taps + tap
            total = total + tap_ref[tap : tap + 1, :] * padded[start : start + rows, :]
        conv_ref[:, width + 2 * columns :] = total
        sums_ref[0:1, :] = jnp.sum(total, 0, keepdims=True)
        sums_ref[1:2, :] = jnp.sum(total * total, 0, keepdims=True)

    return on_chip(
        body,
        "conv_forward",
        (kept, own, other, gains, weights, depth_kernel),
        (((rows, width + 3 * columns), F32), ((2, columns), F32)),
        scratch=(pltpu.VMEM((rows + 2 * PAD, columns), F32),),
    )


def batch_norm(conv_ref, sums_ref, batch_ref, token_count):
    columns = sums_ref.shape[1]
    column_mean = sums_ref[0:1, :] / token_count
    inverse = lax.rsqrt(sums_ref[1:2, :] / token_count - column_mean * column_mean + EPSILON)
    standard = (conv_ref[:, conv_ref.shape[1] - columns :] - column_mean) * inverse
    return standard, inverse, standard * batch_ref[0:1, :] + batch_ref[1:2, :]


def norm_forward(conv_kept, sums, batch, weights, token_count):
    rows = conv_kept.shape[0]
    columns = sums.shape[1]
    width = weights.shape[0]

    def body(ins, outs, _):
        conv_ref, sums_ref, batch_ref, weight_ref = ins
        _, _, shifted = batch_norm(conv_ref, sums_ref, batch_ref, token_count)
        activated = (shifted * jax.nn.sigmoid(shifted)).astype(BF16)
        outs[0][...] = right_transposed(activated, weight_ref[:, 7 * columns :]).astype(BF16)

    return on_chip(
        body, "norm_forward", (conv_kept, sums, batch, weights), (((rows, width), BF16),)
    )[0]


def second_block(conv_kept, own, other, cotangent, gains, weights, mixed, sums, batch, count):
    rows, width = own.shape
    columns = sums.shape[1]
    half = weights.shape[1] // 4

    def body(ins, outs, _):
        conv_ref, own_ref, other_ref, cot_ref, gain_ref, weight_ref, mixed_ref = ins[:7]
        sums_ref, batch_ref = ins[7:]
        out_ref, grads_ref, rows_ref, grad_sums_ref, last_gain_ref, gain_grad_ref = outs
        residual = conv_ref[:, :width] + both_parts(own_ref, other_ref)
        normed, factor = norm_parts(residual)
        entries = (normed * gain_ref[3:4, :]).astype(BF16)
        rows_ref[:, width : 2 * width] = entries
        inner, branch_sum = [], 0.0
        for part in range(2):
            left = 2 * part * half
            pre = matmul(entries, weight_ref[:, left : left + half])
            sigma = jax.nn.sigmoid(pre)
            hidden = (pre * sigma).astype(BF16)
            inner.append(swish_slope(pre, sigma))
            if part == 0:
                rows_ref[:, 2 * width + half :] = hidden
            branch_sum += right_transposed(hidden, weight_ref[:, left + half : left + 2 * half])
        after = residual + 0.5 * branch_sum
        last_normed, last_factor = norm_parts(after)
        last_gain = gain_ref[4:5, :]
        out_ref[...] = own_half(last_normed * last_gain).astype(BF16)
        gradient, last_grad = norm_back(
            cot_ref[...].astype(F32), last_normed, last_factor, last_gain
        )
        last_gain_ref[...] = 0.5 * last_grad
        branch = (0.5 * gradient).astype(BF16)
        rows_ref[:, :width] = branch
        entry_grad = 0.0
        for part in range(2):
            left = 2 * part * half
            grad_hidden = matmul(branch, weight_ref[:, left + half : left + 2 * half])
            grad_pre = (grad_hidden * inner[part]).astype(BF16)
            if part == 0:
                rows_ref[:, 2 * width : 2 * width + half] = grad_pre
            entry_grad += right_transposed(grad_pre, weight_ref[:, left : left + half])
        passed, gain_grad = norm_back(entry_grad, normed, factor, gain_ref[3:4, :])
        gain_grad_ref[...] = 0.5 * gain_grad
        total = gradient + passed
        grads_ref[:, :width] = total
        standard, _, shifted = batch_norm(conv_ref, sums_ref, batch_ref, count)
        grad_shifted = matmul(total.astype(BF16), mixed_ref[:, 7 * columns :]) * swish_slope(
            shifted, jax.nn.sigmoid(shifted)
        )
        grads_ref[:, width:] = grad_shifted
        grad_sums_ref[0:1, :] = jnp.sum(grad_shifted, 0, keepdims=True)
        grad_sums_ref[1:2, :] = jnp.sum(grad_shifted * standard, 0, keepdims=True)

    return on_chip(
        body,
        "second_block",
        (conv_kept, own, other, cotangent, gains, weights, mixed, sums, batch),
        (
            ((rows // 2, width), BF16),
            ((rows, width + columns), F32),
            ((rows, 2 * width + 2 * half), BF16),
            ((2, columns), F32),
            ((1, width), F32),
            ((1, width), F32),
        ),
    )


def conv_backward(norm_grads, grad_sums, conv_kept, sums, batch, weights, depth_kernel, count):
    rows = conv_kept.shape[0]
    columns = sums.shape[1]
    width = weights.shape[0]
    taps = depth_kernel.shape[0]
    half_taps = (taps - 1) // 2

    def body(ins, outs, scratch):
        grads_ref, grad_sums_ref, conv_ref, sums_ref, batch_ref, weight_ref, tap_ref = ins
        grad_conv_ref, joined_ref, part_ref = outs
        padded = scratch[0]
        standard, inverse, _ = batch_norm(conv_ref, sums_ref, batch_ref, count)
        grad_conv = (inverse * batch_ref[0:1, :]) * (
            grads_ref[:, width:]
            - grad_sums_ref[0:1, :] / count
            - standard * (grad_sums_ref[1:2, :] / count)
        )
        grad_conv_ref[...] = grad_conv
        pad_rows(padded, rows, columns, grad_conv)
        total = jnp.zeros((rows, columns), F32)
        for tap in range(taps):
            start = PAD + half_taps - tap
            total = total + tap_ref[tap : tap + 1, :] * padded[start : start + rows, :]
        gate_sigma = conv_ref[:, width + columns : width + 2 * columns]
        grad_value = total * gate_sigma
        grad_gate = grad_value * conv_ref[:, width : width + columns] * (1.0 - gate_sigma)
        joined = jnp.concatenate([grad_value, grad_gate], 1).astype(BF16)
        joined_ref[...] = joined
        part_ref[...] = right_transposed(
            joined, weight_ref[:, 5 * columns : 7 * columns]
        ).astype(BF16)

    return on_chip(
        body,
        "conv_backward",
        (norm_grads, grad_sums, conv_kept, sums, batch, weights, depth_kernel),
        (((rows, columns), F32), ((rows, 2 * columns), BF16), ((rows, width), BF16)),
        scratch=(pltpu.VMEM((rows + 2 * PAD, columns), F32),),
    )


def conv_weight_grads(norm_grads, grad_conv, joined, conv_kept, sums, batch, gains, taps, count):
    rows, columns = grad_conv.shape
    width = gains.shape[1]
    half_taps = (taps - 1) // 2

    def body(ins, outs, scratch):
        grads_ref, grad_ref, joined_ref, conv_ref, sums_ref, batch_ref, gain_ref = ins
        padded = scratch[0]
        entries = entries_of(conv_ref[:, :width], gain_ref[2:3, :])
        outs[0][:, : 2 * columns] = left_transposed(entries, joined_ref[...]).astype(BF16)
        _, _, shifted = batch_norm(conv_ref, sums_ref, batch_ref, count)
        activated = (shifted * jax.nn.sigmoid(shifted)).astype(BF16)
        outs[0][:, 2 * columns :] = left_transposed(
            grads_ref[:, :width].astype(BF16), activated
        ).astype(BF16)
        value = conv_ref[:, width : width + columns]
        gate = conv_ref[:, width + columns : width + 2 * columns]
        pad_rows(padded, rows, columns, value * gate)
        grad_conv_value = grad_ref[...]
        for tap in range(taps):
            start = PAD - half_taps + tap
            outs[1][tap : tap + 1, :] = jnp.sum(
                padded[start : start + rows, :] * grad_conv_value, 0, keepdims=True
            )

    return on_chip(
        body,
        "conv_weight_grads",
        (norm_grads, grad_conv, joined, conv_kept, sums, batch, gains),
        (((width, 3 * columns), BF16), ((taps, columns), F32)),
        scratch=(pltpu.VMEM((rows + 2 * PAD, columns), F32),),
    )


def first_back(gradient, own, other, kept, pre, gains, weights):
    rows, width = gradient.shape
    hidden = weights.shape[1] // 2

    def body(ins, outs, _):
        grad_ref, own_ref, other_ref, kept_ref, pre_ref, gain_ref, weight_ref = ins
        grads_ref, keep_ref, send_ref, gain_grad_ref = outs
        normed, factor = norm_parts(kept_residual(kept_ref, width))
        passed, gain_grad = norm_back(
            both_parts(own_ref, other_ref), normed, factor, gain_ref[1:2, :]
        )
        gain_grad_ref[...] = 0.5 * gain_grad
        total = grad_ref[...] + passed
        keep_ref[:, :width] = own_half(total)
        part = ff_back_body(total, pre_ref[...], weight_ref, grads_ref)
        keep_ref[:, width:] = own_half(part)
        send_ref[...] = other_half(part).astype(BF16)

    return on_chip(
        body,
        "first_back",
        (gradient, own, other, kept, pre, gains, weights),
        (
            ((rows, width + 2 * hidden), BF16),
            ((rows // 2, 2 * width), F32),
            ((rows // 2, width), BF16),
            ((1, width), F32),
        ),
    )


def input_back(keep, other, tokens, gains, gain_grads, tap_grads, bias_grads):
    rows, width = tokens.shape
    taps, columns = tap_grads.shape
    upper = (taps + 1) // 2
    packed_rows = -(-(6 + upper) // 8) * 8

    def body(ins, outs, _):
        keep_ref, other_ref, x_ref, gain_ref = ins[:4]
        tap_ref, bias_ref = ins[8:]
        packed = outs[1]
        normed, factor = norm_parts(x_ref[...].astype(F32))
        passed, gain_grad = norm_back(
            keep_ref[:, width:] + other_ref[...].astype(F32), normed, factor, gain_ref[0:1, :]
        )
        outs[0][...] = keep_ref[:, :width] + passed
        packed[...] = jnp.zeros((packed_rows, 2 * columns), F32)
        packed[0:1, :] = gain_grad
        for place in range(4):
            packed[place + 1 : place + 2, :] = ins[4 + place][...]
        packed[5:6, :columns] = bias_ref[0:1, :]
        packed[5:6, columns:] = bias_ref[1:2, :]
        packed[6 : 6 + upper, :columns] = tap_ref[:upper, :]
        packed[6 : 6 + taps - upper, columns:] = tap_ref[upper:, :]

    return on_chip(
        body,
        "input_back",
        (keep, other, tokens, gains) + tuple(gain_grads) + (tap_grads, bias_grads),
        (((rows, width), F32), ((packed_rows, 2 * columns), F32)),
        flops=1_000_000,
    )


def reduce_plain(grads):
    return lax.psum_scatter(grads.astype(BF16), "dp", scatter_dimension=0, tiled=True).astype(F32)


def stacked_columns(pieces, count):
    width = pieces.shape[1] // count
    return jnp.stack([pieces[:, index * width : (index + 1) * width] for index in range(count)])


def unstacked(stacked):
    return [stacked[index] for index in range(stacked.shape[0])]


def body(
    tokens,
    norm_gains,
    first_in,
    first_out,
    attention_in,
    attention_out,
    head_biases,
    gated_in,
    pointwise_out,
    depth_kernel,
    batch_scale,
    batch_shift,
    second_in,
    second_out,
    cotangent,
):
    local_heads = HEAD_TOTAL // lax.axis_size("tensor")
    length = tokens.shape[0] * lax.axis_size("tensor")
    token_count = float(length * lax.axis_size("dp"))
    columns = attention_out.shape[1]
    hidden = first_in.shape[1]
    width = tokens.shape[1]
    table = sinusoid(length, width).astype(BF16)
    batch = jnp.stack([batch_scale, batch_shift])
    split = doubling()

    def gather(pieces):
        return lax.all_gather(jnp.concatenate(pieces, 1), "dp", axis=0, tiled=True)

    tokens_all = both_halves(tokens)
    cotangent_all = both_halves(cotangent)

    second_own = jnp.concatenate([second_in, second_out], 1)
    second_pair = jnp.concatenate([second_own, swap(second_own)], 1)
    if split:
        batch_one = (first_in, first_out)
        batch_two = (
            attention_in.reshape(-1, columns),
            jnp.concatenate([attention_out, gated_in.reshape(-1, columns), pointwise_out], 0),
        )
        batch_one = gather_join(batch_one, gather_send(batch_one, 0))
        arrived_one = gather_send(batch_one, 1)
        arrived_two = gather_send(tie(batch_two, batch_one), 0)
        batch_one = gather_join(batch_one, arrived_one)
        arrived_one = gather_send(batch_one, 2)
        batch_two = gather_join(batch_two, tie(arrived_two, batch_one))
        arrived_two = gather_send(batch_two, 1)
        batch_one = gather_join(batch_one, tie(arrived_one, batch_two))
        second_pair = tie(second_pair, batch_one)
        batch_two = gather_join(batch_two, tie(arrived_two, batch_one))
        arrived_two = gather_send(batch_two, 2)
        batch_one = gather_last(batch_one)
    else:
        batch_one = gather([first_in, first_out])
        mixed_weights = gather(
            unstacked(attention_in) + [attention_out] + unstacked(gated_in) + [pointwise_out]
        )
        positions = position_forward(table, mixed_weights, columns)
    second_weights = gather([second_pair])

    pre1, part1, first_weights = first_forward(tokens_all, norm_gains, batch_one)
    other1 = swap(part1)
    if split:
        batch_two = gather_last(gather_join(batch_two, tie(arrived_two, other1)))
        mixed_weights, positions = mixed_assemble(batch_two, table, width)
    kept, part2 = attention_forward(
        tokens_all, part1, other1, norm_gains, mixed_weights, positions, head_biases, local_heads
    )
    other2 = swap(part2)
    conv_kept, sums = conv_forward(
        kept, part2, other2, norm_gains, mixed_weights, depth_kernel
    )
    sums = tie(sum_over(sums, "dp"), second_weights)
    part3 = norm_forward(conv_kept, sums, batch, mixed_weights, token_count)
    other3 = swap(part3)
    block_out, norm_grads, second_rows, grad_sums, gain5, gain4 = second_block(
        conv_kept,
        part3,
        other3,
        cotangent_all,
        norm_gains,
        second_weights,
        mixed_weights,
        sums,
        batch,
        token_count,
    )
    second_grads = second_weight_grads(second_rows, width)
    reduced_second = reduce_plain(second_grads)
    grad_sums = sum_over(grad_sums, "dp")
    grad_sums = tie(grad_sums, second_grads)
    grad_conv, joined3, part6 = conv_backward(
        norm_grads, grad_sums, conv_kept, sums, batch, mixed_weights, depth_kernel, token_count
    )
    other6 = swap(part6)
    conv_grads, tap_grads = conv_weight_grads(
        norm_grads,
        grad_conv,
        joined3,
        conv_kept,
        sums,
        batch,
        norm_gains,
        depth_kernel.shape[0],
        token_count,
    )
    other6 = tie(other6, conv_grads)
    grad2, joined2, table_grad, part7, gain3, bias_grads = attention_back(
        norm_grads,
        part6,
        other6,
        conv_kept,
        norm_gains,
        mixed_weights,
        positions,
        kept,
        local_heads,
    )
    other7 = swap(part7)
    mixed_grads = mixed_weight_grads(
        joined2, table, table_grad, grad2, kept, norm_gains, conv_grads, split
    )
    if split:
        keeps, sends = mixed_grads
        mixed_keeps, sends = scatter_add(keeps, scatter_send(sends, 0), 0, "mixed_sum")
        mixed_arrived = scatter_send(sends, 1)
        other7 = tie(other7, mixed_arrived)
    first_rows, keep8, send8, gain2 = first_back(
        grad2, part7, other7, kept, pre1, norm_gains, first_weights
    )
    other8 = swap(send8)
    small = ((gain2, gain3, gain4, gain5), tap_grads, bias_grads)
    if split:
        mixed_keeps, sends = scatter_add(mixed_keeps, mixed_arrived, 1, "mixed_sum")
        mixed_arrived = scatter_send(sends, 2)
        keeps, sends = ff_weight_split(
            tie(first_rows, mixed_keeps), tokens_all, norm_gains, 0, "first_weight_grads"
        )
        first_arrived = scatter_send(sends, 0)
        first_arrived = tie(first_arrived, mixed_arrived)
        first_keeps, sends = scatter_add(keeps, first_arrived, 0, "first_sum")
        first_arrived = scatter_send(sends, 1)
        mixed_keeps, sends = scatter_add(
            mixed_keeps, tie(mixed_arrived, first_keeps), 2, "mixed_sum"
        )
        mixed_arrived = scatter_send(sends, 3)
        first_arrived = tie(first_arrived, mixed_arrived)
        first_keeps, sends = scatter_add(first_keeps, first_arrived, 1, "first_sum")
        first_arrived = scatter_send(sends, 2)
        (mixed_a, mixed_b), _ = scatter_add(
            mixed_keeps, tie(mixed_arrived, first_keeps), 3, "mixed_sum"
        )
        other8 = tie(other8, mixed_a)
        grad_start, packed = input_back(keep8, other8, tokens, norm_gains, *small)
        first_arrived = tie(first_arrived, packed)
        first_keeps, sends = scatter_add(first_keeps, first_arrived, 2, "first_sum")
        first_arrived = scatter_send(sends, 3)
        (reduced_in, reduced_out), _ = scatter_add(first_keeps, first_arrived, 3, "first_sum")
        rows = mixed_a.shape[0] // 4
        reduced_attention = mixed_a.reshape(4, rows, columns)
        reduced_mixing = mixed_b[:rows]
        reduced_gated = mixed_b[rows : 3 * rows].reshape(2, rows, columns)
        reduced_pointwise = mixed_b[3 * rows :]
    else:
        grad_start, packed = input_back(keep8, other8, tokens, norm_gains, *small)
        first_grads = reduce_plain(
            ff_weight_grads(first_rows, tokens_all, norm_gains, 0, "first_weight_grads")
        )
        reduced_in, reduced_out = first_grads[:, :hidden], first_grads[:, hidden:]
        mixed = reduce_plain(mixed_grads)
        reduced_attention = stacked_columns(mixed[:, : 4 * columns], 4)
        reduced_mixing = mixed[:, 4 * columns : 5 * columns]
        reduced_gated = stacked_columns(mixed[:, 5 * columns : 7 * columns], 2)
        reduced_pointwise = mixed[:, 7 * columns :]
    packed = sum_over(packed, "dp")
    gain_total = sum_over(packed[:5], "tensor")
    bias_total = packed[5].reshape(bias_grads.shape)
    taps = tap_grads.shape[0]
    upper = (taps + 1) // 2
    tap_total = jnp.concatenate(
        [packed[6 : 6 + upper, :columns], packed[6 : 6 + taps - upper, columns:]], 0
    )
    return (
        block_out,
        grad_start,
        gain_total,
        reduced_in,
        reduced_out,
        reduced_attention,
        reduced_mixing,
        bias_total,
        reduced_gated,
        reduced_pointwise,
        tap_total,
        grad_sums[1],
        grad_sums[0],
        reduced_second[:, :hidden],
        reduced_second[:, hidden:],
    )


def solution(mesh):
    placed = (
        P(("dp", "tensor"), None),
        P(),
        P("dp", "tensor"),
        P("dp", "tensor"),
        P(None, "dp", "tensor"),
        P("dp", "tensor"),
        P(None, "tensor"),
        P(None, "dp", "tensor"),
        P("dp", "tensor"),
        P(None, "tensor"),
        P("tensor"),
        P("tensor"),
        P("dp", "tensor"),
        P("dp", "tensor"),
        P(("dp", "tensor"), None),
    )
    return jax.shard_map(
        body,
        mesh=mesh,
        in_specs=placed,
        out_specs=(
            P(("dp", "tensor"), None),
            P(("dp", "tensor"), None),
            P(),
            P("dp", "tensor"),
            P("dp", "tensor"),
            P(None, "dp", "tensor"),
            P("dp", "tensor"),
            P(None, "tensor"),
            P(None, "dp", "tensor"),
            P("dp", "tensor"),
            P(None, "tensor"),
            P("tensor"),
            P("tensor"),
            P("dp", "tensor"),
            P("dp", "tensor"),
        ),
        check_vma=False,
    )
```

time: 255 us -> 207 us (0.81)
  local copies, waits for them, and re-layouts: 49.4 us -> 15.1 us
  starting transfers between devices: 64.1 us -> 56.3 us
  Pallas kernels: 30.8 us -> 26 us
    unnamed x192 -> x76, local copies, waits for them, and re-layouts: 41.9 us -> 11 us
    ppermute x10 -> x9, waiting for transfers between devices: 34.4 us -> 20.2 us  [swap(): return lax.ppermute(value, 'tensor', [(0, 1), (1, 0)])]
    ppermute x48, waiting for transfers between devices: 49.4 us -> 62.7 us  [shift(): lax.ppermute(value, axis, [(k, k ^ mask) for k in range(lax.axis_size(axi...]
    pallas_call x26 -> x28, Pallas kernels: 30.8 us -> 26 us  [on_chip(): pl.pallas_call(kernel, out_shape=[jax.ShapeDtypeStruct(shape, kind) for s...]
    ppermute x48, starting transfers between devices: 54.1 us -> 49.7 us  [shift(): lax.ppermute(value, axis, [(k, k ^ mask) for k in range(lax.axis_size(axi...]
    ppermute x10 -> x9, starting transfers between devices: 9.92 us -> 6.52 us  [swap(): return lax.ppermute(value, 'tensor', [(0, 1), (1, 0)])]
    reshape x6 -> x0, local copies, waits for them, and re-layouts: 3.19 us -> none  [the longest x3 1.97 us: body(): jnp.reshape(value, (-1, 128))]
  transfers between devices with their start and end apart: 60 -> 59, of which waited for: 35 -> 33; matrix products, arithmetic and copies ran while one was open for 7% -> 7% of each run, Pallas kernels for 11% -> 11%
where the time goes in v4:
time: 207 us
  waiting for transfers between devices  83 us (40%)
  starting transfers between devices  56.3 us (27%)
  Pallas kernels  26 us (13%)
  local copies, waits for them, and re-layouts  15.1 us (7%)
  between operations  14.6 us (7%)
  other arithmetic  11.7 us (6%)
    ppermute x48, waiting for transfers between devices, shift(): lax.ppermute(value, axis, [(k, k ^ mask) for k in range(lax.axis_size(axi...  62.7 us
    ppermute x48, starting transfers between devices, shift(): lax.ppermute(value, axis, [(k, k ^ mask) for k in range(lax.axis_size(axi...  49.7 us
    pallas_call x28, Pallas kernels, on_chip(): pl.pallas_call(kernel, out_shape=[jax.ShapeDtypeStruct(shape, kind) for s...  26 us
    ppermute x9, waiting for transfers between devices, swap(): return lax.ppermute(value, 'tensor', [(0, 1), (1, 0)])  20.2 us
    unnamed x76, local copies, waits for them, and re-layouts  11 us
    ppermute x9, starting transfers between devices, swap(): return lax.ppermute(value, 'tensor', [(0, 1), (1, 0)])  6.52 us
  transfers between devices with their start and end apart: 59, of which 33 were waited for; matrix products, arithmetic and copies ran while one was open for 7% of the time, Pallas kernels for 11%

profile of v4, /device:TPU:0, one launch (start us, length us, event | category | flops | bytes accessed | tf_op | source)
XLA Modules:
  0.0 206.6 jit_solution(13248751700499042589)
XLA Ops:
  7.2 4.1 %collective-permute-start.1 = (bf16[32,1024]{1,0:T(8,128)(2,1)}, bf16[32,1024]{1,0:T(8,128)(2,1)S(1)}, u32[]{:S(2)}, u32[]{:S(2)}) collective-permute-start(bf16[32,1024]{1,0:T(8,128)(2,1)} %refs_0_.1), channel_id=1, source_target_pairs={{0,16},{2,18},{4,20},{6,22},{8,24},{10,26},{12,28},{14,30},{16,0},... | collective-permute-start | bytes 196616 | tf_op jit(solution)/shard_map/ppermute | solution.py:103
  11.4 3.8 %collective-permute-done.1.refs_2_ = bf16[32,1024]{1,0:T(8,128)(2,1)S(1)} collective-permute-done((bf16[32,1024]{1,0:T(8,128)(2,1)}, bf16[32,1024]{1,0:T(8,128)(2,1)S(1)}, u32[]{:S(2)}, u32[]{:S(2)}) %collective-permute-start.1) | collective-permute-done | bytes 65568 | tf_op jit(solution)/shard_map/ppermute | solution.py:103
  15.2 2.8 %collective-permute-done.2.refs_3_ = bf16[32,1024]{1,0:T(8,128)(2,1)S(1)} collective-permute-done((bf16[32,1024]{1,0:T(8,128)(2,1)}, bf16[32,1024]{1,0:T(8,128)(2,1)S(1)}, u32[]{:S(2)}, u32[]{:S(2)}) %collective-permute-start.2) | collective-permute-done | bytes 65568 | tf_op jit(solution)/shard_map/ppermute | solution.py:103
  20.5 1.5 collective-permute-start.4
  22.8 1.6 collective-permute-start.24
  25.2 3.3 %collective-permute-start.7 = (bf16[128,256]{1,0:T(8,128)(2,1)}, bf16[128,256]{1,0:T(8,128)(2,1)S(1)}, u32[]{:S(2)}, u32[]{:S(2)}) collective-permute-start(bf16[128,256]{1,0:T(8,128)(2,1)} %bitcast.8), channel_id=1, source_target_pairs={{0,16},{2,18},{4,20},{6,22},{8,24},{10,26},{12,28},{14,30},{16,0},... | collective-permute-start | bytes 196616 | tf_op jit(solution)/shard_map/ppermute | solution.py:103
  29.2 1.1 collective-permute-start.6
  30.3 1.6 pad_maximum_fusion.1
  32.7 1.8 collective-permute-done.8.refs_3_
  35.8 2.2 %collective-permute-done.6.refs_3_ = bf16[128,1024]{1,0:T(8,128)(2,1)S(1)} collective-permute-done((bf16[128,1024]{1,0:T(8,128)(2,1)S(1)}, bf16[128,1024]{1,0:T(8,128)(2,1)S(1)}, u32[]{:S(2)}, u32[]{:S(2)}) %collective-permute-start.6) | collective-permute-done | bytes 262176 | tf_op jit(solution)/shard_map/ppermute | solution.py:103
  39.2 1.5 collective-permute-start
  41.7 3.3 %collective-permute-done.26 = bf16[128,512]{1,0:T(8,128)(2,1)S(1)} collective-permute-done((bf16[128,512]{1,0:T(8,128)(2,1)S(1)}, bf16[128,512]{1,0:T(8,128)(2,1)S(1)}, u32[]{:S(2)}, u32[]{:S(2)}) %collective-permute-start.26) | collective-permute-done | bytes 131104 | tf_op jit(solution)/shard_map/ppermute | solution.py:83
  45.0 1.1 collective-permute-start.13
  47.7 4.5 %collective-permute-done.13.refs_3_ = bf16[256,256]{1,0:T(8,128)(2,1)S(1)} collective-permute-done((bf16[256,256]{1,0:T(8,128)(2,1)S(1)}, bf16[256,256]{1,0:T(8,128)(2,1)S(1)}, u32[]{:S(2)}, u32[]{:S(2)}) %collective-permute-start.13) | collective-permute-done | bytes 131104 | tf_op jit(solution)/shard_map/ppermute | solution.py:103
  52.8 2.0 collective-permute-start.15
  55.8 1.3 copy-done.11
  57.7 1.1 collective-permute-done.14.refs_2_
  58.8 4.5 %collective-permute-done.15.refs_3_ = bf16[512,256]{1,0:T(8,128)(2,1)S(1)} collective-permute-done((bf16[512,256]{1,0:T(8,128)(2,1)S(1)}, bf16[512,256]{1,0:T(8,128)(2,1)S(1)}, u32[]{:S(2)}, u32[]{:S(2)}) %collective-permute-start.15) | collective-permute-done | bytes 262176 | tf_op jit(solution)/shard_map/ppermute | solution.py:103
  64.2 2.4 %multiply_sine_fusion = (bf16[512,256]{1,0:T(8,128)(2,1)S(1)}, bf16[512,256]{1,0:T(8,128)(2,1)S(1)}) fusion(f32[256]{0:T(256)S(1)} %multiply_exponential_fusion, f32[512]{0:T(512)S(1)} %iota_add_fusion), kind=kLoop, calls=%fused_computation.3 | loop fusion | flops 393216 | bytes 527360 | tf_op jit(solution)/shard_map/sin | solution.py:57
  67.6 3.3 %attention_forward.1 = (bf16[256,3328]{1,0:T(8,128)(2,1)S(1)}, bf16[256,512]{1,0:T(8,128)(2,1)S(1)}) custom-call(bf16[256,512]{1,0:T(8,128)(2,1)S(1)} %pad_maximum_fusion.refs_0_.refs_1_, bf16[256,512]{1,0:T(8,128)(2,1)S(1)} %get-tuple-element.136.refs_1_, bf16[256,512]{1,0:T(8,128)(2,1)S(1)} %collective-permute-done.11.refs_2_, f32[5,512]{1,0:T(8,128)S(1)} %copy-done.13, ...), custom_call_target="tpu_custom_call" | custom-call | flops 300000000 | bytes 5124096 | tf_op jit(solution)/shard_map/attention_forward/pallas_call | solution.py:70
  71.5 7.8 %collective-permute-done.18.refs_2_ = bf16[256,512]{1,0:T(8,128)(2,1)S(1)} collective-permute-done((bf16[256,512]{1,0:T(8,128)(2,1)S(1)}, bf16[256,512]{1,0:T(8,128)(2,1)S(1)}, u32[]{:S(2)}, u32[]{:S(2)}) %collective-permute-start.18) | collective-permute-done | bytes 262176 | tf_op jit(solution)/shard_map/ppermute | solution.py:83
  79.3 1.9 conv_forward.1
  81.3 1.1 collective-permute-done.19
  82.5 1.5 collective-permute-start.20
  84.0 2.1 %collective-permute-done.20 = f32[2,256]{1,0:T(2,128)S(1)} collective-permute-done((f32[2,256]{1,0:T(2,128)S(1)}, f32[2,256]{1,0:T(2,128)S(1)}, u32[]{:S(2)}, u32[]{:S(2)}) %collective-permute-start.20) | collective-permute-done | bytes 2080 | tf_op jit(solution)/shard_map/ppermute | solution.py:103
  86.1 2.5 %collective-permute-start.23 = (f32[2,256]{1,0:T(2,128)S(1)}, f32[2,256]{1,0:T(2,128)S(1)}, u32[]{:S(2)}, u32[]{:S(2)}) collective-permute-start(f32[2,256]{1,0:T(2,128)S(1)} %add.59), channel_id=1, source_target_pairs={{0,24},{2,26},{4,28},{6,30},{8,16},{10,18},{12,20},{14,22},{16,8},... | collective-permute-start | bytes 6152 | tf_op jit(solution)/shard_map/ppermute | solution.py:103
  88.5 1.9 collective-permute-start.21
  91.4 1.6 collective-permute-done.22
  95.6 1.3 pad_maximum_fusion.2.refs_3_
  96.9 4.9 %collective-permute-done.25.refs_2_ = bf16[256,512]{1,0:T(8,128)(2,1)S(1)} collective-permute-done((bf16[256,512]{1,0:T(8,128)(2,1)S(1)}, bf16[256,512]{1,0:T(8,128)(2,1)S(1)}, u32[]{:S(2)}, u32[]{:S(2)}) %collective-permute-start.25) | collective-permute-done | bytes 262176 | tf_op jit(solution)/shard_map/ppermute | solution.py:83
  101.8 3.8 %second_block.1 = (bf16[128,512]{1,0:T(8,128)(2,1)}, f32[256,768]{1,0:T(8,128)S(1)}, bf16[256,3072]{1,0:T(8,128)(2,1)S(1)}, f32[2,256]{1,0:T(2,128)S(1)}, f32[1,512]{1,0:T(1,128)S(1)}, /*index=5*/f32[1,512]{1,0:T(1,128)S(1)}) custom-call(f32[256,1280]{1,0:T(8,128)S(1)} %get-tuple-element.149.refs_0_.refs_2_.refs_3_, ...), custom_call_target="tpu_custom_call" | custom-call | flops 300000000 | bytes 10899456 | tf_op jit(solution)/shard_map/second_block/pallas_call | solution.py:70
  106.6 1.2 collective-permute-done.27
  107.7 1.4 collective-permute-start.28
  109.1 2.2 %collective-permute-done.28 = f32[2,256]{1,0:T(2,128)S(1)} collective-permute-done((f32[2,256]{1,0:T(2,128)S(1)}, f32[2,256]{1,0:T(2,128)S(1)}, u32[]{:S(2)}, u32[]{:S(2)}) %collective-permute-start.28) | collective-permute-done | bytes 2080 | tf_op jit(solution)/shard_map/ppermute | solution.py:103
  111.9 1.8 collective-permute-start.31
  114.2 2.0 collective-permute-start.29
  117.0 1.3 copy-done.2
  119.2 1.1 copy-done.4
  122.4 1.6 conv_backward.1
  125.1 2.3 %conv_weight_grads.1 = (bf16[512,768]{1,0:T(8,128)(2,1)S(1)}, f32[31,256]{1,0:T(8,128)S(1)}) custom-call(f32[256,768]{1,0:T(8,128)S(1)} %copy-done.5, f32[256,256]{1,0:T(8,128)S(1)} %get-tuple-element.159.refs_1_, bf16[256,512]{1,0:T(8,128)(2,1)S(1)} %get-tuple-element.160.refs_2_, f32[256,1280]{1,0:T(8,128)S(1)} %get-tuple-element.149.refs_0_.refs_2_.refs_3_, ...), custom_call_target="tpu_custom_call" | custom-call | flops 300000000 | bytes 3453952 | tf_op jit(solution)/shard_map/conv_weight_grads/pallas_call | solution.py:70
  127.4 3.1 %collective-permute-done.32.refs_2_ = bf16[256,512]{1,0:T(8,128)(2,1)S(1)} collective-permute-done((bf16[256,512]{1,0:T(8,128)(2,1)S(1)}, bf16[256,512]{1,0:T(8,128)(2,1)S(1)}, u32[]{:S(2)}, u32[]{:S(2)}) %collective-permute-start.32) | collective-permute-done | bytes 262176 | tf_op jit(solution)/shard_map/ppermute | solution.py:83
  130.5 3.6 %attention_back.1 = (f32[256,512]{1,0:T(8,128)S(1)}, bf16[256,768]{1,0:T(8,128)(2,1)S(1)}, bf16[512,256]{1,0:T(8,128)(2,1)S(1)}, bf16[256,512]{1,0:T(8,128)(2,1)...) custom-call(f32[256,768]{1,0:T(8,128)S(1)} %copy-done.5, bf16[256,512]{1,0:T(8,128)(2,1)S(1)} %get-tuple-element.158.refs_1_, ...), custom_call_target="tpu_custom_call" | custom-call | flops 300000000 | bytes 8140800 | tf_op jit(solution)/shard_map/attention_back/pallas_call | solution.py:70
  134.1 1.1 mixed_weight_grads.1
  135.8 1.4 collective-permute-done.34.refs_2_
  138.2 1.4 collective-permute-start.36
  139.5 1.8 collective-permute-start.37
  141.6 5.5 %collective-permute-done.36.refs_2_ = bf16[512,256]{1,0:T(8,128)(2,1)S(1)} collective-permute-done((bf16[512,256]{1,0:T(8,128)(2,1)S(1)}, bf16[512,256]{1,0:T(8,128)(2,1)S(1)}, u32[]{:S(2)}, u32[]{:S(2)}) %collective-permute-start.36) | collective-permute-done | bytes 262176 | tf_op jit(solution)/shard_map/ppermute | solution.py:103
  147.1 3.3 %collective-permute-done.37.refs_3_ = bf16[512,256]{1,0:T(8,128)(2,1)S(1)} collective-permute-done((bf16[512,256]{1,0:T(8,128)(2,1)S(1)}, bf16[512,256]{1,0:T(8,128)(2,1)S(1)}, u32[]{:S(2)}, u32[]{:S(2)}) %collective-permute-start.37) | collective-permute-done | bytes 262176 | tf_op jit(solution)/shard_map/ppermute | solution.py:103
  150.6 1.2 first_back.1
  151.8 1.3 first_weight_grads.1
  153.7 2.2 %collective-permute-start.39 = (bf16[256,256]{1,0:T(8,128)(2,1)S(1)}, bf16[256,256]{1,0:T(8,128)(2,1)S(1)}, u32[]{:S(2)}, u32[]{:S(2)}) collective-permute-start(bf16[256,256]{1,0:T(8,128)(2,1)S(1)} %get-tuple-element.182), channel_id=1, source_target_pairs={{0,8},{2,10},{4,12},{6,14},{8,0},{10,2},{12,4},{14,6},{16,24},{18,... | collective-permute-start | bytes 393224 | tf_op jit(solution)/shard_map/ppermute | solution.py:103
  155.9 6.0 %collective-permute-done.39.refs_2_ = bf16[256,256]{1,0:T(8,128)(2,1)S(1)} collective-permute-done((bf16[256,256]{1,0:T(8,128)(2,1)S(1)}, bf16[256,256]{1,0:T(8,128)(2,1)S(1)}, u32[]{:S(2)}, u32[]{:S(2)}) %collective-permute-start.39) | collective-permute-done | bytes 131104 | tf_op jit(solution)/shard_map/ppermute | solution.py:103
  163.9 1.6 collective-permute-start.43
  165.5 1.4 collective-permute-start.44
  166.9 6.6 %collective-permute-done.43.refs_2_ = bf16[128,256]{1,0:T(8,128)(2,1)S(1)} collective-permute-done((bf16[128,256]{1,0:T(8,128)(2,1)S(1)}, bf16[128,256]{1,0:T(8,128)(2,1)S(1)}, u32[]{:S(2)}, u32[]{:S(2)}) %collective-permute-start.43) | collective-permute-done | bytes 65568 | tf_op jit(solution)/shard_map/ppermute | solution.py:103
  174.5 2.5 %collective-permute-done.46.refs_3_ = bf16[128,1024]{1,0:T(8,128)(2,1)S(1)} collective-permute-done((bf16[128,1024]{1,0:T(8,128)(2,1)S(1)}, bf16[128,1024]{1,0:T(8,128)(2,1)S(1)}, u32[]{:S(2)}, u32[]{:S(2)}) %collective-permute-start.46) | collective-permute-done | bytes 262176 | tf_op jit(solution)/shard_map/ppermute | solution.py:103
  178.8 1.2 collective-permute-done.47
  180.0 1.3 collective-permute-start.48
  182.7 1.5 collective-permute-done.48
  184.2 1.2 collective-permute-start.51
  186.3 2.4 %collective-permute-start.49 = (f32[24,512]{1,0:T(8,128)S(1)}, f32[24,512]{1,0:T(8,128)S(1)}, u32[]{:S(2)}, u32[]{:S(2)}) collective-permute-start(f32[24,512]{1,0:T(8,128)S(1)} %add.69), channel_id=1, source_target_pairs={{0,8},{2,10},{4,12},{6,14},{8,0},{10,2},{12,4},{14,6},{16,24},{18,... | collective-permute-start | bytes 147464 | tf_op jit(solution)/shard_map/ppermute | solution.py:103
  190.1 2.9 %collective-permute-start.56 = (bf16[32,1024]{1,0:T(8,128)(2,1)S(1)}, bf16[32,1024]{1,0:T(8,128)(2,1)S(1)}, u32[]{:S(2)}, u32[]{:S(2)}) collective-permute-start(bf16[32,1024]{1,0:T(8,128)(2,1)S(1)} %get-tuple-element.225), channel_id=1, source_target_pairs={{0,16},{2,18},{4,20},{6,22},{8,24},{10,26},{12,28},{14,30},{16,0},... | collective-permute-start | bytes 196616 | tf_op jit(solution)/shard_map/ppermute | solution.py:103
  194.5 2.3 %collective-permute-done.52 = f32[5,512]{1,0:T(8,128)S(1)} collective-permute-done((f32[5,512]{1,0:T(8,128)S(1)}, f32[5,512]{1,0:T(8,128)S(1)}, u32[]{:S(2)}, u32[]{:S(2)}) %collective-permute-start.52) | collective-permute-done | bytes 10272 | tf_op jit(solution)/shard_map/ppermute | solution.py:103
  198.2 1.6 fusion.1
  (192 shorter events, 39.4 us)
Async XLA Ops:
  7.2 32.0 %copy-start.18 = (bf16[128,512]{1,0:T(8,128)(2,1)S(1)}, bf16[128,512]{1,0:T(8,128)(2,1)}, u32[]{:S(2)}) copy-start(bf16[128,512]{1,0:T(8,128)(2,1)} %refs_2_.3) | copy-start | bytes 393220
  7.2 86.4 %all-gather.2.cloned.1.call-start = ((), (), s32[]{:S(2)}) async-start(), calls=%async_computation.1 | async-start | bytes 4456448 | tf_op jit(solution)/shard_map/all_gather | solution.py:855
  7.2 8.0 %collective-permute-start.1 = (bf16[32,1024]{1,0:T(8,128)(2,1)}, bf16[32,1024]{1,0:T(8,128)(2,1)S(1)}, u32[]{:S(2)}, u32[]{:S(2)}) collective-permute-start(bf16[32,1024]{1,0:T(8,128)(2,1)} %refs_0_.1), channel_id=1, source_target_pairs={{0,16},{2,18},{4,20},{6,22},{8,24},{10,26},{12,28},{14,30},{16,0},... | collective-permute-start | bytes 196616 | tf_op jit(solution)/shard_map/ppermute | solution.py:103
  11.3 6.7 %collective-permute-start.2 = (bf16[32,1024]{1,0:T(8,128)(2,1)}, bf16[32,1024]{1,0:T(8,128)(2,1)S(1)}, u32[]{:S(2)}, u32[]{:S(2)}) collective-permute-start(bf16[32,1024]{1,0:T(8,128)(2,1)} %refs_1_.2), channel_id=1, source_target_pairs={{0,16},{2,18},{4,20},{6,22},{8,24},{10,26},{12,28},{14,30},{16,0},... | collective-permute-start | bytes 196616 | tf_op jit(solution)/shard_map/ppermute | solution.py:103
  19.7 19.0 %copy-start.35 = (bf16[128,512]{1,0:T(8,128)(2,1)S(1)}, bf16[128,512]{1,0:T(8,128)(2,1)}, u32[]{:S(2)}) copy-start(bf16[128,512]{1,0:T(8,128)(2,1)} %param.29) | copy-start | bytes 393220
  19.7 8.8 %collective-permute-start.3 = (bf16[64,1024]{1,0:T(8,128)(2,1)S(1)}, bf16[64,1024]{1,0:T(8,128)(2,1)S(1)}, u32[]{:S(2)}, u32[]{:S(2)}) collective-permute-start(bf16[64,1024]{1,0:T(8,128)(2,1)S(1)} %get-tuple-element.122.refs_0_), channel_id=1, source_target_pairs={{0,8},{2,10},{4,12},{6,14},{8,0},{10,2},{12,4},{14,6},{16,24},{18,... | collective-permute-start | bytes 393224 | tf_op jit(solution)/shard_map/ppermute | solution.py:103
  20.5 8.1 %collective-permute-start.4 = (bf16[64,1024]{1,0:T(8,128)(2,1)S(1)}, bf16[64,1024]{1,0:T(8,128)(2,1)S(1)}, u32[]{:S(2)}, u32[]{:S(2)}) collective-permute-start(bf16[64,1024]{1,0:T(8,128)(2,1)S(1)} %get-tuple-element.123.refs_1_), channel_id=1, source_target_pairs={{0,4},{2,6},{4,0},{6,2},{8,12},{10,14},{12,8},{14,10},{16,20},{18,... | collective-permute-start | bytes 393224 | tf_op jit(solution)/shard_map/ppermute | solution.py:103
  22.8 7.5 %collective-permute-start.24 = (bf16[32,2048]{1,0:T(8,128)(2,1)S(1)}, bf16[32,2048]{1,0:T(8,128)(2,1)S(1)}, u32[]{:S(2)}, u32[]{:S(2)}) collective-permute-start(bf16[32,2048]{1,0:T(8,128)(2,1)S(1)} %pad_maximum_fusion.3), channel_id=1, source_target_pairs={{0,1},{1,0},{2,3},{3,2},{4,5},{5,4},{6,7},{7,6},{8,9},{9,8},{10,11... | collective-permute-start | bytes 393224 | tf_op jit(solution)/shard_map/ppermute | solution.py:83
  25.2 7.5 %collective-permute-start.7 = (bf16[128,256]{1,0:T(8,128)(2,1)}, bf16[128,256]{1,0:T(8,128)(2,1)S(1)}, u32[]{:S(2)}, u32[]{:S(2)}) collective-permute-start(bf16[128,256]{1,0:T(8,128)(2,1)} %bitcast.8), channel_id=1, source_target_pairs={{0,16},{2,18},{4,20},{6,22},{8,24},{10,26},{12,28},{14,30},{16,0},... | collective-permute-start | bytes 196616 | tf_op jit(solution)/shard_map/ppermute | solution.py:103
  28.5 6.0 %collective-permute-start.8 = (bf16[128,256]{1,0:T(8,128)(2,1)S(1)}, bf16[128,256]{1,0:T(8,128)(2,1)S(1)}, u32[]{:S(2)}, u32[]{:S(2)}) collective-permute-start(bf16[128,256]{1,0:T(8,128)(2,1)S(1)} %pad_maximum_fusion.4.refs_1_), channel_id=1, source_target_pairs={{0,16},{2,18},{4,20},{6,22},{8,24},{10,26},{12,28},{14,30},{16,0},... | collective-permute-start | bytes 196616 | tf_op jit(solution)/shard_map/ppermute | solution.py:103
  28.6 7.2 %collective-permute-start.5 = (bf16[128,1024]{1,0:T(8,128)(2,1)S(1)}, bf16[128,1024]{1,0:T(8,128)(2,1)S(1)}, u32[]{:S(2)}, u32[]{:S(2)}) collective-permute-start(bf16[128,1024]{1,0:T(8,128)(2,1)S(1)} %get-tuple-element.124.refs_0_), channel_id=1, source_target_pairs={{0,4},{2,6},{4,0},{6,2},{8,12},{10,14},{12,8},{14,10},{16,20},{18,... | collective-permute-start | bytes 786440 | tf_op jit(solution)/shard_map/ppermute | solution.py:103
  29.2 25.6 %copy-start.13 = (f32[5,512]{1,0:T(8,128)S(1)}, f32[5,512]{1,0:T(8,128)}, u32[]{:S(2)}) copy-start(f32[5,512]{1,0:T(8,128)} %refs_3_.5) | copy-start | bytes 30724
  29.2 8.8 %collective-permute-start.6 = (bf16[128,1024]{1,0:T(8,128)(2,1)S(1)}, bf16[128,1024]{1,0:T(8,128)(2,1)S(1)}, u32[]{:S(2)}, u32[]{:S(2)}) collective-permute-start(bf16[128,1024]{1,0:T(8,128)(2,1)S(1)} %get-tuple-element.125.refs_1_), channel_id=1, source_target_pairs={{0,8},{2,10},{4,12},{6,14},{8,0},{10,2},{12,4},{14,6},{16,24},{18,... | collective-permute-start | bytes 786440 | tf_op jit(solution)/shard_map/ppermute | solution.py:103
  38.0 160.2 %reduce-scatter.2.cloned.1.call-start = ((), (), s32[]{:S(2)}) async-start(), calls=%async_computation.2 | async-start | bytes 2228224 | tf_op jit(solution)/shard_map/reduce_scatter | solution.py:815
  38.1 16.7 %collective-permute-start.9 = (bf16[256,1024]{1,0:T(8,128)(2,1)S(1)}, bf16[256,1024]{1,0:T(8,128)(2,1)S(1)}, u32[]{:S(2)}, u32[]{:S(2)}) collective-permute-start(bf16[256,1024]{1,0:T(8,128)(2,1)S(1)} %get-tuple-element.134.refs_2_), channel_id=1, source_target_pairs={{0,2},{2,0},{4,6},{6,4},{8,10},{10,8},{12,14},{14,12},{16,18},{18,... | collective-permute-start | bytes 1572872 | tf_op jit(solution)/shard_map/ppermute | solution.py:103
  38.2 16.6 %collective-permute-start.10 = (bf16[256,1024]{1,0:T(8,128)(2,1)S(1)}, bf16[256,1024]{1,0:T(8,128)(2,1)S(1)}, u32[]{:S(2)}, u32[]{:S(2)}) collective-permute-start(bf16[256,1024]{1,0:T(8,128)(2,1)S(1)} %get-tuple-element.135.refs_4_), channel_id=1, source_target_pairs={{0,2},{2,0},{4,6},{6,4},{8,10},{10,8},{12,14},{14,12},{16,18},{18,... | collective-permute-start | bytes 1572872 | tf_op jit(solution)/shard_map/ppermute | solution.py:103
  38.7 6.4 %collective-permute-start.26 = (bf16[128,512]{1,0:T(8,128)(2,1)S(1)}, bf16[128,512]{1,0:T(8,128)(2,1)S(1)}, u32[]{:S(2)}, u32[]{:S(2)}) collective-permute-start(bf16[128,512]{1,0:T(8,128)(2,1)S(1)} %copy-done.35), channel_id=1, source_target_pairs={{0,1},{1,0},{2,3},{3,2},{4,5},{5,4},{6,7},{7,6},{8,9},{9,8},{10,11... | collective-permute-start | bytes 393224 | tf_op jit(solution)/shard_map/ppermute | solution.py:83
  39.2 7.8 %collective-permute-start = (bf16[128,512]{1,0:T(8,128)(2,1)S(1)}, bf16[128,512]{1,0:T(8,128)(2,1)S(1)}, u32[]{:S(2)}, u32[]{:S(2)}) collective-permute-start(bf16[128,512]{1,0:T(8,128)(2,1)S(1)} %copy-done.18), channel_id=1, source_target_pairs={{0,1},{1,0},{2,3},{3,2},{4,5},{5,4},{6,7},{7,6},{8,9},{9,8},{10,11... | collective-permute-start | bytes 393224 | tf_op jit(solution)/shard_map/ppermute | solution.py:83
  40.7 7.0 %collective-permute-start.12 = (bf16[256,256]{1,0:T(8,128)(2,1)S(1)}, bf16[256,256]{1,0:T(8,128)(2,1)S(1)}, u32[]{:S(2)}, u32[]{:S(2)}) collective-permute-start(bf16[256,256]{1,0:T(8,128)(2,1)S(1)} %get-tuple-element.130.refs_0_), channel_id=1, source_target_pairs={{0,8},{2,10},{4,12},{6,14},{8,0},{10,2},{12,4},{14,6},{16,24},{18,... | collective-permute-start | bytes 393224 | tf_op jit(solution)/shard_map/ppermute | solution.py:103
  45.0 7.3 %collective-permute-start.13 = (bf16[256,256]{1,0:T(8,128)(2,1)S(1)}, bf16[256,256]{1,0:T(8,128)(2,1)S(1)}, u32[]{:S(2)}, u32[]{:S(2)}) collective-permute-start(bf16[256,256]{1,0:T(8,128)(2,1)S(1)} %get-tuple-element.131.refs_1_), channel_id=1, source_target_pairs={{0,4},{2,6},{4,0},{6,2},{8,12},{10,14},{12,8},{14,10},{16,20},{18,... | collective-permute-start | bytes 393224 | tf_op jit(solution)/shard_map/ppermute | solution.py:103
  47.7 19.9 %copy-start.8 = (bf16[256,512]{1,0:T(8,128)(2,1)}, bf16[256,512]{1,0:T(8,128)(2,1)S(1)}, u32[]{:S(2)}) copy-start(bf16[256,512]{1,0:T(8,128)(2,1)S(1)} %pad_maximum_fusion.refs_0_.refs_1_) | copy-start | bytes 786436
  52.3 6.4 %collective-permute-start.14 = (bf16[512,256]{1,0:T(8,128)(2,1)S(1)}, bf16[512,256]{1,0:T(8,128)(2,1)S(1)}, u32[]{:S(2)}, u32[]{:S(2)}) collective-permute-start(bf16[512,256]{1,0:T(8,128)(2,1)S(1)} %get-tuple-element.139.refs_0_), channel_id=1, source_target_pairs={{0,4},{2,6},{4,0},{6,2},{8,12},{10,14},{12,8},{14,10},{16,20},{18,... | collective-permute-start | bytes 786440 | tf_op jit(solution)/shard_map/ppermute | solution.py:103
  52.8 10.4 %collective-permute-start.15 = (bf16[512,256]{1,0:T(8,128)(2,1)S(1)}, bf16[512,256]{1,0:T(8,128)(2,1)S(1)}, u32[]{:S(2)}, u32[]{:S(2)}) collective-permute-start(bf16[512,256]{1,0:T(8,128)(2,1)S(1)} %get-tuple-element.140.refs_1_), channel_id=1, source_target_pairs={{0,8},{2,10},{4,12},{6,14},{8,0},{10,2},{12,4},{14,6},{16,24},{18,... | collective-permute-start | bytes 786440 | tf_op jit(solution)/shard_map/ppermute | solution.py:103
  57.2 6.4 %collective-permute-start.11 = (bf16[256,512]{1,0:T(8,128)(2,1)S(1)}, bf16[256,512]{1,0:T(8,128)(2,1)S(1)}, u32[]{:S(2)}, u32[]{:S(2)}) collective-permute-start(bf16[256,512]{1,0:T(8,128)(2,1)S(1)} %get-tuple-element.136.refs_1_), channel_id=1, source_target_pairs={{0,1},{1,0},{2,3},{3,2},{4,5},{5,4},{6,7},{7,6},{8,9},{9,8},{10,11... | collective-permute-start | bytes 786440 | tf_op jit(solution)/shard_map/ppermute | solution.py:83
  63.6 3.2 %collective-permute-start.16 = (bf16[1024,256]{1,0:T(8,128)(2,1)S(1)}, bf16[1024,256]{1,0:T(8,128)(2,1)S(1)}, u32[]{:S(2)}, u32[]{:S(2)}) collective-permute-start(bf16[1024,256]{1,0:T(8,128)(2,1)S(1)} %get-tuple-element.143.refs_0_), channel_id=1, source_target_pairs={{0,2},{2,0},{4,6},{6,4},{8,10},{10,8},{12,14},{14,12},{16,18},{18,... | collective-permute-start | bytes 1572872 | tf_op jit(solution)/shard_map/ppermute | solution.py:103
  63.7 3.2 %collective-permute-start.17 = (bf16[1024,256]{1,0:T(8,128)(2,1)S(1)}, bf16[1024,256]{1,0:T(8,128)(2,1)S(1)}, u32[]{:S(2)}, u32[]{:S(2)}) collective-permute-start(bf16[1024,256]{1,0:T(8,128)(2,1)S(1)} %get-tuple-element.144.refs_2_), channel_id=1, source_target_pairs={{0,2},{2,0},{4,6},{6,4},{8,10},{10,8},{12,14},{14,12},{16,18},{18,... | collective-permute-start | bytes 1572872 | tf_op jit(solution)/shard_map/ppermute | solution.py:103
  71.0 8.3 %collective-permute-start.18 = (bf16[256,512]{1,0:T(8,128)(2,1)S(1)}, bf16[256,512]{1,0:T(8,128)(2,1)S(1)}, u32[]{:S(2)}, u32[]{:S(2)}) collective-permute-start(bf16[256,512]{1,0:T(8,128)(2,1)S(1)} %get-tuple-element.148.refs_1_), channel_id=1, source_target_pairs={{0,1},{1,0},{2,3},{3,2},{4,5},{5,4},{6,7},{7,6},{8,9},{9,8},{10,11... | collective-permute-start | bytes 786440 | tf_op jit(solution)/shard_map/ppermute | solution.py:83
  81.2 1.2 collective-permute-start.19
  82.5 3.6 %collective-permute-start.20 = (f32[2,256]{1,0:T(2,128)S(1)}, f32[2,256]{1,0:T(2,128)S(1)}, u32[]{:S(2)}, u32[]{:S(2)}) collective-permute-start(f32[2,256]{1,0:T(2,128)S(1)} %add.58), channel_id=1, source_target_pairs={{0,4},{2,6},{4,0},{6,2},{8,12},{10,14},{12,8},{14,10},{16,20},{18,... | collective-permute-start | bytes 6152 | tf_op jit(solution)/shard_map/ppermute | solution.py:103
  86.1 5.4 %collective-permute-start.23 = (f32[2,256]{1,0:T(2,128)S(1)}, f32[2,256]{1,0:T(2,128)S(1)}, u32[]{:S(2)}, u32[]{:S(2)}) collective-permute-start(f32[2,256]{1,0:T(2,128)S(1)} %add.59), channel_id=1, source_target_pairs={{0,24},{2,26},{4,28},{6,30},{8,16},{10,18},{12,20},{14,22},{16,8},... | collective-permute-start | bytes 6152 | tf_op jit(solution)/shard_map/ppermute | solution.py:103
  88.5 4.5 %collective-permute-start.22 = (f32[2,256]{1,0:T(2,128)S(1)}, f32[2,256]{1,0:T(2,128)S(1)}, u32[]{:S(2)}, u32[]{:S(2)}) collective-permute-start(f32[2,256]{1,0:T(2,128)S(1)} %add.59), channel_id=1, source_target_pairs={{0,16},{2,18},{4,20},{6,22},{8,24},{10,26},{12,28},{14,30},{16,0},... | collective-permute-start | bytes 6152 | tf_op jit(solution)/shard_map/ppermute | solution.py:103
  88.5 4.5 %collective-permute-start.21 = (f32[2,256]{1,0:T(2,128)S(1)}, f32[2,256]{1,0:T(2,128)S(1)}, u32[]{:S(2)}, u32[]{:S(2)}) collective-permute-start(f32[2,256]{1,0:T(2,128)S(1)} %add.59), channel_id=1, source_target_pairs={{0,8},{2,10},{4,12},{6,14},{8,0},{10,2},{12,4},{14,6},{16,24},{18,... | collective-permute-start | bytes 6152 | tf_op jit(solution)/shard_map/ppermute | solution.py:103
  95.3 6.6 %collective-permute-start.25 = (bf16[256,512]{1,0:T(8,128)(2,1)S(1)}, bf16[256,512]{1,0:T(8,128)(2,1)S(1)}, u32[]{:S(2)}, u32[]{:S(2)}) collective-permute-start(bf16[256,512]{1,0:T(8,128)(2,1)S(1)} %norm_forward.1.refs_1_), channel_id=1, source_target_pairs={{0,1},{1,0},{2,3},{3,2},{4,5},{5,4},{6,7},{7,6},{8,9},{9,8},{10,11... | collective-permute-start | bytes 786440 | tf_op jit(solution)/shard_map/ppermute | solution.py:83
  106.6 1.2 collective-permute-start.27
  107.7 3.6 %collective-permute-start.28 = (f32[2,256]{1,0:T(2,128)S(1)}, f32[2,256]{1,0:T(2,128)S(1)}, u32[]{:S(2)}, u32[]{:S(2)}) collective-permute-start(f32[2,256]{1,0:T(2,128)S(1)} %add.63), channel_id=1, source_target_pairs={{0,4},{2,6},{4,0},{6,2},{8,12},{10,14},{12,8},{14,10},{16,20},{18,... | collective-permute-start | bytes 6152 | tf_op jit(solution)/shard_map/ppermute | solution.py:103
  111.9 6.5 %collective-permute-start.31 = (f32[2,256]{1,0:T(2,128)}, f32[2,256]{1,0:T(2,128)}, u32[]{:S(2)}, u32[]{:S(2)}) collective-permute-start(f32[2,256]{1,0:T(2,128)} %add.64), channel_id=1, source_target_pairs={{0,24},{2,26},{4,28},{6,30},{8,16},{10,18},{12,20},{14,22},{16,8},... | collective-permute-start | bytes 6152 | tf_op jit(solution)/shard_map/ppermute | solution.py:103
  113.6 4.8 %collective-permute-start.30 = (f32[2,256]{1,0:T(2,128)}, f32[2,256]{1,0:T(2,128)}, u32[]{:S(2)}, u32[]{:S(2)}) collective-permute-start(f32[2,256]{1,0:T(2,128)} %add.64), channel_id=1, source_target_pairs={{0,16},{2,18},{4,20},{6,22},{8,24},{10,26},{12,28},{14,30},{16,0},... | collective-permute-start | bytes 6152 | tf_op jit(solution)/shard_map/ppermute | solution.py:103
  114.2 4.2 %collective-permute-start.29 = (f32[2,256]{1,0:T(2,128)}, f32[2,256]{1,0:T(2,128)}, u32[]{:S(2)}, u32[]{:S(2)}) collective-permute-start(f32[2,256]{1,0:T(2,128)} %add.64), channel_id=1, source_target_pairs={{0,8},{2,10},{4,12},{6,14},{8,0},{10,2},{12,4},{14,6},{16,24},{18,... | collective-permute-start | bytes 6152 | tf_op jit(solution)/shard_map/ppermute | solution.py:103
  124.1 6.4 %collective-permute-start.32 = (bf16[256,512]{1,0:T(8,128)(2,1)S(1)}, bf16[256,512]{1,0:T(8,128)(2,1)S(1)}, u32[]{:S(2)}, u32[]{:S(2)}) collective-permute-start(bf16[256,512]{1,0:T(8,128)(2,1)S(1)} %get-tuple-element.158.refs_1_), channel_id=1, source_target_pairs={{0,1},{1,0},{2,3},{3,2},{4,5},{5,4},{6,7},{7,6},{8,9},{9,8},{10,11... | collective-permute-start | bytes 786440 | tf_op jit(solution)/shard_map/ppermute | solution.py:83
  135.3 2.0 collective-permute-start.34
  135.3 2.6 %collective-permute-start.35 = (bf16[1024,256]{1,0:T(8,128)(2,1)S(1)}, bf16[1024,256]{1,0:T(8,128)(2,1)S(1)}, u32[]{:S(2)}, u32[]{:S(2)}) collective-permute-start(bf16[1024,256]{1,0:T(8,128)(2,1)S(1)} %get-tuple-element.170), channel_id=1, source_target_pairs={{0,2},{2,0},{4,6},{6,4},{8,10},{10,8},{12,14},{14,12},{16,18},{18,... | collective-permute-start | bytes 1572872 | tf_op jit(solution)/shard_map/ppermute | solution.py:103
  138.2 8.9 %collective-permute-start.36 = (bf16[512,256]{1,0:T(8,128)(2,1)S(1)}, bf16[512,256]{1,0:T(8,128)(2,1)S(1)}, u32[]{:S(2)}, u32[]{:S(2)}) collective-permute-start(bf16[512,256]{1,0:T(8,128)(2,1)S(1)} %get-tuple-element.171), channel_id=1, source_target_pairs={{0,4},{2,6},{4,0},{6,2},{8,12},{10,14},{12,8},{14,10},{16,20},{18,... | collective-permute-start | bytes 786440 | tf_op jit(solution)/shard_map/ppermute | solution.py:103
  139.5 10.9 %collective-permute-start.37 = (bf16[512,256]{1,0:T(8,128)(2,1)S(1)}, bf16[512,256]{1,0:T(8,128)(2,1)S(1)}, u32[]{:S(2)}, u32[]{:S(2)}) collective-permute-start(bf16[512,256]{1,0:T(8,128)(2,1)S(1)} %get-tuple-element.172), channel_id=1, source_target_pairs={{0,8},{2,10},{4,12},{6,14},{8,0},{10,2},{12,4},{14,6},{16,24},{18,... | collective-permute-start | bytes 786440 | tf_op jit(solution)/shard_map/ppermute | solution.py:103
  141.3 9.2 %collective-permute-start.33 = (bf16[256,512]{1,0:T(8,128)(2,1)S(1)}, bf16[256,512]{1,0:T(8,128)(2,1)S(1)}, u32[]{:S(2)}, u32[]{:S(2)}) collective-permute-start(bf16[256,512]{1,0:T(8,128)(2,1)S(1)} %get-tuple-element.164.refs_1_), channel_id=1, source_target_pairs={{0,1},{1,0},{2,3},{3,2},{4,5},{5,4},{6,7},{7,6},{8,9},{9,8},{10,11... | collective-permute-start | bytes 786440 | tf_op jit(solution)/shard_map/ppermute | solution.py:83
  153.1 8.8 %collective-permute-start.41 = (bf16[256,1024]{1,0:T(8,128)(2,1)S(1)}, bf16[256,1024]{1,0:T(8,128)(2,1)S(1)}, u32[]{:S(2)}, u32[]{:S(2)}) collective-permute-start(bf16[256,1024]{1,0:T(8,128)(2,1)S(1)} %get-tuple-element.188), channel_id=1, source_target_pairs={{0,2},{2,0},{4,6},{6,4},{8,10},{10,8},{12,14},{14,12},{16,18},{18,... | collective-permute-start | bytes 1572872 | tf_op jit(solution)/shard_map/ppermute | solution.py:103
  153.2 8.7 %collective-permute-start.42 = (bf16[256,1024]{1,0:T(8,128)(2,1)S(1)}, bf16[256,1024]{1,0:T(8,128)(2,1)S(1)}, u32[]{:S(2)}, u32[]{:S(2)}) collective-permute-start(bf16[256,1024]{1,0:T(8,128)(2,1)S(1)} %get-tuple-element.189), channel_id=1, source_target_pairs={{0,2},{2,0},{4,6},{6,4},{8,10},{10,8},{12,14},{14,12},{16,18},{18,... | collective-permute-start | bytes 1572872 | tf_op jit(solution)/shard_map/ppermute | solution.py:103
  153.7 8.2 %collective-permute-start.39 = (bf16[256,256]{1,0:T(8,128)(2,1)S(1)}, bf16[256,256]{1,0:T(8,128)(2,1)S(1)}, u32[]{:S(2)}, u32[]{:S(2)}) collective-permute-start(bf16[256,256]{1,0:T(8,128)(2,1)S(1)} %get-tuple-element.182), channel_id=1, source_target_pairs={{0,8},{2,10},{4,12},{6,14},{8,0},{10,2},{12,4},{14,6},{16,24},{18,... | collective-permute-start | bytes 393224 | tf_op jit(solution)/shard_map/ppermute | solution.py:103
  155.9 6.0 %collective-permute-start.40 = (bf16[256,256]{1,0:T(8,128)(2,1)S(1)}, bf16[256,256]{1,0:T(8,128)(2,1)S(1)}, u32[]{:S(2)}, u32[]{:S(2)}) collective-permute-start(bf16[256,256]{1,0:T(8,128)(2,1)S(1)} %get-tuple-element.183), channel_id=1, source_target_pairs={{0,4},{2,6},{4,0},{6,2},{8,12},{10,14},{12,8},{14,10},{16,20},{18,... | collective-permute-start | bytes 393224 | tf_op jit(solution)/shard_map/ppermute | solution.py:103
  162.0 15.7 %copy-start.31 = (f32[1,512]{1,0:T(1,128)S(1)}, f32[1,512]{1,0:T(1,128)}, u32[]{:S(2)}) copy-start(f32[1,512]{1,0:T(1,128)} %copy-done.30) | copy-start | bytes 6148
  162.1 12.4 %collective-permute-start.45 = (bf16[128,1024]{1,0:T(8,128)(2,1)S(1)}, bf16[128,1024]{1,0:T(8,128)(2,1)S(1)}, u32[]{:S(2)}, u32[]{:S(2)}) collective-permute-start(bf16[128,1024]{1,0:T(8,128)(2,1)S(1)} %get-tuple-element.200), channel_id=1, source_target_pairs={{0,4},{2,6},{4,0},{6,2},{8,12},{10,14},{12,8},{14,10},{16,20},{18,... | collective-permute-start | bytes 786440 | tf_op jit(solution)/shard_map/ppermute | solution.py:103
  163.0 14.0 %collective-permute-start.46 = (bf16[128,1024]{1,0:T(8,128)(2,1)S(1)}, bf16[128,1024]{1,0:T(8,128)(2,1)S(1)}, u32[]{:S(2)}, u32[]{:S(2)}) collective-permute-start(bf16[128,1024]{1,0:T(8,128)(2,1)S(1)} %get-tuple-element.201), channel_id=1, source_target_pairs={{0,8},{2,10},{4,12},{6,14},{8,0},{10,2},{12,4},{14,6},{16,24},{18,... | collective-permute-start | bytes 786440 | tf_op jit(solution)/shard_map/ppermute | solution.py:103
  163.6 14.2 %collective-permute-start.38 = (bf16[128,512]{1,0:T(8,128)(2,1)S(1)}, bf16[128,512]{1,0:T(8,128)(2,1)S(1)}, u32[]{:S(2)}, u32[]{:S(2)}) collective-permute-start(bf16[128,512]{1,0:T(8,128)(2,1)S(1)} %get-tuple-element.177), channel_id=1, source_target_pairs={{0,1},{1,0},{2,3},{3,2},{4,5},{5,4},{6,7},{7,6},{8,9},{9,8},{10,11... | collective-permute-start | bytes 393224 | tf_op jit(solution)/shard_map/ppermute | solution.py:83
  163.9 9.5 %collective-permute-start.43 = (bf16[128,256]{1,0:T(8,128)(2,1)S(1)}, bf16[128,256]{1,0:T(8,128)(2,1)S(1)}, u32[]{:S(2)}, u32[]{:S(2)}) collective-permute-start(bf16[128,256]{1,0:T(8,128)(2,1)S(1)} %get-tuple-element.198), channel_id=1, source_target_pairs={{0,16},{2,18},{4,20},{6,22},{8,24},{10,26},{12,28},{14,30},{16,0},... | collective-permute-start | bytes 196616 | tf_op jit(solution)/shard_map/ppermute | solution.py:103
  165.5 9.0 %collective-permute-start.44 = (bf16[128,256]{1,0:T(8,128)(2,1)S(1)}, bf16[128,256]{1,0:T(8,128)(2,1)S(1)}, u32[]{:S(2)}, u32[]{:S(2)}) collective-permute-start(bf16[128,256]{1,0:T(8,128)(2,1)S(1)} %get-tuple-element.199), channel_id=1, source_target_pairs={{0,16},{2,18},{4,20},{6,22},{8,24},{10,26},{12,28},{14,30},{16,0},... | collective-permute-start | bytes 196616 | tf_op jit(solution)/shard_map/ppermute | solution.py:103
  178.8 1.2 collective-permute-start.47
  180.0 4.2 %collective-permute-start.48 = (f32[24,512]{1,0:T(8,128)S(1)}, f32[24,512]{1,0:T(8,128)S(1)}, u32[]{:S(2)}, u32[]{:S(2)}) collective-permute-start(f32[24,512]{1,0:T(8,128)S(1)} %add.68), channel_id=1, source_target_pairs={{0,4},{2,6},{4,0},{6,2},{8,12},{10,14},{12,8},{14,10},{16,20},{18,... | collective-permute-start | bytes 147464 | tf_op jit(solution)/shard_map/ppermute | solution.py:103
  181.9 8.1 %collective-permute-start.53 = (bf16[64,1024]{1,0:T(8,128)(2,1)S(1)}, bf16[64,1024]{1,0:T(8,128)(2,1)S(1)}, u32[]{:S(2)}, u32[]{:S(2)}) collective-permute-start(bf16[64,1024]{1,0:T(8,128)(2,1)S(1)} %get-tuple-element.218), channel_id=1, source_target_pairs={{0,8},{2,10},{4,12},{6,14},{8,0},{10,2},{12,4},{14,6},{16,24},{18,... | collective-permute-start | bytes 393224 | tf_op jit(solution)/shard_map/ppermute | solution.py:103
  182.1 7.8 %collective-permute-start.54 = (bf16[64,1024]{1,0:T(8,128)(2,1)S(1)}, bf16[64,1024]{1,0:T(8,128)(2,1)S(1)}, u32[]{:S(2)}, u32[]{:S(2)}) collective-permute-start(bf16[64,1024]{1,0:T(8,128)(2,1)S(1)} %get-tuple-element.219), channel_id=1, source_target_pairs={{0,4},{2,6},{4,0},{6,2},{8,12},{10,14},{12,8},{14,10},{16,20},{18,... | collective-permute-start | bytes 393224 | tf_op jit(solution)/shard_map/ppermute | solution.py:103
  184.2 8.8 %collective-permute-start.51 = (f32[24,512]{1,0:T(8,128)S(1)}, f32[24,512]{1,0:T(8,128)S(1)}, u32[]{:S(2)}, u32[]{:S(2)}) collective-permute-start(f32[24,512]{1,0:T(8,128)S(1)} %add.69), channel_id=1, source_target_pairs={{0,24},{2,26},{4,28},{6,30},{8,16},{10,18},{12,20},{14,22},{16,8},... | collective-permute-start | bytes 147464 | tf_op jit(solution)/shard_map/ppermute | solution.py:103
  185.4 7.6 %collective-permute-start.50 = (f32[24,512]{1,0:T(8,128)S(1)}, f32[24,512]{1,0:T(8,128)S(1)}, u32[]{:S(2)}, u32[]{:S(2)}) collective-permute-start(f32[24,512]{1,0:T(8,128)S(1)} %add.69), channel_id=1, source_target_pairs={{0,16},{2,18},{4,20},{6,22},{8,24},{10,26},{12,28},{14,30},{16,0},... | collective-permute-start | bytes 147464 | tf_op jit(solution)/shard_map/ppermute | solution.py:103
  186.3 6.7 %collective-permute-start.49 = (f32[24,512]{1,0:T(8,128)S(1)}, f32[24,512]{1,0:T(8,128)S(1)}, u32[]{:S(2)}, u32[]{:S(2)}) collective-permute-start(f32[24,512]{1,0:T(8,128)S(1)} %add.69), channel_id=1, source_target_pairs={{0,8},{2,10},{4,12},{6,14},{8,0},{10,2},{12,4},{14,6},{16,24},{18,... | collective-permute-start | bytes 147464 | tf_op jit(solution)/shard_map/ppermute | solution.py:103
  190.0 7.5 %collective-permute-start.55 = (bf16[32,1024]{1,0:T(8,128)(2,1)S(1)}, bf16[32,1024]{1,0:T(8,128)(2,1)S(1)}, u32[]{:S(2)}, u32[]{:S(2)}) collective-permute-start(bf16[32,1024]{1,0:T(8,128)(2,1)S(1)} %get-tuple-element.224), channel_id=1, source_target_pairs={{0,16},{2,18},{4,20},{6,22},{8,24},{10,26},{12,28},{14,30},{16,0},... | collective-permute-start | bytes 196616 | tf_op jit(solution)/shard_map/ppermute | solution.py:103
  190.1 7.4 %collective-permute-start.56 = (bf16[32,1024]{1,0:T(8,128)(2,1)S(1)}, bf16[32,1024]{1,0:T(8,128)(2,1)S(1)}, u32[]{:S(2)}, u32[]{:S(2)}) collective-permute-start(bf16[32,1024]{1,0:T(8,128)(2,1)S(1)} %get-tuple-element.225), channel_id=1, source_target_pairs={{0,16},{2,18},{4,20},{6,22},{8,24},{10,26},{12,28},{14,30},{16,0},... | collective-permute-start | bytes 196616 | tf_op jit(solution)/shard_map/ppermute | solution.py:103
  193.1 3.8 %collective-permute-start.52 = (f32[5,512]{1,0:T(8,128)S(1)}, f32[5,512]{1,0:T(8,128)S(1)}, u32[]{:S(2)}, u32[]{:S(2)}) collective-permute-start(f32[5,512]{1,0:T(8,128)S(1)} %slice.44), channel_id=1, source_target_pairs={{0,1},{1,0},{2,3},{3,2},{4,5},{5,4},{6,7},{7,6},{8,9},{9,8},{10,11... | collective-permute-start | bytes 30728 | tf_op jit(solution)/shard_map/ppermute | solution.py:103
  (33 other events, 173.9 us)
Sparse Core Ops, SparseCore 0:
  38.2 52.6 all-gather.1
  118.5 61.2 reduce-scatter.1

commit v5 on v4

--- a/solution.py
+++ b/solution.py
@@ -103,13 +103,13 @@
     return lax.ppermute(value, axis, [(k, k ^ mask) for k in range(lax.axis_size(axis))])
 
 
-def sum_over(value, axis):
+def sum_over(value, axis, step=1, stop=None):
     size = lax.axis_size(axis)
     if size & (size - 1):
         return lax.psum(value, axis)
-    step = 1
-    while step < size:
-        if step >= 4 and step * 4 <= size:
+    stop = stop or size
+    while step < stop:
+        if step >= 4 and step * 4 <= stop:
             near, far, both = (shift(value, axis, step * times) for times in (1, 2, 3))
             value = (value + near) + (far + both)
             step *= 4
@@ -138,32 +138,36 @@
     return distances(order[::-1])
 
 
-def gather_send(pair, stage):
-    return tuple(shift(value, "dp", order[stage]) for value, order in zip(pair, GATHER_ORDERS))
-
-
-def gather_join(pair, arrived):
+def gather_send(values, stage):
+    return tuple(shift(value, "dp", order[stage]) for value, order in zip(values, GATHER_ORDERS))
+
+
+def gather_join(pair, arrived, joint=False):
+    sizes = [value.shape[0] for value in pair]
+
     def body(ins, outs, _):
         for group in range(2):
-            rows = ins[group].shape[0]
-            outs[group][:rows, :] = ins[group][...]
-            outs[group][rows:, :] = ins[2 + group][...]
-
-    results = tuple(((2 * value.shape[0], value.shape[1]), value.dtype) for value in pair)
+            rows = sizes[group]
+            target, start = (outs[0], 2 * rows * group) if joint else (outs[group], 0)
+            source, begin = (ins[2], rows * group) if len(arrived) == 1 else (ins[2 + group], 0)
+            target[start : start + rows, :] = ins[group][...]
+            target[start + rows : start + 2 * rows, :] = source[begin : begin + rows, :]
+
+    columns, kind = pair[0].shape[1], pair[0].dtype
+    if joint:
+        results = (((2 * sum(sizes), columns), kind),)
+    else:
+        results = tuple(((2 * rows, columns), kind) for rows in sizes)
     return tuple(on_chip(body, "gather_join", tuple(pair) + arrived, results, flops=1_000))
-
-
-def gather_last(pair):
-    return tuple((value, shift(value, "dp", 1)) for value in pair)
 
 
 def tie(values, *others):
     return lax.optimization_barrier((values, others))[0]
 
 
-def assemble(ref, target_ref, order, half, matrices, first_column):
+def assemble(ref, target_ref, group, half, matrices, first_column):
     device = lax.axis_index("dp")
-    blocks = distances(order)
+    blocks = distances(GATHER_ORDERS[group])
     count = len(blocks) // 2
     rows = target_ref.shape[0] // len(blocks)
     columns = ref.shape[1]
@@ -171,17 +175,18 @@
         owner = device ^ blocks[half * count + place]
         target = pl.ds(pl.multiple_of(owner * rows, rows), rows)
         for matrix in range(matrices):
-            start = (place * matrices + matrix) * rows
+            start = ((group * count + place) * matrices + matrix) * rows
             left = first_column + matrix * columns
             target_ref[target, left : left + columns] = ref[start : start + rows, :]
 
 
-def scatter_split(total_ref, keep_ref, send_ref, order, matrices):
+def scatter_split(total_ref, keep_ref, send_ref, group, matrices):
     device = lax.axis_index("dp")
-    blocks = halving(order)
+    blocks = halving(SCATTER_ORDERS[group])
     count = len(blocks) // 2
     rows = total_ref.shape[0] // len(blocks)
     columns = keep_ref.shape[1]
+    first = group * keep_ref.shape[0]
     for place, block in enumerate(blocks):
         source = pl.ds(pl.multiple_of((device ^ block) * rows, rows), rows)
         for matrix in range(matrices):
@@ -190,39 +195,42 @@
             if place < count:
                 keep_ref[start : start + rows, :] = piece
             else:
-                send_ref[start : start + rows, :] = piece.astype(BF16)
+                send_ref[first + start : first + start + rows, :] = piece.astype(BF16)
 
 
 def scatter_send(sends, stage):
     return tuple(shift(send, "dp", order[stage]) for send, order in zip(sends, SCATTER_ORDERS))
 
 
+def arrived_part(refs, group, rows):
+    if len(refs) == 1:
+        return refs[0][group * rows : (group + 1) * rows, :].astype(F32)
+    return refs[group][...].astype(F32)
+
+
 def scatter_add(keeps, arrived, stage, name):
-    groups = len(keeps)
+    rows, columns = keeps[0].shape
+    half = rows // 2
     last = stage == len(SCATTER_ORDERS[0]) - 1
-    results = []
-    for keep in keeps:
-        rows, columns = keep.shape
-        if last:
-            results.append(((rows, columns), F32))
-        else:
-            results.append(((rows // 2, columns), F32))
-            results.append(((rows // 2, columns), BF16))
-
-    def body(ins, outs, _):
-        for group in range(groups):
-            total = ins[group][...] + ins[groups + group][...].astype(F32)
+    joint = stage == len(SCATTER_ORDERS[0]) - 2
+    results = (((rows if last else half, columns), F32),) * 2
+    if not last:
+        results += (((rows, columns), BF16),) if joint else (((half, columns), BF16),) * 2
+
+    def body(ins, outs, _):
+        for group in range(2):
+            total = ins[group][...] + arrived_part(ins[2:], group, rows)
             if last:
                 outs[group][...] = total
+                continue
+            outs[group][...] = total[:half]
+            if joint:
+                outs[2][group * half : (group + 1) * half, :] = total[half:].astype(BF16)
             else:
-                half = total.shape[0] // 2
-                outs[2 * group][...] = total[:half]
-                outs[2 * group + 1][...] = total[half:].astype(BF16)
-
-    values = on_chip(body, name, tuple(keeps) + tuple(arrived), tuple(results), flops=1_000)
-    if last:
-        return values, ()
-    return values[0::2], values[1::2]
+                outs[2 + group][...] = total[half:].astype(BF16)
+
+    values = on_chip(body, name, tuple(keeps) + tuple(arrived), results, flops=1_000)
+    return values[:2], values[2:]
 
 
 def entries_of(residual, gain):
@@ -244,7 +252,7 @@
 def first_forward(tokens, gains, weights):
     rows, width = tokens.shape
     split = isinstance(weights, tuple)
-    pieces = weights[0] + weights[1] if split else (weights,)
+    pieces = weights if split else (weights,)
     hidden = pieces[0].shape[1] if split else weights.shape[1] // 2
 
     def body(ins, outs, _):
@@ -253,8 +261,7 @@
             weight_ref = outs[2]
             for group in range(2):
                 for half in range(2):
-                    piece = ins[2 + 2 * group + half]
-                    assemble(piece, weight_ref, GATHER_ORDERS[group], half, 1, group * hidden)
+                    assemble(ins[2 + half], weight_ref, group, half, 1, group * hidden)
         entries = entries_of(ins[0][...].astype(F32), ins[1][0:1, :])
         outs[0][...] = ff_forward_body(entries, weight_ref, outs[1])
 
@@ -263,6 +270,26 @@
         results += (((width, 2 * hidden), BF16),)
     values = on_chip(body, "first_forward", (tokens, gains) + pieces, results)
     return values if split else tuple(values) + (weights,)
+
+
+def second_forward(conv_kept, own, other, gains, weights):
+    rows, width = own.shape
+    hidden = weights.shape[1] // 2
+
+    def body(ins, outs, _):
+        kept_ref, part_ref = outs
+        after = ins[0][:, :width] + both_parts(ins[1], ins[2])
+        kept_ref[:, :width] = after
+        kept_ref[:, width:] = ff_forward_body(
+            entries_of(after, ins[3][3:4, :]), ins[4], part_ref
+        )
+
+    return on_chip(
+        body,
+        "second_forward",
+        (conv_kept, own, other, gains, weights),
+        (((rows, width + hidden), F32), ((rows, width), BF16)),
+    )
 
 
 def ff_back_body(gradient, pre, weight_ref, grads_ref):
@@ -278,19 +305,36 @@
     return right_transposed(grad_pre, weight_ref[:, :half])
 
 
-def second_weight_grads(rows_kept, width):
-    half = (rows_kept.shape[1] - 2 * width) // 2
-
-    def body(ins, outs, _):
-        rows_ref = ins[0]
-        outs[0][:, :half] = left_transposed(
-            rows_ref[:, width : 2 * width], rows_ref[:, 2 * width : 2 * width + half]
+def second_back(kept, own, other, cotangent, gains, weights):
+    rows, width = own.shape
+    hidden = weights.shape[1] // 2
+
+    def body(ins, outs, _):
+        kept_ref, own_ref, other_ref, cot_ref, gain_ref, weight_ref = ins
+        out_ref, grad_ref, grads_ref, part_ref, gain_grad_ref = outs
+        after = kept_ref[:, :width] + 0.5 * both_parts(own_ref, other_ref)
+        normed, factor = norm_parts(after)
+        gain = gain_ref[4:5, :]
+        out_ref[...] = own_half(normed * gain).astype(BF16)
+        gradient, gain_grad = norm_back(cot_ref[...].astype(F32), normed, factor, gain)
+        gain_grad_ref[...] = 0.5 * gain_grad
+        grad_ref[...] = gradient
+        part_ref[...] = ff_back_body(
+            gradient, kept_ref[:, width:], weight_ref, grads_ref
         ).astype(BF16)
-        outs[0][:, half:] = left_transposed(
-            rows_ref[:, :width], rows_ref[:, 2 * width + half :]
-        ).astype(BF16)
-
-    return on_chip(body, "second_weight_grads", (rows_kept,), (((width, 2 * half), BF16),))[0]
+
+    return on_chip(
+        body,
+        "second_back",
+        (kept, own, other, cotangent, gains, weights),
+        (
+            ((rows // 2, width), BF16),
+            ((rows, width), F32),
+            ((rows, width + 2 * hidden), BF16),
+            ((rows, width), BF16),
+            ((1, width), F32),
+        ),
+    )
 
 
 def ff_weight_grads(grads, residual, gains, row, name):
@@ -318,19 +362,18 @@
         grads_ref, x_ref, gain_ref = ins
         entries = entries_of(x_ref[:, :width].astype(F32), gain_ref[row : row + 1, :])
         scratch[0][...] = left_transposed(entries, grads_ref[:, width : width + half])
-        scatter_split(scratch[0], outs[0], outs[1], SCATTER_ORDERS[0], 1)
+        scatter_split(scratch[0], outs[0], outs[2], 0, 1)
         scratch[0][...] = left_transposed(grads_ref[:, :width], grads_ref[:, width + half :])
-        scatter_split(scratch[0], outs[2], outs[3], SCATTER_ORDERS[1], 1)
-
-    halves = (((width // 2, half), F32), ((width // 2, half), BF16))
+        scatter_split(scratch[0], outs[1], outs[2], 1, 1)
+
     values = on_chip(
         body,
         name,
         (grads, residual, gains),
-        halves + halves,
+        (((width // 2, half), F32),) * 2 + (((width, half), BF16),),
         scratch=(pltpu.VMEM((width, half), F32),),
     )
-    return values[0::2], values[1::2]
+    return values[:2], values[2:]
 
 
 def kept_residual(kept_ref, width):
@@ -471,26 +514,32 @@
     )
 
 
-def mixed_assemble(pairs, table, width):
-    columns = pairs[0][0].shape[1]
+def second_assemble(halves, width):
+    columns = halves[0].shape[1]
 
     def body(ins, outs, _):
         for group in range(2):
             for half in range(2):
-                assemble(
-                    ins[2 * group + half],
-                    outs[0],
-                    GATHER_ORDERS[group],
-                    half,
-                    4,
-                    4 * group * columns,
-                )
-        outs[1][...] = matmul(ins[4][...], outs[0][:, 3 * columns : 4 * columns]).astype(BF16)
+                assemble(ins[half], outs[0], group, half, 1, group * columns)
+
+    return on_chip(
+        body, "second_assemble", halves, (((width, 2 * columns), BF16),), flops=1_000
+    )[0]
+
+
+def mixed_assemble(halves, table, width):
+    columns = halves[0].shape[1]
+
+    def body(ins, outs, _):
+        for group in range(2):
+            for half in range(2):
+                assemble(ins[half], outs[0], group, half, 4, 4 * group * columns)
+        outs[1][...] = matmul(ins[2][...], outs[0][:, 3 * columns : 4 * columns]).astype(BF16)
 
     return on_chip(
         body,
         "mixed_assemble",
-        pairs[0] + pairs[1] + (table,),
+        halves + (table,),
         (((width, 8 * columns), BF16), ((table.shape[0], columns), BF16)),
     )
 
@@ -519,21 +568,71 @@
         whole(ins, scratch[0])
         for group in range(2):
             part = scratch[0].at[:, 4 * group * columns : 4 * (group + 1) * columns]
-            scatter_split(part, outs[2 * group], outs[2 * group + 1], SCATTER_ORDERS[group], 4)
+            scatter_split(part, outs[group], outs[2], group, 4)
 
     operands = (joined, table, table_grad, total, kept, gains, conv_grads)
     if not split:
         results = (((width, 8 * columns), F32),)
         return on_chip(body, "mixed_weight_grads", operands, results)[0]
-    halves = (((2 * width, columns), F32), ((2 * width, columns), BF16))
     values = on_chip(
         body,
         "mixed_weight_grads",
         operands,
-        halves + halves,
+        (((2 * width, columns), F32),) * 2 + (((4 * width, columns), BF16),),
         scratch=(pltpu.VMEM((width, 8 * columns), F32),),
     )
-    return values[0::2], values[1::2]
+    return values[:2], values[2:]
+
+
+def mixed_finish(keeps, arrived):
+    rows, columns = keeps[0].shape
+    one = rows // 4
+
+    def body(ins, outs, _):
+        first = ins[0][...] + arrived_part(ins[2:], 0, rows)
+        for matrix in range(4):
+            outs[0][matrix] = first[matrix * one : (matrix + 1) * one]
+        second = ins[1][...] + arrived_part(ins[2:], 1, rows)
+        outs[1][...] = second[:one]
+        outs[2][0] = second[one : 2 * one]
+        outs[2][1] = second[2 * one : 3 * one]
+        outs[3][...] = second[3 * one :]
+
+    return on_chip(
+        body,
+        "mixed_finish",
+        tuple(keeps) + tuple(arrived),
+        (
+            ((4, one, columns), F32),
+            ((one, columns), F32),
+            ((2, one, columns), F32),
+            ((one, columns), F32),
+        ),
+        flops=1_000,
+    )
+
+
+def unpack_small(parts, taps, columns):
+    upper = (taps + 1) // 2
+    width = parts[0].shape[1]
+
+    def body(ins, outs, scratch):
+        total = scratch[0]
+        total[...] = (ins[0][...] + ins[1][...]) + (ins[2][...] + ins[3][...])
+        outs[0][...] = total[:5, :]
+        outs[1][:upper, :] = total[9 : 9 + upper, :columns]
+        outs[1][upper:, :] = total[9 : 9 + taps - upper, columns:]
+        outs[2][0:1, :] = total[8:9, :columns]
+        outs[2][1:2, :] = total[8:9, columns:]
+
+    return on_chip(
+        body,
+        "unpack_small",
+        parts,
+        (((5, width), F32), ((taps, columns), F32), ((2, columns), F32)),
+        scratch=(pltpu.VMEM(parts[0].shape, F32),),
+        flops=1_000,
+    )
 
 
 PAD = 16
@@ -604,71 +703,35 @@
     )[0]
 
 
-def second_block(conv_kept, own, other, cotangent, gains, weights, mixed, sums, batch, count):
-    rows, width = own.shape
+def norm_backward(gradient, own, other, kept, gains, weights, conv_kept, sums, batch, count):
+    rows, width = gradient.shape
     columns = sums.shape[1]
-    half = weights.shape[1] // 4
-
-    def body(ins, outs, _):
-        conv_ref, own_ref, other_ref, cot_ref, gain_ref, weight_ref, mixed_ref = ins[:7]
-        sums_ref, batch_ref = ins[7:]
-        out_ref, grads_ref, rows_ref, grad_sums_ref, last_gain_ref, gain_grad_ref = outs
-        residual = conv_ref[:, :width] + both_parts(own_ref, other_ref)
-        normed, factor = norm_parts(residual)
-        entries = (normed * gain_ref[3:4, :]).astype(BF16)
-        rows_ref[:, width : 2 * width] = entries
-        inner, branch_sum = [], 0.0
-        for part in range(2):
-            left = 2 * part * half
-            pre = matmul(entries, weight_ref[:, left : left + half])
-            sigma = jax.nn.sigmoid(pre)
-            hidden = (pre * sigma).astype(BF16)
-            inner.append(swish_slope(pre, sigma))
-            if part == 0:
-                rows_ref[:, 2 * width + half :] = hidden
-            branch_sum += right_transposed(hidden, weight_ref[:, left + half : left + 2 * half])
-        after = residual + 0.5 * branch_sum
-        last_normed, last_factor = norm_parts(after)
-        last_gain = gain_ref[4:5, :]
-        out_ref[...] = own_half(last_normed * last_gain).astype(BF16)
-        gradient, last_grad = norm_back(
-            cot_ref[...].astype(F32), last_normed, last_factor, last_gain
-        )
-        last_gain_ref[...] = 0.5 * last_grad
-        branch = (0.5 * gradient).astype(BF16)
-        rows_ref[:, :width] = branch
-        entry_grad = 0.0
-        for part in range(2):
-            left = 2 * part * half
-            grad_hidden = matmul(branch, weight_ref[:, left + half : left + 2 * half])
-            grad_pre = (grad_hidden * inner[part]).astype(BF16)
-            if part == 0:
-                rows_ref[:, 2 * width : 2 * width + half] = grad_pre
-            entry_grad += right_transposed(grad_pre, weight_ref[:, left : left + half])
-        passed, gain_grad = norm_back(entry_grad, normed, factor, gain_ref[3:4, :])
+
+    def body(ins, outs, _):
+        grad_ref, own_ref, other_ref, x_ref, gain_ref, weight_ref, conv_ref, sums_ref, batch_ref = (
+            ins
+        )
+        grads_ref, grad_sums_ref, gain_grad_ref = outs
+        normed, factor = norm_parts(x_ref[:, :width])
+        passed, gain_grad = norm_back(
+            both_parts(own_ref, other_ref), normed, factor, gain_ref[3:4, :]
+        )
         gain_grad_ref[...] = 0.5 * gain_grad
-        total = gradient + passed
+        total = grad_ref[...] + passed
         grads_ref[:, :width] = total
         standard, _, shifted = batch_norm(conv_ref, sums_ref, batch_ref, count)
-        grad_shifted = matmul(total.astype(BF16), mixed_ref[:, 7 * columns :]) * swish_slope(
-            shifted, jax.nn.sigmoid(shifted)
-        )
+        grad_shifted = matmul(
+            total.astype(BF16), weight_ref[:, 7 * columns :]
+        ) * swish_slope(shifted, jax.nn.sigmoid(shifted))
         grads_ref[:, width:] = grad_shifted
         grad_sums_ref[0:1, :] = jnp.sum(grad_shifted, 0, keepdims=True)
         grad_sums_ref[1:2, :] = jnp.sum(grad_shifted * standard, 0, keepdims=True)
 
     return on_chip(
         body,
-        "second_block",
-        (conv_kept, own, other, cotangent, gains, weights, mixed, sums, batch),
-        (
-            ((rows // 2, width), BF16),
-            ((rows, width + columns), F32),
-            ((rows, 2 * width + 2 * half), BF16),
-            ((2, columns), F32),
-            ((1, width), F32),
-            ((1, width), F32),
-        ),
+        "norm_backward",
+        (gradient, own, other, kept, gains, weights, conv_kept, sums, batch),
+        (((rows, width + columns), F32), ((2, columns), F32), ((1, width), F32)),
     )
 
 
@@ -782,7 +845,7 @@
     rows, width = tokens.shape
     taps, columns = tap_grads.shape
     upper = (taps + 1) // 2
-    packed_rows = -(-(6 + upper) // 8) * 8
+    packed_rows = 8 + -(-(1 + upper) // 8) * 8
 
     def body(ins, outs, _):
         keep_ref, other_ref, x_ref, gain_ref = ins[:4]
@@ -797,10 +860,10 @@
         packed[0:1, :] = gain_grad
         for place in range(4):
             packed[place + 1 : place + 2, :] = ins[4 + place][...]
-        packed[5:6, :columns] = bias_ref[0:1, :]
-        packed[5:6, columns:] = bias_ref[1:2, :]
-        packed[6 : 6 + upper, :columns] = tap_ref[:upper, :]
-        packed[6 : 6 + taps - upper, columns:] = tap_ref[upper:, :]
+        packed[8:9, :columns] = bias_ref[0:1, :]
+        packed[8:9, columns:] = bias_ref[1:2, :]
+        packed[9 : 9 + upper, :columns] = tap_ref[:upper, :]
+        packed[9 : 9 + taps - upper, columns:] = tap_ref[upper:, :]
 
     return on_chip(
         body,
@@ -857,65 +920,113 @@
     tokens_all = both_halves(tokens)
     cotangent_all = both_halves(cotangent)
 
-    second_own = jnp.concatenate([second_in, second_out], 1)
-    second_pair = jnp.concatenate([second_own, swap(second_own)], 1)
     if split:
         batch_one = (first_in, first_out)
-        batch_two = (
-            attention_in.reshape(-1, columns),
-            jnp.concatenate([attention_out, gated_in.reshape(-1, columns), pointwise_out], 0),
-        )
-        batch_one = gather_join(batch_one, gather_send(batch_one, 0))
+        joint_two = jnp.concatenate(
+            [
+                attention_in.reshape(-1, columns),
+                attention_out,
+                gated_in.reshape(-1, columns),
+                pointwise_out,
+            ],
+            0,
+        )
+        batch_two = (joint_two[: joint_two.shape[0] // 2], joint_two[joint_two.shape[0] // 2 :])
+        batch_three = (second_in, second_out)
+        joint_three = jnp.concatenate(batch_three, 0)
+        arrived_one = gather_send(batch_one, 0)
+        batch_one = on_chip(
+            lambda ins, outs, _: (
+                outs[0].__setitem__(..., ins[0][...]),
+                outs[1].__setitem__(..., ins[1][...]),
+            ),
+            "first_copy",
+            batch_one,
+            tuple((value.shape, value.dtype) for value in batch_one),
+            flops=1_000,
+        )
+        arrived_one = tie(arrived_one, (batch_one, table))
+        arrived_two = gather_send((tie(joint_two, arrived_one),), 0)
+        batch_one = gather_join(tuple(batch_one), tuple(arrived_one))
         arrived_one = gather_send(batch_one, 1)
-        arrived_two = gather_send(tie(batch_two, batch_one), 0)
-        batch_one = gather_join(batch_one, arrived_one)
+        batch_one = gather_join(batch_one, tie(arrived_one, tokens_all))
         arrived_one = gather_send(batch_one, 2)
         batch_two = gather_join(batch_two, tie(arrived_two, batch_one))
         arrived_two = gather_send(batch_two, 1)
-        batch_one = gather_join(batch_one, tie(arrived_one, batch_two))
-        second_pair = tie(second_pair, batch_one)
-        batch_two = gather_join(batch_two, tie(arrived_two, batch_one))
-        arrived_two = gather_send(batch_two, 2)
-        batch_one = gather_last(batch_one)
+        batch_one = gather_join(
+            batch_one, tie(arrived_one, (batch_two, cotangent_all)), joint=True
+        )
+        arrived_three = gather_send((tie(joint_three, batch_one),), 0)
+        batch_one += (shift(batch_one[0], "dp", 1),)
     else:
         batch_one = gather([first_in, first_out])
         mixed_weights = gather(
             unstacked(attention_in) + [attention_out] + unstacked(gated_in) + [pointwise_out]
         )
         positions = position_forward(table, mixed_weights, columns)
-    second_weights = gather([second_pair])
+        second_weights = gather([second_in, second_out])
 
     pre1, part1, first_weights = first_forward(tokens_all, norm_gains, batch_one)
     other1 = swap(part1)
     if split:
-        batch_two = gather_last(gather_join(batch_two, tie(arrived_two, other1)))
+        batch_two = gather_join(batch_two, tie(arrived_two, part1))
+        arrived_two = gather_send(batch_two, 2)
+        batch_three = gather_join(batch_three, tie(arrived_three, batch_two))
+        arrived_three = gather_send(batch_three, 1)
+        batch_two = gather_join(batch_two, tie(arrived_two, (other1, batch_three)), joint=True)
+        batch_two += (shift(batch_two[0], "dp", 1),)
         mixed_weights, positions = mixed_assemble(batch_two, table, width)
     kept, part2 = attention_forward(
         tokens_all, part1, other1, norm_gains, mixed_weights, positions, head_biases, local_heads
     )
     other2 = swap(part2)
+    if split:
+        batch_three = gather_join(batch_three, tie(arrived_three, part2))
+        arrived_three = gather_send(batch_three, 2)
     conv_kept, sums = conv_forward(
         kept, part2, other2, norm_gains, mixed_weights, depth_kernel
     )
-    sums = tie(sum_over(sums, "dp"), second_weights)
+    if split:
+        batch_three = gather_join(batch_three, tie(arrived_three, sums), joint=True)
+        batch_three += (shift(batch_three[0], "dp", 1),)
+        second_weights = second_assemble(batch_three, width)
+    sums = sum_over(sums, "dp")
     part3 = norm_forward(conv_kept, sums, batch, mixed_weights, token_count)
     other3 = swap(part3)
-    block_out, norm_grads, second_rows, grad_sums, gain5, gain4 = second_block(
+    other3 = tie(other3, second_weights)
+    second_kept, part4 = second_forward(conv_kept, part3, other3, norm_gains, second_weights)
+    other4 = swap(part4)
+    block_out, grad4, second_rows, part5, gain5 = second_back(
+        second_kept, part4, other4, cotangent_all, norm_gains, second_weights
+    )
+    other5 = swap(part5)
+    second_name = "second_weight_grads"
+    if split:
+        keeps, sends = ff_weight_split(second_rows, second_kept, norm_gains, 3, second_name)
+        second_keeps, sends = scatter_add(keeps, scatter_send(sends, 0), 0, "second_sum")
+        second_arrived = scatter_send(sends, 1)
+        other5 = tie(other5, second_keeps)
+    else:
+        second_grads = reduce_plain(
+            ff_weight_grads(second_rows, second_kept, norm_gains, 3, second_name)
+        )
+        second_reduced = (second_grads[:, :hidden], second_grads[:, hidden:])
+    norm_grads, grad_sums, gain4 = norm_backward(
+        grad4,
+        part5,
+        other5,
+        second_kept,
+        norm_gains,
+        mixed_weights,
         conv_kept,
-        part3,
-        other3,
-        cotangent_all,
-        norm_gains,
-        second_weights,
-        mixed_weights,
         sums,
         batch,
         token_count,
     )
-    second_grads = second_weight_grads(second_rows, width)
-    reduced_second = reduce_plain(second_grads)
     grad_sums = sum_over(grad_sums, "dp")
-    grad_sums = tie(grad_sums, second_grads)
+    if split:
+        second_keeps, sends = scatter_add(second_keeps, second_arrived, 1, "second_sum")
+        grad_sums = tie(grad_sums, second_keeps)
     grad_conv, joined3, part6 = conv_backward(
         norm_grads, grad_sums, conv_kept, sums, batch, mixed_weights, depth_kernel, token_count
     )
@@ -932,6 +1043,12 @@
         token_count,
     )
     other6 = tie(other6, conv_grads)
+    if split:
+        second_arrived = scatter_send(tie(sends, part6), 2)
+        second_arrived = tie(second_arrived, conv_grads)
+        second_keeps, sends = scatter_add(second_keeps, second_arrived, 2, "second_sum")
+        second_arrived = scatter_send(sends, 3)
+        other6 = tie(other6, second_keeps)
     grad2, joined2, table_grad, part7, gain3, bias_grads = attention_back(
         norm_grads,
         part6,
@@ -951,7 +1068,7 @@
         keeps, sends = mixed_grads
         mixed_keeps, sends = scatter_add(keeps, scatter_send(sends, 0), 0, "mixed_sum")
         mixed_arrived = scatter_send(sends, 1)
-        other7 = tie(other7, mixed_arrived)
+        other7 = tie(other7, mixed_keeps)
     first_rows, keep8, send8, gain2 = first_back(
         grad2, part7, other7, kept, pre1, norm_gains, first_weights
     )
@@ -964,30 +1081,31 @@
             tie(first_rows, mixed_keeps), tokens_all, norm_gains, 0, "first_weight_grads"
         )
         first_arrived = scatter_send(sends, 0)
-        first_arrived = tie(first_arrived, mixed_arrived)
         first_keeps, sends = scatter_add(keeps, first_arrived, 0, "first_sum")
         first_arrived = scatter_send(sends, 1)
+        second_reduced, _ = scatter_add(
+            second_keeps, tie(second_arrived, first_keeps), 3, "second_sum"
+        )
         mixed_keeps, sends = scatter_add(
             mixed_keeps, tie(mixed_arrived, first_keeps), 2, "mixed_sum"
         )
         mixed_arrived = scatter_send(sends, 3)
-        first_arrived = tie(first_arrived, mixed_arrived)
+        other8 = tie(other8, mixed_keeps)
+        grad_start, packed = input_back(keep8, other8, tokens, norm_gains, *small)
+        first_arrived = tie(first_arrived, packed)
         first_keeps, sends = scatter_add(first_keeps, first_arrived, 1, "first_sum")
         first_arrived = scatter_send(sends, 2)
-        (mixed_a, mixed_b), _ = scatter_add(
-            mixed_keeps, tie(mixed_arrived, first_keeps), 3, "mixed_sum"
-        )
-        other8 = tie(other8, mixed_a)
-        grad_start, packed = input_back(keep8, other8, tokens, norm_gains, *small)
-        first_arrived = tie(first_arrived, packed)
+        packed = jnp.concatenate([sum_over(packed[:8], "tensor"), packed[8:]], 0)
+        packed = sum_over(tie(packed, first_keeps), "dp", 1, 4)
+        reduced_attention, reduced_mixing, reduced_gated, reduced_pointwise = mixed_finish(
+            mixed_keeps, tie(mixed_arrived, first_keeps)
+        )
+        first_arrived = tie(first_arrived, (reduced_mixing, packed))
         first_keeps, sends = scatter_add(first_keeps, first_arrived, 2, "first_sum")
         first_arrived = scatter_send(sends, 3)
+        packed = tie(packed, first_keeps)
+        parts = (packed,) + tuple(shift(packed, "dp", mask) for mask in (4, 8, 12))
         (reduced_in, reduced_out), _ = scatter_add(first_keeps, first_arrived, 3, "first_sum")
-        rows = mixed_a.shape[0] // 4
-        reduced_attention = mixed_a.reshape(4, rows, columns)
-        reduced_mixing = mixed_b[:rows]
-        reduced_gated = mixed_b[rows : 3 * rows].reshape(2, rows, columns)
-        reduced_pointwise = mixed_b[3 * rows :]
     else:
         grad_start, packed = input_back(keep8, other8, tokens, norm_gains, *small)
         first_grads = reduce_plain(
@@ -999,14 +1117,10 @@
         reduced_mixing = mixed[:, 4 * columns : 5 * columns]
         reduced_gated = stacked_columns(mixed[:, 5 * columns : 7 * columns], 2)
         reduced_pointwise = mixed[:, 7 * columns :]
-    packed = sum_over(packed, "dp")
-    gain_total = sum_over(packed[:5], "tensor")
-    bias_total = packed[5].reshape(bias_grads.shape)
-    taps = tap_grads.shape[0]
-    upper = (taps + 1) // 2
-    tap_total = jnp.concatenate(
-        [packed[6 : 6 + upper, :columns], packed[6 : 6 + taps - upper, columns:]], 0
-    )
+        packed = jnp.concatenate([sum_over(packed[:8], "tensor"), packed[8:]], 0)
+        packed = sum_over(packed, "dp")
+        parts = (packed,) + (jnp.zeros_like(packed),) * 3
+    gain_total, tap_total, bias_total = unpack_small(parts, depth_kernel.shape[0], columns)
     return (
         block_out,
         grad_start,
@@ -1021,8 +1135,7 @@
         tap_total,
         grad_sums[1],
         grad_sums[0],
-        reduced_second[:, :hidden],
-        reduced_second[:, hidden:],
+        *second_reduced,
     )
 
 

time: 207 us -> 191 us (0.923)
  between operations: 14.6 us -> 1.21 us
  local copies, waits for them, and re-layouts: 15.1 us -> 2.33 us
  starting transfers between devices: 56.3 us -> 67.2 us
  other arithmetic: 11.7 us -> 2.63 us
  waiting for transfers between devices: 83 us -> 88.7 us
  Pallas kernels: 26 us -> 28.6 us
    unnamed x76 -> x30, local copies, waits for them, and re-layouts: 11 us -> 1.75 us
    ppermute x9 -> x10, starting transfers between devices: 6.52 us -> 12.5 us  [swap(): return lax.ppermute(value, 'tensor', [(0, 1), (1, 0)])]
    ppermute x48 -> x53, starting transfers between devices: 49.7 us -> 54.7 us  [shift(): lax.ppermute(value, axis, [(k, k ^ mask) for k in range(lax.axis_size(axi...]
    concatenate x4, other arithmetic: 3.87 us -> 0.03 us  [the longest x2 0.02 us: body(): jnp.concatenate([attention_in.reshape(-1, columns), attention_out, gated_...]
    ppermute x48 -> x53, waiting for transfers between devices: 62.7 us -> 66.1 us  [shift(): lax.ppermute(value, axis, [(k, k ^ mask) for k in range(lax.axis_size(axi...]
    slice x7 -> x2, local copies, waits for them, and re-layouts: 2.88 us -> 0.01 us  [body(): packed = jnp.concatenate([sum_over(packed[:8], 'tensor'), packed[8:]], 0)]
    pallas_call x28 -> x40, Pallas kernels: 26 us -> 28.6 us  [on_chip(): pl.pallas_call(kernel, out_shape=[jax.ShapeDtypeStruct(shape, kind) for s...]
    ppermute x9 -> x10, waiting for transfers between devices: 20.2 us -> 22.5 us  [swap(): return lax.ppermute(value, 'tensor', [(0, 1), (1, 0)])]
  transfers between devices with their start and end apart: 59 -> 63, of which waited for: 33 -> 39; matrix products, arithmetic and copies ran while one was open for 7% -> 2% of each run, Pallas kernels for 11% -> 8%
where the time goes in v5:
time: 191 us
  waiting for transfers between devices  88.7 us (46%)
  starting transfers between devices  67.2 us (35%)
  Pallas kernels  28.6 us (15%)
  other arithmetic  2.63 us (1%)
  local copies, waits for them, and re-layouts  2.33 us (1%)
    ppermute x53, waiting for transfers between devices, shift(): lax.ppermute(value, axis, [(k, k ^ mask) for k in range(lax.axis_size(axi...  66.1 us
    ppermute x53, starting transfers between devices, shift(): lax.ppermute(value, axis, [(k, k ^ mask) for k in range(lax.axis_size(axi...  54.7 us
    pallas_call x40, Pallas kernels, on_chip(): pl.pallas_call(kernel, out_shape=[jax.ShapeDtypeStruct(shape, kind) for s...  28.6 us
    ppermute x10, waiting for transfers between devices, swap(): return lax.ppermute(value, 'tensor', [(0, 1), (1, 0)])  22.5 us
    ppermute x10, starting transfers between devices, swap(): return lax.ppermute(value, 'tensor', [(0, 1), (1, 0)])  12.5 us
  transfers between devices with their start and end apart: 63, of which 39 were waited for; matrix products, arithmetic and copies ran while one was open for 2% of the time, Pallas kernels for 8%

profile of v5, /device:TPU:0, one launch (start us, length us, event | category | flops | bytes accessed | tf_op | source)
XLA Modules:
  0.0 190.6 jit_solution(6418247230211070764)
XLA Ops:
  0.7 4.1 %collective-permute-start.1 = (bf16[32,1024]{1,0:T(8,128)(2,1)}, bf16[32,1024]{1,0:T(8,128)(2,1)S(1)}, u32[]{:S(2)}, u32[]{:S(2)}) collective-permute-start(bf16[32,1024]{1,0:T(8,128)(2,1)} %refs_0_.2), channel_id=1, source_target_pairs={{0,16},{2,18},{4,20},{6,22},{8,24},{10,26},{12,28},{14,30},{16,0},... | collective-permute-start | bytes 196616 | tf_op jit(solution)/shard_map/ppermute | solution.py:103
  4.8 1.8 collective-permute-start
  6.9 2.2 %multiply_sine_fusion = (bf16[512,256]{1,0:T(8,128)(2,1)S(1)}, bf16[512,256]{1,0:T(8,128)(2,1)S(1)}) fusion(f32[256]{0:T(256)S(1)} %multiply_exponential_fusion, f32[512]{0:T(512)S(1)} %iota_add_fusion), kind=kLoop, calls=%fused_computation.3 | loop fusion | flops 393216 | bytes 527360 | tf_op jit(solution)/shard_map/sin | solution.py:57
  11.5 1.6 collective-permute-start.3
  13.0 1.5 collective-permute-start.4
  14.6 1.9 collective-permute-done.3.refs_2_
  16.5 1.5 collective-permute-done.4.refs_3_
  18.1 1.6 collective-permute-start.5
  20.4 2.4 %collective-permute-start.7 = (bf16[256,256]{1,0:T(8,128)(2,1)S(1)}, bf16[256,256]{1,0:T(8,128)(2,1)S(1)}, u32[]{:S(2)}, u32[]{:S(2)}) collective-permute-start(bf16[256,256]{1,0:T(8,128)(2,1)S(1)} %pad_maximum_fusion.2), channel_id=1, source_target_pairs={{0,16},{2,18},{4,20},{6,22},{8,24},{10,26},{12,28},{14,30},{16,0},... | collective-permute-start | bytes 393224 | tf_op jit(solution)/shard_map/ppermute | solution.py:103
  22.8 4.5 %collective-permute-done.7.refs_2_ = bf16[256,256]{1,0:T(8,128)(2,1)S(1)} collective-permute-done((bf16[256,256]{1,0:T(8,128)(2,1)S(1)}, bf16[256,256]{1,0:T(8,128)(2,1)S(1)}, u32[]{:S(2)}, u32[]{:S(2)}) %collective-permute-start.7) | collective-permute-done | bytes 131104 | tf_op jit(solution)/shard_map/ppermute | solution.py:103
  28.6 3.3 %collective-permute-start.11 = (bf16[256,256]{1,0:T(8,128)(2,1)S(1)}, bf16[256,256]{1,0:T(8,128)(2,1)S(1)}, u32[]{:S(2)}, u32[]{:S(2)}) collective-permute-start(bf16[256,256]{1,0:T(8,128)(2,1)S(1)} %get-tuple-element.170.refs_0_), channel_id=1, source_target_pairs={{0,8},{2,10},{4,12},{6,14},{8,0},{10,2},{12,4},{14,6},{16,24},{18,... | collective-permute-start | bytes 393224 | tf_op jit(solution)/shard_map/ppermute | solution.py:103
  33.5 2.5 %collective-permute-done.11.refs_2_ = bf16[256,256]{1,0:T(8,128)(2,1)S(1)} collective-permute-done((bf16[256,256]{1,0:T(8,128)(2,1)S(1)}, bf16[256,256]{1,0:T(8,128)(2,1)S(1)}, u32[]{:S(2)}, u32[]{:S(2)}) %collective-permute-start.11) | collective-permute-done | bytes 131104 | tf_op jit(solution)/shard_map/ppermute | solution.py:103
  36.0 1.5 collective-permute-done.12.refs_3_
  38.4 1.5 collective-permute-start.10
  40.8 6.0 %collective-permute-done.15.refs_2_ = bf16[64,1024]{1,0:T(8,128)(2,1)S(1)} collective-permute-done((bf16[64,1024]{1,0:T(8,128)(2,1)S(1)}, bf16[64,1024]{1,0:T(8,128)(2,1)S(1)}, u32[]{:S(2)}, u32[]{:S(2)}) %collective-permute-start.15) | collective-permute-done | bytes 131104 | tf_op jit(solution)/shard_map/ppermute | solution.py:103
  46.8 1.4 collective-permute-done.14.refs_3_
  49.0 1.5 collective-permute-start.25
  51.5 3.3 %attention_forward.1 = (bf16[256,3328]{1,0:T(8,128)(2,1)S(1)}, bf16[256,512]{1,0:T(8,128)(2,1)S(1)}) custom-call(bf16[256,512]{1,0:T(8,128)(2,1)S(1)} %pad_maximum_fusion.refs_0_.refs_1_, bf16[256,512]{1,0:T(8,128)(2,1)S(1)} %get-tuple-element.174.refs_1_, bf16[256,512]{1,0:T(8,128)(2,1)S(1)} %collective-permute-done.10.refs_2_, f32[5,512]{1,0:T(8,128)S(1)} %copy-done, ...), custom_call_target="tpu_custom_call" | custom-call | flops 300000000 | bytes 5124096 | tf_op jit(solution)/shard_map/attention_forward/pallas_call | solution.py:70
  54.8 1.6 collective-permute-start.17
  56.4 1.6 collective-permute-start.26
  58.6 4.6 %collective-permute-done.17.refs_2_ = bf16[256,512]{1,0:T(8,128)(2,1)S(1)} collective-permute-done((bf16[256,512]{1,0:T(8,128)(2,1)S(1)}, bf16[256,512]{1,0:T(8,128)(2,1)S(1)}, u32[]{:S(2)}, u32[]{:S(2)}) %collective-permute-start.17) | collective-permute-done | bytes 262176 | tf_op jit(solution)/shard_map/ppermute | solution.py:83
  63.2 1.9 %conv_forward.1 = (f32[256,1280]{1,0:T(8,128)S(1)}, f32[2,256]{1,0:T(2,128)S(1)}) custom-call(bf16[256,3328]{1,0:T(8,128)(2,1)S(1)} %get-tuple-element.187.refs_0_.refs_7_.refs_4_.refs_3_, bf16[256,512]{1,0:T(8,128)(2,1)S(1)} %get-tuple-element.188.refs_1_, bf16[256,512]{1,0:T(8,128)(2,1)S(1)} %collective-permute-done.17.refs_2_, f32[5,512]{1,0:T(8,128)S(1)} %copy-done, ...), custom_call_target="tpu_custom_call" | custom-call | flops 300000000 | bytes 5680128 | tf_op jit(solution)/shard_map/conv_forward/pallas_call | solution.py:70
  66.4 2.1 %collective-permute-done.18 = f32[2,256]{1,0:T(2,128)S(1)} collective-permute-done((f32[2,256]{1,0:T(2,128)S(1)}, f32[2,256]{1,0:T(2,128)S(1)}, u32[]{:S(2)}, u32[]{:S(2)}) %collective-permute-start.18) | collective-permute-done | bytes 2080 | tf_op jit(solution)/shard_map/ppermute | solution.py:103
  69.5 2.7 %collective-permute-done.19 = f32[2,256]{1,0:T(2,128)S(1)} collective-permute-done((f32[2,256]{1,0:T(2,128)S(1)}, f32[2,256]{1,0:T(2,128)S(1)}, u32[]{:S(2)}, u32[]{:S(2)}) %collective-permute-start.19) | collective-permute-done | bytes 2080 | tf_op jit(solution)/shard_map/ppermute | solution.py:103
  72.8 1.2 collective-permute-start.21
  74.0 2.5 %collective-permute-start.22 = (f32[2,256]{1,0:T(2,128)S(1)}, f32[2,256]{1,0:T(2,128)S(1)}, u32[]{:S(2)}, u32[]{:S(2)}) collective-permute-start(f32[2,256]{1,0:T(2,128)S(1)} %add.48), channel_id=1, source_target_pairs={{0,24},{2,26},{4,28},{6,30},{8,16},{10,18},{12,20},{14,22},{16,8},... | collective-permute-start | bytes 6152 | tf_op jit(solution)/shard_map/ppermute | solution.py:103
  77.3 2.1 %collective-permute-done.22 = f32[2,256]{1,0:T(2,128)S(1)} collective-permute-done((f32[2,256]{1,0:T(2,128)S(1)}, f32[2,256]{1,0:T(2,128)S(1)}, u32[]{:S(2)}, u32[]{:S(2)}) %collective-permute-start.22) | collective-permute-done | bytes 2080 | tf_op jit(solution)/shard_map/ppermute | solution.py:103
  79.7 1.4 collective-permute-start.23
  81.3 5.0 %collective-permute-done.23.refs_2_ = bf16[256,512]{1,0:T(8,128)(2,1)S(1)} collective-permute-done((bf16[256,512]{1,0:T(8,128)(2,1)S(1)}, bf16[256,512]{1,0:T(8,128)(2,1)S(1)}, u32[]{:S(2)}, u32[]{:S(2)}) %collective-permute-start.23) | collective-permute-done | bytes 262176 | tf_op jit(solution)/shard_map/ppermute | solution.py:83
  87.3 1.4 collective-permute-start.29
  88.7 5.0 %collective-permute-done.29.refs_2_ = bf16[256,512]{1,0:T(8,128)(2,1)S(1)} collective-permute-done((bf16[256,512]{1,0:T(8,128)(2,1)S(1)}, bf16[256,512]{1,0:T(8,128)(2,1)S(1)}, u32[]{:S(2)}, u32[]{:S(2)}) %collective-permute-start.29) | collective-permute-done | bytes 262176 | tf_op jit(solution)/shard_map/ppermute | solution.py:83
  93.7 1.8 second_back.1
  95.5 1.3 second_weight_grads.1
  96.8 1.4 collective-permute-start.30
  98.2 1.2 collective-permute-done.31.refs_2_
  100.9 4.6 %collective-permute-done.30.refs_2_ = bf16[256,512]{1,0:T(8,128)(2,1)S(1)} collective-permute-done((bf16[256,512]{1,0:T(8,128)(2,1)S(1)}, bf16[256,512]{1,0:T(8,128)(2,1)S(1)}, u32[]{:S(2)}, u32[]{:S(2)}) %collective-permute-start.30) | collective-permute-done | bytes 262176 | tf_op jit(solution)/shard_map/ppermute | solution.py:83
  108.3 2.6 %collective-permute-done.33 = f32[2,256]{1,0:T(2,128)S(1)} collective-permute-done((f32[2,256]{1,0:T(2,128)S(1)}, f32[2,256]{1,0:T(2,128)S(1)}, u32[]{:S(2)}, u32[]{:S(2)}) %collective-permute-start.33) | collective-permute-done | bytes 2080 | tf_op jit(solution)/shard_map/ppermute | solution.py:103
  111.0 3.1 %collective-permute-start.35 = (f32[2,256]{1,0:T(2,128)S(1)}, f32[2,256]{1,0:T(2,128)S(1)}, u32[]{:S(2)}, u32[]{:S(2)}) collective-permute-start(f32[2,256]{1,0:T(2,128)S(1)} %add.53), channel_id=1, source_target_pairs={{0,16},{2,18},{4,20},{6,22},{8,24},{10,26},{12,28},{14,30},{16,0},... | collective-permute-start | bytes 6152 | tf_op jit(solution)/shard_map/ppermute | solution.py:103
  114.1 1.3 collective-permute-start.36
  115.6 3.8 %collective-permute-done.36 = f32[2,256]{1,0:T(2,128)S(1)} collective-permute-done((f32[2,256]{1,0:T(2,128)S(1)}, f32[2,256]{1,0:T(2,128)S(1)}, u32[]{:S(2)}, u32[]{:S(2)}) %collective-permute-start.36) | collective-permute-done | bytes 2080 | tf_op jit(solution)/shard_map/ppermute | solution.py:103
  119.6 1.6 conv_backward.1
  122.3 1.5 collective-permute-start.41
  123.8 2.1 %conv_weight_grads.1 = (bf16[512,768]{1,0:T(8,128)(2,1)S(1)}, f32[31,256]{1,0:T(8,128)S(1)}) custom-call(f32[256,768]{1,0:T(8,128)S(1)} %get-tuple-element.210.refs_0_, f32[256,256]{1,0:T(8,128)S(1)} %get-tuple-element.218.refs_1_, bf16[256,512]{1,0:T(8,128)(2,1)S(1)} %get-tuple-element.219.refs_2_, ...), custom_call_target="tpu_custom_call" | custom-call | flops 300000000 | bytes 3453952 | tf_op jit(solution)/shard_map/conv_weight_grads/pallas_call | solution.py:70
  125.9 1.3 collective-permute-done.40.refs_2_
  127.7 3.6 %attention_back.1 = (f32[256,512]{1,0:T(8,128)S(1)}, bf16[256,768]{1,0:T(8,128)(2,1)S(1)}, bf16[512,256]{1,0:T(8,128)(2,1)S(1)}, bf16[256,512]{1,0:T(8,128)(2,1)...) custom-call(f32[256,768]{1,0:T(8,128)S(1)} %get-tuple-element.210.refs_0_, ...), custom_call_target="tpu_custom_call" | custom-call | flops 300000000 | bytes 8140800 | tf_op jit(solution)/shard_map/attention_back/pallas_call | solution.py:70
  133.6 1.6 collective-permute-done.43.refs_2_
  135.4 1.2 collective-permute-start.45
  136.6 2.0 %collective-permute-start.46 = (bf16[512,256]{1,0:T(8,128)(2,1)S(1)}, bf16[512,256]{1,0:T(8,128)(2,1)S(1)}, u32[]{:S(2)}, u32[]{:S(2)}) collective-permute-start(bf16[512,256]{1,0:T(8,128)(2,1)S(1)} %get-tuple-element.246), channel_id=1, source_target_pairs={{0,8},{2,10},{4,12},{6,14},{8,0},{10,2},{12,4},{14,6},{16,24},{18,... | collective-permute-start | bytes 786440 | tf_op jit(solution)/shard_map/ppermute | solution.py:103
  138.6 2.7 %collective-permute-done.42.refs_2_ = bf16[256,512]{1,0:T(8,128)(2,1)S(1)} collective-permute-done((bf16[256,512]{1,0:T(8,128)(2,1)S(1)}, bf16[256,512]{1,0:T(8,128)(2,1)S(1)}, u32[]{:S(2)}, u32[]{:S(2)}) %collective-permute-start.42) | collective-permute-done | bytes 262176 | tf_op jit(solution)/shard_map/ppermute | solution.py:83
  141.3 1.3 first_back.1
  142.6 1.3 collective-permute-done.45.refs_2_
  145.0 1.5 first_weight_grads.1
  146.6 1.8 collective-permute-start.47
  150.2 2.3 %collective-permute-done.47.refs_2_ = bf16[256,256]{1,0:T(8,128)(2,1)S(1)} collective-permute-done((bf16[256,256]{1,0:T(8,128)(2,1)S(1)}, bf16[256,256]{1,0:T(8,128)(2,1)S(1)}, u32[]{:S(2)}, u32[]{:S(2)}) %collective-permute-start.47) | collective-permute-done | bytes 131104 | tf_op jit(solution)/shard_map/ppermute | solution.py:103
  152.5 1.5 collective-permute-done.48.refs_3_
  159.2 4.1 %collective-permute-done.51.refs_2_ = bf16[128,1024]{1,0:T(8,128)(2,1)S(1)} collective-permute-done((bf16[128,1024]{1,0:T(8,128)(2,1)S(1)}, bf16[128,1024]{1,0:T(8,128)(2,1)S(1)}, u32[]{:S(2)}, u32[]{:S(2)}) %collective-permute-start.51) | collective-permute-done | bytes 262176 | tf_op jit(solution)/shard_map/ppermute | solution.py:103
  163.3 3.5 %collective-permute-done.52.refs_3_ = bf16[128,1024]{1,0:T(8,128)(2,1)S(1)} collective-permute-done((bf16[128,1024]{1,0:T(8,128)(2,1)S(1)}, bf16[128,1024]{1,0:T(8,128)(2,1)S(1)}, u32[]{:S(2)}, u32[]{:S(2)}) %collective-permute-start.52) | collective-permute-done | bytes 262176 | tf_op jit(solution)/shard_map/ppermute | solution.py:103
  167.0 1.2 collective-permute-start.56
  169.3 1.7 collective-permute-start.62
  171.7 2.5 %collective-permute-done.54 = f32[32,512]{1,0:T(8,128)S(1)} collective-permute-done((f32[32,512]{1,0:T(8,128)S(1)}, f32[32,512]{1,0:T(8,128)S(1)}, u32[]{:S(2)}, u32[]{:S(2)}) %collective-permute-start.54) | collective-permute-done | bytes 65568 | tf_op jit(solution)/shard_map/ppermute | solution.py:103
  174.3 1.8 collective-permute-start.58
  176.3 2.5 %collective-permute-start.60 = (f32[32,512]{1,0:T(8,128)S(1)}, f32[32,512]{1,0:T(8,128)S(1)}, u32[]{:S(2)}, u32[]{:S(2)}) collective-permute-start(f32[32,512]{1,0:T(8,128)S(1)} %add.59.refs_0_), channel_id=1, source_target_pairs={{0,24},{2,26},{4,28},{6,30},{8,16},{10,18},{12,20},{14,22},{16,8},... | collective-permute-start | bytes 196616 | tf_op jit(solution)/shard_map/ppermute | solution.py:103
  181.1 5.4 %collective-permute-done.59.refs_2_ = f32[32,512]{1,0:T(8,128)S(1)} collective-permute-done((f32[32,512]{1,0:T(8,128)S(1)}, f32[32,512]{1,0:T(8,128)S(1)}, u32[]{:S(2)}, u32[]{:S(2)}) %collective-permute-start.59) | collective-permute-done | bytes 65568 | tf_op jit(solution)/shard_map/ppermute | solution.py:103
  187.1 2.8 %collective-permute-done.61.refs_2_ = bf16[64,1024]{1,0:T(8,128)(2,1)S(1)} collective-permute-done((bf16[64,1024]{1,0:T(8,128)(2,1)S(1)}, bf16[64,1024]{1,0:T(8,128)(2,1)S(1)}, u32[]{:S(2)}, u32[]{:S(2)}) %collective-permute-start.61) | collective-permute-done | bytes 131104 | tf_op jit(solution)/shard_map/ppermute | solution.py:103
  (157 shorter events, 38.2 us)
Async XLA Ops:
  0.7 10.4 %collective-permute-start.1 = (bf16[32,1024]{1,0:T(8,128)(2,1)}, bf16[32,1024]{1,0:T(8,128)(2,1)S(1)}, u32[]{:S(2)}, u32[]{:S(2)}) collective-permute-start(bf16[32,1024]{1,0:T(8,128)(2,1)} %refs_0_.2), channel_id=1, source_target_pairs={{0,16},{2,18},{4,20},{6,22},{8,24},{10,26},{12,28},{14,30},{16,0},... | collective-permute-start | bytes 196616 | tf_op jit(solution)/shard_map/ppermute | solution.py:103
  4.8 6.7 %collective-permute-start.2 = (bf16[32,1024]{1,0:T(8,128)(2,1)}, bf16[32,1024]{1,0:T(8,128)(2,1)S(1)}, u32[]{:S(2)}, u32[]{:S(2)}) collective-permute-start(bf16[32,1024]{1,0:T(8,128)(2,1)} %refs_1_.3), channel_id=1, source_target_pairs={{0,16},{2,18},{4,20},{6,22},{8,24},{10,26},{12,28},{14,30},{16,0},... | collective-permute-start | bytes 196616 | tf_op jit(solution)/shard_map/ppermute | solution.py:103
  4.8 9.7 %collective-permute-start = (bf16[128,512]{1,0:T(8,128)(2,1)}, bf16[128,512]{1,0:T(8,128)(2,1)S(1)}, u32[]{:S(2)}, u32[]{:S(2)}) collective-permute-start(bf16[128,512]{1,0:T(8,128)(2,1)} %refs_2_.5), channel_id=1, source_target_pairs={{0,1},{1,0},{2,3},{3,2},{4,5},{5,4},{6,7},{7,6},{8,9},{9,8},{10,11... | collective-permute-start | bytes 393224 | tf_op jit(solution)/shard_map/ppermute | solution.py:83
  6.6 7.9 %collective-permute-start.8 = (bf16[128,512]{1,0:T(8,128)(2,1)}, bf16[128,512]{1,0:T(8,128)(2,1)S(1)}, u32[]{:S(2)}, u32[]{:S(2)}) collective-permute-start(bf16[128,512]{1,0:T(8,128)(2,1)} %param.29), channel_id=1, source_target_pairs={{0,1},{1,0},{2,3},{3,2},{4,5},{5,4},{6,7},{7,6},{8,9},{9,8},{10,11... | collective-permute-start | bytes 393224 | tf_op jit(solution)/shard_map/ppermute | solution.py:83
  11.5 5.0 %collective-permute-start.3 = (bf16[64,1024]{1,0:T(8,128)(2,1)S(1)}, bf16[64,1024]{1,0:T(8,128)(2,1)S(1)}, u32[]{:S(2)}, u32[]{:S(2)}) collective-permute-start(bf16[64,1024]{1,0:T(8,128)(2,1)S(1)} %get-tuple-element.162.refs_0_), channel_id=1, source_target_pairs={{0,8},{2,10},{4,12},{6,14},{8,0},{10,2},{12,4},{14,6},{16,24},{18,... | collective-permute-start | bytes 393224 | tf_op jit(solution)/shard_map/ppermute | solution.py:103
  13.0 5.0 %collective-permute-start.4 = (bf16[64,1024]{1,0:T(8,128)(2,1)S(1)}, bf16[64,1024]{1,0:T(8,128)(2,1)S(1)}, u32[]{:S(2)}, u32[]{:S(2)}) collective-permute-start(bf16[64,1024]{1,0:T(8,128)(2,1)S(1)} %get-tuple-element.163.refs_1_), channel_id=1, source_target_pairs={{0,4},{2,6},{4,0},{6,2},{8,12},{10,14},{12,8},{14,10},{16,20},{18,... | collective-permute-start | bytes 393224 | tf_op jit(solution)/shard_map/ppermute | solution.py:103
  18.1 14.4 %copy-start = (f32[5,512]{1,0:T(8,128)S(1)}, f32[5,512]{1,0:T(8,128)}, u32[]{:S(2)}) copy-start(f32[5,512]{1,0:T(8,128)} %refs_3_.7) | copy-start | bytes 30724
  18.1 9.2 %collective-permute-start.5 = (bf16[128,1024]{1,0:T(8,128)(2,1)S(1)}, bf16[128,1024]{1,0:T(8,128)(2,1)S(1)}, u32[]{:S(2)}, u32[]{:S(2)}) collective-permute-start(bf16[128,1024]{1,0:T(8,128)(2,1)S(1)} %get-tuple-element.166.refs_0_), channel_id=1, source_target_pairs={{0,4},{2,6},{4,0},{6,2},{8,12},{10,14},{12,8},{14,10},{16,20},{18,... | collective-permute-start | bytes 786440 | tf_op jit(solution)/shard_map/ppermute | solution.py:103
  19.6 8.8 %collective-permute-start.6 = (bf16[128,1024]{1,0:T(8,128)(2,1)S(1)}, bf16[128,1024]{1,0:T(8,128)(2,1)S(1)}, u32[]{:S(2)}, u32[]{:S(2)}) collective-permute-start(bf16[128,1024]{1,0:T(8,128)(2,1)S(1)} %get-tuple-element.167.refs_1_), channel_id=1, source_target_pairs={{0,8},{2,10},{4,12},{6,14},{8,0},{10,2},{12,4},{14,6},{16,24},{18,... | collective-permute-start | bytes 786440 | tf_op jit(solution)/shard_map/ppermute | solution.py:103
  20.4 6.9 %collective-permute-start.7 = (bf16[256,256]{1,0:T(8,128)(2,1)S(1)}, bf16[256,256]{1,0:T(8,128)(2,1)S(1)}, u32[]{:S(2)}, u32[]{:S(2)}) collective-permute-start(bf16[256,256]{1,0:T(8,128)(2,1)S(1)} %pad_maximum_fusion.2), channel_id=1, source_target_pairs={{0,16},{2,18},{4,20},{6,22},{8,24},{10,26},{12,28},{14,30},{16,0},... | collective-permute-start | bytes 393224 | tf_op jit(solution)/shard_map/ppermute | solution.py:103
  28.5 3.9 %collective-permute-start.9 = (bf16[512,1024]{1,0:T(8,128)(2,1)S(1)}, bf16[512,1024]{1,0:T(8,128)(2,1)S(1)}, u32[]{:S(2)}, u32[]{:S(2)}) collective-permute-start(bf16[512,1024]{1,0:T(8,128)(2,1)S(1)} %gather_join.12.refs_2_), channel_id=1, source_target_pairs={{0,2},{2,0},{4,6},{6,4},{8,10},{10,8},{12,14},{14,12},{16,18},{18,... | collective-permute-start | bytes 3145736 | tf_op jit(solution)/shard_map/ppermute | solution.py:103
  28.6 7.4 %collective-permute-start.11 = (bf16[256,256]{1,0:T(8,128)(2,1)S(1)}, bf16[256,256]{1,0:T(8,128)(2,1)S(1)}, u32[]{:S(2)}, u32[]{:S(2)}) collective-permute-start(bf16[256,256]{1,0:T(8,128)(2,1)S(1)} %get-tuple-element.170.refs_0_), channel_id=1, source_target_pairs={{0,8},{2,10},{4,12},{6,14},{8,0},{10,2},{12,4},{14,6},{16,24},{18,... | collective-permute-start | bytes 393224 | tf_op jit(solution)/shard_map/ppermute | solution.py:103
  31.9 5.6 %collective-permute-start.12 = (bf16[256,256]{1,0:T(8,128)(2,1)S(1)}, bf16[256,256]{1,0:T(8,128)(2,1)S(1)}, u32[]{:S(2)}, u32[]{:S(2)}) collective-permute-start(bf16[256,256]{1,0:T(8,128)(2,1)S(1)} %get-tuple-element.171.refs_1_), channel_id=1, source_target_pairs={{0,4},{2,6},{4,0},{6,2},{8,12},{10,14},{12,8},{14,10},{16,20},{18,... | collective-permute-start | bytes 393224 | tf_op jit(solution)/shard_map/ppermute | solution.py:103
  37.5 9.3 %collective-permute-start.13 = (bf16[512,256]{1,0:T(8,128)(2,1)S(1)}, bf16[512,256]{1,0:T(8,128)(2,1)S(1)}, u32[]{:S(2)}, u32[]{:S(2)}) collective-permute-start(bf16[512,256]{1,0:T(8,128)(2,1)S(1)} %get-tuple-element.177.refs_0_), channel_id=1, source_target_pairs={{0,4},{2,6},{4,0},{6,2},{8,12},{10,14},{12,8},{14,10},{16,20},{18,... | collective-permute-start | bytes 786440 | tf_op jit(solution)/shard_map/ppermute | solution.py:103
  38.1 10.1 %collective-permute-start.14 = (bf16[512,256]{1,0:T(8,128)(2,1)S(1)}, bf16[512,256]{1,0:T(8,128)(2,1)S(1)}, u32[]{:S(2)}, u32[]{:S(2)}) collective-permute-start(bf16[512,256]{1,0:T(8,128)(2,1)S(1)} %get-tuple-element.178.refs_1_), channel_id=1, source_target_pairs={{0,8},{2,10},{4,12},{6,14},{8,0},{10,2},{12,4},{14,6},{16,24},{18,... | collective-permute-start | bytes 786440 | tf_op jit(solution)/shard_map/ppermute | solution.py:103
  38.4 9.8 %collective-permute-start.10 = (bf16[256,512]{1,0:T(8,128)(2,1)S(1)}, bf16[256,512]{1,0:T(8,128)(2,1)S(1)}, u32[]{:S(2)}, u32[]{:S(2)}) collective-permute-start(bf16[256,512]{1,0:T(8,128)(2,1)S(1)} %get-tuple-element.174.refs_1_), channel_id=1, source_target_pairs={{0,1},{1,0},{2,3},{3,2},{4,5},{5,4},{6,7},{7,6},{8,9},{9,8},{10,11... | collective-permute-start | bytes 786440 | tf_op jit(solution)/shard_map/ppermute | solution.py:83
  39.9 6.9 %collective-permute-start.15 = (bf16[64,1024]{1,0:T(8,128)(2,1)S(1)}, bf16[64,1024]{1,0:T(8,128)(2,1)S(1)}, u32[]{:S(2)}, u32[]{:S(2)}) collective-permute-start(bf16[64,1024]{1,0:T(8,128)(2,1)S(1)} %pad_maximum_fusion.3), channel_id=1, source_target_pairs={{0,16},{2,18},{4,20},{6,22},{8,24},{10,26},{12,28},{14,30},{16,0},... | collective-permute-start | bytes 393224 | tf_op jit(solution)/shard_map/ppermute | solution.py:103
  48.3 2.7 %collective-permute-start.16 = (bf16[2048,256]{1,0:T(8,128)(2,1)S(1)}, bf16[2048,256]{1,0:T(8,128)(2,1)S(1)}, u32[]{:S(2)}, u32[]{:S(2)}) collective-permute-start(bf16[2048,256]{1,0:T(8,128)(2,1)S(1)} %gather_join.15.refs_0_), channel_id=1, source_target_pairs={{0,2},{2,0},{4,6},{6,4},{8,10},{10,8},{12,14},{14,12},{16,18},{18,... | collective-permute-start | bytes 3145736 | tf_op jit(solution)/shard_map/ppermute | solution.py:103
  48.4 8.0 %collective-permute-start.24 = (bf16[64,1024]{1,0:T(8,128)(2,1)S(1)}, bf16[64,1024]{1,0:T(8,128)(2,1)S(1)}, u32[]{:S(2)}, u32[]{:S(2)}) collective-permute-start(bf16[64,1024]{1,0:T(8,128)(2,1)S(1)} %get-tuple-element.181.refs_0_), channel_id=1, source_target_pairs={{0,8},{2,10},{4,12},{6,14},{8,0},{10,2},{12,4},{14,6},{16,24},{18,... | collective-permute-start | bytes 393224 | tf_op jit(solution)/shard_map/ppermute | solution.py:103
  49.0 7.4 %collective-permute-start.25 = (bf16[64,1024]{1,0:T(8,128)(2,1)S(1)}, bf16[64,1024]{1,0:T(8,128)(2,1)S(1)}, u32[]{:S(2)}, u32[]{:S(2)}) collective-permute-start(bf16[64,1024]{1,0:T(8,128)(2,1)S(1)} %get-tuple-element.182.refs_1_), channel_id=1, source_target_pairs={{0,4},{2,6},{4,0},{6,2},{8,12},{10,14},{12,8},{14,10},{16,20},{18,... | collective-permute-start | bytes 393224 | tf_op jit(solution)/shard_map/ppermute | solution.py:103
  54.8 8.4 %collective-permute-start.17 = (bf16[256,512]{1,0:T(8,128)(2,1)S(1)}, bf16[256,512]{1,0:T(8,128)(2,1)S(1)}, u32[]{:S(2)}, u32[]{:S(2)}) collective-permute-start(bf16[256,512]{1,0:T(8,128)(2,1)S(1)} %get-tuple-element.188.refs_1_), channel_id=1, source_target_pairs={{0,1},{1,0},{2,3},{3,2},{4,5},{5,4},{6,7},{7,6},{8,9},{9,8},{10,11... | collective-permute-start | bytes 786440 | tf_op jit(solution)/shard_map/ppermute | solution.py:83
  56.4 8.7 %collective-permute-start.26 = (bf16[128,1024]{1,0:T(8,128)(2,1)S(1)}, bf16[128,1024]{1,0:T(8,128)(2,1)S(1)}, u32[]{:S(2)}, u32[]{:S(2)}) collective-permute-start(bf16[128,1024]{1,0:T(8,128)(2,1)S(1)} %get-tuple-element.193.refs_0_), channel_id=1, source_target_pairs={{0,4},{2,6},{4,0},{6,2},{8,12},{10,14},{12,8},{14,10},{16,20},{18,... | collective-permute-start | bytes 786440 | tf_op jit(solution)/shard_map/ppermute | solution.py:103
  58.0 7.8 %collective-permute-start.27 = (bf16[128,1024]{1,0:T(8,128)(2,1)S(1)}, bf16[128,1024]{1,0:T(8,128)(2,1)S(1)}, u32[]{:S(2)}, u32[]{:S(2)}) collective-permute-start(bf16[128,1024]{1,0:T(8,128)(2,1)S(1)} %get-tuple-element.194.refs_1_), channel_id=1, source_target_pairs={{0,8},{2,10},{4,12},{6,14},{8,0},{10,2},{12,4},{14,6},{16,24},{18,... | collective-permute-start | bytes 786440 | tf_op jit(solution)/shard_map/ppermute | solution.py:103
  65.9 15.2 %collective-permute-start.28 = (bf16[512,1024]{1,0:T(8,128)(2,1)S(1)}, bf16[512,1024]{1,0:T(8,128)(2,1)S(1)}, u32[]{:S(2)}, u32[]{:S(2)}) collective-permute-start(bf16[512,1024]{1,0:T(8,128)(2,1)S(1)} %gather_join.17.refs_0_), channel_id=1, source_target_pairs={{0,2},{2,0},{4,6},{6,4},{8,10},{10,8},{12,14},{14,12},{16,18},{18,... | collective-permute-start | bytes 3145736 | tf_op jit(solution)/shard_map/ppermute | solution.py:103
  65.9 2.6 %collective-permute-start.18 = (f32[2,256]{1,0:T(2,128)S(1)}, f32[2,256]{1,0:T(2,128)S(1)}, u32[]{:S(2)}, u32[]{:S(2)}) collective-permute-start(f32[2,256]{1,0:T(2,128)S(1)} %get-tuple-element.190), channel_id=1, source_target_pairs={{0,2},{2,0},{4,6},{6,4},{8,10},{10,8},{12,14},{14,12},{16,18},{18,... | collective-permute-start | bytes 6152 | tf_op jit(solution)/shard_map/ppermute | solution.py:103
  68.6 3.6 %collective-permute-start.19 = (f32[2,256]{1,0:T(2,128)S(1)}, f32[2,256]{1,0:T(2,128)S(1)}, u32[]{:S(2)}, u32[]{:S(2)}) collective-permute-start(f32[2,256]{1,0:T(2,128)S(1)} %add.47), channel_id=1, source_target_pairs={{0,4},{2,6},{4,0},{6,2},{8,12},{10,14},{12,8},{14,10},{16,20},{18,... | collective-permute-start | bytes 6152 | tf_op jit(solution)/shard_map/ppermute | solution.py:103
  72.2 4.4 %collective-permute-start.20 = (f32[2,256]{1,0:T(2,128)S(1)}, f32[2,256]{1,0:T(2,128)S(1)}, u32[]{:S(2)}, u32[]{:S(2)}) collective-permute-start(f32[2,256]{1,0:T(2,128)S(1)} %add.48), channel_id=1, source_target_pairs={{0,8},{2,10},{4,12},{6,14},{8,0},{10,2},{12,4},{14,6},{16,24},{18,... | collective-permute-start | bytes 6152 | tf_op jit(solution)/shard_map/ppermute | solution.py:103
  72.8 4.5 %collective-permute-start.21 = (f32[2,256]{1,0:T(2,128)S(1)}, f32[2,256]{1,0:T(2,128)S(1)}, u32[]{:S(2)}, u32[]{:S(2)}) collective-permute-start(f32[2,256]{1,0:T(2,128)S(1)} %add.48), channel_id=1, source_target_pairs={{0,16},{2,18},{4,20},{6,22},{8,24},{10,26},{12,28},{14,30},{16,0},... | collective-permute-start | bytes 6152 | tf_op jit(solution)/shard_map/ppermute | solution.py:103
  74.0 5.4 %collective-permute-start.22 = (f32[2,256]{1,0:T(2,128)S(1)}, f32[2,256]{1,0:T(2,128)S(1)}, u32[]{:S(2)}, u32[]{:S(2)}) collective-permute-start(f32[2,256]{1,0:T(2,128)S(1)} %add.48), channel_id=1, source_target_pairs={{0,24},{2,26},{4,28},{6,30},{8,16},{10,18},{12,20},{14,22},{16,8},... | collective-permute-start | bytes 6152 | tf_op jit(solution)/shard_map/ppermute | solution.py:103
  79.7 6.6 %collective-permute-start.23 = (bf16[256,512]{1,0:T(8,128)(2,1)S(1)}, bf16[256,512]{1,0:T(8,128)(2,1)S(1)}, u32[]{:S(2)}, u32[]{:S(2)}) collective-permute-start(bf16[256,512]{1,0:T(8,128)(2,1)S(1)} %norm_forward.1.refs_1_), channel_id=1, source_target_pairs={{0,1},{1,0},{2,3},{3,2},{4,5},{5,4},{6,7},{7,6},{8,9},{9,8},{10,11... | collective-permute-start | bytes 786440 | tf_op jit(solution)/shard_map/ppermute | solution.py:83
  87.3 6.4 %collective-permute-start.29 = (bf16[256,512]{1,0:T(8,128)(2,1)S(1)}, bf16[256,512]{1,0:T(8,128)(2,1)S(1)}, u32[]{:S(2)}, u32[]{:S(2)}) collective-permute-start(bf16[256,512]{1,0:T(8,128)(2,1)S(1)} %get-tuple-element.199.refs_1_), channel_id=1, source_target_pairs={{0,1},{1,0},{2,3},{3,2},{4,5},{5,4},{6,7},{7,6},{8,9},{9,8},{10,11... | collective-permute-start | bytes 786440 | tf_op jit(solution)/shard_map/ppermute | solution.py:83
  96.8 2.7 %collective-permute-start.31 = (bf16[512,1024]{1,0:T(8,128)(2,1)S(1)}, bf16[512,1024]{1,0:T(8,128)(2,1)S(1)}, u32[]{:S(2)}, u32[]{:S(2)}) collective-permute-start(bf16[512,1024]{1,0:T(8,128)(2,1)S(1)} %get-tuple-element.206), channel_id=1, source_target_pairs={{0,2},{2,0},{4,6},{6,4},{8,10},{10,8},{12,14},{14,12},{16,18},{18,... | collective-permute-start | bytes 3145736 | tf_op jit(solution)/shard_map/ppermute | solution.py:103
  96.8 8.7 %collective-permute-start.30 = (bf16[256,512]{1,0:T(8,128)(2,1)S(1)}, bf16[256,512]{1,0:T(8,128)(2,1)S(1)}, u32[]{:S(2)}, u32[]{:S(2)}) collective-permute-start(bf16[256,512]{1,0:T(8,128)(2,1)S(1)} %get-tuple-element.202.refs_1_), channel_id=1, source_target_pairs={{0,1},{1,0},{2,3},{3,2},{4,5},{5,4},{6,7},{7,6},{8,9},{9,8},{10,11... | collective-permute-start | bytes 786440 | tf_op jit(solution)/shard_map/ppermute | solution.py:83
  99.9 19.6 %collective-permute-start.37 = (bf16[128,1024]{1,0:T(8,128)(2,1)S(1)}, bf16[128,1024]{1,0:T(8,128)(2,1)S(1)}, u32[]{:S(2)}, u32[]{:S(2)}) collective-permute-start(bf16[128,1024]{1,0:T(8,128)(2,1)S(1)} %get-tuple-element.212), channel_id=1, source_target_pairs={{0,4},{2,6},{4,0},{6,2},{8,12},{10,14},{12,8},{14,10},{16,20},{18,... | collective-permute-start | bytes 786440 | tf_op jit(solution)/shard_map/ppermute | solution.py:103
  100.9 18.5 %collective-permute-start.38 = (bf16[128,1024]{1,0:T(8,128)(2,1)S(1)}, bf16[128,1024]{1,0:T(8,128)(2,1)S(1)}, u32[]{:S(2)}, u32[]{:S(2)}) collective-permute-start(bf16[128,1024]{1,0:T(8,128)(2,1)S(1)} %get-tuple-element.213), channel_id=1, source_target_pairs={{0,8},{2,10},{4,12},{6,14},{8,0},{10,2},{12,4},{14,6},{16,24},{18,... | collective-permute-start | bytes 786440 | tf_op jit(solution)/shard_map/ppermute | solution.py:103
  106.2 1.2 collective-permute-start.32
  107.4 3.6 %collective-permute-start.33 = (f32[2,256]{1,0:T(2,128)S(1)}, f32[2,256]{1,0:T(2,128)S(1)}, u32[]{:S(2)}, u32[]{:S(2)}) collective-permute-start(f32[2,256]{1,0:T(2,128)S(1)} %add.52), channel_id=1, source_target_pairs={{0,4},{2,6},{4,0},{6,2},{8,12},{10,14},{12,8},{14,10},{16,20},{18,... | collective-permute-start | bytes 6152 | tf_op jit(solution)/shard_map/ppermute | solution.py:103
  111.0 4.4 %collective-permute-start.34 = (f32[2,256]{1,0:T(2,128)S(1)}, f32[2,256]{1,0:T(2,128)S(1)}, u32[]{:S(2)}, u32[]{:S(2)}) collective-permute-start(f32[2,256]{1,0:T(2,128)S(1)} %add.53), channel_id=1, source_target_pairs={{0,8},{2,10},{4,12},{6,14},{8,0},{10,2},{12,4},{14,6},{16,24},{18,... | collective-permute-start | bytes 6152 | tf_op jit(solution)/shard_map/ppermute | solution.py:103
  111.0 4.7 %collective-permute-start.35 = (f32[2,256]{1,0:T(2,128)S(1)}, f32[2,256]{1,0:T(2,128)S(1)}, u32[]{:S(2)}, u32[]{:S(2)}) collective-permute-start(f32[2,256]{1,0:T(2,128)S(1)} %add.53), channel_id=1, source_target_pairs={{0,16},{2,18},{4,20},{6,22},{8,24},{10,26},{12,28},{14,30},{16,0},... | collective-permute-start | bytes 6152 | tf_op jit(solution)/shard_map/ppermute | solution.py:103
  114.1 5.4 %collective-permute-start.36 = (f32[2,256]{1,0:T(2,128)S(1)}, f32[2,256]{1,0:T(2,128)S(1)}, u32[]{:S(2)}, u32[]{:S(2)}) collective-permute-start(f32[2,256]{1,0:T(2,128)S(1)} %add.53), channel_id=1, source_target_pairs={{0,24},{2,26},{4,28},{6,30},{8,16},{10,18},{12,20},{14,22},{16,8},... | collective-permute-start | bytes 6152 | tf_op jit(solution)/shard_map/ppermute | solution.py:103
  121.3 6.4 %collective-permute-start.39 = (bf16[256,512]{1,0:T(8,128)(2,1)S(1)}, bf16[256,512]{1,0:T(8,128)(2,1)S(1)}, u32[]{:S(2)}, u32[]{:S(2)}) collective-permute-start(bf16[256,512]{1,0:T(8,128)(2,1)S(1)} %get-tuple-element.217.refs_1_), channel_id=1, source_target_pairs={{0,1},{1,0},{2,3},{3,2},{4,5},{5,4},{6,7},{7,6},{8,9},{9,8},{10,11... | collective-permute-start | bytes 786440 | tf_op jit(solution)/shard_map/ppermute | solution.py:83
  122.3 5.0 %collective-permute-start.40 = (bf16[64,1024]{1,0:T(8,128)(2,1)S(1)}, bf16[64,1024]{1,0:T(8,128)(2,1)S(1)}, u32[]{:S(2)}, u32[]{:S(2)}) collective-permute-start(bf16[64,1024]{1,0:T(8,128)(2,1)S(1)} %get-tuple-element.224), channel_id=1, source_target_pairs={{0,8},{2,10},{4,12},{6,14},{8,0},{10,2},{12,4},{14,6},{16,24},{18,... | collective-permute-start | bytes 393224 | tf_op jit(solution)/shard_map/ppermute | solution.py:103
  122.3 5.0 %collective-permute-start.41 = (bf16[64,1024]{1,0:T(8,128)(2,1)S(1)}, bf16[64,1024]{1,0:T(8,128)(2,1)S(1)}, u32[]{:S(2)}, u32[]{:S(2)}) collective-permute-start(bf16[64,1024]{1,0:T(8,128)(2,1)S(1)} %get-tuple-element.225), channel_id=1, source_target_pairs={{0,4},{2,6},{4,0},{6,2},{8,12},{10,14},{12,8},{14,10},{16,20},{18,... | collective-permute-start | bytes 393224 | tf_op jit(solution)/shard_map/ppermute | solution.py:103
  132.5 2.7 %collective-permute-start.43 = (bf16[2048,256]{1,0:T(8,128)(2,1)S(1)}, bf16[2048,256]{1,0:T(8,128)(2,1)S(1)}, u32[]{:S(2)}, u32[]{:S(2)}) collective-permute-start(bf16[2048,256]{1,0:T(8,128)(2,1)S(1)} %get-tuple-element.237), channel_id=1, source_target_pairs={{0,2},{2,0},{4,6},{6,4},{8,10},{10,8},{12,14},{14,12},{16,18},{18,... | collective-permute-start | bytes 3145736 | tf_op jit(solution)/shard_map/ppermute | solution.py:103
  132.6 8.7 %collective-permute-start.42 = (bf16[256,512]{1,0:T(8,128)(2,1)S(1)}, bf16[256,512]{1,0:T(8,128)(2,1)S(1)}, u32[]{:S(2)}, u32[]{:S(2)}) collective-permute-start(bf16[256,512]{1,0:T(8,128)(2,1)S(1)} %get-tuple-element.232.refs_1_), channel_id=1, source_target_pairs={{0,1},{1,0},{2,3},{3,2},{4,5},{5,4},{6,7},{7,6},{8,9},{9,8},{10,11... | collective-permute-start | bytes 786440 | tf_op jit(solution)/shard_map/ppermute | solution.py:83
  135.4 8.4 %collective-permute-start.45 = (bf16[512,256]{1,0:T(8,128)(2,1)S(1)}, bf16[512,256]{1,0:T(8,128)(2,1)S(1)}, u32[]{:S(2)}, u32[]{:S(2)}) collective-permute-start(bf16[512,256]{1,0:T(8,128)(2,1)S(1)} %get-tuple-element.245), channel_id=1, source_target_pairs={{0,4},{2,6},{4,0},{6,2},{8,12},{10,14},{12,8},{14,10},{16,20},{18,... | collective-permute-start | bytes 786440 | tf_op jit(solution)/shard_map/ppermute | solution.py:103
  136.6 8.3 %collective-permute-start.46 = (bf16[512,256]{1,0:T(8,128)(2,1)S(1)}, bf16[512,256]{1,0:T(8,128)(2,1)S(1)}, u32[]{:S(2)}, u32[]{:S(2)}) collective-permute-start(bf16[512,256]{1,0:T(8,128)(2,1)S(1)} %get-tuple-element.246), channel_id=1, source_target_pairs={{0,8},{2,10},{4,12},{6,14},{8,0},{10,2},{12,4},{14,6},{16,24},{18,... | collective-permute-start | bytes 786440 | tf_op jit(solution)/shard_map/ppermute | solution.py:103
  146.5 3.5 %collective-permute-start.49 = (bf16[512,1024]{1,0:T(8,128)(2,1)S(1)}, bf16[512,1024]{1,0:T(8,128)(2,1)S(1)}, u32[]{:S(2)}, u32[]{:S(2)}) collective-permute-start(bf16[512,1024]{1,0:T(8,128)(2,1)S(1)} %get-tuple-element.255), channel_id=1, source_target_pairs={{0,2},{2,0},{4,6},{6,4},{8,10},{10,8},{12,14},{14,12},{16,18},{18,... | collective-permute-start | bytes 3145736 | tf_op jit(solution)/shard_map/ppermute | solution.py:103
  146.6 5.9 %collective-permute-start.47 = (bf16[256,256]{1,0:T(8,128)(2,1)S(1)}, bf16[256,256]{1,0:T(8,128)(2,1)S(1)}, u32[]{:S(2)}, u32[]{:S(2)}) collective-permute-start(bf16[256,256]{1,0:T(8,128)(2,1)S(1)} %get-tuple-element.249), channel_id=1, source_target_pairs={{0,8},{2,10},{4,12},{6,14},{8,0},{10,2},{12,4},{14,6},{16,24},{18,... | collective-permute-start | bytes 393224 | tf_op jit(solution)/shard_map/ppermute | solution.py:103
  148.4 5.6 %collective-permute-start.48 = (bf16[256,256]{1,0:T(8,128)(2,1)S(1)}, bf16[256,256]{1,0:T(8,128)(2,1)S(1)}, u32[]{:S(2)}, u32[]{:S(2)}) collective-permute-start(bf16[256,256]{1,0:T(8,128)(2,1)S(1)} %get-tuple-element.250), channel_id=1, source_target_pairs={{0,4},{2,6},{4,0},{6,2},{8,12},{10,14},{12,8},{14,10},{16,20},{18,... | collective-permute-start | bytes 393224 | tf_op jit(solution)/shard_map/ppermute | solution.py:103
  149.0 5.3 %collective-permute-start.44 = (bf16[128,512]{1,0:T(8,128)(2,1)S(1)}, bf16[128,512]{1,0:T(8,128)(2,1)S(1)}, u32[]{:S(2)}, u32[]{:S(2)}) collective-permute-start(bf16[128,512]{1,0:T(8,128)(2,1)S(1)} %get-tuple-element.244), channel_id=1, source_target_pairs={{0,1},{1,0},{2,3},{3,2},{4,5},{5,4},{6,7},{7,6},{8,9},{9,8},{10,11... | collective-permute-start | bytes 393224 | tf_op jit(solution)/shard_map/ppermute | solution.py:83
  155.3 3.9 %collective-permute-start.50 = (f32[8,512]{1,0:T(8,128)S(1)}, f32[8,512]{1,0:T(8,128)S(1)}, u32[]{:S(2)}, u32[]{:S(2)}) collective-permute-start(f32[8,512]{1,0:T(8,128)S(1)} %slice.14), channel_id=1, source_target_pairs={{0,1},{1,0},{2,3},{3,2},{4,5},{5,4},{6,7},{7,6},{8,9},{9,8},{10,11... | collective-permute-start | bytes 49160 | tf_op jit(solution)/shard_map/ppermute | solution.py:103
  156.4 6.9 %collective-permute-start.51 = (bf16[128,1024]{1,0:T(8,128)(2,1)S(1)}, bf16[128,1024]{1,0:T(8,128)(2,1)S(1)}, u32[]{:S(2)}, u32[]{:S(2)}) collective-permute-start(bf16[128,1024]{1,0:T(8,128)(2,1)S(1)} %get-tuple-element.271), channel_id=1, source_target_pairs={{0,4},{2,6},{4,0},{6,2},{8,12},{10,14},{12,8},{14,10},{16,20},{18,... | collective-permute-start | bytes 786440 | tf_op jit(solution)/shard_map/ppermute | solution.py:103
  157.3 9.5 %collective-permute-start.52 = (bf16[128,1024]{1,0:T(8,128)(2,1)S(1)}, bf16[128,1024]{1,0:T(8,128)(2,1)S(1)}, u32[]{:S(2)}, u32[]{:S(2)}) collective-permute-start(bf16[128,1024]{1,0:T(8,128)(2,1)S(1)} %get-tuple-element.272), channel_id=1, source_target_pairs={{0,8},{2,10},{4,12},{6,14},{8,0},{10,2},{12,4},{14,6},{16,24},{18,... | collective-permute-start | bytes 786440 | tf_op jit(solution)/shard_map/ppermute | solution.py:103
  158.1 12.9 %collective-permute-start.57 = (bf16[256,256]{1,0:T(8,128)(2,1)S(1)}, bf16[256,256]{1,0:T(8,128)(2,1)S(1)}, u32[]{:S(2)}, u32[]{:S(2)}) collective-permute-start(bf16[256,256]{1,0:T(8,128)(2,1)S(1)} %get-tuple-element.280), channel_id=1, source_target_pairs={{0,16},{2,18},{4,20},{6,22},{8,24},{10,26},{12,28},{14,30},{16,0},... | collective-permute-start | bytes 393224 | tf_op jit(solution)/shard_map/ppermute | solution.py:103
  166.8 1.3 collective-permute-start.53
  166.9 7.3 %collective-permute-start.55 = (bf16[64,1024]{1,0:T(8,128)(2,1)S(1)}, bf16[64,1024]{1,0:T(8,128)(2,1)S(1)}, u32[]{:S(2)}, u32[]{:S(2)}) collective-permute-start(bf16[64,1024]{1,0:T(8,128)(2,1)S(1)} %get-tuple-element.278), channel_id=1, source_target_pairs={{0,8},{2,10},{4,12},{6,14},{8,0},{10,2},{12,4},{14,6},{16,24},{18,... | collective-permute-start | bytes 393224 | tf_op jit(solution)/shard_map/ppermute | solution.py:103
  167.0 7.3 %collective-permute-start.56 = (bf16[64,1024]{1,0:T(8,128)(2,1)S(1)}, bf16[64,1024]{1,0:T(8,128)(2,1)S(1)}, u32[]{:S(2)}, u32[]{:S(2)}) collective-permute-start(bf16[64,1024]{1,0:T(8,128)(2,1)S(1)} %get-tuple-element.279), channel_id=1, source_target_pairs={{0,4},{2,6},{4,0},{6,2},{8,12},{10,14},{12,8},{14,10},{16,20},{18,... | collective-permute-start | bytes 393224 | tf_op jit(solution)/shard_map/ppermute | solution.py:103
  168.2 6.0 %collective-permute-start.54 = (f32[32,512]{1,0:T(8,128)S(1)}, f32[32,512]{1,0:T(8,128)S(1)}, u32[]{:S(2)}, u32[]{:S(2)}) collective-permute-start(f32[32,512]{1,0:T(8,128)S(1)} %add.58), channel_id=1, source_target_pairs={{0,4},{2,6},{4,0},{6,2},{8,12},{10,14},{12,8},{14,10},{16,20},{18,... | collective-permute-start | bytes 196616 | tf_op jit(solution)/shard_map/ppermute | solution.py:103
  169.3 10.7 %collective-permute-start.62 = (bf16[64,1024]{1,0:T(8,128)(2,1)S(1)}, bf16[64,1024]{1,0:T(8,128)(2,1)S(1)}, u32[]{:S(2)}, u32[]{:S(2)}) collective-permute-start(bf16[64,1024]{1,0:T(8,128)(2,1)S(1)} %get-tuple-element.297), channel_id=1, source_target_pairs={{0,16},{2,18},{4,20},{6,22},{8,24},{10,26},{12,28},{14,30},{16,0},... | collective-permute-start | bytes 393224 | tf_op jit(solution)/shard_map/ppermute | solution.py:103
  174.3 6.8 %collective-permute-start.58 = (f32[32,512]{1,0:T(8,128)S(1)}, f32[32,512]{1,0:T(8,128)S(1)}, u32[]{:S(2)}, u32[]{:S(2)}) collective-permute-start(f32[32,512]{1,0:T(8,128)S(1)} %add.59.refs_0_), channel_id=1, source_target_pairs={{0,8},{2,10},{4,12},{6,14},{8,0},{10,2},{12,4},{14,6},{16,24},{18,... | collective-permute-start | bytes 196616 | tf_op jit(solution)/shard_map/ppermute | solution.py:103
  176.1 10.3 %collective-permute-start.59 = (f32[32,512]{1,0:T(8,128)S(1)}, f32[32,512]{1,0:T(8,128)S(1)}, u32[]{:S(2)}, u32[]{:S(2)}) collective-permute-start(f32[32,512]{1,0:T(8,128)S(1)} %add.59.refs_0_), channel_id=1, source_target_pairs={{0,16},{2,18},{4,20},{6,22},{8,24},{10,26},{12,28},{14,30},{16,0},... | collective-permute-start | bytes 196616 | tf_op jit(solution)/shard_map/ppermute | solution.py:103
  176.3 10.1 %collective-permute-start.60 = (f32[32,512]{1,0:T(8,128)S(1)}, f32[32,512]{1,0:T(8,128)S(1)}, u32[]{:S(2)}, u32[]{:S(2)}) collective-permute-start(f32[32,512]{1,0:T(8,128)S(1)} %add.59.refs_0_), channel_id=1, source_target_pairs={{0,24},{2,26},{4,28},{6,30},{8,16},{10,18},{12,20},{14,22},{16,8},... | collective-permute-start | bytes 196616 | tf_op jit(solution)/shard_map/ppermute | solution.py:103
  178.8 11.1 %collective-permute-start.61 = (bf16[64,1024]{1,0:T(8,128)(2,1)S(1)}, bf16[64,1024]{1,0:T(8,128)(2,1)S(1)}, u32[]{:S(2)}, u32[]{:S(2)}) collective-permute-start(bf16[64,1024]{1,0:T(8,128)(2,1)S(1)} %get-tuple-element.289), channel_id=1, source_target_pairs={{0,16},{2,18},{4,20},{6,22},{8,24},{10,26},{12,28},{14,30},{16,0},... | collective-permute-start | bytes 393224 | tf_op jit(solution)/shard_map/ppermute | solution.py:103
  (14 other events, 134.8 us)

commit v6 on v5

--- a/solution.py
+++ b/solution.py
@@ -94,11 +94,6 @@
     return jnp.where(lax.axis_index("tensor") == 0, value[:half], value[half:])
 
 
-def other_half(value):
-    half = value.shape[0] // 2
-    return jnp.where(lax.axis_index("tensor") == 0, value[half:], value[:half])
-
-
 def shift(value, axis, mask):
     return lax.ppermute(value, axis, [(k, k ^ mask) for k in range(lax.axis_size(axis))])
 
@@ -109,7 +104,7 @@
         return lax.psum(value, axis)
     stop = stop or size
     while step < stop:
-        if step >= 4 and step * 4 <= stop:
+        if step * 4 <= stop:
             near, far, both = (shift(value, axis, step * times) for times in (1, 2, 3))
             value = (value + near) + (far + both)
             step *= 4
@@ -317,7 +312,7 @@
         gain = gain_ref[4:5, :]
         out_ref[...] = own_half(normed * gain).astype(BF16)
         gradient, gain_grad = norm_back(cot_ref[...].astype(F32), normed, factor, gain)
-        gain_grad_ref[...] = 0.5 * gain_grad
+        gain_grad_ref[...] = gain_grad
         grad_ref[...] = gradient
         part_ref[...] = ff_back_body(
             gradient, kept_ref[:, width:], weight_ref, grads_ref
@@ -454,7 +449,7 @@
         passed, gain_grad = norm_back(
             both_parts(own_ref, other_ref), normed, factor, gain_ref[2:3, :]
         )
-        gain_grad_ref[...] = 0.5 * gain_grad
+        gain_grad_ref[...] = gain_grad
         total = grad_ref[:, :width] + passed
         total_ref[...] = total
         grad_mixed = matmul(
@@ -716,7 +711,7 @@
         passed, gain_grad = norm_back(
             both_parts(own_ref, other_ref), normed, factor, gain_ref[3:4, :]
         )
-        gain_grad_ref[...] = 0.5 * gain_grad
+        gain_grad_ref[...] = gain_grad
         total = grad_ref[...] + passed
         grads_ref[:, :width] = total
         standard, _, shifted = batch_norm(conv_ref, sums_ref, batch_ref, count)
@@ -816,17 +811,15 @@
 
     def body(ins, outs, _):
         grad_ref, own_ref, other_ref, kept_ref, pre_ref, gain_ref, weight_ref = ins
-        grads_ref, keep_ref, send_ref, gain_grad_ref = outs
+        grads_ref, total_ref, part_ref, gain_grad_ref = outs
         normed, factor = norm_parts(kept_residual(kept_ref, width))
         passed, gain_grad = norm_back(
             both_parts(own_ref, other_ref), normed, factor, gain_ref[1:2, :]
         )
-        gain_grad_ref[...] = 0.5 * gain_grad
+        gain_grad_ref[...] = gain_grad
         total = grad_ref[...] + passed
-        keep_ref[:, :width] = own_half(total)
-        part = ff_back_body(total, pre_ref[...], weight_ref, grads_ref)
-        keep_ref[:, width:] = own_half(part)
-        send_ref[...] = other_half(part).astype(BF16)
+        total_ref[...] = total
+        part_ref[...] = ff_back_body(total, pre_ref[...], weight_ref, grads_ref).astype(BF16)
 
     return on_chip(
         body,
@@ -834,32 +827,32 @@
         (gradient, own, other, kept, pre, gains, weights),
         (
             ((rows, width + 2 * hidden), BF16),
-            ((rows // 2, 2 * width), F32),
-            ((rows // 2, width), BF16),
+            ((rows, width), F32),
+            ((rows, width), BF16),
             ((1, width), F32),
         ),
     )
 
 
-def input_back(keep, other, tokens, gains, gain_grads, tap_grads, bias_grads):
+def input_back(total, own, other, tokens, gains, gain_grads, tap_grads, bias_grads):
     rows, width = tokens.shape
     taps, columns = tap_grads.shape
     upper = (taps + 1) // 2
     packed_rows = 8 + -(-(1 + upper) // 8) * 8
 
     def body(ins, outs, _):
-        keep_ref, other_ref, x_ref, gain_ref = ins[:4]
-        tap_ref, bias_ref = ins[8:]
+        total_ref, own_ref, other_ref, x_ref, gain_ref = ins[:5]
+        tap_ref, bias_ref = ins[9:]
         packed = outs[1]
         normed, factor = norm_parts(x_ref[...].astype(F32))
         passed, gain_grad = norm_back(
-            keep_ref[:, width:] + other_ref[...].astype(F32), normed, factor, gain_ref[0:1, :]
-        )
-        outs[0][...] = keep_ref[:, :width] + passed
+            both_parts(own_ref, other_ref), normed, factor, gain_ref[0:1, :]
+        )
+        outs[0][...] = own_half(total_ref[...] + passed)
         packed[...] = jnp.zeros((packed_rows, 2 * columns), F32)
         packed[0:1, :] = gain_grad
         for place in range(4):
-            packed[place + 1 : place + 2, :] = ins[4 + place][...]
+            packed[place + 1 : place + 2, :] = ins[5 + place][...]
         packed[8:9, :columns] = bias_ref[0:1, :]
         packed[8:9, columns:] = bias_ref[1:2, :]
         packed[9 : 9 + upper, :columns] = tap_ref[:upper, :]
@@ -868,8 +861,8 @@
     return on_chip(
         body,
         "input_back",
-        (keep, other, tokens, gains) + tuple(gain_grads) + (tap_grads, bias_grads),
-        (((rows, width), F32), ((packed_rows, 2 * columns), F32)),
+        (total, own, other, tokens, gains) + tuple(gain_grads) + (tap_grads, bias_grads),
+        (((rows // 2, width), F32), ((packed_rows, 2 * columns), F32)),
         flops=1_000_000,
     )
 
@@ -1069,10 +1062,10 @@
         mixed_keeps, sends = scatter_add(keeps, scatter_send(sends, 0), 0, "mixed_sum")
         mixed_arrived = scatter_send(sends, 1)
         other7 = tie(other7, mixed_keeps)
-    first_rows, keep8, send8, gain2 = first_back(
+    first_rows, grad1, part8, gain2 = first_back(
         grad2, part7, other7, kept, pre1, norm_gains, first_weights
     )
-    other8 = swap(send8)
+    other8 = swap(part8)
     small = ((gain2, gain3, gain4, gain5), tap_grads, bias_grads)
     if split:
         mixed_keeps, sends = scatter_add(mixed_keeps, mixed_arrived, 1, "mixed_sum")
@@ -1091,23 +1084,22 @@
         )
         mixed_arrived = scatter_send(sends, 3)
         other8 = tie(other8, mixed_keeps)
-        grad_start, packed = input_back(keep8, other8, tokens, norm_gains, *small)
+        grad_start, packed = input_back(grad1, part8, other8, tokens_all, norm_gains, *small)
         first_arrived = tie(first_arrived, packed)
         first_keeps, sends = scatter_add(first_keeps, first_arrived, 1, "first_sum")
         first_arrived = scatter_send(sends, 2)
-        packed = jnp.concatenate([sum_over(packed[:8], "tensor"), packed[8:]], 0)
-        packed = sum_over(tie(packed, first_keeps), "dp", 1, 4)
+        packed = sum_over(tie(sum_over(packed, "dp", 1, 2), first_keeps), "dp", 2, 4)
         reduced_attention, reduced_mixing, reduced_gated, reduced_pointwise = mixed_finish(
             mixed_keeps, tie(mixed_arrived, first_keeps)
         )
-        first_arrived = tie(first_arrived, (reduced_mixing, packed))
+        first_arrived = tie(first_arrived, reduced_mixing)
         first_keeps, sends = scatter_add(first_keeps, first_arrived, 2, "first_sum")
         first_arrived = scatter_send(sends, 3)
         packed = tie(packed, first_keeps)
         parts = (packed,) + tuple(shift(packed, "dp", mask) for mask in (4, 8, 12))
         (reduced_in, reduced_out), _ = scatter_add(first_keeps, first_arrived, 3, "first_sum")
     else:
-        grad_start, packed = input_back(keep8, other8, tokens, norm_gains, *small)
+        grad_start, packed = input_back(grad1, part8, other8, tokens_all, norm_gains, *small)
         first_grads = reduce_plain(
             ff_weight_grads(first_rows, tokens_all, norm_gains, 0, "first_weight_grads")
         )
@@ -1117,7 +1109,6 @@
         reduced_mixing = mixed[:, 4 * columns : 5 * columns]
         reduced_gated = stacked_columns(mixed[:, 5 * columns : 7 * columns], 2)
         reduced_pointwise = mixed[:, 7 * columns :]
-        packed = jnp.concatenate([sum_over(packed[:8], "tensor"), packed[8:]], 0)
         packed = sum_over(packed, "dp")
         parts = (packed,) + (jnp.zeros_like(packed),) * 3
     gain_total, tap_total, bias_total = unpack_small(parts, depth_kernel.shape[0], columns)

time: 191 us -> 186 us (0.974)
  waiting for transfers between devices: 88.7 us -> 81.6 us
  starting transfers between devices: 67.2 us -> 69.5 us
    ppermute x53 -> x54, waiting for transfers between devices: 66.1 us -> 57.5 us  [shift(): lax.ppermute(value, axis, [(k, k ^ mask) for k in range(lax.axis_size(axi...]
    ppermute x53 -> x54, starting transfers between devices: 54.7 us -> 55.8 us  [shift(): lax.ppermute(value, axis, [(k, k ^ mask) for k in range(lax.axis_size(axi...]
  transfers between devices with their start and end apart: 63 -> 64, of which waited for: 39 -> 38; matrix products, arithmetic and copies ran while one was open for 2% -> 2% of each run, Pallas kernels for 8% -> 8%
where the time goes in v6:
time: 186 us
  waiting for transfers between devices  81.6 us (44%)
  starting transfers between devices  69.5 us (37%)
  Pallas kernels  28.7 us (15%)
  other arithmetic  2.61 us (1%)
  local copies, waits for them, and re-layouts  2.32 us (1%)
    ppermute x54, waiting for transfers between devices, shift(): lax.ppermute(value, axis, [(k, k ^ mask) for k in range(lax.axis_size(axi...  57.5 us
    ppermute x54, starting transfers between devices, shift(): lax.ppermute(value, axis, [(k, k ^ mask) for k in range(lax.axis_size(axi...  55.8 us
    pallas_call x40, Pallas kernels, on_chip(): pl.pallas_call(kernel, out_shape=[jax.ShapeDtypeStruct(shape, kind) for s...  28.7 us
    ppermute x10, waiting for transfers between devices, swap(): return lax.ppermute(value, 'tensor', [(0, 1), (1, 0)])  24.1 us
    ppermute x10, starting transfers between devices, swap(): return lax.ppermute(value, 'tensor', [(0, 1), (1, 0)])  13.6 us
  transfers between devices with their start and end apart: 64, of which 38 were waited for; matrix products, arithmetic and copies ran while one was open for 2% of the time, Pallas kernels for 8%

profile of v6, /device:TPU:0, one launch (start us, length us, event | category | flops | bytes accessed | tf_op | source)
XLA Modules:
  0.0 185.9 jit_solution(3741628346711842264)
XLA Ops:
  0.7 4.1 %collective-permute-start.1 = (bf16[32,1024]{1,0:T(8,128)(2,1)}, bf16[32,1024]{1,0:T(8,128)(2,1)S(1)}, u32[]{:S(2)}, u32[]{:S(2)}) collective-permute-start(bf16[32,1024]{1,0:T(8,128)(2,1)} %refs_0_.2), channel_id=1, source_target_pairs={{0,16},{2,18},{4,20},{6,22},{8,24},{10,26},{12,28},{14,30},{16,0},... | collective-permute-start | bytes 196616 | tf_op jit(solution)/shard_map/ppermute | solution.py:98
  4.8 1.8 collective-permute-start
  6.9 2.2 %multiply_sine_fusion = (bf16[512,256]{1,0:T(8,128)(2,1)S(1)}, bf16[512,256]{1,0:T(8,128)(2,1)S(1)}) fusion(f32[256]{0:T(256)S(1)} %multiply_exponential_fusion, f32[512]{0:T(512)S(1)} %iota_add_fusion), kind=kLoop, calls=%fused_computation.3 | loop fusion | flops 393216 | bytes 527360 | tf_op jit(solution)/shard_map/sin | solution.py:57
  11.5 1.6 collective-permute-start.3
  13.0 1.5 collective-permute-start.4
  14.6 1.9 collective-permute-done.3.refs_2_
  16.5 1.5 collective-permute-done.4.refs_3_
  18.1 1.6 collective-permute-start.5
  20.4 2.4 %collective-permute-start.7 = (bf16[256,256]{1,0:T(8,128)(2,1)S(1)}, bf16[256,256]{1,0:T(8,128)(2,1)S(1)}, u32[]{:S(2)}, u32[]{:S(2)}) collective-permute-start(bf16[256,256]{1,0:T(8,128)(2,1)S(1)} %pad_maximum_fusion.2), channel_id=1, source_target_pairs={{0,16},{2,18},{4,20},{6,22},{8,24},{10,26},{12,28},{14,30},{16,0},... | collective-permute-start | bytes 393224 | tf_op jit(solution)/shard_map/ppermute | solution.py:98
  22.8 4.5 %collective-permute-done.7.refs_2_ = bf16[256,256]{1,0:T(8,128)(2,1)S(1)} collective-permute-done((bf16[256,256]{1,0:T(8,128)(2,1)S(1)}, bf16[256,256]{1,0:T(8,128)(2,1)S(1)}, u32[]{:S(2)}, u32[]{:S(2)}) %collective-permute-start.7) | collective-permute-done | bytes 131104 | tf_op jit(solution)/shard_map/ppermute | solution.py:98
  28.6 3.3 %collective-permute-start.11 = (bf16[256,256]{1,0:T(8,128)(2,1)S(1)}, bf16[256,256]{1,0:T(8,128)(2,1)S(1)}, u32[]{:S(2)}, u32[]{:S(2)}) collective-permute-start(bf16[256,256]{1,0:T(8,128)(2,1)S(1)} %get-tuple-element.170.refs_0_), channel_id=1, source_target_pairs={{0,8},{2,10},{4,12},{6,14},{8,0},{10,2},{12,4},{14,6},{16,24},{18,... | collective-permute-start | bytes 393224 | tf_op jit(solution)/shard_map/ppermute | solution.py:98
  33.5 2.5 %collective-permute-done.11.refs_2_ = bf16[256,256]{1,0:T(8,128)(2,1)S(1)} collective-permute-done((bf16[256,256]{1,0:T(8,128)(2,1)S(1)}, bf16[256,256]{1,0:T(8,128)(2,1)S(1)}, u32[]{:S(2)}, u32[]{:S(2)}) %collective-permute-start.11) | collective-permute-done | bytes 131104 | tf_op jit(solution)/shard_map/ppermute | solution.py:98
  36.0 1.5 collective-permute-done.12.refs_3_
  38.4 1.5 collective-permute-start.10
  40.8 6.0 %collective-permute-done.15.refs_2_ = bf16[64,1024]{1,0:T(8,128)(2,1)S(1)} collective-permute-done((bf16[64,1024]{1,0:T(8,128)(2,1)S(1)}, bf16[64,1024]{1,0:T(8,128)(2,1)S(1)}, u32[]{:S(2)}, u32[]{:S(2)}) %collective-permute-start.15) | collective-permute-done | bytes 131104 | tf_op jit(solution)/shard_map/ppermute | solution.py:98
  46.8 1.4 collective-permute-done.14.refs_3_
  49.0 1.5 collective-permute-start.26
  51.5 3.3 %attention_forward.1 = (bf16[256,3328]{1,0:T(8,128)(2,1)S(1)}, bf16[256,512]{1,0:T(8,128)(2,1)S(1)}) custom-call(bf16[256,512]{1,0:T(8,128)(2,1)S(1)} %pad_maximum_fusion.refs_0_.refs_1_.refs_3_, bf16[256,512]{1,0:T(8,128)(2,1)S(1)} %get-tuple-element.174.refs_1_, bf16[256,512]{1,0:T(8,128)(2,1)S(1)} %collective-permute-done.10.refs_2_, ...), custom_call_target="tpu_custom_call" | custom-call | flops 300000000 | bytes 5124096 | tf_op jit(solution)/shard_map/attention_forward/pallas_call | solution.py:70
  54.8 1.6 collective-permute-start.17
  56.4 1.6 collective-permute-start.27
  58.6 4.6 %collective-permute-done.17.refs_2_ = bf16[256,512]{1,0:T(8,128)(2,1)S(1)} collective-permute-done((bf16[256,512]{1,0:T(8,128)(2,1)S(1)}, bf16[256,512]{1,0:T(8,128)(2,1)S(1)}, u32[]{:S(2)}, u32[]{:S(2)}) %collective-permute-start.17) | collective-permute-done | bytes 262176 | tf_op jit(solution)/shard_map/ppermute | solution.py:83
  63.2 1.9 %conv_forward.1 = (f32[256,1280]{1,0:T(8,128)S(1)}, f32[2,256]{1,0:T(2,128)S(1)}) custom-call(bf16[256,3328]{1,0:T(8,128)(2,1)S(1)} %get-tuple-element.187.refs_0_.refs_7_.refs_4_.refs_3_, bf16[256,512]{1,0:T(8,128)(2,1)S(1)} %get-tuple-element.188.refs_1_, bf16[256,512]{1,0:T(8,128)(2,1)S(1)} %collective-permute-done.17.refs_2_, f32[5,512]{1,0:T(8,128)S(1)} %copy-done, ...), custom_call_target="tpu_custom_call" | custom-call | flops 300000000 | bytes 5680128 | tf_op jit(solution)/shard_map/conv_forward/pallas_call | solution.py:70
  68.6 1.4 collective-permute-done.19
  71.0 1.3 collective-permute-start.22
  72.2 2.5 %collective-permute-start.23 = (f32[2,256]{1,0:T(2,128)S(1)}, f32[2,256]{1,0:T(2,128)S(1)}, u32[]{:S(2)}, u32[]{:S(2)}) collective-permute-start(f32[2,256]{1,0:T(2,128)S(1)} %add_add_fusion.3), channel_id=1, source_target_pairs={{0,24},{2,26},{4,28},{6,30},{8,16},{10,18},{12,20},{14,22},{16,8},... | collective-permute-start | bytes 6152 | tf_op jit(solution)/shard_map/ppermute | solution.py:98
  75.5 2.2 %collective-permute-done.23 = f32[2,256]{1,0:T(2,128)S(1)} collective-permute-done((f32[2,256]{1,0:T(2,128)S(1)}, f32[2,256]{1,0:T(2,128)S(1)}, u32[]{:S(2)}, u32[]{:S(2)}) %collective-permute-start.23) | collective-permute-done | bytes 2080 | tf_op jit(solution)/shard_map/ppermute | solution.py:98
  77.9 1.3 collective-permute-start.24
  79.4 4.9 %collective-permute-done.24.refs_2_ = bf16[256,512]{1,0:T(8,128)(2,1)S(1)} collective-permute-done((bf16[256,512]{1,0:T(8,128)(2,1)S(1)}, bf16[256,512]{1,0:T(8,128)(2,1)S(1)}, u32[]{:S(2)}, u32[]{:S(2)}) %collective-permute-start.24) | collective-permute-done | bytes 262176 | tf_op jit(solution)/shard_map/ppermute | solution.py:83
  85.3 1.5 collective-permute-start.30
  86.9 4.9 %collective-permute-done.30.refs_2_ = bf16[256,512]{1,0:T(8,128)(2,1)S(1)} collective-permute-done((bf16[256,512]{1,0:T(8,128)(2,1)S(1)}, bf16[256,512]{1,0:T(8,128)(2,1)S(1)}, u32[]{:S(2)}, u32[]{:S(2)}) %collective-permute-start.30) | collective-permute-done | bytes 262176 | tf_op jit(solution)/shard_map/ppermute | solution.py:83
  91.8 1.8 second_back.1
  93.6 1.3 second_weight_grads.1
  94.9 1.5 collective-permute-start.31
  98.0 5.7 %collective-permute-done.31.refs_2_ = bf16[256,512]{1,0:T(8,128)(2,1)S(1)} collective-permute-done((bf16[256,512]{1,0:T(8,128)(2,1)S(1)}, bf16[256,512]{1,0:T(8,128)(2,1)S(1)}, u32[]{:S(2)}, u32[]{:S(2)}) %collective-permute-start.31) | collective-permute-done | bytes 262176 | tf_op jit(solution)/shard_map/ppermute | solution.py:83
  104.3 1.1 collective-permute-start.34
  109.4 2.2 %collective-permute-start.37 = (f32[2,256]{1,0:T(2,128)S(1)}, f32[2,256]{1,0:T(2,128)S(1)}, u32[]{:S(2)}, u32[]{:S(2)}) collective-permute-start(f32[2,256]{1,0:T(2,128)S(1)} %add_add_fusion.1), channel_id=1, source_target_pairs={{0,16},{2,18},{4,20},{6,22},{8,24},{10,26},{12,28},{14,30},{16,0},... | collective-permute-start | bytes 6152 | tf_op jit(solution)/shard_map/ppermute | solution.py:98
  111.6 1.3 collective-permute-start.38
  112.9 2.8 %collective-permute-done.36 = f32[2,256]{1,0:T(2,128)S(1)} collective-permute-done((f32[2,256]{1,0:T(2,128)S(1)}, f32[2,256]{1,0:T(2,128)S(1)}, u32[]{:S(2)}, u32[]{:S(2)}) %collective-permute-start.36) | collective-permute-done | bytes 2080 | tf_op jit(solution)/shard_map/ppermute | solution.py:98
  115.7 1.4 collective-permute-done.38
  117.2 1.6 conv_backward.1
  118.8 1.3 collective-permute-start.41
  120.1 1.2 collective-permute-start.43
  121.3 2.1 %conv_weight_grads.1 = (bf16[512,768]{1,0:T(8,128)(2,1)S(1)}, f32[31,256]{1,0:T(8,128)S(1)}) custom-call(f32[256,768]{1,0:T(8,128)S(1)} %get-tuple-element.210.refs_0_, f32[256,256]{1,0:T(8,128)S(1)} %get-tuple-element.218.refs_1_, bf16[256,512]{1,0:T(8,128)(2,1)S(1)} %get-tuple-element.219.refs_2_, ...), custom_call_target="tpu_custom_call" | custom-call | flops 300000000 | bytes 3453952 | tf_op jit(solution)/shard_map/conv_weight_grads/pallas_call | solution.py:70
  123.5 1.6 collective-permute-done.42.refs_2_
  125.8 3.6 %attention_back.1 = (f32[256,512]{1,0:T(8,128)S(1)}, bf16[256,768]{1,0:T(8,128)(2,1)S(1)}, bf16[512,256]{1,0:T(8,128)(2,1)S(1)}, bf16[256,512]{1,0:T(8,128)(2,1)...) custom-call(f32[256,768]{1,0:T(8,128)S(1)} %get-tuple-element.210.refs_0_, ...), custom_call_target="tpu_custom_call" | custom-call | flops 300000000 | bytes 8140800 | tf_op jit(solution)/shard_map/attention_back/pallas_call | solution.py:70
  130.7 1.3 collective-permute-start.44
  132.0 1.4 collective-permute-done.45.refs_2_
  134.6 1.6 collective-permute-start.48
  136.2 3.3 %collective-permute-done.44.refs_2_ = bf16[256,512]{1,0:T(8,128)(2,1)S(1)} collective-permute-done((bf16[256,512]{1,0:T(8,128)(2,1)S(1)}, bf16[256,512]{1,0:T(8,128)(2,1)S(1)}, u32[]{:S(2)}, u32[]{:S(2)}) %collective-permute-start.44) | collective-permute-done | bytes 262176 | tf_op jit(solution)/shard_map/ppermute | solution.py:83
  139.4 1.2 first_back.1
  140.7 1.3 collective-permute-done.47.refs_2_
  142.7 1.5 first_weight_grads.1
  144.3 1.6 collective-permute-start.46
  147.1 1.2 collective-permute-start.53
  148.3 1.3 collective-permute-start.54
  151.2 8.0 %collective-permute-done.49.refs_2_ = bf16[256,256]{1,0:T(8,128)(2,1)S(1)} collective-permute-done((bf16[256,256]{1,0:T(8,128)(2,1)S(1)}, bf16[256,256]{1,0:T(8,128)(2,1)S(1)}, u32[]{:S(2)}, u32[]{:S(2)}) %collective-permute-start.49) | collective-permute-done | bytes 131104 | tf_op jit(solution)/shard_map/ppermute | solution.py:98
  159.3 1.3 collective-permute-start.58
  163.8 1.2 collective-permute-start.55
  165.0 1.9 %collective-permute-start.63 = (bf16[64,1024]{1,0:T(8,128)(2,1)S(1)}, bf16[64,1024]{1,0:T(8,128)(2,1)S(1)}, u32[]{:S(2)}, u32[]{:S(2)}) collective-permute-start(bf16[64,1024]{1,0:T(8,128)(2,1)S(1)} %get-tuple-element.297), channel_id=1, source_target_pairs={{0,16},{2,18},{4,20},{6,22},{8,24},{10,26},{12,28},{14,30},{16,0},... | collective-permute-start | bytes 393224 | tf_op jit(solution)/shard_map/ppermute | solution.py:98
  168.2 1.7 collective-permute-done.55
  171.1 2.3 %collective-permute-start.60 = (f32[32,512]{1,0:T(8,128)S(1)}, f32[32,512]{1,0:T(8,128)S(1)}, u32[]{:S(2)}, u32[]{:S(2)}) collective-permute-start(f32[32,512]{1,0:T(8,128)S(1)} %add.63.refs_0_), channel_id=1, source_target_pairs={{0,16},{2,18},{4,20},{6,22},{8,24},{10,26},{12,28},{14,30},{16,0},... | collective-permute-start | bytes 196616 | tf_op jit(solution)/shard_map/ppermute | solution.py:98
  173.4 1.1 collective-permute-start.61
  176.8 5.0 %collective-permute-done.60.refs_2_ = f32[32,512]{1,0:T(8,128)S(1)} collective-permute-done((f32[32,512]{1,0:T(8,128)S(1)}, f32[32,512]{1,0:T(8,128)S(1)}, u32[]{:S(2)}, u32[]{:S(2)}) %collective-permute-start.60) | collective-permute-done | bytes 65568 | tf_op jit(solution)/shard_map/ppermute | solution.py:98
  182.5 2.6 %collective-permute-done.62.refs_2_ = bf16[64,1024]{1,0:T(8,128)(2,1)S(1)} collective-permute-done((bf16[64,1024]{1,0:T(8,128)(2,1)S(1)}, bf16[64,1024]{1,0:T(8,128)(2,1)S(1)}, u32[]{:S(2)}, u32[]{:S(2)}) %collective-permute-start.62) | collective-permute-done | bytes 131104 | tf_op jit(solution)/shard_map/ppermute | solution.py:98
  (153 shorter events, 39.5 us)
Async XLA Ops:
  0.7 10.4 %collective-permute-start.1 = (bf16[32,1024]{1,0:T(8,128)(2,1)}, bf16[32,1024]{1,0:T(8,128)(2,1)S(1)}, u32[]{:S(2)}, u32[]{:S(2)}) collective-permute-start(bf16[32,1024]{1,0:T(8,128)(2,1)} %refs_0_.2), channel_id=1, source_target_pairs={{0,16},{2,18},{4,20},{6,22},{8,24},{10,26},{12,28},{14,30},{16,0},... | collective-permute-start | bytes 196616 | tf_op jit(solution)/shard_map/ppermute | solution.py:98
  4.8 6.7 %collective-permute-start.2 = (bf16[32,1024]{1,0:T(8,128)(2,1)}, bf16[32,1024]{1,0:T(8,128)(2,1)S(1)}, u32[]{:S(2)}, u32[]{:S(2)}) collective-permute-start(bf16[32,1024]{1,0:T(8,128)(2,1)} %refs_1_.3), channel_id=1, source_target_pairs={{0,16},{2,18},{4,20},{6,22},{8,24},{10,26},{12,28},{14,30},{16,0},... | collective-permute-start | bytes 196616 | tf_op jit(solution)/shard_map/ppermute | solution.py:98
  4.8 9.7 %collective-permute-start = (bf16[128,512]{1,0:T(8,128)(2,1)}, bf16[128,512]{1,0:T(8,128)(2,1)S(1)}, u32[]{:S(2)}, u32[]{:S(2)}) collective-permute-start(bf16[128,512]{1,0:T(8,128)(2,1)} %param.15), channel_id=1, source_target_pairs={{0,1},{1,0},{2,3},{3,2},{4,5},{5,4},{6,7},{7,6},{8,9},{9,8},{10,11... | collective-permute-start | bytes 393224 | tf_op jit(solution)/shard_map/ppermute | solution.py:83
  6.6 7.9 %collective-permute-start.8 = (bf16[128,512]{1,0:T(8,128)(2,1)}, bf16[128,512]{1,0:T(8,128)(2,1)S(1)}, u32[]{:S(2)}, u32[]{:S(2)}) collective-permute-start(bf16[128,512]{1,0:T(8,128)(2,1)} %param.29), channel_id=1, source_target_pairs={{0,1},{1,0},{2,3},{3,2},{4,5},{5,4},{6,7},{7,6},{8,9},{9,8},{10,11... | collective-permute-start | bytes 393224 | tf_op jit(solution)/shard_map/ppermute | solution.py:83
  11.5 5.0 %collective-permute-start.3 = (bf16[64,1024]{1,0:T(8,128)(2,1)S(1)}, bf16[64,1024]{1,0:T(8,128)(2,1)S(1)}, u32[]{:S(2)}, u32[]{:S(2)}) collective-permute-start(bf16[64,1024]{1,0:T(8,128)(2,1)S(1)} %get-tuple-element.162.refs_0_), channel_id=1, source_target_pairs={{0,8},{2,10},{4,12},{6,14},{8,0},{10,2},{12,4},{14,6},{16,24},{18,... | collective-permute-start | bytes 393224 | tf_op jit(solution)/shard_map/ppermute | solution.py:98
  13.0 5.0 %collective-permute-start.4 = (bf16[64,1024]{1,0:T(8,128)(2,1)S(1)}, bf16[64,1024]{1,0:T(8,128)(2,1)S(1)}, u32[]{:S(2)}, u32[]{:S(2)}) collective-permute-start(bf16[64,1024]{1,0:T(8,128)(2,1)S(1)} %get-tuple-element.163.refs_1_), channel_id=1, source_target_pairs={{0,4},{2,6},{4,0},{6,2},{8,12},{10,14},{12,8},{14,10},{16,20},{18,... | collective-permute-start | bytes 393224 | tf_op jit(solution)/shard_map/ppermute | solution.py:98
  18.1 9.2 %collective-permute-start.5 = (bf16[128,1024]{1,0:T(8,128)(2,1)S(1)}, bf16[128,1024]{1,0:T(8,128)(2,1)S(1)}, u32[]{:S(2)}, u32[]{:S(2)}) collective-permute-start(bf16[128,1024]{1,0:T(8,128)(2,1)S(1)} %get-tuple-element.166.refs_0_), channel_id=1, source_target_pairs={{0,4},{2,6},{4,0},{6,2},{8,12},{10,14},{12,8},{14,10},{16,20},{18,... | collective-permute-start | bytes 786440 | tf_op jit(solution)/shard_map/ppermute | solution.py:98
  19.6 8.8 %collective-permute-start.6 = (bf16[128,1024]{1,0:T(8,128)(2,1)S(1)}, bf16[128,1024]{1,0:T(8,128)(2,1)S(1)}, u32[]{:S(2)}, u32[]{:S(2)}) collective-permute-start(bf16[128,1024]{1,0:T(8,128)(2,1)S(1)} %get-tuple-element.167.refs_1_), channel_id=1, source_target_pairs={{0,8},{2,10},{4,12},{6,14},{8,0},{10,2},{12,4},{14,6},{16,24},{18,... | collective-permute-start | bytes 786440 | tf_op jit(solution)/shard_map/ppermute | solution.py:98
  20.4 6.9 %collective-permute-start.7 = (bf16[256,256]{1,0:T(8,128)(2,1)S(1)}, bf16[256,256]{1,0:T(8,128)(2,1)S(1)}, u32[]{:S(2)}, u32[]{:S(2)}) collective-permute-start(bf16[256,256]{1,0:T(8,128)(2,1)S(1)} %pad_maximum_fusion.2), channel_id=1, source_target_pairs={{0,16},{2,18},{4,20},{6,22},{8,24},{10,26},{12,28},{14,30},{16,0},... | collective-permute-start | bytes 393224 | tf_op jit(solution)/shard_map/ppermute | solution.py:98
  28.5 3.9 %collective-permute-start.9 = (bf16[512,1024]{1,0:T(8,128)(2,1)S(1)}, bf16[512,1024]{1,0:T(8,128)(2,1)S(1)}, u32[]{:S(2)}, u32[]{:S(2)}) collective-permute-start(bf16[512,1024]{1,0:T(8,128)(2,1)S(1)} %gather_join.12.refs_2_), channel_id=1, source_target_pairs={{0,2},{2,0},{4,6},{6,4},{8,10},{10,8},{12,14},{14,12},{16,18},{18,... | collective-permute-start | bytes 3145736 | tf_op jit(solution)/shard_map/ppermute | solution.py:98
  28.6 7.4 %collective-permute-start.11 = (bf16[256,256]{1,0:T(8,128)(2,1)S(1)}, bf16[256,256]{1,0:T(8,128)(2,1)S(1)}, u32[]{:S(2)}, u32[]{:S(2)}) collective-permute-start(bf16[256,256]{1,0:T(8,128)(2,1)S(1)} %get-tuple-element.170.refs_0_), channel_id=1, source_target_pairs={{0,8},{2,10},{4,12},{6,14},{8,0},{10,2},{12,4},{14,6},{16,24},{18,... | collective-permute-start | bytes 393224 | tf_op jit(solution)/shard_map/ppermute | solution.py:98
  31.9 5.6 %collective-permute-start.12 = (bf16[256,256]{1,0:T(8,128)(2,1)S(1)}, bf16[256,256]{1,0:T(8,128)(2,1)S(1)}, u32[]{:S(2)}, u32[]{:S(2)}) collective-permute-start(bf16[256,256]{1,0:T(8,128)(2,1)S(1)} %get-tuple-element.171.refs_1_), channel_id=1, source_target_pairs={{0,4},{2,6},{4,0},{6,2},{8,12},{10,14},{12,8},{14,10},{16,20},{18,... | collective-permute-start | bytes 393224 | tf_op jit(solution)/shard_map/ppermute | solution.py:98
  37.5 9.3 %collective-permute-start.13 = (bf16[512,256]{1,0:T(8,128)(2,1)S(1)}, bf16[512,256]{1,0:T(8,128)(2,1)S(1)}, u32[]{:S(2)}, u32[]{:S(2)}) collective-permute-start(bf16[512,256]{1,0:T(8,128)(2,1)S(1)} %get-tuple-element.177.refs_0_), channel_id=1, source_target_pairs={{0,4},{2,6},{4,0},{6,2},{8,12},{10,14},{12,8},{14,10},{16,20},{18,... | collective-permute-start | bytes 786440 | tf_op jit(solution)/shard_map/ppermute | solution.py:98
  38.1 10.1 %collective-permute-start.14 = (bf16[512,256]{1,0:T(8,128)(2,1)S(1)}, bf16[512,256]{1,0:T(8,128)(2,1)S(1)}, u32[]{:S(2)}, u32[]{:S(2)}) collective-permute-start(bf16[512,256]{1,0:T(8,128)(2,1)S(1)} %get-tuple-element.178.refs_1_), channel_id=1, source_target_pairs={{0,8},{2,10},{4,12},{6,14},{8,0},{10,2},{12,4},{14,6},{16,24},{18,... | collective-permute-start | bytes 786440 | tf_op jit(solution)/shard_map/ppermute | solution.py:98
  38.4 9.8 %collective-permute-start.10 = (bf16[256,512]{1,0:T(8,128)(2,1)S(1)}, bf16[256,512]{1,0:T(8,128)(2,1)S(1)}, u32[]{:S(2)}, u32[]{:S(2)}) collective-permute-start(bf16[256,512]{1,0:T(8,128)(2,1)S(1)} %get-tuple-element.174.refs_1_), channel_id=1, source_target_pairs={{0,1},{1,0},{2,3},{3,2},{4,5},{5,4},{6,7},{7,6},{8,9},{9,8},{10,11... | collective-permute-start | bytes 786440 | tf_op jit(solution)/shard_map/ppermute | solution.py:83
  39.9 6.9 %collective-permute-start.15 = (bf16[64,1024]{1,0:T(8,128)(2,1)S(1)}, bf16[64,1024]{1,0:T(8,128)(2,1)S(1)}, u32[]{:S(2)}, u32[]{:S(2)}) collective-permute-start(bf16[64,1024]{1,0:T(8,128)(2,1)S(1)} %pad_maximum_fusion.3), channel_id=1, source_target_pairs={{0,16},{2,18},{4,20},{6,22},{8,24},{10,26},{12,28},{14,30},{16,0},... | collective-permute-start | bytes 393224 | tf_op jit(solution)/shard_map/ppermute | solution.py:98
  48.3 2.7 %collective-permute-start.16 = (bf16[2048,256]{1,0:T(8,128)(2,1)S(1)}, bf16[2048,256]{1,0:T(8,128)(2,1)S(1)}, u32[]{:S(2)}, u32[]{:S(2)}) collective-permute-start(bf16[2048,256]{1,0:T(8,128)(2,1)S(1)} %gather_join.15.refs_0_), channel_id=1, source_target_pairs={{0,2},{2,0},{4,6},{6,4},{8,10},{10,8},{12,14},{14,12},{16,18},{18,... | collective-permute-start | bytes 3145736 | tf_op jit(solution)/shard_map/ppermute | solution.py:98
  48.4 8.0 %collective-permute-start.25 = (bf16[64,1024]{1,0:T(8,128)(2,1)S(1)}, bf16[64,1024]{1,0:T(8,128)(2,1)S(1)}, u32[]{:S(2)}, u32[]{:S(2)}) collective-permute-start(bf16[64,1024]{1,0:T(8,128)(2,1)S(1)} %get-tuple-element.181.refs_0_), channel_id=1, source_target_pairs={{0,8},{2,10},{4,12},{6,14},{8,0},{10,2},{12,4},{14,6},{16,24},{18,... | collective-permute-start | bytes 393224 | tf_op jit(solution)/shard_map/ppermute | solution.py:98
  49.0 7.4 %collective-permute-start.26 = (bf16[64,1024]{1,0:T(8,128)(2,1)S(1)}, bf16[64,1024]{1,0:T(8,128)(2,1)S(1)}, u32[]{:S(2)}, u32[]{:S(2)}) collective-permute-start(bf16[64,1024]{1,0:T(8,128)(2,1)S(1)} %get-tuple-element.182.refs_1_), channel_id=1, source_target_pairs={{0,4},{2,6},{4,0},{6,2},{8,12},{10,14},{12,8},{14,10},{16,20},{18,... | collective-permute-start | bytes 393224 | tf_op jit(solution)/shard_map/ppermute | solution.py:98
  54.8 8.4 %collective-permute-start.17 = (bf16[256,512]{1,0:T(8,128)(2,1)S(1)}, bf16[256,512]{1,0:T(8,128)(2,1)S(1)}, u32[]{:S(2)}, u32[]{:S(2)}) collective-permute-start(bf16[256,512]{1,0:T(8,128)(2,1)S(1)} %get-tuple-element.188.refs_1_), channel_id=1, source_target_pairs={{0,1},{1,0},{2,3},{3,2},{4,5},{5,4},{6,7},{7,6},{8,9},{9,8},{10,11... | collective-permute-start | bytes 786440 | tf_op jit(solution)/shard_map/ppermute | solution.py:83
  56.4 8.7 %collective-permute-start.27 = (bf16[128,1024]{1,0:T(8,128)(2,1)S(1)}, bf16[128,1024]{1,0:T(8,128)(2,1)S(1)}, u32[]{:S(2)}, u32[]{:S(2)}) collective-permute-start(bf16[128,1024]{1,0:T(8,128)(2,1)S(1)} %get-tuple-element.193.refs_0_), channel_id=1, source_target_pairs={{0,4},{2,6},{4,0},{6,2},{8,12},{10,14},{12,8},{14,10},{16,20},{18,... | collective-permute-start | bytes 786440 | tf_op jit(solution)/shard_map/ppermute | solution.py:98
  58.0 7.8 %collective-permute-start.28 = (bf16[128,1024]{1,0:T(8,128)(2,1)S(1)}, bf16[128,1024]{1,0:T(8,128)(2,1)S(1)}, u32[]{:S(2)}, u32[]{:S(2)}) collective-permute-start(bf16[128,1024]{1,0:T(8,128)(2,1)S(1)} %get-tuple-element.194.refs_1_), channel_id=1, source_target_pairs={{0,8},{2,10},{4,12},{6,14},{8,0},{10,2},{12,4},{14,6},{16,24},{18,... | collective-permute-start | bytes 786440 | tf_op jit(solution)/shard_map/ppermute | solution.py:98
  65.9 13.4 %collective-permute-start.29 = (bf16[512,1024]{1,0:T(8,128)(2,1)S(1)}, bf16[512,1024]{1,0:T(8,128)(2,1)S(1)}, u32[]{:S(2)}, u32[]{:S(2)}) collective-permute-start(bf16[512,1024]{1,0:T(8,128)(2,1)S(1)} %gather_join.17.refs_0_), channel_id=1, source_target_pairs={{0,2},{2,0},{4,6},{6,4},{8,10},{10,8},{12,14},{14,12},{16,18},{18,... | collective-permute-start | bytes 3145736 | tf_op jit(solution)/shard_map/ppermute | solution.py:98
  65.9 2.6 %collective-permute-start.18 = (f32[2,256]{1,0:T(2,128)S(1)}, f32[2,256]{1,0:T(2,128)S(1)}, u32[]{:S(2)}, u32[]{:S(2)}) collective-permute-start(f32[2,256]{1,0:T(2,128)S(1)} %get-tuple-element.190), channel_id=1, source_target_pairs={{0,2},{2,0},{4,6},{6,4},{8,10},{10,8},{12,14},{14,12},{16,18},{18,... | collective-permute-start | bytes 6152 | tf_op jit(solution)/shard_map/ppermute | solution.py:98
  66.4 3.6 %collective-permute-start.19 = (f32[2,256]{1,0:T(2,128)S(1)}, f32[2,256]{1,0:T(2,128)S(1)}, u32[]{:S(2)}, u32[]{:S(2)}) collective-permute-start(f32[2,256]{1,0:T(2,128)S(1)} %get-tuple-element.190), channel_id=1, source_target_pairs={{0,4},{2,6},{4,0},{6,2},{8,12},{10,14},{12,8},{14,10},{16,20},{18,... | collective-permute-start | bytes 6152 | tf_op jit(solution)/shard_map/ppermute | solution.py:98
  67.3 3.0 %collective-permute-start.20 = (f32[2,256]{1,0:T(2,128)S(1)}, f32[2,256]{1,0:T(2,128)S(1)}, u32[]{:S(2)}, u32[]{:S(2)}) collective-permute-start(f32[2,256]{1,0:T(2,128)S(1)} %get-tuple-element.190), channel_id=1, source_target_pairs={{0,6},{2,4},{4,2},{6,0},{8,14},{10,12},{12,10},{14,8},{16,22},{18,... | collective-permute-start | bytes 6152 | tf_op jit(solution)/shard_map/ppermute | solution.py:98
  70.4 4.4 %collective-permute-start.21 = (f32[2,256]{1,0:T(2,128)S(1)}, f32[2,256]{1,0:T(2,128)S(1)}, u32[]{:S(2)}, u32[]{:S(2)}) collective-permute-start(f32[2,256]{1,0:T(2,128)S(1)} %add_add_fusion.3), channel_id=1, source_target_pairs={{0,8},{2,10},{4,12},{6,14},{8,0},{10,2},{12,4},{14,6},{16,24},{18,... | collective-permute-start | bytes 6152 | tf_op jit(solution)/shard_map/ppermute | solution.py:98
  71.0 4.5 %collective-permute-start.22 = (f32[2,256]{1,0:T(2,128)S(1)}, f32[2,256]{1,0:T(2,128)S(1)}, u32[]{:S(2)}, u32[]{:S(2)}) collective-permute-start(f32[2,256]{1,0:T(2,128)S(1)} %add_add_fusion.3), channel_id=1, source_target_pairs={{0,16},{2,18},{4,20},{6,22},{8,24},{10,26},{12,28},{14,30},{16,0},... | collective-permute-start | bytes 6152 | tf_op jit(solution)/shard_map/ppermute | solution.py:98
  72.2 5.4 %collective-permute-start.23 = (f32[2,256]{1,0:T(2,128)S(1)}, f32[2,256]{1,0:T(2,128)S(1)}, u32[]{:S(2)}, u32[]{:S(2)}) collective-permute-start(f32[2,256]{1,0:T(2,128)S(1)} %add_add_fusion.3), channel_id=1, source_target_pairs={{0,24},{2,26},{4,28},{6,30},{8,16},{10,18},{12,20},{14,22},{16,8},... | collective-permute-start | bytes 6152 | tf_op jit(solution)/shard_map/ppermute | solution.py:98
  77.9 6.4 %collective-permute-start.24 = (bf16[256,512]{1,0:T(8,128)(2,1)S(1)}, bf16[256,512]{1,0:T(8,128)(2,1)S(1)}, u32[]{:S(2)}, u32[]{:S(2)}) collective-permute-start(bf16[256,512]{1,0:T(8,128)(2,1)S(1)} %norm_forward.1.refs_1_), channel_id=1, source_target_pairs={{0,1},{1,0},{2,3},{3,2},{4,5},{5,4},{6,7},{7,6},{8,9},{9,8},{10,11... | collective-permute-start | bytes 786440 | tf_op jit(solution)/shard_map/ppermute | solution.py:83
  85.3 6.4 %collective-permute-start.30 = (bf16[256,512]{1,0:T(8,128)(2,1)S(1)}, bf16[256,512]{1,0:T(8,128)(2,1)S(1)}, u32[]{:S(2)}, u32[]{:S(2)}) collective-permute-start(bf16[256,512]{1,0:T(8,128)(2,1)S(1)} %get-tuple-element.199.refs_1_), channel_id=1, source_target_pairs={{0,1},{1,0},{2,3},{3,2},{4,5},{5,4},{6,7},{7,6},{8,9},{9,8},{10,11... | collective-permute-start | bytes 786440 | tf_op jit(solution)/shard_map/ppermute | solution.py:83
  94.8 2.7 %collective-permute-start.32 = (bf16[512,1024]{1,0:T(8,128)(2,1)S(1)}, bf16[512,1024]{1,0:T(8,128)(2,1)S(1)}, u32[]{:S(2)}, u32[]{:S(2)}) collective-permute-start(bf16[512,1024]{1,0:T(8,128)(2,1)S(1)} %get-tuple-element.206), channel_id=1, source_target_pairs={{0,2},{2,0},{4,6},{6,4},{8,10},{10,8},{12,14},{14,12},{16,18},{18,... | collective-permute-start | bytes 3145736 | tf_op jit(solution)/shard_map/ppermute | solution.py:98
  94.9 8.7 %collective-permute-start.31 = (bf16[256,512]{1,0:T(8,128)(2,1)S(1)}, bf16[256,512]{1,0:T(8,128)(2,1)S(1)}, u32[]{:S(2)}, u32[]{:S(2)}) collective-permute-start(bf16[256,512]{1,0:T(8,128)(2,1)S(1)} %get-tuple-element.202.refs_1_), channel_id=1, source_target_pairs={{0,1},{1,0},{2,3},{3,2},{4,5},{5,4},{6,7},{7,6},{8,9},{9,8},{10,11... | collective-permute-start | bytes 786440 | tf_op jit(solution)/shard_map/ppermute | solution.py:83
  104.3 3.0 %collective-permute-start.33 = (f32[2,256]{1,0:T(2,128)S(1)}, f32[2,256]{1,0:T(2,128)S(1)}, u32[]{:S(2)}, u32[]{:S(2)}) collective-permute-start(f32[2,256]{1,0:T(2,128)S(1)} %get-tuple-element.211), channel_id=1, source_target_pairs={{0,2},{2,0},{4,6},{6,4},{8,10},{10,8},{12,14},{14,12},{16,18},{18,... | collective-permute-start | bytes 6152 | tf_op jit(solution)/shard_map/ppermute | solution.py:98
  104.3 3.7 %collective-permute-start.34 = (f32[2,256]{1,0:T(2,128)S(1)}, f32[2,256]{1,0:T(2,128)S(1)}, u32[]{:S(2)}, u32[]{:S(2)}) collective-permute-start(f32[2,256]{1,0:T(2,128)S(1)} %get-tuple-element.211), channel_id=1, source_target_pairs={{0,4},{2,6},{4,0},{6,2},{8,12},{10,14},{12,8},{14,10},{16,20},{18,... | collective-permute-start | bytes 6152 | tf_op jit(solution)/shard_map/ppermute | solution.py:98
  105.5 3.0 %collective-permute-start.35 = (f32[2,256]{1,0:T(2,128)S(1)}, f32[2,256]{1,0:T(2,128)S(1)}, u32[]{:S(2)}, u32[]{:S(2)}) collective-permute-start(f32[2,256]{1,0:T(2,128)S(1)} %get-tuple-element.211), channel_id=1, source_target_pairs={{0,6},{2,4},{4,2},{6,0},{8,14},{10,12},{12,10},{14,8},{16,22},{18,... | collective-permute-start | bytes 6152 | tf_op jit(solution)/shard_map/ppermute | solution.py:98
  106.2 10.8 %collective-permute-start.39 = (bf16[128,1024]{1,0:T(8,128)(2,1)S(1)}, bf16[128,1024]{1,0:T(8,128)(2,1)S(1)}, u32[]{:S(2)}, u32[]{:S(2)}) collective-permute-start(bf16[128,1024]{1,0:T(8,128)(2,1)S(1)} %get-tuple-element.212), channel_id=1, source_target_pairs={{0,4},{2,6},{4,0},{6,2},{8,12},{10,14},{12,8},{14,10},{16,20},{18,... | collective-permute-start | bytes 786440 | tf_op jit(solution)/shard_map/ppermute | solution.py:98
  107.3 9.8 %collective-permute-start.40 = (bf16[128,1024]{1,0:T(8,128)(2,1)S(1)}, bf16[128,1024]{1,0:T(8,128)(2,1)S(1)}, u32[]{:S(2)}, u32[]{:S(2)}) collective-permute-start(bf16[128,1024]{1,0:T(8,128)(2,1)S(1)} %get-tuple-element.213), channel_id=1, source_target_pairs={{0,8},{2,10},{4,12},{6,14},{8,0},{10,2},{12,4},{14,6},{16,24},{18,... | collective-permute-start | bytes 786440 | tf_op jit(solution)/shard_map/ppermute | solution.py:98
  108.5 7.1 %collective-permute-start.36 = (f32[2,256]{1,0:T(2,128)S(1)}, f32[2,256]{1,0:T(2,128)S(1)}, u32[]{:S(2)}, u32[]{:S(2)}) collective-permute-start(f32[2,256]{1,0:T(2,128)S(1)} %add_add_fusion.1), channel_id=1, source_target_pairs={{0,8},{2,10},{4,12},{6,14},{8,0},{10,2},{12,4},{14,6},{16,24},{18,... | collective-permute-start | bytes 6152 | tf_op jit(solution)/shard_map/ppermute | solution.py:98
  109.4 6.2 %collective-permute-start.37 = (f32[2,256]{1,0:T(2,128)S(1)}, f32[2,256]{1,0:T(2,128)S(1)}, u32[]{:S(2)}, u32[]{:S(2)}) collective-permute-start(f32[2,256]{1,0:T(2,128)S(1)} %add_add_fusion.1), channel_id=1, source_target_pairs={{0,16},{2,18},{4,20},{6,22},{8,24},{10,26},{12,28},{14,30},{16,0},... | collective-permute-start | bytes 6152 | tf_op jit(solution)/shard_map/ppermute | solution.py:98
  111.6 5.4 %collective-permute-start.38 = (f32[2,256]{1,0:T(2,128)S(1)}, f32[2,256]{1,0:T(2,128)S(1)}, u32[]{:S(2)}, u32[]{:S(2)}) collective-permute-start(f32[2,256]{1,0:T(2,128)S(1)} %add_add_fusion.1), channel_id=1, source_target_pairs={{0,24},{2,26},{4,28},{6,30},{8,16},{10,18},{12,20},{14,22},{16,8},... | collective-permute-start | bytes 6152 | tf_op jit(solution)/shard_map/ppermute | solution.py:98
  118.8 7.0 %collective-permute-start.41 = (bf16[256,512]{1,0:T(8,128)(2,1)S(1)}, bf16[256,512]{1,0:T(8,128)(2,1)S(1)}, u32[]{:S(2)}, u32[]{:S(2)}) collective-permute-start(bf16[256,512]{1,0:T(8,128)(2,1)S(1)} %get-tuple-element.217.refs_1_), channel_id=1, source_target_pairs={{0,1},{1,0},{2,3},{3,2},{4,5},{5,4},{6,7},{7,6},{8,9},{9,8},{10,11... | collective-permute-start | bytes 786440 | tf_op jit(solution)/shard_map/ppermute | solution.py:83
  120.1 5.0 %collective-permute-start.42 = (bf16[64,1024]{1,0:T(8,128)(2,1)S(1)}, bf16[64,1024]{1,0:T(8,128)(2,1)S(1)}, u32[]{:S(2)}, u32[]{:S(2)}) collective-permute-start(bf16[64,1024]{1,0:T(8,128)(2,1)S(1)} %get-tuple-element.224), channel_id=1, source_target_pairs={{0,8},{2,10},{4,12},{6,14},{8,0},{10,2},{12,4},{14,6},{16,24},{18,... | collective-permute-start | bytes 393224 | tf_op jit(solution)/shard_map/ppermute | solution.py:98
  120.1 5.0 %collective-permute-start.43 = (bf16[64,1024]{1,0:T(8,128)(2,1)S(1)}, bf16[64,1024]{1,0:T(8,128)(2,1)S(1)}, u32[]{:S(2)}, u32[]{:S(2)}) collective-permute-start(bf16[64,1024]{1,0:T(8,128)(2,1)S(1)} %get-tuple-element.225), channel_id=1, source_target_pairs={{0,4},{2,6},{4,0},{6,2},{8,12},{10,14},{12,8},{14,10},{16,20},{18,... | collective-permute-start | bytes 393224 | tf_op jit(solution)/shard_map/ppermute | solution.py:98
  130.6 2.7 %collective-permute-start.45 = (bf16[2048,256]{1,0:T(8,128)(2,1)S(1)}, bf16[2048,256]{1,0:T(8,128)(2,1)S(1)}, u32[]{:S(2)}, u32[]{:S(2)}) collective-permute-start(bf16[2048,256]{1,0:T(8,128)(2,1)S(1)} %get-tuple-element.237), channel_id=1, source_target_pairs={{0,2},{2,0},{4,6},{6,4},{8,10},{10,8},{12,14},{14,12},{16,18},{18,... | collective-permute-start | bytes 3145736 | tf_op jit(solution)/shard_map/ppermute | solution.py:98
  130.7 8.7 %collective-permute-start.44 = (bf16[256,512]{1,0:T(8,128)(2,1)S(1)}, bf16[256,512]{1,0:T(8,128)(2,1)S(1)}, u32[]{:S(2)}, u32[]{:S(2)}) collective-permute-start(bf16[256,512]{1,0:T(8,128)(2,1)S(1)} %get-tuple-element.232.refs_1_), channel_id=1, source_target_pairs={{0,1},{1,0},{2,3},{3,2},{4,5},{5,4},{6,7},{7,6},{8,9},{9,8},{10,11... | collective-permute-start | bytes 786440 | tf_op jit(solution)/shard_map/ppermute | solution.py:83
  133.6 8.4 %collective-permute-start.47 = (bf16[512,256]{1,0:T(8,128)(2,1)S(1)}, bf16[512,256]{1,0:T(8,128)(2,1)S(1)}, u32[]{:S(2)}, u32[]{:S(2)}) collective-permute-start(bf16[512,256]{1,0:T(8,128)(2,1)S(1)} %get-tuple-element.245), channel_id=1, source_target_pairs={{0,4},{2,6},{4,0},{6,2},{8,12},{10,14},{12,8},{14,10},{16,20},{18,... | collective-permute-start | bytes 786440 | tf_op jit(solution)/shard_map/ppermute | solution.py:98
  134.6 8.1 %collective-permute-start.48 = (bf16[512,256]{1,0:T(8,128)(2,1)S(1)}, bf16[512,256]{1,0:T(8,128)(2,1)S(1)}, u32[]{:S(2)}, u32[]{:S(2)}) collective-permute-start(bf16[512,256]{1,0:T(8,128)(2,1)S(1)} %get-tuple-element.246), channel_id=1, source_target_pairs={{0,8},{2,10},{4,12},{6,14},{8,0},{10,2},{12,4},{14,6},{16,24},{18,... | collective-permute-start | bytes 786440 | tf_op jit(solution)/shard_map/ppermute | solution.py:98
  144.2 2.7 %collective-permute-start.51 = (bf16[512,1024]{1,0:T(8,128)(2,1)S(1)}, bf16[512,1024]{1,0:T(8,128)(2,1)S(1)}, u32[]{:S(2)}, u32[]{:S(2)}) collective-permute-start(bf16[512,1024]{1,0:T(8,128)(2,1)S(1)} %get-tuple-element.255), channel_id=1, source_target_pairs={{0,2},{2,0},{4,6},{6,4},{8,10},{10,8},{12,14},{14,12},{16,18},{18,... | collective-permute-start | bytes 3145736 | tf_op jit(solution)/shard_map/ppermute | solution.py:98
  144.3 15.0 %collective-permute-start.46 = (bf16[256,512]{1,0:T(8,128)(2,1)S(1)}, bf16[256,512]{1,0:T(8,128)(2,1)S(1)}, u32[]{:S(2)}, u32[]{:S(2)}) collective-permute-start(bf16[256,512]{1,0:T(8,128)(2,1)S(1)} %get-tuple-element.244.refs_1_), channel_id=1, source_target_pairs={{0,1},{1,0},{2,3},{3,2},{4,5},{5,4},{6,7},{7,6},{8,9},{9,8},{10,11... | collective-permute-start | bytes 786440 | tf_op jit(solution)/shard_map/ppermute | solution.py:83
  147.1 14.6 %collective-permute-start.53 = (bf16[128,1024]{1,0:T(8,128)(2,1)S(1)}, bf16[128,1024]{1,0:T(8,128)(2,1)S(1)}, u32[]{:S(2)}, u32[]{:S(2)}) collective-permute-start(bf16[128,1024]{1,0:T(8,128)(2,1)S(1)} %get-tuple-element.271), channel_id=1, source_target_pairs={{0,4},{2,6},{4,0},{6,2},{8,12},{10,14},{12,8},{14,10},{16,20},{18,... | collective-permute-start | bytes 786440 | tf_op jit(solution)/shard_map/ppermute | solution.py:98
  148.3 13.4 %collective-permute-start.54 = (bf16[128,1024]{1,0:T(8,128)(2,1)S(1)}, bf16[128,1024]{1,0:T(8,128)(2,1)S(1)}, u32[]{:S(2)}, u32[]{:S(2)}) collective-permute-start(bf16[128,1024]{1,0:T(8,128)(2,1)S(1)} %get-tuple-element.272), channel_id=1, source_target_pairs={{0,8},{2,10},{4,12},{6,14},{8,0},{10,2},{12,4},{14,6},{16,24},{18,... | collective-permute-start | bytes 786440 | tf_op jit(solution)/shard_map/ppermute | solution.py:98
  149.6 9.6 %collective-permute-start.49 = (bf16[256,256]{1,0:T(8,128)(2,1)S(1)}, bf16[256,256]{1,0:T(8,128)(2,1)S(1)}, u32[]{:S(2)}, u32[]{:S(2)}) collective-permute-start(bf16[256,256]{1,0:T(8,128)(2,1)S(1)} %get-tuple-element.249), channel_id=1, source_target_pairs={{0,8},{2,10},{4,12},{6,14},{8,0},{10,2},{12,4},{14,6},{16,24},{18,... | collective-permute-start | bytes 393224 | tf_op jit(solution)/shard_map/ppermute | solution.py:98
  150.3 8.9 %collective-permute-start.50 = (bf16[256,256]{1,0:T(8,128)(2,1)S(1)}, bf16[256,256]{1,0:T(8,128)(2,1)S(1)}, u32[]{:S(2)}, u32[]{:S(2)}) collective-permute-start(bf16[256,256]{1,0:T(8,128)(2,1)S(1)} %get-tuple-element.250), channel_id=1, source_target_pairs={{0,4},{2,6},{4,0},{6,2},{8,12},{10,14},{12,8},{14,10},{16,20},{18,... | collective-permute-start | bytes 393224 | tf_op jit(solution)/shard_map/ppermute | solution.py:98
  159.3 8.3 %collective-permute-start.58 = (bf16[256,256]{1,0:T(8,128)(2,1)S(1)}, bf16[256,256]{1,0:T(8,128)(2,1)S(1)}, u32[]{:S(2)}, u32[]{:S(2)}) collective-permute-start(bf16[256,256]{1,0:T(8,128)(2,1)S(1)} %get-tuple-element.280), channel_id=1, source_target_pairs={{0,16},{2,18},{4,20},{6,22},{8,24},{10,26},{12,28},{14,30},{16,0},... | collective-permute-start | bytes 393224 | tf_op jit(solution)/shard_map/ppermute | solution.py:98
  161.7 2.1 %collective-permute-start.52 = (f32[32,512]{1,0:T(8,128)S(1)}, f32[32,512]{1,0:T(8,128)S(1)}, u32[]{:S(2)}, u32[]{:S(2)}) collective-permute-start(f32[32,512]{1,0:T(8,128)S(1)} %get-tuple-element.270), channel_id=1, source_target_pairs={{0,2},{2,0},{4,6},{6,4},{8,10},{10,8},{12,14},{14,12},{16,18},{18,... | collective-permute-start | bytes 196616 | tf_op jit(solution)/shard_map/ppermute | solution.py:98
  161.8 8.2 %collective-permute-start.56 = (bf16[64,1024]{1,0:T(8,128)(2,1)S(1)}, bf16[64,1024]{1,0:T(8,128)(2,1)S(1)}, u32[]{:S(2)}, u32[]{:S(2)}) collective-permute-start(bf16[64,1024]{1,0:T(8,128)(2,1)S(1)} %get-tuple-element.278), channel_id=1, source_target_pairs={{0,8},{2,10},{4,12},{6,14},{8,0},{10,2},{12,4},{14,6},{16,24},{18,... | collective-permute-start | bytes 393224 | tf_op jit(solution)/shard_map/ppermute | solution.py:98
  162.9 7.1 %collective-permute-start.57 = (bf16[64,1024]{1,0:T(8,128)(2,1)S(1)}, bf16[64,1024]{1,0:T(8,128)(2,1)S(1)}, u32[]{:S(2)}, u32[]{:S(2)}) collective-permute-start(bf16[64,1024]{1,0:T(8,128)(2,1)S(1)} %get-tuple-element.279), channel_id=1, source_target_pairs={{0,4},{2,6},{4,0},{6,2},{8,12},{10,14},{12,8},{14,10},{16,20},{18,... | collective-permute-start | bytes 393224 | tf_op jit(solution)/shard_map/ppermute | solution.py:98
  163.8 6.1 %collective-permute-start.55 = (f32[32,512]{1,0:T(8,128)S(1)}, f32[32,512]{1,0:T(8,128)S(1)}, u32[]{:S(2)}, u32[]{:S(2)}) collective-permute-start(f32[32,512]{1,0:T(8,128)S(1)} %add.62), channel_id=1, source_target_pairs={{0,4},{2,6},{4,0},{6,2},{8,12},{10,14},{12,8},{14,10},{16,20},{18,... | collective-permute-start | bytes 196616 | tf_op jit(solution)/shard_map/ppermute | solution.py:98
  165.0 11.1 %collective-permute-start.63 = (bf16[64,1024]{1,0:T(8,128)(2,1)S(1)}, bf16[64,1024]{1,0:T(8,128)(2,1)S(1)}, u32[]{:S(2)}, u32[]{:S(2)}) collective-permute-start(bf16[64,1024]{1,0:T(8,128)(2,1)S(1)} %get-tuple-element.297), channel_id=1, source_target_pairs={{0,16},{2,18},{4,20},{6,22},{8,24},{10,26},{12,28},{14,30},{16,0},... | collective-permute-start | bytes 393224 | tf_op jit(solution)/shard_map/ppermute | solution.py:98
  170.1 6.8 %collective-permute-start.59 = (f32[32,512]{1,0:T(8,128)S(1)}, f32[32,512]{1,0:T(8,128)S(1)}, u32[]{:S(2)}, u32[]{:S(2)}) collective-permute-start(f32[32,512]{1,0:T(8,128)S(1)} %add.63.refs_0_), channel_id=1, source_target_pairs={{0,8},{2,10},{4,12},{6,14},{8,0},{10,2},{12,4},{14,6},{16,24},{18,... | collective-permute-start | bytes 196616 | tf_op jit(solution)/shard_map/ppermute | solution.py:98
  171.1 10.8 %collective-permute-start.60 = (f32[32,512]{1,0:T(8,128)S(1)}, f32[32,512]{1,0:T(8,128)S(1)}, u32[]{:S(2)}, u32[]{:S(2)}) collective-permute-start(f32[32,512]{1,0:T(8,128)S(1)} %add.63.refs_0_), channel_id=1, source_target_pairs={{0,16},{2,18},{4,20},{6,22},{8,24},{10,26},{12,28},{14,30},{16,0},... | collective-permute-start | bytes 196616 | tf_op jit(solution)/shard_map/ppermute | solution.py:98
  173.4 8.5 %collective-permute-start.61 = (f32[32,512]{1,0:T(8,128)S(1)}, f32[32,512]{1,0:T(8,128)S(1)}, u32[]{:S(2)}, u32[]{:S(2)}) collective-permute-start(f32[32,512]{1,0:T(8,128)S(1)} %add.63.refs_0_), channel_id=1, source_target_pairs={{0,24},{2,26},{4,28},{6,30},{8,16},{10,18},{12,20},{14,22},{16,8},... | collective-permute-start | bytes 196616 | tf_op jit(solution)/shard_map/ppermute | solution.py:98
  174.5 10.6 %collective-permute-start.62 = (bf16[64,1024]{1,0:T(8,128)(2,1)S(1)}, bf16[64,1024]{1,0:T(8,128)(2,1)S(1)}, u32[]{:S(2)}, u32[]{:S(2)}) collective-permute-start(bf16[64,1024]{1,0:T(8,128)(2,1)S(1)} %get-tuple-element.289), channel_id=1, source_target_pairs={{0,16},{2,18},{4,20},{6,22},{8,24},{10,26},{12,28},{14,30},{16,0},... | collective-permute-start | bytes 393224 | tf_op jit(solution)/shard_map/ppermute | solution.py:98
  (15 other events, 145.5 us)

commit v7 on v6

--- a/solution.py
+++ b/solution.py
@@ -910,11 +910,23 @@
     def gather(pieces):
         return lax.all_gather(jnp.concatenate(pieces, 1), "dp", axis=0, tiled=True)
 
-    tokens_all = both_halves(tokens)
+    batch_one = None
+    if split:
+        batch_one = on_chip(
+            lambda ins, outs, _: (
+                outs[0].__setitem__(..., ins[0][...]),
+                outs[1].__setitem__(..., ins[1][...]),
+            ),
+            "first_copy",
+            (first_in, first_out),
+            tuple((value.shape, value.dtype) for value in (first_in, first_out)),
+            flops=1_000,
+        )
+        batch_one = tuple(batch_one)
+    tokens_all = both_halves(tie(tokens, batch_one))
     cotangent_all = both_halves(cotangent)
 
     if split:
-        batch_one = (first_in, first_out)
         joint_two = jnp.concatenate(
             [
                 attention_in.reshape(-1, columns),
@@ -927,22 +939,12 @@
         batch_two = (joint_two[: joint_two.shape[0] // 2], joint_two[joint_two.shape[0] // 2 :])
         batch_three = (second_in, second_out)
         joint_three = jnp.concatenate(batch_three, 0)
-        arrived_one = gather_send(batch_one, 0)
-        batch_one = on_chip(
-            lambda ins, outs, _: (
-                outs[0].__setitem__(..., ins[0][...]),
-                outs[1].__setitem__(..., ins[1][...]),
-            ),
-            "first_copy",
-            batch_one,
-            tuple((value.shape, value.dtype) for value in batch_one),
-            flops=1_000,
-        )
-        arrived_one = tie(arrived_one, (batch_one, table))
+        arrived_one = gather_send((first_in, first_out), 0)
+        arrived_one = tie(arrived_one, batch_one)
         arrived_two = gather_send((tie(joint_two, arrived_one),), 0)
-        batch_one = gather_join(tuple(batch_one), tuple(arrived_one))
+        batch_one = gather_join(batch_one, tuple(arrived_one))
         arrived_one = gather_send(batch_one, 1)
-        batch_one = gather_join(batch_one, tie(arrived_one, tokens_all))
+        batch_one = gather_join(batch_one, tie(arrived_one, table))
         arrived_one = gather_send(batch_one, 2)
         batch_two = gather_join(batch_two, tie(arrived_two, batch_one))
         arrived_two = gather_send(batch_two, 1)

time: 186 us -> 184 us (0.989)
  waiting for transfers between devices: 81.6 us -> 78 us
    ppermute x54, waiting for transfers between devices: 57.5 us -> 54.1 us  [shift(): lax.ppermute(value, axis, [(k, k ^ mask) for k in range(lax.axis_size(axi...]
    ppermute x54, starting transfers between devices: 55.8 us -> 59.2 us  [shift(): lax.ppermute(value, axis, [(k, k ^ mask) for k in range(lax.axis_size(axi...]
where the time goes in v7:
time: 184 us
  waiting for transfers between devices  78 us (42%)
  starting transfers between devices  71.3 us (39%)
  Pallas kernels  28.7 us (16%)
  other arithmetic  2.61 us (1%)
  local copies, waits for them, and re-layouts  2.31 us (1%)
    ppermute x54, starting transfers between devices, shift(): lax.ppermute(value, axis, [(k, k ^ mask) for k in range(lax.axis_size(axi...  59.2 us
    ppermute x54, waiting for transfers between devices, shift(): lax.ppermute(value, axis, [(k, k ^ mask) for k in range(lax.axis_size(axi...  54.1 us
    pallas_call x40, Pallas kernels, on_chip(): pl.pallas_call(kernel, out_shape=[jax.ShapeDtypeStruct(shape, kind) for s...  28.7 us
    ppermute x10, waiting for transfers between devices, swap(): return lax.ppermute(value, 'tensor', [(0, 1), (1, 0)])  23.9 us
    ppermute x10, starting transfers between devices, swap(): return lax.ppermute(value, 'tensor', [(0, 1), (1, 0)])  12 us
  transfers between devices with their start and end apart: 64, of which 38 were waited for; matrix products, arithmetic and copies ran while one was open for 2% of the time, Pallas kernels for 8%

profile of v7, /device:TPU:0, one launch (start us, length us, event | category | flops | bytes accessed | tf_op | source)
XLA Modules:
  0.0 184.0 jit_solution(8056723468018405659)
XLA Ops:
  0.7 4.1 %collective-permute-start.1 = (bf16[32,1024]{1,0:T(8,128)(2,1)}, bf16[32,1024]{1,0:T(8,128)(2,1)S(1)}, u32[]{:S(2)}, u32[]{:S(2)}) collective-permute-start(bf16[32,1024]{1,0:T(8,128)(2,1)} %refs_0_.2), channel_id=1, source_target_pairs={{0,16},{2,18},{4,20},{6,22},{8,24},{10,26},{12,28},{14,30},{16,0},... | collective-permute-start | bytes 196616 | tf_op jit(solution)/shard_map/ppermute | solution.py:98
  6.6 1.8 %collective-permute-start = (bf16[128,512]{1,0:T(8,128)(2,1)}, bf16[128,512]{1,0:T(8,128)(2,1)S(1)}, u32[]{:S(2)}, u32[]{:S(2)}) collective-permute-start(bf16[128,512]{1,0:T(8,128)(2,1)} %param.15), channel_id=1, source_target_pairs={{0,1},{1,0},{2,3},{3,2},{4,5},{5,4},{6,7},{7,6},{8,9},{9,8},{10,11... | collective-permute-start | bytes 393224 | tf_op jit(solution)/shard_map/ppermute | solution.py:83
  8.7 2.2 %multiply_sine_fusion = (bf16[512,256]{1,0:T(8,128)(2,1)S(1)}, bf16[512,256]{1,0:T(8,128)(2,1)S(1)}) fusion(f32[256]{0:T(256)S(1)} %multiply_exponential_fusion, f32[512]{0:T(512)S(1)} %iota_add_fusion), kind=kLoop, calls=%fused_computation.3 | loop fusion | flops 393216 | bytes 527360 | tf_op jit(solution)/shard_map/sin | solution.py:57
  11.4 1.6 collective-permute-start.3
  13.1 1.5 collective-permute-start.4
  14.6 2.7 %collective-permute-start.7 = (bf16[256,256]{1,0:T(8,128)(2,1)S(1)}, bf16[256,256]{1,0:T(8,128)(2,1)S(1)}, u32[]{:S(2)}, u32[]{:S(2)}) collective-permute-start(bf16[256,256]{1,0:T(8,128)(2,1)S(1)} %pad_maximum_fusion.2), channel_id=1, source_target_pairs={{0,16},{2,18},{4,20},{6,22},{8,24},{10,26},{12,28},{14,30},{16,0},... | collective-permute-start | bytes 393224 | tf_op jit(solution)/shard_map/ppermute | solution.py:98
  18.1 1.8 collective-permute-start.5
  20.4 2.7 %collective-permute-done.7.refs_2_ = bf16[256,256]{1,0:T(8,128)(2,1)S(1)} collective-permute-done((bf16[256,256]{1,0:T(8,128)(2,1)S(1)}, bf16[256,256]{1,0:T(8,128)(2,1)S(1)}, u32[]{:S(2)}, u32[]{:S(2)}) %collective-permute-start.7) | collective-permute-done | bytes 131104 | tf_op jit(solution)/shard_map/ppermute | solution.py:98
  23.1 1.4 collective-permute-done.5.refs_2_
  24.6 2.6 %collective-permute-done.6.refs_3_ = bf16[128,1024]{1,0:T(8,128)(2,1)S(1)} collective-permute-done((bf16[128,1024]{1,0:T(8,128)(2,1)S(1)}, bf16[128,1024]{1,0:T(8,128)(2,1)S(1)}, u32[]{:S(2)}, u32[]{:S(2)}) %collective-permute-start.6) | collective-permute-done | bytes 262176 | tf_op jit(solution)/shard_map/ppermute | solution.py:98
  28.6 1.3 collective-permute-done.9.refs_3_
  31.0 2.2 %collective-permute-done.11.refs_2_ = bf16[256,256]{1,0:T(8,128)(2,1)S(1)} collective-permute-done((bf16[256,256]{1,0:T(8,128)(2,1)S(1)}, bf16[256,256]{1,0:T(8,128)(2,1)S(1)}, u32[]{:S(2)}, u32[]{:S(2)}) %collective-permute-start.11) | collective-permute-done | bytes 131104 | tf_op jit(solution)/shard_map/ppermute | solution.py:98
  35.4 1.5 collective-permute-start.10
  36.9 2.6 %collective-permute-start.15 = (bf16[64,1024]{1,0:T(8,128)(2,1)S(1)}, bf16[64,1024]{1,0:T(8,128)(2,1)S(1)}, u32[]{:S(2)}, u32[]{:S(2)}) collective-permute-start(bf16[64,1024]{1,0:T(8,128)(2,1)S(1)} %pad_maximum_fusion.3), channel_id=1, source_target_pairs={{0,16},{2,18},{4,20},{6,22},{8,24},{10,26},{12,28},{14,30},{16,0},... | collective-permute-start | bytes 393224 | tf_op jit(solution)/shard_map/ppermute | solution.py:98
  39.5 3.9 %collective-permute-done.15.refs_2_ = bf16[64,1024]{1,0:T(8,128)(2,1)S(1)} collective-permute-done((bf16[64,1024]{1,0:T(8,128)(2,1)S(1)}, bf16[64,1024]{1,0:T(8,128)(2,1)S(1)}, u32[]{:S(2)}, u32[]{:S(2)}) %collective-permute-start.15) | collective-permute-done | bytes 131104 | tf_op jit(solution)/shard_map/ppermute | solution.py:98
  44.5 3.4 %collective-permute-start.25 = (bf16[64,1024]{1,0:T(8,128)(2,1)S(1)}, bf16[64,1024]{1,0:T(8,128)(2,1)S(1)}, u32[]{:S(2)}, u32[]{:S(2)}) collective-permute-start(bf16[64,1024]{1,0:T(8,128)(2,1)S(1)} %get-tuple-element.183.refs_0_), channel_id=1, source_target_pairs={{0,8},{2,10},{4,12},{6,14},{8,0},{10,2},{12,4},{14,6},{16,24},{18,... | collective-permute-start | bytes 393224 | tf_op jit(solution)/shard_map/ppermute | solution.py:98
  47.9 1.6 collective-permute-start.26
  50.0 3.3 %attention_forward.1 = (bf16[256,3328]{1,0:T(8,128)(2,1)S(1)}, bf16[256,512]{1,0:T(8,128)(2,1)S(1)}) custom-call(bf16[256,512]{1,0:T(8,128)(2,1)S(1)} %pad_maximum_fusion.refs_0_.refs_1_.refs_3_, bf16[256,512]{1,0:T(8,128)(2,1)S(1)} %get-tuple-element.176.refs_1_, bf16[256,512]{1,0:T(8,128)(2,1)S(1)} %collective-permute-done.10.refs_2_, ...), custom_call_target="tpu_custom_call" | custom-call | flops 300000000 | bytes 5124096 | tf_op jit(solution)/shard_map/attention_forward/pallas_call | solution.py:70
  53.4 1.6 collective-permute-start.17
  55.5 2.1 %collective-permute-start.28 = (bf16[128,1024]{1,0:T(8,128)(2,1)S(1)}, bf16[128,1024]{1,0:T(8,128)(2,1)S(1)}, u32[]{:S(2)}, u32[]{:S(2)}) collective-permute-start(bf16[128,1024]{1,0:T(8,128)(2,1)S(1)} %get-tuple-element.196.refs_1_), channel_id=1, source_target_pairs={{0,8},{2,10},{4,12},{6,14},{8,0},{10,2},{12,4},{14,6},{16,24},{18,... | collective-permute-start | bytes 786440 | tf_op jit(solution)/shard_map/ppermute | solution.py:98
  57.7 3.9 %collective-permute-done.17.refs_2_ = bf16[256,512]{1,0:T(8,128)(2,1)S(1)} collective-permute-done((bf16[256,512]{1,0:T(8,128)(2,1)S(1)}, bf16[256,512]{1,0:T(8,128)(2,1)S(1)}, u32[]{:S(2)}, u32[]{:S(2)}) %collective-permute-start.17) | collective-permute-done | bytes 262176 | tf_op jit(solution)/shard_map/ppermute | solution.py:83
  61.5 1.9 %conv_forward.1 = (f32[256,1280]{1,0:T(8,128)S(1)}, f32[2,256]{1,0:T(2,128)S(1)}) custom-call(bf16[256,3328]{1,0:T(8,128)(2,1)S(1)} %get-tuple-element.189.refs_0_.refs_7_.refs_4_.refs_3_, bf16[256,512]{1,0:T(8,128)(2,1)S(1)} %get-tuple-element.190.refs_1_, bf16[256,512]{1,0:T(8,128)(2,1)S(1)} %collective-permute-done.17.refs_2_, f32[5,512]{1,0:T(8,128)S(1)} %copy-done, ...), custom_call_target="tpu_custom_call" | custom-call | flops 300000000 | bytes 5680128 | tf_op jit(solution)/shard_map/conv_forward/pallas_call | solution.py:70
  66.5 1.4 collective-permute-done.19
  68.3 1.7 collective-permute-start.21
  70.0 1.2 collective-permute-start.22
  71.2 1.5 collective-permute-start.23
  72.7 1.8 collective-permute-done.22
  74.5 2.1 %collective-permute-done.23 = f32[2,256]{1,0:T(2,128)S(1)} collective-permute-done((f32[2,256]{1,0:T(2,128)S(1)}, f32[2,256]{1,0:T(2,128)S(1)}, u32[]{:S(2)}, u32[]{:S(2)}) %collective-permute-start.23) | collective-permute-done | bytes 2080 | tf_op jit(solution)/shard_map/ppermute | solution.py:98
  78.0 5.3 %collective-permute-done.24.refs_2_ = bf16[256,512]{1,0:T(8,128)(2,1)S(1)} collective-permute-done((bf16[256,512]{1,0:T(8,128)(2,1)S(1)}, bf16[256,512]{1,0:T(8,128)(2,1)S(1)}, u32[]{:S(2)}, u32[]{:S(2)}) %collective-permute-start.24) | collective-permute-done | bytes 262176 | tf_op jit(solution)/shard_map/ppermute | solution.py:83
  85.2 5.5 %collective-permute-done.30.refs_2_ = bf16[256,512]{1,0:T(8,128)(2,1)S(1)} collective-permute-done((bf16[256,512]{1,0:T(8,128)(2,1)S(1)}, bf16[256,512]{1,0:T(8,128)(2,1)S(1)}, u32[]{:S(2)}, u32[]{:S(2)}) %collective-permute-start.30) | collective-permute-done | bytes 262176 | tf_op jit(solution)/shard_map/ppermute | solution.py:83
  90.7 1.8 second_back.1
  92.5 1.3 second_weight_grads.1
  94.8 1.7 collective-permute-done.32.refs_2_
  96.9 5.7 %collective-permute-done.31.refs_2_ = bf16[256,512]{1,0:T(8,128)(2,1)S(1)} collective-permute-done((bf16[256,512]{1,0:T(8,128)(2,1)S(1)}, bf16[256,512]{1,0:T(8,128)(2,1)S(1)}, u32[]{:S(2)}, u32[]{:S(2)}) %collective-permute-start.31) | collective-permute-done | bytes 262176 | tf_op jit(solution)/shard_map/ppermute | solution.py:83
  108.1 1.5 collective-permute-start.37
  109.6 2.0 %collective-permute-start.38 = (f32[2,256]{1,0:T(2,128)S(1)}, f32[2,256]{1,0:T(2,128)S(1)}, u32[]{:S(2)}, u32[]{:S(2)}) collective-permute-start(f32[2,256]{1,0:T(2,128)S(1)} %add_add_fusion.1), channel_id=1, source_target_pairs={{0,24},{2,26},{4,28},{6,30},{8,16},{10,18},{12,20},{14,22},{16,8},... | collective-permute-start | bytes 6152 | tf_op jit(solution)/shard_map/ppermute | solution.py:98
  111.6 2.8 %collective-permute-done.36 = f32[2,256]{1,0:T(2,128)S(1)} collective-permute-done((f32[2,256]{1,0:T(2,128)S(1)}, f32[2,256]{1,0:T(2,128)S(1)}, u32[]{:S(2)}, u32[]{:S(2)}) %collective-permute-start.36) | collective-permute-done | bytes 2080 | tf_op jit(solution)/shard_map/ppermute | solution.py:98
  115.1 1.6 conv_backward.1
  116.7 1.4 collective-permute-start.41
  119.3 2.1 %conv_weight_grads.1 = (bf16[512,768]{1,0:T(8,128)(2,1)S(1)}, f32[31,256]{1,0:T(8,128)S(1)}) custom-call(f32[256,768]{1,0:T(8,128)S(1)} %get-tuple-element.212.refs_0_, f32[256,256]{1,0:T(8,128)S(1)} %get-tuple-element.220.refs_1_, bf16[256,512]{1,0:T(8,128)(2,1)S(1)} %get-tuple-element.221.refs_2_, ...), custom_call_target="tpu_custom_call" | custom-call | flops 300000000 | bytes 3453952 | tf_op jit(solution)/shard_map/conv_weight_grads/pallas_call | solution.py:70
  121.4 1.7 collective-permute-done.42.refs_2_
  123.7 3.6 %attention_back.1 = (f32[256,512]{1,0:T(8,128)S(1)}, bf16[256,768]{1,0:T(8,128)(2,1)S(1)}, bf16[512,256]{1,0:T(8,128)(2,1)S(1)}, bf16[256,512]{1,0:T(8,128)(2,1)...) custom-call(f32[256,768]{1,0:T(8,128)S(1)} %get-tuple-element.212.refs_0_, ...), custom_call_target="tpu_custom_call" | custom-call | flops 300000000 | bytes 8140800 | tf_op jit(solution)/shard_map/attention_back/pallas_call | solution.py:70
  127.3 1.1 mixed_weight_grads.1
  128.5 1.4 collective-permute-start.44
  129.9 1.3 collective-permute-done.45.refs_2_
  131.4 1.3 collective-permute-start.47
  132.7 1.4 collective-permute-start.48
  134.1 3.2 %collective-permute-done.44.refs_2_ = bf16[256,512]{1,0:T(8,128)(2,1)S(1)} collective-permute-done((bf16[256,512]{1,0:T(8,128)(2,1)S(1)}, bf16[256,512]{1,0:T(8,128)(2,1)S(1)}, u32[]{:S(2)}, u32[]{:S(2)}) %collective-permute-start.44) | collective-permute-done | bytes 262176 | tf_op jit(solution)/shard_map/ppermute | solution.py:83
  137.2 1.2 first_back.1
  138.5 1.3 collective-permute-done.47.refs_2_
  140.8 1.5 first_weight_grads.1
  142.4 1.2 collective-permute-start.46
  143.6 1.5 collective-permute-done.51.refs_2_
  146.1 1.5 collective-permute-start.54
  148.1 1.2 collective-permute-start.50
  149.4 7.6 %collective-permute-done.49.refs_2_ = bf16[256,256]{1,0:T(8,128)(2,1)S(1)} collective-permute-done((bf16[256,256]{1,0:T(8,128)(2,1)S(1)}, bf16[256,256]{1,0:T(8,128)(2,1)S(1)}, u32[]{:S(2)}, u32[]{:S(2)}) %collective-permute-start.49) | collective-permute-done | bytes 131104 | tf_op jit(solution)/shard_map/ppermute | solution.py:98
  157.1 1.8 collective-permute-start.58
  158.8 1.1 input_back.1
  161.1 1.2 collective-permute-start.57
  163.3 1.8 collective-permute-start.63
  166.0 2.1 %collective-permute-done.55 = f32[32,512]{1,0:T(8,128)S(1)} collective-permute-done((f32[32,512]{1,0:T(8,128)S(1)}, f32[32,512]{1,0:T(8,128)S(1)}, u32[]{:S(2)}, u32[]{:S(2)}) %collective-permute-start.55) | collective-permute-done | bytes 65568 | tf_op jit(solution)/shard_map/ppermute | solution.py:98
  169.3 2.3 %collective-permute-start.60 = (f32[32,512]{1,0:T(8,128)S(1)}, f32[32,512]{1,0:T(8,128)S(1)}, u32[]{:S(2)}, u32[]{:S(2)}) collective-permute-start(f32[32,512]{1,0:T(8,128)S(1)} %add.63.refs_0_), channel_id=1, source_target_pairs={{0,16},{2,18},{4,20},{6,22},{8,24},{10,26},{12,28},{14,30},{16,0},... | collective-permute-start | bytes 196616 | tf_op jit(solution)/shard_map/ppermute | solution.py:98
  174.9 5.3 %collective-permute-done.60.refs_2_ = f32[32,512]{1,0:T(8,128)S(1)} collective-permute-done((f32[32,512]{1,0:T(8,128)S(1)}, f32[32,512]{1,0:T(8,128)S(1)}, u32[]{:S(2)}, u32[]{:S(2)}) %collective-permute-start.60) | collective-permute-done | bytes 65568 | tf_op jit(solution)/shard_map/ppermute | solution.py:98
  180.8 2.5 %collective-permute-done.62.refs_2_ = bf16[64,1024]{1,0:T(8,128)(2,1)S(1)} collective-permute-done((bf16[64,1024]{1,0:T(8,128)(2,1)S(1)}, bf16[64,1024]{1,0:T(8,128)(2,1)S(1)}, u32[]{:S(2)}, u32[]{:S(2)}) %collective-permute-start.62) | collective-permute-done | bytes 131104 | tf_op jit(solution)/shard_map/ppermute | solution.py:98
  (153 shorter events, 38.6 us)
Async XLA Ops:
  0.7 10.5 %collective-permute-start.1 = (bf16[32,1024]{1,0:T(8,128)(2,1)}, bf16[32,1024]{1,0:T(8,128)(2,1)S(1)}, u32[]{:S(2)}, u32[]{:S(2)}) collective-permute-start(bf16[32,1024]{1,0:T(8,128)(2,1)} %refs_0_.2), channel_id=1, source_target_pairs={{0,16},{2,18},{4,20},{6,22},{8,24},{10,26},{12,28},{14,30},{16,0},... | collective-permute-start | bytes 196616 | tf_op jit(solution)/shard_map/ppermute | solution.py:98
  4.8 6.7 %collective-permute-start.2 = (bf16[32,1024]{1,0:T(8,128)(2,1)}, bf16[32,1024]{1,0:T(8,128)(2,1)S(1)}, u32[]{:S(2)}, u32[]{:S(2)}) collective-permute-start(bf16[32,1024]{1,0:T(8,128)(2,1)} %refs_1_.3), channel_id=1, source_target_pairs={{0,16},{2,18},{4,20},{6,22},{8,24},{10,26},{12,28},{14,30},{16,0},... | collective-permute-start | bytes 196616 | tf_op jit(solution)/shard_map/ppermute | solution.py:98
  6.6 13.8 %collective-permute-start = (bf16[128,512]{1,0:T(8,128)(2,1)}, bf16[128,512]{1,0:T(8,128)(2,1)S(1)}, u32[]{:S(2)}, u32[]{:S(2)}) collective-permute-start(bf16[128,512]{1,0:T(8,128)(2,1)} %param.15), channel_id=1, source_target_pairs={{0,1},{1,0},{2,3},{3,2},{4,5},{5,4},{6,7},{7,6},{8,9},{9,8},{10,11... | collective-permute-start | bytes 393224 | tf_op jit(solution)/shard_map/ppermute | solution.py:83
  8.4 11.9 %collective-permute-start.8 = (bf16[128,512]{1,0:T(8,128)(2,1)}, bf16[128,512]{1,0:T(8,128)(2,1)S(1)}, u32[]{:S(2)}, u32[]{:S(2)}) collective-permute-start(bf16[128,512]{1,0:T(8,128)(2,1)} %param.29), channel_id=1, source_target_pairs={{0,1},{1,0},{2,3},{3,2},{4,5},{5,4},{6,7},{7,6},{8,9},{9,8},{10,11... | collective-permute-start | bytes 393224 | tf_op jit(solution)/shard_map/ppermute | solution.py:83
  11.4 5.8 %collective-permute-start.3 = (bf16[64,1024]{1,0:T(8,128)(2,1)S(1)}, bf16[64,1024]{1,0:T(8,128)(2,1)S(1)}, u32[]{:S(2)}, u32[]{:S(2)}) collective-permute-start(bf16[64,1024]{1,0:T(8,128)(2,1)S(1)} %get-tuple-element.164.refs_0_), channel_id=1, source_target_pairs={{0,8},{2,10},{4,12},{6,14},{8,0},{10,2},{12,4},{14,6},{16,24},{18,... | collective-permute-start | bytes 393224 | tf_op jit(solution)/shard_map/ppermute | solution.py:98
  13.1 5.0 %collective-permute-start.4 = (bf16[64,1024]{1,0:T(8,128)(2,1)S(1)}, bf16[64,1024]{1,0:T(8,128)(2,1)S(1)}, u32[]{:S(2)}, u32[]{:S(2)}) collective-permute-start(bf16[64,1024]{1,0:T(8,128)(2,1)S(1)} %get-tuple-element.165.refs_1_), channel_id=1, source_target_pairs={{0,4},{2,6},{4,0},{6,2},{8,12},{10,14},{12,8},{14,10},{16,20},{18,... | collective-permute-start | bytes 393224 | tf_op jit(solution)/shard_map/ppermute | solution.py:98
  14.6 8.5 %collective-permute-start.7 = (bf16[256,256]{1,0:T(8,128)(2,1)S(1)}, bf16[256,256]{1,0:T(8,128)(2,1)S(1)}, u32[]{:S(2)}, u32[]{:S(2)}) collective-permute-start(bf16[256,256]{1,0:T(8,128)(2,1)S(1)} %pad_maximum_fusion.2), channel_id=1, source_target_pairs={{0,16},{2,18},{4,20},{6,22},{8,24},{10,26},{12,28},{14,30},{16,0},... | collective-permute-start | bytes 393224 | tf_op jit(solution)/shard_map/ppermute | solution.py:98
  18.1 6.5 %collective-permute-start.5 = (bf16[128,1024]{1,0:T(8,128)(2,1)S(1)}, bf16[128,1024]{1,0:T(8,128)(2,1)S(1)}, u32[]{:S(2)}, u32[]{:S(2)}) collective-permute-start(bf16[128,1024]{1,0:T(8,128)(2,1)S(1)} %get-tuple-element.168.refs_0_), channel_id=1, source_target_pairs={{0,4},{2,6},{4,0},{6,2},{8,12},{10,14},{12,8},{14,10},{16,20},{18,... | collective-permute-start | bytes 786440 | tf_op jit(solution)/shard_map/ppermute | solution.py:98
  19.8 7.3 %collective-permute-start.6 = (bf16[128,1024]{1,0:T(8,128)(2,1)S(1)}, bf16[128,1024]{1,0:T(8,128)(2,1)S(1)}, u32[]{:S(2)}, u32[]{:S(2)}) collective-permute-start(bf16[128,1024]{1,0:T(8,128)(2,1)S(1)} %get-tuple-element.169.refs_1_), channel_id=1, source_target_pairs={{0,8},{2,10},{4,12},{6,14},{8,0},{10,2},{12,4},{14,6},{16,24},{18,... | collective-permute-start | bytes 786440 | tf_op jit(solution)/shard_map/ppermute | solution.py:98
  27.3 2.7 %collective-permute-start.9 = (bf16[512,1024]{1,0:T(8,128)(2,1)S(1)}, bf16[512,1024]{1,0:T(8,128)(2,1)S(1)}, u32[]{:S(2)}, u32[]{:S(2)}) collective-permute-start(bf16[512,1024]{1,0:T(8,128)(2,1)S(1)} %gather_join.12.refs_2_), channel_id=1, source_target_pairs={{0,2},{2,0},{4,6},{6,4},{8,10},{10,8},{12,14},{14,12},{16,18},{18,... | collective-permute-start | bytes 3145736 | tf_op jit(solution)/shard_map/ppermute | solution.py:98
  27.3 5.9 %collective-permute-start.11 = (bf16[256,256]{1,0:T(8,128)(2,1)S(1)}, bf16[256,256]{1,0:T(8,128)(2,1)S(1)}, u32[]{:S(2)}, u32[]{:S(2)}) collective-permute-start(bf16[256,256]{1,0:T(8,128)(2,1)S(1)} %get-tuple-element.172.refs_0_), channel_id=1, source_target_pairs={{0,8},{2,10},{4,12},{6,14},{8,0},{10,2},{12,4},{14,6},{16,24},{18,... | collective-permute-start | bytes 393224 | tf_op jit(solution)/shard_map/ppermute | solution.py:98
  28.1 5.6 %collective-permute-start.12 = (bf16[256,256]{1,0:T(8,128)(2,1)S(1)}, bf16[256,256]{1,0:T(8,128)(2,1)S(1)}, u32[]{:S(2)}, u32[]{:S(2)}) collective-permute-start(bf16[256,256]{1,0:T(8,128)(2,1)S(1)} %get-tuple-element.173.refs_1_), channel_id=1, source_target_pairs={{0,4},{2,6},{4,0},{6,2},{8,12},{10,14},{12,8},{14,10},{16,20},{18,... | collective-permute-start | bytes 393224 | tf_op jit(solution)/shard_map/ppermute | solution.py:98
  33.7 9.7 %collective-permute-start.13 = (bf16[512,256]{1,0:T(8,128)(2,1)S(1)}, bf16[512,256]{1,0:T(8,128)(2,1)S(1)}, u32[]{:S(2)}, u32[]{:S(2)}) collective-permute-start(bf16[512,256]{1,0:T(8,128)(2,1)S(1)} %get-tuple-element.179.refs_0_), channel_id=1, source_target_pairs={{0,4},{2,6},{4,0},{6,2},{8,12},{10,14},{12,8},{14,10},{16,20},{18,... | collective-permute-start | bytes 786440 | tf_op jit(solution)/shard_map/ppermute | solution.py:98
  34.3 10.1 %collective-permute-start.14 = (bf16[512,256]{1,0:T(8,128)(2,1)S(1)}, bf16[512,256]{1,0:T(8,128)(2,1)S(1)}, u32[]{:S(2)}, u32[]{:S(2)}) collective-permute-start(bf16[512,256]{1,0:T(8,128)(2,1)S(1)} %get-tuple-element.180.refs_1_), channel_id=1, source_target_pairs={{0,8},{2,10},{4,12},{6,14},{8,0},{10,2},{12,4},{14,6},{16,24},{18,... | collective-permute-start | bytes 786440 | tf_op jit(solution)/shard_map/ppermute | solution.py:98
  35.4 9.0 %collective-permute-start.10 = (bf16[256,512]{1,0:T(8,128)(2,1)S(1)}, bf16[256,512]{1,0:T(8,128)(2,1)S(1)}, u32[]{:S(2)}, u32[]{:S(2)}) collective-permute-start(bf16[256,512]{1,0:T(8,128)(2,1)S(1)} %get-tuple-element.176.refs_1_), channel_id=1, source_target_pairs={{0,1},{1,0},{2,3},{3,2},{4,5},{5,4},{6,7},{7,6},{8,9},{9,8},{10,11... | collective-permute-start | bytes 786440 | tf_op jit(solution)/shard_map/ppermute | solution.py:83
  36.9 6.5 %collective-permute-start.15 = (bf16[64,1024]{1,0:T(8,128)(2,1)S(1)}, bf16[64,1024]{1,0:T(8,128)(2,1)S(1)}, u32[]{:S(2)}, u32[]{:S(2)}) collective-permute-start(bf16[64,1024]{1,0:T(8,128)(2,1)S(1)} %pad_maximum_fusion.3), channel_id=1, source_target_pairs={{0,16},{2,18},{4,20},{6,22},{8,24},{10,26},{12,28},{14,30},{16,0},... | collective-permute-start | bytes 393224 | tf_op jit(solution)/shard_map/ppermute | solution.py:98
  44.5 5.1 %collective-permute-start.16 = (bf16[2048,256]{1,0:T(8,128)(2,1)S(1)}, bf16[2048,256]{1,0:T(8,128)(2,1)S(1)}, u32[]{:S(2)}, u32[]{:S(2)}) collective-permute-start(bf16[2048,256]{1,0:T(8,128)(2,1)S(1)} %gather_join.15.refs_0_), channel_id=1, source_target_pairs={{0,2},{2,0},{4,6},{6,4},{8,10},{10,8},{12,14},{14,12},{16,18},{18,... | collective-permute-start | bytes 3145736 | tf_op jit(solution)/shard_map/ppermute | solution.py:98
  44.5 10.4 %collective-permute-start.25 = (bf16[64,1024]{1,0:T(8,128)(2,1)S(1)}, bf16[64,1024]{1,0:T(8,128)(2,1)S(1)}, u32[]{:S(2)}, u32[]{:S(2)}) collective-permute-start(bf16[64,1024]{1,0:T(8,128)(2,1)S(1)} %get-tuple-element.183.refs_0_), channel_id=1, source_target_pairs={{0,8},{2,10},{4,12},{6,14},{8,0},{10,2},{12,4},{14,6},{16,24},{18,... | collective-permute-start | bytes 393224 | tf_op jit(solution)/shard_map/ppermute | solution.py:98
  47.9 7.0 %collective-permute-start.26 = (bf16[64,1024]{1,0:T(8,128)(2,1)S(1)}, bf16[64,1024]{1,0:T(8,128)(2,1)S(1)}, u32[]{:S(2)}, u32[]{:S(2)}) collective-permute-start(bf16[64,1024]{1,0:T(8,128)(2,1)S(1)} %get-tuple-element.184.refs_1_), channel_id=1, source_target_pairs={{0,4},{2,6},{4,0},{6,2},{8,12},{10,14},{12,8},{14,10},{16,20},{18,... | collective-permute-start | bytes 393224 | tf_op jit(solution)/shard_map/ppermute | solution.py:98
  53.4 8.2 %collective-permute-start.17 = (bf16[256,512]{1,0:T(8,128)(2,1)S(1)}, bf16[256,512]{1,0:T(8,128)(2,1)S(1)}, u32[]{:S(2)}, u32[]{:S(2)}) collective-permute-start(bf16[256,512]{1,0:T(8,128)(2,1)S(1)} %get-tuple-element.190.refs_1_), channel_id=1, source_target_pairs={{0,1},{1,0},{2,3},{3,2},{4,5},{5,4},{6,7},{7,6},{8,9},{9,8},{10,11... | collective-permute-start | bytes 786440 | tf_op jit(solution)/shard_map/ppermute | solution.py:83
  55.0 8.5 %collective-permute-start.27 = (bf16[128,1024]{1,0:T(8,128)(2,1)S(1)}, bf16[128,1024]{1,0:T(8,128)(2,1)S(1)}, u32[]{:S(2)}, u32[]{:S(2)}) collective-permute-start(bf16[128,1024]{1,0:T(8,128)(2,1)S(1)} %get-tuple-element.195.refs_0_), channel_id=1, source_target_pairs={{0,4},{2,6},{4,0},{6,2},{8,12},{10,14},{12,8},{14,10},{16,20},{18,... | collective-permute-start | bytes 786440 | tf_op jit(solution)/shard_map/ppermute | solution.py:98
  55.5 8.2 %collective-permute-start.28 = (bf16[128,1024]{1,0:T(8,128)(2,1)S(1)}, bf16[128,1024]{1,0:T(8,128)(2,1)S(1)}, u32[]{:S(2)}, u32[]{:S(2)}) collective-permute-start(bf16[128,1024]{1,0:T(8,128)(2,1)S(1)} %get-tuple-element.196.refs_1_), channel_id=1, source_target_pairs={{0,8},{2,10},{4,12},{6,14},{8,0},{10,2},{12,4},{14,6},{16,24},{18,... | collective-permute-start | bytes 786440 | tf_op jit(solution)/shard_map/ppermute | solution.py:98
  63.8 14.1 %collective-permute-start.29 = (bf16[512,1024]{1,0:T(8,128)(2,1)S(1)}, bf16[512,1024]{1,0:T(8,128)(2,1)S(1)}, u32[]{:S(2)}, u32[]{:S(2)}) collective-permute-start(bf16[512,1024]{1,0:T(8,128)(2,1)S(1)} %gather_join.17.refs_0_), channel_id=1, source_target_pairs={{0,2},{2,0},{4,6},{6,4},{8,10},{10,8},{12,14},{14,12},{16,18},{18,... | collective-permute-start | bytes 3145736 | tf_op jit(solution)/shard_map/ppermute | solution.py:98
  63.9 2.6 %collective-permute-start.18 = (f32[2,256]{1,0:T(2,128)S(1)}, f32[2,256]{1,0:T(2,128)S(1)}, u32[]{:S(2)}, u32[]{:S(2)}) collective-permute-start(f32[2,256]{1,0:T(2,128)S(1)} %get-tuple-element.192), channel_id=1, source_target_pairs={{0,2},{2,0},{4,6},{6,4},{8,10},{10,8},{12,14},{14,12},{16,18},{18,... | collective-permute-start | bytes 6152 | tf_op jit(solution)/shard_map/ppermute | solution.py:98
  64.4 3.6 %collective-permute-start.19 = (f32[2,256]{1,0:T(2,128)S(1)}, f32[2,256]{1,0:T(2,128)S(1)}, u32[]{:S(2)}, u32[]{:S(2)}) collective-permute-start(f32[2,256]{1,0:T(2,128)S(1)} %get-tuple-element.192), channel_id=1, source_target_pairs={{0,4},{2,6},{4,0},{6,2},{8,12},{10,14},{12,8},{14,10},{16,20},{18,... | collective-permute-start | bytes 6152 | tf_op jit(solution)/shard_map/ppermute | solution.py:98
  65.3 3.0 %collective-permute-start.20 = (f32[2,256]{1,0:T(2,128)S(1)}, f32[2,256]{1,0:T(2,128)S(1)}, u32[]{:S(2)}, u32[]{:S(2)}) collective-permute-start(f32[2,256]{1,0:T(2,128)S(1)} %get-tuple-element.192), channel_id=1, source_target_pairs={{0,6},{2,4},{4,2},{6,0},{8,14},{10,12},{12,10},{14,8},{16,22},{18,... | collective-permute-start | bytes 6152 | tf_op jit(solution)/shard_map/ppermute | solution.py:98
  68.3 4.4 %collective-permute-start.21 = (f32[2,256]{1,0:T(2,128)S(1)}, f32[2,256]{1,0:T(2,128)S(1)}, u32[]{:S(2)}, u32[]{:S(2)}) collective-permute-start(f32[2,256]{1,0:T(2,128)S(1)} %add_add_fusion.3), channel_id=1, source_target_pairs={{0,8},{2,10},{4,12},{6,14},{8,0},{10,2},{12,4},{14,6},{16,24},{18,... | collective-permute-start | bytes 6152 | tf_op jit(solution)/shard_map/ppermute | solution.py:98
  70.0 4.5 %collective-permute-start.22 = (f32[2,256]{1,0:T(2,128)S(1)}, f32[2,256]{1,0:T(2,128)S(1)}, u32[]{:S(2)}, u32[]{:S(2)}) collective-permute-start(f32[2,256]{1,0:T(2,128)S(1)} %add_add_fusion.3), channel_id=1, source_target_pairs={{0,16},{2,18},{4,20},{6,22},{8,24},{10,26},{12,28},{14,30},{16,0},... | collective-permute-start | bytes 6152 | tf_op jit(solution)/shard_map/ppermute | solution.py:98
  71.2 5.4 %collective-permute-start.23 = (f32[2,256]{1,0:T(2,128)S(1)}, f32[2,256]{1,0:T(2,128)S(1)}, u32[]{:S(2)}, u32[]{:S(2)}) collective-permute-start(f32[2,256]{1,0:T(2,128)S(1)} %add_add_fusion.3), channel_id=1, source_target_pairs={{0,24},{2,26},{4,28},{6,30},{8,16},{10,18},{12,20},{14,22},{16,8},... | collective-permute-start | bytes 6152 | tf_op jit(solution)/shard_map/ppermute | solution.py:98
  76.9 6.4 %collective-permute-start.24 = (bf16[256,512]{1,0:T(8,128)(2,1)S(1)}, bf16[256,512]{1,0:T(8,128)(2,1)S(1)}, u32[]{:S(2)}, u32[]{:S(2)}) collective-permute-start(bf16[256,512]{1,0:T(8,128)(2,1)S(1)} %norm_forward.1.refs_1_), channel_id=1, source_target_pairs={{0,1},{1,0},{2,3},{3,2},{4,5},{5,4},{6,7},{7,6},{8,9},{9,8},{10,11... | collective-permute-start | bytes 786440 | tf_op jit(solution)/shard_map/ppermute | solution.py:83
  84.3 6.4 %collective-permute-start.30 = (bf16[256,512]{1,0:T(8,128)(2,1)S(1)}, bf16[256,512]{1,0:T(8,128)(2,1)S(1)}, u32[]{:S(2)}, u32[]{:S(2)}) collective-permute-start(bf16[256,512]{1,0:T(8,128)(2,1)S(1)} %get-tuple-element.201.refs_1_), channel_id=1, source_target_pairs={{0,1},{1,0},{2,3},{3,2},{4,5},{5,4},{6,7},{7,6},{8,9},{9,8},{10,11... | collective-permute-start | bytes 786440 | tf_op jit(solution)/shard_map/ppermute | solution.py:83
  93.8 2.7 %collective-permute-start.32 = (bf16[512,1024]{1,0:T(8,128)(2,1)S(1)}, bf16[512,1024]{1,0:T(8,128)(2,1)S(1)}, u32[]{:S(2)}, u32[]{:S(2)}) collective-permute-start(bf16[512,1024]{1,0:T(8,128)(2,1)S(1)} %get-tuple-element.208), channel_id=1, source_target_pairs={{0,2},{2,0},{4,6},{6,4},{8,10},{10,8},{12,14},{14,12},{16,18},{18,... | collective-permute-start | bytes 3145736 | tf_op jit(solution)/shard_map/ppermute | solution.py:98
  93.9 8.7 %collective-permute-start.31 = (bf16[256,512]{1,0:T(8,128)(2,1)S(1)}, bf16[256,512]{1,0:T(8,128)(2,1)S(1)}, u32[]{:S(2)}, u32[]{:S(2)}) collective-permute-start(bf16[256,512]{1,0:T(8,128)(2,1)S(1)} %get-tuple-element.204.refs_1_), channel_id=1, source_target_pairs={{0,1},{1,0},{2,3},{3,2},{4,5},{5,4},{6,7},{7,6},{8,9},{9,8},{10,11... | collective-permute-start | bytes 786440 | tf_op jit(solution)/shard_map/ppermute | solution.py:83
  103.2 2.8 %collective-permute-start.33 = (f32[2,256]{1,0:T(2,128)S(1)}, f32[2,256]{1,0:T(2,128)S(1)}, u32[]{:S(2)}, u32[]{:S(2)}) collective-permute-start(f32[2,256]{1,0:T(2,128)S(1)} %get-tuple-element.213), channel_id=1, source_target_pairs={{0,2},{2,0},{4,6},{6,4},{8,10},{10,8},{12,14},{14,12},{16,18},{18,... | collective-permute-start | bytes 6152 | tf_op jit(solution)/shard_map/ppermute | solution.py:98
  103.3 3.7 %collective-permute-start.34 = (f32[2,256]{1,0:T(2,128)S(1)}, f32[2,256]{1,0:T(2,128)S(1)}, u32[]{:S(2)}, u32[]{:S(2)}) collective-permute-start(f32[2,256]{1,0:T(2,128)S(1)} %get-tuple-element.213), channel_id=1, source_target_pairs={{0,4},{2,6},{4,0},{6,2},{8,12},{10,14},{12,8},{14,10},{16,20},{18,... | collective-permute-start | bytes 6152 | tf_op jit(solution)/shard_map/ppermute | solution.py:98
  104.2 3.0 %collective-permute-start.35 = (f32[2,256]{1,0:T(2,128)S(1)}, f32[2,256]{1,0:T(2,128)S(1)}, u32[]{:S(2)}, u32[]{:S(2)}) collective-permute-start(f32[2,256]{1,0:T(2,128)S(1)} %get-tuple-element.213), channel_id=1, source_target_pairs={{0,6},{2,4},{4,2},{6,0},{8,14},{10,12},{12,10},{14,8},{16,22},{18,... | collective-permute-start | bytes 6152 | tf_op jit(solution)/shard_map/ppermute | solution.py:98
  105.1 9.8 %collective-permute-start.39 = (bf16[128,1024]{1,0:T(8,128)(2,1)S(1)}, bf16[128,1024]{1,0:T(8,128)(2,1)S(1)}, u32[]{:S(2)}, u32[]{:S(2)}) collective-permute-start(bf16[128,1024]{1,0:T(8,128)(2,1)S(1)} %get-tuple-element.214), channel_id=1, source_target_pairs={{0,4},{2,6},{4,0},{6,2},{8,12},{10,14},{12,8},{14,10},{16,20},{18,... | collective-permute-start | bytes 786440 | tf_op jit(solution)/shard_map/ppermute | solution.py:98
  106.0 9.0 %collective-permute-start.40 = (bf16[128,1024]{1,0:T(8,128)(2,1)S(1)}, bf16[128,1024]{1,0:T(8,128)(2,1)S(1)}, u32[]{:S(2)}, u32[]{:S(2)}) collective-permute-start(bf16[128,1024]{1,0:T(8,128)(2,1)S(1)} %get-tuple-element.215), channel_id=1, source_target_pairs={{0,8},{2,10},{4,12},{6,14},{8,0},{10,2},{12,4},{14,6},{16,24},{18,... | collective-permute-start | bytes 786440 | tf_op jit(solution)/shard_map/ppermute | solution.py:98
  107.2 7.2 %collective-permute-start.36 = (f32[2,256]{1,0:T(2,128)S(1)}, f32[2,256]{1,0:T(2,128)S(1)}, u32[]{:S(2)}, u32[]{:S(2)}) collective-permute-start(f32[2,256]{1,0:T(2,128)S(1)} %add_add_fusion.1), channel_id=1, source_target_pairs={{0,8},{2,10},{4,12},{6,14},{8,0},{10,2},{12,4},{14,6},{16,24},{18,... | collective-permute-start | bytes 6152 | tf_op jit(solution)/shard_map/ppermute | solution.py:98
  108.1 6.3 %collective-permute-start.37 = (f32[2,256]{1,0:T(2,128)S(1)}, f32[2,256]{1,0:T(2,128)S(1)}, u32[]{:S(2)}, u32[]{:S(2)}) collective-permute-start(f32[2,256]{1,0:T(2,128)S(1)} %add_add_fusion.1), channel_id=1, source_target_pairs={{0,16},{2,18},{4,20},{6,22},{8,24},{10,26},{12,28},{14,30},{16,0},... | collective-permute-start | bytes 6152 | tf_op jit(solution)/shard_map/ppermute | solution.py:98
  109.6 5.4 %collective-permute-start.38 = (f32[2,256]{1,0:T(2,128)S(1)}, f32[2,256]{1,0:T(2,128)S(1)}, u32[]{:S(2)}, u32[]{:S(2)}) collective-permute-start(f32[2,256]{1,0:T(2,128)S(1)} %add_add_fusion.1), channel_id=1, source_target_pairs={{0,24},{2,26},{4,28},{6,30},{8,16},{10,18},{12,20},{14,22},{16,8},... | collective-permute-start | bytes 6152 | tf_op jit(solution)/shard_map/ppermute | solution.py:98
  116.7 6.9 %collective-permute-start.41 = (bf16[256,512]{1,0:T(8,128)(2,1)S(1)}, bf16[256,512]{1,0:T(8,128)(2,1)S(1)}, u32[]{:S(2)}, u32[]{:S(2)}) collective-permute-start(bf16[256,512]{1,0:T(8,128)(2,1)S(1)} %get-tuple-element.219.refs_1_), channel_id=1, source_target_pairs={{0,1},{1,0},{2,3},{3,2},{4,5},{5,4},{6,7},{7,6},{8,9},{9,8},{10,11... | collective-permute-start | bytes 786440 | tf_op jit(solution)/shard_map/ppermute | solution.py:83
  118.1 5.0 %collective-permute-start.42 = (bf16[64,1024]{1,0:T(8,128)(2,1)S(1)}, bf16[64,1024]{1,0:T(8,128)(2,1)S(1)}, u32[]{:S(2)}, u32[]{:S(2)}) collective-permute-start(bf16[64,1024]{1,0:T(8,128)(2,1)S(1)} %get-tuple-element.226), channel_id=1, source_target_pairs={{0,8},{2,10},{4,12},{6,14},{8,0},{10,2},{12,4},{14,6},{16,24},{18,... | collective-permute-start | bytes 393224 | tf_op jit(solution)/shard_map/ppermute | solution.py:98
  118.2 5.0 %collective-permute-start.43 = (bf16[64,1024]{1,0:T(8,128)(2,1)S(1)}, bf16[64,1024]{1,0:T(8,128)(2,1)S(1)}, u32[]{:S(2)}, u32[]{:S(2)}) collective-permute-start(bf16[64,1024]{1,0:T(8,128)(2,1)S(1)} %get-tuple-element.227), channel_id=1, source_target_pairs={{0,4},{2,6},{4,0},{6,2},{8,12},{10,14},{12,8},{14,10},{16,20},{18,... | collective-permute-start | bytes 393224 | tf_op jit(solution)/shard_map/ppermute | solution.py:98
  128.4 2.7 %collective-permute-start.45 = (bf16[2048,256]{1,0:T(8,128)(2,1)S(1)}, bf16[2048,256]{1,0:T(8,128)(2,1)S(1)}, u32[]{:S(2)}, u32[]{:S(2)}) collective-permute-start(bf16[2048,256]{1,0:T(8,128)(2,1)S(1)} %get-tuple-element.239), channel_id=1, source_target_pairs={{0,2},{2,0},{4,6},{6,4},{8,10},{10,8},{12,14},{14,12},{16,18},{18,... | collective-permute-start | bytes 3145736 | tf_op jit(solution)/shard_map/ppermute | solution.py:98
  128.5 8.7 %collective-permute-start.44 = (bf16[256,512]{1,0:T(8,128)(2,1)S(1)}, bf16[256,512]{1,0:T(8,128)(2,1)S(1)}, u32[]{:S(2)}, u32[]{:S(2)}) collective-permute-start(bf16[256,512]{1,0:T(8,128)(2,1)S(1)} %get-tuple-element.234.refs_1_), channel_id=1, source_target_pairs={{0,1},{1,0},{2,3},{3,2},{4,5},{5,4},{6,7},{7,6},{8,9},{9,8},{10,11... | collective-permute-start | bytes 786440 | tf_op jit(solution)/shard_map/ppermute | solution.py:83
  131.4 8.4 %collective-permute-start.47 = (bf16[512,256]{1,0:T(8,128)(2,1)S(1)}, bf16[512,256]{1,0:T(8,128)(2,1)S(1)}, u32[]{:S(2)}, u32[]{:S(2)}) collective-permute-start(bf16[512,256]{1,0:T(8,128)(2,1)S(1)} %get-tuple-element.247), channel_id=1, source_target_pairs={{0,4},{2,6},{4,0},{6,2},{8,12},{10,14},{12,8},{14,10},{16,20},{18,... | collective-permute-start | bytes 786440 | tf_op jit(solution)/shard_map/ppermute | solution.py:98
  132.7 8.1 %collective-permute-start.48 = (bf16[512,256]{1,0:T(8,128)(2,1)S(1)}, bf16[512,256]{1,0:T(8,128)(2,1)S(1)}, u32[]{:S(2)}, u32[]{:S(2)}) collective-permute-start(bf16[512,256]{1,0:T(8,128)(2,1)S(1)} %get-tuple-element.248), channel_id=1, source_target_pairs={{0,8},{2,10},{4,12},{6,14},{8,0},{10,2},{12,4},{14,6},{16,24},{18,... | collective-permute-start | bytes 786440 | tf_op jit(solution)/shard_map/ppermute | solution.py:98
  142.3 2.7 %collective-permute-start.51 = (bf16[512,1024]{1,0:T(8,128)(2,1)S(1)}, bf16[512,1024]{1,0:T(8,128)(2,1)S(1)}, u32[]{:S(2)}, u32[]{:S(2)}) collective-permute-start(bf16[512,1024]{1,0:T(8,128)(2,1)S(1)} %get-tuple-element.257), channel_id=1, source_target_pairs={{0,2},{2,0},{4,6},{6,4},{8,10},{10,8},{12,14},{14,12},{16,18},{18,... | collective-permute-start | bytes 3145736 | tf_op jit(solution)/shard_map/ppermute | solution.py:98
  142.4 14.6 %collective-permute-start.46 = (bf16[256,512]{1,0:T(8,128)(2,1)S(1)}, bf16[256,512]{1,0:T(8,128)(2,1)S(1)}, u32[]{:S(2)}, u32[]{:S(2)}) collective-permute-start(bf16[256,512]{1,0:T(8,128)(2,1)S(1)} %get-tuple-element.246.refs_1_), channel_id=1, source_target_pairs={{0,1},{1,0},{2,3},{3,2},{4,5},{5,4},{6,7},{7,6},{8,9},{9,8},{10,11... | collective-permute-start | bytes 786440 | tf_op jit(solution)/shard_map/ppermute | solution.py:83
  145.2 14.7 %collective-permute-start.53 = (bf16[128,1024]{1,0:T(8,128)(2,1)S(1)}, bf16[128,1024]{1,0:T(8,128)(2,1)S(1)}, u32[]{:S(2)}, u32[]{:S(2)}) collective-permute-start(bf16[128,1024]{1,0:T(8,128)(2,1)S(1)} %get-tuple-element.273), channel_id=1, source_target_pairs={{0,4},{2,6},{4,0},{6,2},{8,12},{10,14},{12,8},{14,10},{16,20},{18,... | collective-permute-start | bytes 786440 | tf_op jit(solution)/shard_map/ppermute | solution.py:98
  146.1 13.8 %collective-permute-start.54 = (bf16[128,1024]{1,0:T(8,128)(2,1)S(1)}, bf16[128,1024]{1,0:T(8,128)(2,1)S(1)}, u32[]{:S(2)}, u32[]{:S(2)}) collective-permute-start(bf16[128,1024]{1,0:T(8,128)(2,1)S(1)} %get-tuple-element.274), channel_id=1, source_target_pairs={{0,8},{2,10},{4,12},{6,14},{8,0},{10,2},{12,4},{14,6},{16,24},{18,... | collective-permute-start | bytes 786440 | tf_op jit(solution)/shard_map/ppermute | solution.py:98
  147.7 9.3 %collective-permute-start.49 = (bf16[256,256]{1,0:T(8,128)(2,1)S(1)}, bf16[256,256]{1,0:T(8,128)(2,1)S(1)}, u32[]{:S(2)}, u32[]{:S(2)}) collective-permute-start(bf16[256,256]{1,0:T(8,128)(2,1)S(1)} %get-tuple-element.251), channel_id=1, source_target_pairs={{0,8},{2,10},{4,12},{6,14},{8,0},{10,2},{12,4},{14,6},{16,24},{18,... | collective-permute-start | bytes 393224 | tf_op jit(solution)/shard_map/ppermute | solution.py:98
  148.1 8.9 %collective-permute-start.50 = (bf16[256,256]{1,0:T(8,128)(2,1)S(1)}, bf16[256,256]{1,0:T(8,128)(2,1)S(1)}, u32[]{:S(2)}, u32[]{:S(2)}) collective-permute-start(bf16[256,256]{1,0:T(8,128)(2,1)S(1)} %get-tuple-element.252), channel_id=1, source_target_pairs={{0,4},{2,6},{4,0},{6,2},{8,12},{10,14},{12,8},{14,10},{16,20},{18,... | collective-permute-start | bytes 393224 | tf_op jit(solution)/shard_map/ppermute | solution.py:98
  157.1 8.3 %collective-permute-start.58 = (bf16[256,256]{1,0:T(8,128)(2,1)S(1)}, bf16[256,256]{1,0:T(8,128)(2,1)S(1)}, u32[]{:S(2)}, u32[]{:S(2)}) collective-permute-start(bf16[256,256]{1,0:T(8,128)(2,1)S(1)} %get-tuple-element.282), channel_id=1, source_target_pairs={{0,16},{2,18},{4,20},{6,22},{8,24},{10,26},{12,28},{14,30},{16,0},... | collective-permute-start | bytes 393224 | tf_op jit(solution)/shard_map/ppermute | solution.py:98
  159.9 2.4 %collective-permute-start.52 = (f32[32,512]{1,0:T(8,128)S(1)}, f32[32,512]{1,0:T(8,128)S(1)}, u32[]{:S(2)}, u32[]{:S(2)}) collective-permute-start(f32[32,512]{1,0:T(8,128)S(1)} %get-tuple-element.272), channel_id=1, source_target_pairs={{0,2},{2,0},{4,6},{6,4},{8,10},{10,8},{12,14},{14,12},{16,18},{18,... | collective-permute-start | bytes 196616 | tf_op jit(solution)/shard_map/ppermute | solution.py:98
  160.1 8.1 %collective-permute-start.56 = (bf16[64,1024]{1,0:T(8,128)(2,1)S(1)}, bf16[64,1024]{1,0:T(8,128)(2,1)S(1)}, u32[]{:S(2)}, u32[]{:S(2)}) collective-permute-start(bf16[64,1024]{1,0:T(8,128)(2,1)S(1)} %get-tuple-element.280), channel_id=1, source_target_pairs={{0,8},{2,10},{4,12},{6,14},{8,0},{10,2},{12,4},{14,6},{16,24},{18,... | collective-permute-start | bytes 393224 | tf_op jit(solution)/shard_map/ppermute | solution.py:98
  161.1 7.1 %collective-permute-start.57 = (bf16[64,1024]{1,0:T(8,128)(2,1)S(1)}, bf16[64,1024]{1,0:T(8,128)(2,1)S(1)}, u32[]{:S(2)}, u32[]{:S(2)}) collective-permute-start(bf16[64,1024]{1,0:T(8,128)(2,1)S(1)} %get-tuple-element.281), channel_id=1, source_target_pairs={{0,4},{2,6},{4,0},{6,2},{8,12},{10,14},{12,8},{14,10},{16,20},{18,... | collective-permute-start | bytes 393224 | tf_op jit(solution)/shard_map/ppermute | solution.py:98
  162.4 5.8 %collective-permute-start.55 = (f32[32,512]{1,0:T(8,128)S(1)}, f32[32,512]{1,0:T(8,128)S(1)}, u32[]{:S(2)}, u32[]{:S(2)}) collective-permute-start(f32[32,512]{1,0:T(8,128)S(1)} %add.62), channel_id=1, source_target_pairs={{0,4},{2,6},{4,0},{6,2},{8,12},{10,14},{12,8},{14,10},{16,20},{18,... | collective-permute-start | bytes 196616 | tf_op jit(solution)/shard_map/ppermute | solution.py:98
  163.3 10.9 %collective-permute-start.63 = (bf16[64,1024]{1,0:T(8,128)(2,1)S(1)}, bf16[64,1024]{1,0:T(8,128)(2,1)S(1)}, u32[]{:S(2)}, u32[]{:S(2)}) collective-permute-start(bf16[64,1024]{1,0:T(8,128)(2,1)S(1)} %get-tuple-element.299), channel_id=1, source_target_pairs={{0,16},{2,18},{4,20},{6,22},{8,24},{10,26},{12,28},{14,30},{16,0},... | collective-permute-start | bytes 393224 | tf_op jit(solution)/shard_map/ppermute | solution.py:98
  168.3 6.6 %collective-permute-start.59 = (f32[32,512]{1,0:T(8,128)S(1)}, f32[32,512]{1,0:T(8,128)S(1)}, u32[]{:S(2)}, u32[]{:S(2)}) collective-permute-start(f32[32,512]{1,0:T(8,128)S(1)} %add.63.refs_0_), channel_id=1, source_target_pairs={{0,8},{2,10},{4,12},{6,14},{8,0},{10,2},{12,4},{14,6},{16,24},{18,... | collective-permute-start | bytes 196616 | tf_op jit(solution)/shard_map/ppermute | solution.py:98
  169.3 10.8 %collective-permute-start.60 = (f32[32,512]{1,0:T(8,128)S(1)}, f32[32,512]{1,0:T(8,128)S(1)}, u32[]{:S(2)}, u32[]{:S(2)}) collective-permute-start(f32[32,512]{1,0:T(8,128)S(1)} %add.63.refs_0_), channel_id=1, source_target_pairs={{0,16},{2,18},{4,20},{6,22},{8,24},{10,26},{12,28},{14,30},{16,0},... | collective-permute-start | bytes 196616 | tf_op jit(solution)/shard_map/ppermute | solution.py:98
  171.7 8.5 %collective-permute-start.61 = (f32[32,512]{1,0:T(8,128)S(1)}, f32[32,512]{1,0:T(8,128)S(1)}, u32[]{:S(2)}, u32[]{:S(2)}) collective-permute-start(f32[32,512]{1,0:T(8,128)S(1)} %add.63.refs_0_), channel_id=1, source_target_pairs={{0,24},{2,26},{4,28},{6,30},{8,16},{10,18},{12,20},{14,22},{16,8},... | collective-permute-start | bytes 196616 | tf_op jit(solution)/shard_map/ppermute | solution.py:98
  172.7 10.6 %collective-permute-start.62 = (bf16[64,1024]{1,0:T(8,128)(2,1)S(1)}, bf16[64,1024]{1,0:T(8,128)(2,1)S(1)}, u32[]{:S(2)}, u32[]{:S(2)}) collective-permute-start(bf16[64,1024]{1,0:T(8,128)(2,1)S(1)} %get-tuple-element.291), channel_id=1, source_target_pairs={{0,16},{2,18},{4,20},{6,22},{8,24},{10,26},{12,28},{14,30},{16,0},... | collective-permute-start | bytes 393224 | tf_op jit(solution)/shard_map/ppermute | solution.py:98
  (15 other events, 129.1 us)
